TPU v7x, 32 devices: a whole 2x2x4 slice. The times are simulated.
32 devices in a mesh: energy: 8 (over z, x), slab: 4 (over y, core).
Axes of the slice: x: 2, y: 2, z: 4, core: 2. Of those that a mesh axis runs over, the one named last changes fastest.
Arguments:
- green_iso: float32 [16, 8, 384, 384], P('energy', 'slab')
- coupling: float32 [8, 384, 384], P('slab')
- lead_green: float32 [16, 384, 384], P('energy')
- energy_weight: float32 [16], P('energy'), may hold values from 0.01875 to 0.1875
- energy_group: int32 [16], P('energy'), may hold values from 0 to 3
- group_charge: float32 [4], replicated, may hold values from 0.02 to 0.2
- orbital_atom: int32 [384], replicated, may hold values from 0 to 47
- atom_cell: int32 [8, 48], P('slab'), may hold values from 0 to 65535
- doping: float32 [64, 64, 128], P('slab', 'energy'), may hold values from -6 to 6
Outputs:
- atom_density: float32 [4, 8, 48], P(None, 'slab')
- potential: float32 [64, 64, 128], P('slab', 'energy')
All inputs are finite; a program needn't handle non-finite values.
Results may differ from a plain program's by a relative error of at most 0.0001.
Values sent between devices are 32-bit elements; how exact they have to be, the bound alone decides.
No kernel may reach another device: no remote copies, remote signals or barrier semaphores. Data moves between devices by JAX's collectives and lax.ppermute only.
A program may use at most 320 MiB of HBM per device.

v0:
```python
import jax
import jax.numpy as jnp
from jax import lax
from jax.sharding import PartitionSpec as P

ITERS = 3


def with_halo(x, sides, width):
    for axis, dim in sides:
        size, length = (lax.axis_size(axis), x.shape[dim])
        up = [(i, (i + 1) % size) for i in range(size - 1)]
        down = [(j, i) for i, j in up]
        last = lax.slice_in_dim(x, length - width, length, axis=dim)
        initial = lax.slice_in_dim(x, 0, width, axis=dim)
        before = lax.ppermute(last, axis, up)
        after = lax.ppermute(initial, axis, down)
        x = jnp.concatenate([before, x, after], axis=dim)
    return x


def shifted(value, axis, steps):
    count = lax.axis_size(axis)
    initial, last = (max(0, -steps), min(count, count - steps))
    return lax.ppermute(value, axis, [(source, source + steps) for source in range(initial, last)])


def matprod(left, right):
    return jnp.matmul(left, right, precision=lax.Precision.HIGHEST)


def affine(propagator, source, state):
    return matprod(matprod(propagator, state), jnp.swapaxes(propagator, -1, -2)) + source


def compose(earlier, later):
    return (matprod(later[0], earlier[0]), affine(later[0], later[1], earlier[1]))


def operate(field):
    padded = with_halo(field, (("energy", 1), ("slab", 0)), 1)
    beside = padded[2:, 1:-1] + padded[:-2, 1:-1] + padded[1:-1, 2:] + padded[1:-1, :-2]
    deeper = jnp.pad(field, ((0, 0), (0, 0), (1, 1)))
    beside = beside + deeper[:, :, 2:] + deeper[:, :, :-2]
    return 6.5 * field - beside


def two_products(residual, image):
    return lax.psum((jnp.sum(residual * residual), jnp.sum(residual * image)), ("energy", "slab"))


def on_device(
    green_iso,
    coupling,
    lead_green,
    energy_weight,
    energy_group,
    group_charge,
    orbital_atom,
    atom_cell,
    doping,
):
    propagators = matprod(green_iso, coupling[None])
    slab_count = green_iso.shape[1]
    local_map = (propagators[:, 0], green_iso[:, 0])
    layer = 1
    local_map = compose(local_map, (propagators[:, layer], green_iso[:, layer]))
    leftmost = lax.axis_index("slab") == 0
    start_state = jnp.where(leftmost, lead_green, jnp.zeros_like(lead_green))

    def relay_turn(turn, incoming):
        outgoing = affine(local_map[0], local_map[1], incoming)
        arrived = shifted(outgoing, "slab", 1)
        return jnp.where(leftmost, lead_green, arrived)

    incoming = lax.fori_loop(0, lax.axis_size("slab") - 1, relay_turn, start_state)
    state = incoming
    diagonals = []
    for layer in range(slab_count):
        state = affine(propagators[:, layer], green_iso[:, layer], state)
        diagonals.append(jnp.diagonal(state, axis1=1, axis2=2))
    diag_stack = jnp.stack(diagonals, 0)
    group_count = group_charge.shape[0]
    weights = energy_weight[:, None] * (
        energy_group[:, None] == jnp.arange(group_count)[None, :]
    ).astype(jnp.float32)
    orbital_density = jnp.einsum(
        "eg,seo->gso", weights, diag_stack, precision=lax.Precision.HIGHEST
    )
    atom_count = atom_cell.shape[1]
    membership = (orbital_atom[:, None] == jnp.arange(atom_count)[None, :]).astype(jnp.float32)
    partial_density = jnp.einsum(
        "gso,oa->gsa", orbital_density, membership, precision=lax.Precision.HIGHEST
    )
    atom_density = lax.psum(partial_density, "energy")
    charge = jnp.einsum("g,gsa->sa", group_charge, atom_density, precision=lax.Precision.HIGHEST)
    depth = doping.shape[2]
    rows_y = doping.shape[1]
    width_x = doping.shape[0] // slab_count
    full_y = rows_y * lax.axis_size("energy")
    y_start = lax.axis_index("energy") * rows_y
    x_part = atom_cell // (full_y * depth)
    y_part = atom_cell // depth % full_y
    z_part = atom_cell % depth
    slab_place = jnp.arange(slab_count, dtype=jnp.int32)[:, None]
    inside = (y_part >= y_start) & (y_part < y_start + rows_y)
    volume = doping.size
    target = ((slab_place * width_x + x_part) * rows_y + (y_part - y_start)) * depth + z_part
    target = jnp.where(inside, target, volume)
    placed = jax.ops.segment_sum(charge.reshape(-1), target.reshape(-1), num_segments=volume + 1)[
        :volume
    ]
    source = doping + placed.reshape(doping.shape)
    potential = jnp.zeros_like(source)
    residual = source
    image = operate(residual)
    norm_now, product = two_products(residual, image)
    alpha = norm_now / product
    direction, along = (residual, image)
    for turn in range(ITERS):
        potential = potential + alpha * direction
        residual = residual - alpha * along
        if turn + 1 < ITERS:
            image = operate(residual)
            norm_next, product = two_products(residual, image)
            ratio = norm_next / norm_now
            alpha = norm_next / (product - ratio * norm_next / alpha)
            direction = residual + ratio * direction
            along = image + ratio * along
            norm_now = norm_next
    return (atom_density, potential)


def solution(mesh):
    in_specs = (
        P("energy", "slab", None, None),
        P("slab", None, None),
        P("energy", None, None),
        P("energy"),
        P("energy"),
        P(),
        P(),
        P("slab", None),
        P("slab", "energy", None),
    )
    out_specs = (P(None, "slab", None), P("slab", "energy", None))
    return jax.shard_map(
        on_device, mesh=mesh, in_specs=in_specs, out_specs=out_specs, check_vma=False
    )
```

profile of v0, /device:TPU:0, one launch (start us, length us, event | category | flops | bytes accessed | tf_op | source)
XLA Modules:
  0.0 401.0 jit_solution(1008519003046152871)
XLA Ops:
  0.7 1.2 copy-done
  1.9 6.4 %convolution_bitcast_fusion = f32[2,2,384,384]{3,2,0,1:T(8,128)S(1)} fusion(f32[2,384,384]{2,1,0:T(8,128)S(1)} %copy-done, f32[2,2,384,384]{3,2,1,0:T(8,128)} %param.11), kind=kOutput, calls=%fused_computation.5 | convolution fusion | flops 2717908992 | bytes 5898240 | tf_op jit(solution)/shard_map/dot_general | solution.py:29
  8.3 2.4 fusion.1
  10.8 2.4 fusion.3
  13.2 0.2 or_reduce_fusion
  13.4 3.6 convolution_add_fusion.3
  17.0 1.3 broadcast_select_fusion.1
  18.4 58.7 %while.10 = (s32[]{:T(128)}, f32[2,384,384]{2,1,0:T(8,128)S(1)}, pred[]{:T(512)}, f32[2,384,384]{2,1,0:T(8,128)S(1)}, f32[2,384,384]{2,1,0:T(8,128)}, /*index=5*/f32[2,384,384]{2,1,0:T(8,128)}, s32[]{:T(128)}) while((s32[]{:T(128)}, f32[2,384,384]{2,1,0:T(8,128)S(1)}, pred[]{:T(512)}, f32[2,384,384]{2,1,0:T(8,128)S(1)}, ...), condition=%wide.region_1.2_spmd, body=%wide.region_0.1_spmd.sunk | while | flops 2718498816 | bytes 21233808 | solution.py:76
  18.4 2.4 fusion.79
  20.8 2.6 convolution_add_fusion.5
  23.4 2.3 collective-permute-start
  25.8 1.6 collective-permute-done
  27.3 1.4 broadcast_select_fusion.3
  28.8 2.4 fusion.79
  31.2 2.6 convolution_add_fusion.5
  33.8 15.9 %collective-permute-start = (f32[2,384,384]{2,1,0:T(8,128)S(1)}, f32[2,384,384]{2,1,0:T(8,128)}, u32[]{:S(2)}, u32[]{:S(2)}) collective-permute-start(f32[2,384,384]{2,1,0:T(8,128)S(1)} %convolution_add_fusion.5), channel_id=1, source_target_pairs={{0,1},{1,2},{2,3},{4,5},{5,6},{6,7},{8,9},{9,10},{10,11},{12,13},{... | collective-permute-start | bytes 3538952 | tf_op jit(solution)/shard_map/while/body/eval_jaxpr/ppermute | solution.py:25
  49.7 1.6 collective-permute-done
  51.3 1.4 broadcast_select_fusion.3
  52.7 2.4 fusion.79
  55.2 2.6 convolution_add_fusion.5
  57.8 16.1 %collective-permute-start = (f32[2,384,384]{2,1,0:T(8,128)S(1)}, f32[2,384,384]{2,1,0:T(8,128)}, u32[]{:S(2)}, u32[]{:S(2)}) collective-permute-start(f32[2,384,384]{2,1,0:T(8,128)S(1)} %convolution_add_fusion.5), channel_id=1, source_target_pairs={{0,1},{1,2},{2,3},{4,5},{5,6},{6,7},{8,9},{9,10},{10,11},{12,13},{... | collective-permute-start | bytes 3538952 | tf_op jit(solution)/shard_map/while/body/eval_jaxpr/ppermute | solution.py:25
  73.8 1.6 collective-permute-done
  75.4 1.4 broadcast_select_fusion.3
  77.0 1.0 copy-done.3
  78.1 4.2 %fusion.2 = f32[2,384,384]{2,1,0:T(8,128)S(1)} fusion(f32[2,384,384]{2,1,0:T(8,128)} %copy-done.3, f32[2,2,384,384]{3,2,0,1:T(8,128)} %copy-done.1), kind=kOutput, calls=%fused_computation.15 | convolution fusion | flops 1358954496 | bytes 3538944 | tf_op jit(solution)/shard_map/dot_general | solution.py:29
  82.3 3.9 convolution_add_fusion.2
  86.2 1.0 copy-done.6
  87.2 3.5 fusion.4
  90.7 35.5 %copy.26 = f32[2,384,384]{0,2,1:T(8,128)} copy(f32[2,384,384]{2,1,0:T(8,128)} %copy-done.6) | data formatting | bytes 2359296 | tf_op jit(solution)/shard_map/add | solution.py:33
  126.1 5.2 %convolution_add_fusion.1 = f32[2,384,384]{2,1,0:T(8,128)} fusion(f32[2,384,384]{2,1,0:T(8,128)} %fusion.4, f32[2,2,384,384]{3,2,0,1:T(8,128)S(1)} %copy-done.2, f32[2,2,384,384]{3,2,1,0:T(8,128)} %param.11), kind=kOutput, calls=%fused_computation.6 | convolution fusion | flops 1359249408 | bytes 4718592 | tf_op jit(solution)/shard_map/dot_general | solution.py:29
  131.3 35.6 %copy.27 = f32[2,384,384]{0,2,1:T(8,128)} copy(f32[2,384,384]{2,1,0:T(8,128)} %convolution_add_fusion.1) | data formatting | bytes 2359296 | tf_op jit(solution)/shard_map/add | solution.py:33
  166.9 8.3 %gather_fusion.1 = f32[384,2]{1,0:T(8,128)S(1)} fusion(f32[2,384,384]{0,2,1:T(8,128)} %copy.27, s32[384]{0:T(512)S(1)} %or_reduce_fusion), kind=kCustom, calls=%fused_computation.1 | custom fusion | bytes 9216 | tf_op jit(solution)/shard_map/jit(diagonal)/gather | solution.py:81
  175.3 8.3 %gather_fusion = f32[384,2]{1,0:T(8,128)S(1)} fusion(f32[2,384,384]{0,2,1:T(8,128)} %copy.26, s32[384]{0:T(512)S(1)} %or_reduce_fusion), kind=kCustom, calls=%fused_computation | custom fusion | bytes 9216 | tf_op jit(solution)/shard_map/jit(diagonal)/gather | solution.py:81
  183.7 0.3 fusion.32
  184.0 0.2 fusion.6
  184.2 21.7 %psum.49 = f32[4,2,48]{2,0,1:T(4,128)S(1)} all-reduce(f32[4,2,48]{2,0,1:T(4,128)S(1)} %fusion.6), channel_id=1, replica_groups=mesh['energy'=8,'slab'=4] {'energy'}, use_global_device_ids=true, to_apply=%region_2.3 | all-reduce | flops 384 | bytes 3072 | tf_op jit(solution)/shard_map/psum | solution.py:95
  205.8 0.1 fusion.41
  206.2 1.2 scatter_custom_fusion
  207.4 1.3 collective-permute-start.1
  208.7 1.3 collective-permute-start.2
  210.1 4.2 %collective-permute-done.2 = f32[16,1,128]{2,1,0:T(1,128)S(1)} collective-permute-done((f32[16,1,128]{2,1,0:T(1,128)S(1)}, f32[16,1,128]{2,1,0:T(1,128)S(1)}, u32[]{:S(2)}, u32[]{:S(2)}) %collective-permute-start.2) | collective-permute-done | bytes 8224 | tf_op jit(solution)/shard_map/ppermute | solution.py:17
  214.3 1.3 collective-permute-start.3
  215.6 10.8 %collective-permute-start.4 = (f32[1,10,128]{2,1,0:T(8,128)S(1)}, f32[1,10,128]{2,1,0:T(8,128)S(1)}, u32[]{:S(2)}, u32[]{:S(2)}) collective-permute-start(f32[1,10,128]{2,1,0:T(8,128)S(1)} %get-tuple-element.72), channel_id=1, source_target_pairs={{0,1},{1,2},{2,3},{4,5},{5,6},{6,7},{8,9},{9,10},{10,11},{12,13},{... | collective-permute-start | bytes 15368 | tf_op jit(solution)/shard_map/ppermute | solution.py:16
  226.4 0.8 collective-permute-done.4
  227.2 0.7 multiply_reduce_fusion.3
  227.9 47.1 %all-reduce.5 = (f32[]{:T(128)}, f32[]{:T(128)}) all-reduce(f32[]{:T(128)} %get-tuple-element.46, f32[]{:T(128)} %get-tuple-element.45), channel_id=1, replica_groups=mesh['energy'=8,'slab'=4] {'energy','slab'}, use_global_device_ids=true, to_apply=%region_5.6 | all-reduce | flops 2 | bytes 16 | tf_op jit(solution)/shard_map/psum | solution.py:49
  276.3 4.2 %collective-permute-start.5 = (f32[16,1,128]{2,1,0:T(1,128)S(1)}, f32[16,1,128]{2,1,0:T(1,128)S(1)}, u32[]{:S(2)}, u32[]{:S(2)}) collective-permute-start(f32[16,1,128]{2,1,0:T(1,128)S(1)} %get-tuple-element.76), channel_id=1, source_target_pairs={{0,4},{4,8},{8,12},{12,16},{16,20},{20,24},{24,28},{1,5},{5,9},{9,... | collective-permute-start | bytes 24584 | tf_op jit(solution)/shard_map/ppermute | solution.py:16
  280.5 1.3 collective-permute-start.6
  281.9 4.2 %collective-permute-done.6 = f32[16,1,128]{2,1,0:T(1,128)S(1)} collective-permute-done((f32[16,1,128]{2,1,0:T(1,128)S(1)}, f32[16,1,128]{2,1,0:T(1,128)S(1)}, u32[]{:S(2)}, u32[]{:S(2)}) %collective-permute-start.6) | collective-permute-done | bytes 8224 | tf_op jit(solution)/shard_map/ppermute | solution.py:17
  286.1 1.3 collective-permute-start.7
  287.4 3.0 collective-permute-start.8
  290.4 0.8 collective-permute-done.8
  291.2 0.7 multiply_reduce_fusion.1
  291.9 43.1 %all-reduce.4 = (f32[]{:T(128)}, f32[]{:T(128)}) all-reduce(f32[]{:T(128)} %get-tuple-element.44, f32[]{:T(128)} %get-tuple-element.43), channel_id=1, replica_groups=mesh['energy'=8,'slab'=4] {'energy','slab'}, use_global_device_ids=true, to_apply=%region_9.10 | all-reduce | flops 2 | bytes 16 | tf_op jit(solution)/shard_map/psum | solution.py:49
  339.6 1.3 collective-permute-start.10
  340.9 4.8 %collective-permute-start.9 = (f32[16,1,128]{2,1,0:T(1,128)S(1)}, f32[16,1,128]{2,1,0:T(1,128)S(1)}, u32[]{:S(2)}, u32[]{:S(2)}) collective-permute-start(f32[16,1,128]{2,1,0:T(1,128)S(1)} %get-tuple-element.74), channel_id=1, source_target_pairs={{0,4},{4,8},{8,12},{12,16},{16,20},{20,24},{24,28},{1,5},{5,9},{9,... | collective-permute-start | bytes 24584 | tf_op jit(solution)/shard_map/ppermute | solution.py:16
  345.8 1.3 collective-permute-done.9
  347.1 1.3 collective-permute-start.11
  348.4 3.0 collective-permute-start.12
  351.4 0.6 copy.30
  352.0 0.2 collective-permute-done.12
  352.3 0.7 fusion.18
  353.0 43.6 %all-reduce.3 = (f32[]{:T(128)}, f32[]{:T(128)}) all-reduce(f32[]{:T(128)} %get-tuple-element.42, f32[]{:T(128)} %get-tuple-element.41), channel_id=1, replica_groups=mesh['energy'=8,'slab'=4] {'energy','slab'}, use_global_device_ids=true, to_apply=%region_13.14 | all-reduce | flops 2 | bytes 16 | tf_op jit(solution)/shard_map/psum | solution.py:49
  400.4 0.7 multiply_add_fusion
  (48 shorter events, 0.7 us)
Async XLA Ops:
  0.6 1.3 copy-start
  0.6 7.7 %copy-start.5 = (f32[2,2,384,384]{3,2,1,0:T(8,128)S(1)}, f32[2,2,384,384]{3,2,1,0:T(8,128)}, u32[]{:S(2)}) copy-start(f32[2,2,384,384]{3,2,1,0:T(8,128)} %param.11) | copy-start | bytes 7077892
  8.3 5.1 %copy-start.1 = (f32[2,2,384,384]{3,2,0,1:T(8,128)}, f32[2,2,384,384]{3,2,0,1:T(8,128)S(1)}, u32[]{:S(2)}) copy-start(f32[2,2,384,384]{3,2,0,1:T(8,128)S(1)} %convolution_bitcast_fusion) | copy-start | bytes 7077892
  18.4 2.5 copy-start.4
  23.4 3.9 collective-permute-start
  28.7 2.5 copy-start.4
  33.8 17.5 %collective-permute-start = (f32[2,384,384]{2,1,0:T(8,128)S(1)}, f32[2,384,384]{2,1,0:T(8,128)}, u32[]{:S(2)}, u32[]{:S(2)}) collective-permute-start(f32[2,384,384]{2,1,0:T(8,128)S(1)} %convolution_add_fusion.5), channel_id=1, source_target_pairs={{0,1},{1,2},{2,3},{4,5},{5,6},{6,7},{8,9},{9,10},{10,11},{12,13},{... | collective-permute-start | bytes 3538952 | tf_op jit(solution)/shard_map/while/body/eval_jaxpr/ppermute | solution.py:25
  52.7 2.5 copy-start.4
  57.8 17.6 %collective-permute-start = (f32[2,384,384]{2,1,0:T(8,128)S(1)}, f32[2,384,384]{2,1,0:T(8,128)}, u32[]{:S(2)}, u32[]{:S(2)}) collective-permute-start(f32[2,384,384]{2,1,0:T(8,128)S(1)} %convolution_add_fusion.5), channel_id=1, source_target_pairs={{0,1},{1,2},{2,3},{4,5},{5,6},{6,7},{8,9},{9,10},{10,11},{12,13},{... | collective-permute-start | bytes 3538952 | tf_op jit(solution)/shard_map/while/body/eval_jaxpr/ppermute | solution.py:25
  77.0 1.0 copy-start.3
  78.1 4.2 %copy-start.2 = (f32[2,2,384,384]{3,2,0,1:T(8,128)S(1)}, f32[2,2,384,384]{3,2,0,1:T(8,128)}, u32[]{:S(2)}) copy-start(f32[2,2,384,384]{3,2,0,1:T(8,128)} %copy-done.1) | copy-start | bytes 7077892
  86.2 1.0 copy-start.6
  131.3 52.4 %copy-start.10 = (f32[2]{0:T(128)S(1)}, f32[2]{0:T(128)}, u32[]{:S(2)}) copy-start(f32[2]{0:T(128)} %param.14) | copy-start | bytes 28
  131.3 52.4 %copy-start.11 = (s32[2]{0:T(128)S(1)}, s32[2]{0:T(128)}, u32[]{:S(2)}) copy-start(s32[2]{0:T(128)} %param.15) | copy-start | bytes 28
  131.3 52.7 %copy-start.9 = (s32[384]{0:T(512)S(1)}, s32[384]{0:T(512)}, u32[]{:S(2)}) copy-start(s32[384]{0:T(512)} %param.17) | copy-start | bytes 4612
  131.3 74.5 %copy-start.12 = (f32[4]{0:T(128)S(1)}, f32[4]{0:T(128)}, u32[]{:S(2)}) copy-start(f32[4]{0:T(128)} %param.16) | copy-start | bytes 52
  131.3 74.7 %copy-start.8 = (s32[2,48]{1,0:T(2,128)S(1)}, s32[2,48]{1,0:T(2,128)}, u32[]{:S(2)}) copy-start(s32[2,48]{1,0:T(2,128)} %param.18) | copy-start | bytes 1156
  131.3 76.1 %copy-start.7 = (f32[16,8,128]{2,1,0:T(8,128)S(1)}, f32[16,8,128]{2,1,0:T(8,128)}, u32[]{:S(2)}) copy-start(f32[16,8,128]{2,1,0:T(8,128)} %param.19) | copy-start | bytes 196612
  207.4 2.6 collective-permute-start.1
  208.7 5.5 %collective-permute-start.2 = (f32[16,1,128]{2,1,0:T(1,128)S(1)}, f32[16,1,128]{2,1,0:T(1,128)S(1)}, u32[]{:S(2)}, u32[]{:S(2)}) collective-permute-start(f32[16,1,128]{2,1,0:T(1,128)S(1)} %get-tuple-element.77), channel_id=1, source_target_pairs={{4,0},{8,4},{12,8},{16,12},{20,16},{24,20},{28,24},{5,1},{9,5},{13... | collective-permute-start | bytes 24584 | tf_op jit(solution)/shard_map/ppermute | solution.py:17
  214.3 12.1 %collective-permute-start.3 = (f32[1,10,128]{2,1,0:T(8,128)S(1)}, f32[1,10,128]{2,1,0:T(8,128)S(1)}, u32[]{:S(2)}, u32[]{:S(2)}) collective-permute-start(f32[1,10,128]{2,1,0:T(8,128)S(1)} %get-tuple-element.71), channel_id=1, source_target_pairs={{1,0},{2,1},{3,2},{5,4},{6,5},{7,6},{9,8},{10,9},{11,10},{13,12},{... | collective-permute-start | bytes 15368 | tf_op jit(solution)/shard_map/ppermute | solution.py:17
  215.6 11.6 %collective-permute-start.4 = (f32[1,10,128]{2,1,0:T(8,128)S(1)}, f32[1,10,128]{2,1,0:T(8,128)S(1)}, u32[]{:S(2)}, u32[]{:S(2)}) collective-permute-start(f32[1,10,128]{2,1,0:T(8,128)S(1)} %get-tuple-element.72), channel_id=1, source_target_pairs={{0,1},{1,2},{2,3},{4,5},{5,6},{6,7},{8,9},{9,10},{10,11},{12,13},{... | collective-permute-start | bytes 15368 | tf_op jit(solution)/shard_map/ppermute | solution.py:16
  276.3 5.5 %collective-permute-start.5 = (f32[16,1,128]{2,1,0:T(1,128)S(1)}, f32[16,1,128]{2,1,0:T(1,128)S(1)}, u32[]{:S(2)}, u32[]{:S(2)}) collective-permute-start(f32[16,1,128]{2,1,0:T(1,128)S(1)} %get-tuple-element.76), channel_id=1, source_target_pairs={{0,4},{4,8},{8,12},{12,16},{16,20},{20,24},{24,28},{1,5},{5,9},{9,... | collective-permute-start | bytes 24584 | tf_op jit(solution)/shard_map/ppermute | solution.py:16
  280.5 5.5 %collective-permute-start.6 = (f32[16,1,128]{2,1,0:T(1,128)S(1)}, f32[16,1,128]{2,1,0:T(1,128)S(1)}, u32[]{:S(2)}, u32[]{:S(2)}) collective-permute-start(f32[16,1,128]{2,1,0:T(1,128)S(1)} %get-tuple-element.75), channel_id=1, source_target_pairs={{4,0},{8,4},{12,8},{16,12},{20,16},{24,20},{28,24},{5,1},{9,5},{13... | collective-permute-start | bytes 24584 | tf_op jit(solution)/shard_map/ppermute | solution.py:17
  286.1 4.3 %collective-permute-start.7 = (f32[1,10,128]{2,1,0:T(8,128)S(1)}, f32[1,10,128]{2,1,0:T(8,128)S(1)}, u32[]{:S(2)}, u32[]{:S(2)}) collective-permute-start(f32[1,10,128]{2,1,0:T(8,128)S(1)} %get-tuple-element.69), channel_id=1, source_target_pairs={{1,0},{2,1},{3,2},{5,4},{6,5},{7,6},{9,8},{10,9},{11,10},{13,12},{... | collective-permute-start | bytes 15368 | tf_op jit(solution)/shard_map/ppermute | solution.py:17
  287.4 3.8 collective-permute-start.8
  339.6 6.1 %collective-permute-start.10 = (f32[16,1,128]{2,1,0:T(1,128)S(1)}, f32[16,1,128]{2,1,0:T(1,128)S(1)}, u32[]{:S(2)}, u32[]{:S(2)}) collective-permute-start(f32[16,1,128]{2,1,0:T(1,128)S(1)} %get-tuple-element.73), channel_id=1, source_target_pairs={{4,0},{8,4},{12,8},{16,12},{20,16},{24,20},{28,24},{5,1},{9,5},{13... | collective-permute-start | bytes 24584 | tf_op jit(solution)/shard_map/ppermute | solution.py:17
  340.9 6.2 %collective-permute-start.9 = (f32[16,1,128]{2,1,0:T(1,128)S(1)}, f32[16,1,128]{2,1,0:T(1,128)S(1)}, u32[]{:S(2)}, u32[]{:S(2)}) collective-permute-start(f32[16,1,128]{2,1,0:T(1,128)S(1)} %get-tuple-element.74), channel_id=1, source_target_pairs={{0,4},{4,8},{8,12},{12,16},{16,20},{20,24},{24,28},{1,5},{5,9},{9,... | collective-permute-start | bytes 24584 | tf_op jit(solution)/shard_map/ppermute | solution.py:16
  347.1 4.9 %collective-permute-start.11 = (f32[1,10,128]{2,1,0:T(8,128)S(1)}, f32[1,10,128]{2,1,0:T(8,128)S(1)}, u32[]{:S(2)}, u32[]{:S(2)}) collective-permute-start(f32[1,10,128]{2,1,0:T(8,128)S(1)} %get-tuple-element.67), channel_id=1, source_target_pairs={{1,0},{2,1},{3,2},{5,4},{6,5},{7,6},{9,8},{10,9},{11,10},{13,12},{... | collective-permute-start | bytes 15368 | tf_op jit(solution)/shard_map/ppermute | solution.py:17
  348.4 3.8 collective-permute-start.12
where the time goes:
time: 403 us; the launch traced here: 401 us
  blocking collectives  155 us (38%)
  local copies, waits for them, and re-layouts  91.9 us (23%)
  starting transfers between devices  69.1 us (17%)
  matrix products  47.3 us (12%)
  waiting for transfers between devices  16.4 us (4%)
  between operations  10.7 us (3%)
  other arithmetic  9.83 us (2%)
    psum x3, blocking collectives, two_products(): lax.psum((jnp.sum(residual * residual), jnp.sum(residual * image)), ('ene...  134 us
    add x2, local copies, waits for them, and re-layouts, affine(): matprod(matprod(propagator, state), jnp.swapaxes(propagator, -1, -2))  71 us
    dot_general x14, matrix products, matprod(): return jnp.matmul(left, right, precision=lax.Precision.HIGHEST)  46.7 us
    ppermute x3, starting transfers between devices, shifted(): lax.ppermute(value, axis, [(source, source + steps) for source in range(i...  34.3 us
    ppermute x6, starting transfers between devices, with_halo(): before = lax.ppermute(last, axis, up)  27.1 us
    psum x1, blocking collectives, on_device(): atom_density = lax.psum(partial_density, 'energy')  21.7 us
    gather x2, local copies, waits for them, and re-layouts, on_device(): diagonals.append(jnp.diagonal(state, axis1=1, axis2=2))  16.6 us
    ppermute x6, waiting for transfers between devices, with_halo(): after = lax.ppermute(initial, axis, down)  8.4 us
  transfers between devices with their start and end apart: 15, of which 9 were waited for; matrix products, arithmetic and copies ran while one was open for 0% of the time, Pallas kernels for 0%

commit v1 on v0

v1 whole, which is shorter than its diff:
```python
import functools

import jax
import jax.numpy as jnp
from jax import lax
from jax.experimental import pallas as pl
from jax.experimental.pallas import tpu as pltpu
from jax.sharding import PartitionSpec as P

ITERS = 3
F32 = jnp.float32
BF16 = jnp.bfloat16
TILE = 128
BOTH = ("energy", "slab")


def split(a):
    high = a.astype(BF16)
    return high, (a - high.astype(F32)).astype(BF16)


def dot(a, b, transposed):
    dims = (((1,), (1 if transposed else 0,)), ((), ()))
    return lax.dot_general(a, b, dims, preferred_element_type=F32)


def product(left, right, transposed=False):
    n = right[0].shape[0 if transposed else 1]
    wide = dot(left[0], jnp.concatenate(right, 0 if transposed else 1), transposed)
    return wide[:, :n] + (wide[:, n:] + dot(left[1], right[0], transposed))


def diagonal_row(matrix):
    n = matrix.shape[0]
    rows = lax.broadcasted_iota(jnp.int32, (n, n), 0)
    columns = lax.broadcasted_iota(jnp.int32, (n, n), 1)
    return jnp.sum(jnp.where(rows == columns, matrix, 0.0), axis=0, keepdims=True)


def block_pairs(count):
    return [(i, j) for i in range(count) for j in range(i, count)]


def pack(matrix, out_ref):
    count = matrix.shape[0] // TILE
    for place, (i, j) in enumerate(block_pairs(count)):
        rows, columns = (slice(i * TILE, (i + 1) * TILE), slice(j * TILE, (j + 1) * TILE))
        out_ref[place] = 0.5 * (matrix[rows, columns] + matrix[columns, rows].T)


def unpack(in_ref, out_ref):
    count = out_ref.shape[0] // TILE
    for place, (i, j) in enumerate(block_pairs(count)):
        rows, columns = (slice(i * TILE, (i + 1) * TILE), slice(j * TILE, (j + 1) * TILE))
        out_ref[rows, columns] = in_ref[place]
        if i != j:
            out_ref[columns, rows] = in_ref[place].T


def copy_all(pairs, sems):
    copies = [pltpu.make_async_copy(src, dst, sems.at[i]) for i, (src, dst) in enumerate(pairs)]
    for copy in copies:
        copy.start()
    return copies


def first_kernel(energy, place_ref, iso, coupling, lead, *refs):
    if energy == 1:
        refs = refs[2:]
    own, sent, packed, diags, c_buf, g_buf, lead_buf, map_buf, sems, out_sem = refs
    place = place_ref[0]
    copies = copy_all(
        [
            (iso.at[energy, 0], g_buf.at[0]),
            (coupling.at[0], c_buf.at[0]),
            (iso.at[energy, 1], g_buf.at[1]),
            (coupling.at[1], c_buf.at[1]),
            (lead.at[energy], lead_buf),
        ],
        sems,
    )
    copies[0].wait()
    copies[1].wait()
    early = product(split(g_buf[0]), split(c_buf[0]))
    early_parts = split(early)
    copies[2].wait()
    copies[3].wait()
    late_parts = split(product(split(g_buf[1]), split(c_buf[1])))
    copies[4].wait()

    @pl.when(place == 0)
    def _():
        state = product(early_parts, split(lead_buf[...]))
        state = product(split(state), early_parts, True) + g_buf[0]
        diags[0:1, :] = diagonal_row(state)
        state = product(late_parts, split(state))
        state = product(split(state), late_parts, True) + g_buf[1]
        diags[1:2, :] = diagonal_row(state)
        pack(state, packed)

    @pl.when(place != 0)
    def _():
        map_buf[0] = early
        map_buf[1] = product(late_parts, early_parts)
        term = product(late_parts, split(g_buf[0]))
        term = product(split(term), late_parts, True) + g_buf[1]
        map_buf[2] = term
        diags[0:1, :] = diagonal_row(g_buf[0])
        diags[1:2, :] = diagonal_row(term)
        core = lax.rem(place, 2)

        @pl.when(core == energy)
        def _():
            copy = pltpu.make_async_copy(map_buf, own, out_sem)
            copy.start()
            copy.wait()

        @pl.when(core != energy)
        def _():
            copy = pltpu.make_async_copy(map_buf, sent, out_sem)
            copy.start()
            copy.wait()


def first_call(energy, place, iso, coupling, lead, maps):
    n = lead.shape[-1]
    blocks = len(block_pairs(n // TILE))
    vmem, hbm = (pl.BlockSpec(memory_space=pltpu.VMEM), pl.BlockSpec(memory_space=pl.ANY))
    smem = pl.BlockSpec(memory_space=pltpu.SMEM)
    map_shape = jax.ShapeDtypeStruct((3, n, n), F32)
    return pl.pallas_call(
        functools.partial(first_kernel, energy),
        out_shape=(
            map_shape,
            map_shape,
            jax.ShapeDtypeStruct((blocks, TILE, TILE), F32),
            jax.ShapeDtypeStruct((8, n), F32),
        ),
        in_specs=[smem, hbm, hbm, hbm] + [hbm] * len(maps),
        out_specs=(hbm, hbm, vmem, vmem),
        input_output_aliases={4: 0, 5: 1} if maps else {},
        scratch_shapes=[
            pltpu.VMEM((2, n, n), F32),
            pltpu.VMEM((2, n, n), F32),
            pltpu.VMEM((n, n), F32),
            pltpu.VMEM((3, n, n), F32),
            pltpu.SemaphoreType.DMA((5,)),
            pltpu.SemaphoreType.DMA,
        ],
        compiler_params=pltpu.CompilerParams(vmem_limit_bytes=24 * 2**20),
        cost_estimate=pl.CostEstimate(flops=36 * n**3, bytes_accessed=24 * n * n, transcendentals=0),
        name=f"slabs_{energy}",
    )(place, iso, coupling, lead, *maps)


def relay_kernel(place_ref, packed, maps, out, diags, state, map_buf, sems):
    @pl.when(place_ref[0] == 1)
    def _():
        copies = copy_all([(maps.at[1], map_buf.at[0]), (maps.at[2], map_buf.at[1])], sems)
        unpack(packed, state)
        copies[0].wait()
        composed = split(map_buf[0])
        term = product(composed, split(state[...]))
        copies[1].wait()
        term = product(split(term), composed, True) + map_buf[1]
        diags[0:1, :] = diagonal_row(term)
        pack(term, out)


def relay_call(place, packed, maps):
    n = maps.shape[-1]
    vmem, hbm = (pl.BlockSpec(memory_space=pltpu.VMEM), pl.BlockSpec(memory_space=pl.ANY))
    smem = pl.BlockSpec(memory_space=pltpu.SMEM)
    return pl.pallas_call(
        relay_kernel,
        out_shape=(
            jax.ShapeDtypeStruct(packed.shape, F32),
            jax.ShapeDtypeStruct((8, n), F32),
        ),
        in_specs=[smem, vmem, hbm],
        out_specs=(vmem, vmem),
        scratch_shapes=[
            pltpu.VMEM((n, n), F32),
            pltpu.VMEM((2, n, n), F32),
            pltpu.SemaphoreType.DMA((2,)),
        ],
        compiler_params=pltpu.CompilerParams(vmem_limit_bytes=16 * 2**20),
        cost_estimate=pl.CostEstimate(flops=12 * n**3, bytes_accessed=12 * n * n, transcendentals=0),
        name="relay",
    )(place, packed, maps)


def pass_kernel(turn, place_ref, packed, own, got, out, state, near_buf, far_buf, sems):
    place = place_ref[0]

    @pl.when((place == 2 * turn) | (place == 2 * turn + 1))
    def _():
        load_maps(lax.rem(place, 2), own, got, near_buf, far_buf, sems)
        unpack(packed, state)
        for buf in (near_buf, far_buf):
            composed = split(buf[1])
            term = product(composed, split(state[...]))
            state[...] = product(split(term), composed, True) + buf[2]
        pack(state[...], out)


def load_maps(core, own, got, near_buf, far_buf, sems):
    @pl.when(core == 0)
    def _():
        for copy in copy_all([(own, near_buf), (got, far_buf)], sems):
            copy.wait()

    @pl.when(core == 1)
    def _():
        for copy in copy_all([(got, near_buf), (own, far_buf)], sems):
            copy.wait()


def pass_call(turn, place, packed, own, got):
    n = own.shape[-1]
    vmem, hbm = (pl.BlockSpec(memory_space=pltpu.VMEM), pl.BlockSpec(memory_space=pl.ANY))
    smem = pl.BlockSpec(memory_space=pltpu.SMEM)
    return pl.pallas_call(
        functools.partial(pass_kernel, turn),
        out_shape=jax.ShapeDtypeStruct(packed.shape, F32),
        in_specs=[smem, vmem, hbm, hbm],
        out_specs=vmem,
        scratch_shapes=[
            pltpu.VMEM((n, n), F32),
            pltpu.VMEM((3, n, n), F32),
            pltpu.VMEM((3, n, n), F32),
            pltpu.SemaphoreType.DMA((2,)),
        ],
        compiler_params=pltpu.CompilerParams(vmem_limit_bytes=24 * 2**20),
        name="pass_on",
    )(place, packed, own, got)


def row_products(left, right):
    return jnp.sum(left * right, axis=1, keepdims=True)


def density_kernel(
    slab_total,
    place_ref,
    weight_ref,
    group_ref,
    orbital_atom,
    first_x,
    second_x,
    first_y,
    second_y,
    own,
    got,
    own_diags,
    got_diags,
    first_diags,
    second_diags,
    first_relayed,
    second_relayed,
    out,
    state,
    near_buf,
    far_buf,
    rows,
    sems,
):
    place = place_ref[0]
    core = lax.rem(place, 2)
    n = state.shape[0]
    rows[...] = jnp.zeros_like(rows)

    def quadratic(matrix, parts):
        return jnp.sum((matrix * product(split(matrix), parts)).T, axis=0, keepdims=True)

    @pl.when(place == 0)
    def _():
        rows[0:2, :] = first_diags[0:2, :]
        rows[2:4, :] = second_diags[0:2, :]

    @pl.when(place == 1)
    def _():
        for copy in copy_all([(got, near_buf), (own, far_buf)], sems):
            copy.wait()
        unpack(first_x, state)
        rows[0:1, :] = first_diags[0:1, :] + quadratic(near_buf[0], split(state[...]))
        rows[1:2, :] = first_relayed[0:1, :]
        unpack(second_x, state)
        rows[2:3, :] = second_diags[0:1, :] + quadratic(far_buf[0], split(state[...]))
        rows[3:4, :] = second_relayed[0:1, :]

    @pl.when(place >= 2)
    def _():
        load_maps(core, own, got, near_buf, far_buf, sems)

        @pl.when(core == 0)
        def _():
            unpack(first_y, state)
            rows[0:2, :] = own_diags[0:2, :]
            rows[2:4, :] = got_diags[0:2, :]

        @pl.when(core == 1)
        def _():
            unpack(second_y, state)
            rows[0:2, :] = got_diags[0:2, :]
            rows[2:4, :] = own_diags[0:2, :]

        parts = split(state[...])
        composed = split(near_buf[1])
        term = product(composed, parts)
        later = product(split(term), composed, True) + near_buf[2]
        rows[0:1, :] += quadratic(near_buf[0], parts)
        rows[1:2, :] += jnp.sum((near_buf[1] * term).T, axis=0, keepdims=True)
        parts = split(later)
        rows[2:3, :] += quadratic(far_buf[0], parts)
        rows[3:4, :] += quadratic(far_buf[1], parts)

    atoms = lax.broadcasted_iota(jnp.int32, (TILE, n), 0)
    member = (atoms == orbital_atom[...]).astype(BF16)
    rest = rows[...]
    folded = jnp.zeros((8, TILE), F32)
    for _ in range(3):
        piece = rest.astype(BF16)
        folded = folded + dot(piece, member, True)
        rest = rest - piece.astype(F32)
    slabs = lax.broadcasted_iota(jnp.int32, (slab_total, TILE), 0)
    for group in range(out.shape[0] // slab_total):
        block = jnp.zeros((slab_total, TILE), F32)
        for row in range(4):
            energy = jnp.where(place < 2, row // 2, core)
            slab = jnp.where(place < 2, 2 * place + row % 2, 2 * (place - core) + row)
            weight = jnp.where(group_ref[energy] == group, weight_ref[energy], 0.0)
            block = block + jnp.where(slabs == slab, weight, 0.0) * folded[row : row + 1, :]
        out[group * slab_total : (group + 1) * slab_total, :] = block


def density_call(place, weight, group, orbital_atom, groups, slab_total, vectors, maps):
    n = orbital_atom.shape[0]
    vmem, hbm = (pl.BlockSpec(memory_space=pltpu.VMEM), pl.BlockSpec(memory_space=pl.ANY))
    smem = pl.BlockSpec(memory_space=pltpu.SMEM)
    return pl.pallas_call(
        functools.partial(density_kernel, slab_total),
        out_shape=jax.ShapeDtypeStruct((groups * slab_total, TILE), F32),
        in_specs=[smem, smem, smem, vmem] + [vmem] * 4 + [hbm] * 2 + [vmem] * 6,
        out_specs=vmem,
        scratch_shapes=[
            pltpu.VMEM((n, n), F32),
            pltpu.VMEM((3, n, n), F32),
            pltpu.VMEM((3, n, n), F32),
            pltpu.VMEM((8, n), F32),
            pltpu.SemaphoreType.DMA((2,)),
        ],
        compiler_params=pltpu.CompilerParams(vmem_limit_bytes=24 * 2**20),
        cost_estimate=pl.CostEstimate(flops=30 * n**3, bytes_accessed=24 * n * n, transcendentals=0),
        name="density",
    )(place, weight, group, orbital_atom.reshape(1, n), *vectors[:4], *maps, *vectors[4:])


def over_slab(value, moves):
    count = lax.axis_size("slab")
    named = dict(moves)
    moves = [(i, named.get(i, i)) for i in range(count)]
    return lax.ppermute(value, "slab", moves)


def pairs_of(count):
    return [(i, i ^ 1) for i in range(count)]


def total_over(value, axis, strides):
    size = 1
    for name in axis if isinstance(axis, tuple) else (axis,):
        size *= lax.axis_size(name)
    got = [lax.ppermute(value, axis, [(i, i ^ k) for i in range(size)]) for k in strides]
    for other in got:
        value = value + other
    return value


def total_over_all(value):
    wires, slabs = (lax.axis_size("energy"), lax.axis_size("slab"))
    value = total_over(value, "slab", (1,))
    stride = 2
    while stride * 2 < slabs:
        value = total_over(value, "slab", (stride,))
        stride *= 2
    value = total_over(value, BOTH, (stride, slabs, stride + slabs))
    stride = 2
    while stride * 4 <= wires:
        value = total_over(value, "energy", (stride, 2 * stride, 3 * stride))
        stride *= 4
    if stride < wires:
        value = total_over(value, "energy", (stride,))
    return value


def with_halo(x, sides, width):
    for axis, dim in sides:
        size, length = (lax.axis_size(axis), x.shape[dim])
        up = [(i, (i + 1) % size) for i in range(size - 1)]
        down = [(j, i) for i, j in up]
        last = lax.slice_in_dim(x, length - width, length, axis=dim)
        initial = lax.slice_in_dim(x, 0, width, axis=dim)
        before = lax.ppermute(last, axis, up)
        after = lax.ppermute(initial, axis, down)
        x = jnp.concatenate([before, x, after], axis=dim)
    return x


def operate(field):
    padded = with_halo(field, (("energy", 1), ("slab", 0)), 1)
    beside = padded[2:, 1:-1] + padded[:-2, 1:-1] + padded[1:-1, 2:] + padded[1:-1, :-2]
    deeper = jnp.pad(field, ((0, 0), (0, 0), (1, 1)))
    beside = beside + deeper[:, :, 2:] + deeper[:, :, :-2]
    return 6.5 * field - beside


def two_products(residual, image):
    pair = jnp.stack([jnp.sum(residual * residual), jnp.sum(residual * image)])
    total = total_over_all(jnp.broadcast_to(pair[:, None], (2, TILE)))
    return total[0, 0], total[1, 0]


def sweep(green_iso, coupling, lead_green, energy_weight, energy_group, groups, orbital_atom):
    devices = lax.axis_size("slab")
    slab_total = devices * green_iso.shape[1]
    place = lax.axis_index("slab").astype(jnp.int32).reshape(1)
    own, sent, packed, first_diags = first_call(0, place, green_iso, coupling, lead_green, ())
    first_x = over_slab(packed, pairs_of(devices))
    own, sent, packed, second_diags = first_call(
        1, place, green_iso, coupling, lead_green, (own, sent)
    )
    second_x = over_slab(packed, pairs_of(devices))
    first_out, first_relayed = relay_call(place, first_x, sent)
    first_y = over_slab(first_out, [(1, 2), (2, 1)])
    got = over_slab(sent, pairs_of(devices)[2:])
    second_out, second_relayed = relay_call(place, second_x, own)
    second_y = over_slab(second_out, [(1, 3), (3, 1)])
    core = lax.rem(place[0], 2)
    own_diags = jnp.where(core == 0, first_diags, second_diags)
    got_diags = lax.ppermute(
        jnp.where(core == 0, second_diags, first_diags), "slab", pairs_of(devices)
    )
    first_in, second_in = (first_y, second_y)
    for turn in range(1, devices // 2 - 1):
        chosen = jnp.where(core == 0, first_in, second_in)
        passed = pass_call(turn, place, chosen, own, got)
        ahead = [(2 * turn + c, 2 * turn + 2 + c) for c in (0, 1)]
        arrived = over_slab(passed, ahead + [(j, i) for i, j in ahead])
        here = place[0] // 2 == turn + 1
        first_in = jnp.where(here, arrived, first_in)
        second_in = jnp.where(here, arrived, second_in)
    vectors = (
        first_x,
        second_x,
        first_in,
        second_in,
        own_diags,
        got_diags,
        first_diags,
        second_diags,
        first_relayed,
        second_relayed,
    )
    return density_call(
        place, energy_weight, energy_group, orbital_atom, groups, slab_total, vectors, (own, got)
    )


def on_device(
    green_iso,
    coupling,
    lead_green,
    energy_weight,
    energy_group,
    group_charge,
    orbital_atom,
    atom_cell,
    doping,
):
    slab_count, atom_count = atom_cell.shape
    groups = group_charge.shape[0]
    partial = sweep(
        green_iso, coupling, lead_green, energy_weight, energy_group, groups, orbital_atom
    )
    density = total_over_all(partial).reshape(groups, -1, TILE)
    atom_density = lax.dynamic_slice(
        density,
        (0, lax.axis_index("slab") * slab_count, 0),
        (groups, slab_count, atom_count),
    )
    charge = jnp.sum(group_charge[:, None, None] * atom_density, axis=0)
    depth = doping.shape[2]
    rows_y = doping.shape[1]
    width_x = doping.shape[0] // slab_count
    full_y = rows_y * lax.axis_size("energy")
    y_start = lax.axis_index("energy") * rows_y
    x_part = atom_cell // (full_y * depth)
    y_part = atom_cell // depth % full_y
    z_part = atom_cell % depth
    slab_place = jnp.arange(slab_count, dtype=jnp.int32)[:, None]
    inside = (y_part >= y_start) & (y_part < y_start + rows_y)
    volume = doping.size
    target = ((slab_place * width_x + x_part) * rows_y + (y_part - y_start)) * depth + z_part
    target = jnp.where(inside, target, volume)
    placed = jax.ops.segment_sum(charge.reshape(-1), target.reshape(-1), num_segments=volume + 1)[
        :volume
    ]
    source = doping + placed.reshape(doping.shape)
    potential = jnp.zeros_like(source)
    residual = source
    image = operate(residual)
    norm_now, product_now = two_products(residual, image)
    alpha = norm_now / product_now
    direction, along = (residual, image)
    for turn in range(ITERS):
        potential = potential + alpha * direction
        residual = residual - alpha * along
        if turn + 1 < ITERS:
            image = operate(residual)
            norm_next, product_now = two_products(residual, image)
            ratio = norm_next / norm_now
            alpha = norm_next / (product_now - ratio * norm_next / alpha)
            direction = residual + ratio * direction
            along = image + ratio * along
            norm_now = norm_next
    return (atom_density, potential)


def solution(mesh):
    in_specs = (
        P("energy", "slab", None, None),
        P("slab", None, None),
        P("energy", None, None),
        P("energy"),
        P("energy"),
        P(),
        P(),
        P("slab", None),
        P("slab", "energy", None),
    )
    out_specs = (P(None, "slab", None), P("slab", "energy", None))
    return jax.shard_map(
        on_device, mesh=mesh, in_specs=in_specs, out_specs=out_specs, check_vma=False
    )
```

time: 403 us -> 180 us (0.45)
  blocking collectives: 155 us -> 0 us
  local copies, waits for them, and re-layouts: 91.9 us -> 12.9 us
  matrix products: 47.3 us -> 0 us
  waiting for transfers between devices: 16.4 us -> 51.8 us
  starting transfers between devices: 69.1 us -> 80.9 us
  Pallas kernels: 0 us -> 11.7 us
    psum x4 -> x0, blocking collectives: 155 us -> none  [the longest x3 134 us: two_products(): lax.psum((jnp.sum(residual * residual), jnp.sum(residual * image)), ('ene...]
    add x2 -> x0, local copies, waits for them, and re-layouts: 71 us -> none  [affine(): matprod(matprod(propagator, state), jnp.swapaxes(propagator, -1, -2))]
    dot_general x17 -> x0, matrix products: 47.3 us -> none  [the longest x14 46.7 us: matprod(): return jnp.matmul(left, right, precision=lax.Precision.HIGHEST)]
    ppermute x3 -> x34, waiting for transfers between devices: 4.71 us -> 36.6 us  [the longest x28 35.3 us: total_over(): lax.ppermute(value, axis, [(i, i ^ k) for i in range(size)])]
    ppermute x3 -> x34, starting transfers between devices: 34.3 us -> 56.7 us  [the longest x28 43.1 us: total_over(): lax.ppermute(value, axis, [(i, i ^ k) for i in range(size)])]
    gather x2 -> x0, local copies, waits for them, and re-layouts: 16.6 us -> none  [on_device(): diagonals.append(jnp.diagonal(state, axis1=1, axis2=2))]
    pallas_call x0 -> x5, Pallas kernels: none -> 11.7 us  [the longest x2 8.66 us: first_call(): pl.pallas_call(functools.partial(first_kernel, energy), out_shape=(map_sh...]
    ppermute x6, starting transfers between devices: 27.1 us -> 16.4 us  [with_halo(): before = lax.ppermute(last, axis, up)]
  transfers between devices with their start and end apart: 15 -> 46, of which waited for: 9 -> 30; matrix products, arithmetic and copies ran while one was open for 0% -> 1% of each run, Pallas kernels for 0% -> 1%
where the time goes in v1:
time: 180 us; the launch traced here: 178 us
  starting transfers between devices  80.9 us (45%)
  waiting for transfers between devices  51.8 us (29%)
  local copies, waits for them, and re-layouts  12.9 us (7%)
  Pallas kernels  11.7 us (6%)
  between operations  10.9 us (6%)
  other arithmetic  9.91 us (6%)
    ppermute x28, starting transfers between devices, total_over(): lax.ppermute(value, axis, [(i, i ^ k) for i in range(size)])  43.1 us
    ppermute x28, waiting for transfers between devices, total_over(): lax.ppermute(value, axis, [(i, i ^ k) for i in range(size)])  35.3 us
    ppermute x6, starting transfers between devices, with_halo(): before = lax.ppermute(last, axis, up)  16.4 us
    ppermute x6, waiting for transfers between devices, with_halo(): after = lax.ppermute(initial, axis, down)  12.6 us
    ppermute x5, starting transfers between devices, over_slab(): return lax.ppermute(value, 'slab', moves)  11.5 us
    unnamed x36, local copies, waits for them, and re-layouts  10.2 us
    pallas_call x2, Pallas kernels, first_call(): pl.pallas_call(functools.partial(first_kernel, energy), out_shape=(map_sh...  8.66 us
    ppermute x6, starting transfers between devices, with_halo(): after = lax.ppermute(initial, axis, down)  7.73 us
  transfers between devices with their start and end apart: 46, of which 30 were waited for; matrix products, arithmetic and copies ran while one was open for 1% of the time, Pallas kernels for 1%

profile of v1, /device:TPU:0, one launch (start us, length us, event | category | flops | bytes accessed | tf_op | source)
XLA Modules:
  0.0 178.1 jit_solution(8011451676326574701)
XLA Ops:
  0.6 1.7 copy-done
  2.3 1.3 copy-done.1
  3.6 1.3 copy-done.2
  4.8 4.3 %slabs_0.1 = (f32[3,384,384]{2,1,0:T(8,128)S(1)}, f32[3,384,384]{2,1,0:T(8,128)S(1)}, f32[6,128,128]{2,1,0:T(8,128)S(1)}, f32[8,384]{1,0:T(8,128)S(1)}) custom-call(s32[1]{0:T(128)} %bitcast.place_ref, f32[2,2,384,384]{3,2,1,0:T(8,128)S(1)} %copy-done, f32[2,384,384]{2,1,0:T(8,128)S(1)} %copy-done.1, f32[2,384,384]{2,1,0:T(8,128)S(1)} %copy-done.2), custom_call_target="tpu_custom_call" | custom-call | flops 2038431744 | bytes 3538944 | tf_op jit(solution)/shard_map/slabs_0/pallas_call | solution.py:131
  9.2 4.3 %slabs_1.1 = (f32[3,384,384]{2,1,0:T(8,128)S(1)}, f32[3,384,384]{2,1,0:T(8,128)S(1)}, f32[6,128,128]{2,1,0:T(8,128)S(1)}, f32[8,384]{1,0:T(8,128)S(1)}) custom-call(s32[1]{0:T(128)} %bitcast.place_ref, f32[2,2,384,384]{3,2,1,0:T(8,128)S(1)} %copy-done, f32[2,384,384]{2,1,0:T(8,128)S(1)} %copy-done.1, ...), custom_call_target="tpu_custom_call", output_to_operand_aliasing={{0}: (4, {}), {1}: (5, {})} | custom-call | flops 2038431744 | bytes 3538944 | tf_op jit(solution)/shard_map/slabs_1/pallas_call | solution.py:131
  13.5 1.9 %collective-permute-start.4 = (f32[3,384,384]{2,1,0:T(8,128)S(1)}, f32[3,384,384]{2,1,0:T(8,128)}, u32[]{:S(2)}, u32[]{:S(2)}) collective-permute-start(f32[3,384,384]{2,1,0:T(8,128)S(1)} %get-tuple-element.18.maps), channel_id=1, source_target_pairs={{0,0},{1,1},{2,3},{3,2},{4,4},{5,5},{6,7},{7,6},{8,8},{9,9},{10,11... | collective-permute-start | bytes 5308424 | tf_op jit(solution)/shard_map/ppermute | solution.py:363
  16.0 1.2 collective-permute-done.1.packed.second_x
  18.6 4.6 %collective-permute-start.3 = (f32[6,128,128]{2,1,0:T(8,128)}, f32[6,128,128]{2,1,0:T(8,128)}, u32[]{:S(2)}, u32[]{:S(2)}) collective-permute-start(f32[6,128,128]{2,1,0:T(8,128)} %get-tuple-element.21), channel_id=1, source_target_pairs={{0,0},{1,3},{2,2},{3,1},{4,4},{5,7},{6,6},{7,5},{8,8},{9,11},{10,1... | collective-permute-start | bytes 1179656 | tf_op jit(solution)/shard_map/ppermute | solution.py:363
  23.2 0.8 relay.2
  24.7 4.5 %collective-permute-start.2 = (f32[6,128,128]{2,1,0:T(8,128)}, f32[6,128,128]{2,1,0:T(8,128)}, u32[]{:S(2)}, u32[]{:S(2)}) collective-permute-start(f32[6,128,128]{2,1,0:T(8,128)} %get-tuple-element.19), channel_id=1, source_target_pairs={{0,0},{1,2},{2,1},{3,3},{4,4},{5,6},{6,5},{7,7},{8,8},{9,10},{10,9... | collective-permute-start | bytes 1179656 | tf_op jit(solution)/shard_map/ppermute | solution.py:363
  29.9 2.1 %collective-permute-start.5 = (f32[8,384]{1,0:T(8,128)S(1)}, f32[8,384]{1,0:T(8,128)S(1)}, u32[]{:S(2)}, u32[]{:S(2)}) collective-permute-start(f32[8,384]{1,0:T(8,128)S(1)} %get-tuple-element.48), channel_id=1, source_target_pairs={{0,1},{1,0},{2,3},{3,2},{4,5},{5,4},{6,7},{7,6},{8,9},{9,8},{10,11... | collective-permute-start | bytes 36872 | tf_op jit(solution)/shard_map/ppermute | solution.py:441
  33.6 1.0 copy-done.6
  34.6 1.0 copy-done.8
  37.6 1.4 density.1
  39.1 8.2 %collective-permute-start.6 = (f32[32,128]{1,0:T(8,128)S(1)}, f32[32,128]{1,0:T(8,128)S(1)}, u32[]{:S(2)}, u32[]{:S(2)}) collective-permute-start(f32[32,128]{1,0:T(8,128)S(1)} %density.1), channel_id=1, source_target_pairs={{0,1},{1,0},{2,3},{3,2},{4,5},{5,4},{6,7},{7,6},{8,9},{9,8},{10,11... | collective-permute-start | bytes 49160 | tf_op jit(solution)/shard_map/ppermute | solution.py:374
  47.2 0.8 collective-permute-done.6
  48.1 2.7 %collective-permute-start.7 = (f32[32,128]{1,0:T(8,128)S(1)}, f32[32,128]{1,0:T(8,128)S(1)}, u32[]{:S(2)}, u32[]{:S(2)}) collective-permute-start(f32[32,128]{1,0:T(8,128)S(1)} %add.187), channel_id=1, source_target_pairs={{0,2},{1,3},{2,0},{3,1},{4,6},{5,7},{6,4},{7,5},{8,10},{9,11},{10,... | collective-permute-start | bytes 49160 | tf_op jit(solution)/shard_map/ppermute | solution.py:374
  50.8 1.5 collective-permute-start.8
  52.5 2.1 %collective-permute-done.8 = f32[32,128]{1,0:T(8,128)S(1)} collective-permute-done((f32[32,128]{1,0:T(8,128)S(1)}, f32[32,128]{1,0:T(8,128)S(1)}, u32[]{:S(2)}, u32[]{:S(2)}) %collective-permute-start.8) | collective-permute-done | bytes 16416 | tf_op jit(solution)/shard_map/ppermute | solution.py:374
  54.6 2.3 %collective-permute-done.9 = f32[32,128]{1,0:T(8,128)S(1)} collective-permute-done((f32[32,128]{1,0:T(8,128)S(1)}, f32[32,128]{1,0:T(8,128)S(1)}, u32[]{:S(2)}, u32[]{:S(2)}) %collective-permute-start.9) | collective-permute-done | bytes 16416 | tf_op jit(solution)/shard_map/ppermute | solution.py:374
  57.0 1.6 collective-permute-start.10
  58.5 2.6 %collective-permute-start.11 = (f32[32,128]{1,0:T(8,128)S(1)}, f32[32,128]{1,0:T(8,128)S(1)}, u32[]{:S(2)}, u32[]{:S(2)}) collective-permute-start(f32[32,128]{1,0:T(8,128)S(1)} %add_add_fusion), channel_id=1, source_target_pairs={{0,16},{4,20},{8,24},{12,28},{16,0},{20,4},{24,8},{28,12},{1,17},{... | collective-permute-start | bytes 49160 | tf_op jit(solution)/shard_map/ppermute | solution.py:374
  61.5 1.7 collective-permute-done.11
  63.2 3.4 %collective-permute-done.12 = f32[32,128]{1,0:T(8,128)S(1)} collective-permute-done((f32[32,128]{1,0:T(8,128)S(1)}, f32[32,128]{1,0:T(8,128)S(1)}, u32[]{:S(2)}, u32[]{:S(2)}) %collective-permute-start.12) | collective-permute-done | bytes 16416 | tf_op jit(solution)/shard_map/ppermute | solution.py:374
  67.4 1.1 scatter_custom_fusion
  68.6 2.5 %collective-permute-start.13 = (f32[16,1,128]{2,1,0:T(1,128)S(1)}, f32[16,1,128]{2,1,0:T(1,128)S(1)}, u32[]{:S(2)}, u32[]{:S(2)}) collective-permute-start(f32[16,1,128]{2,1,0:T(1,128)S(1)} %get-tuple-element.47), channel_id=1, source_target_pairs={{0,4},{4,8},{8,12},{12,16},{16,20},{20,24},{24,28},{1,5},{5,9},{9,... | collective-permute-start | bytes 24584 | tf_op jit(solution)/shard_map/ppermute | solution.py:404
  71.0 1.3 collective-permute-start.14
  72.4 4.2 %collective-permute-done.14 = f32[16,1,128]{2,1,0:T(1,128)S(1)} collective-permute-done((f32[16,1,128]{2,1,0:T(1,128)S(1)}, f32[16,1,128]{2,1,0:T(1,128)S(1)}, u32[]{:S(2)}, u32[]{:S(2)}) %collective-permute-start.14) | collective-permute-done | bytes 8224 | tf_op jit(solution)/shard_map/ppermute | solution.py:405
  76.6 1.3 collective-permute-start.15
  77.9 3.0 %collective-permute-start.16 = (f32[1,10,128]{2,1,0:T(8,128)S(1)}, f32[1,10,128]{2,1,0:T(8,128)S(1)}, u32[]{:S(2)}, u32[]{:S(2)}) collective-permute-start(f32[1,10,128]{2,1,0:T(8,128)S(1)} %get-tuple-element.41), channel_id=1, source_target_pairs={{0,1},{1,2},{2,3},{4,5},{5,6},{6,7},{8,9},{9,10},{10,11},{12,13},{... | collective-permute-start | bytes 15368 | tf_op jit(solution)/shard_map/ppermute | solution.py:404
  82.5 1.4 pad_maximum_fusion.33
  85.1 2.1 %collective-permute-start.18 = (f32[2,128]{1,0:T(2,128)S(1)}, f32[2,128]{1,0:T(2,128)S(1)}, u32[]{:S(2)}, u32[]{:S(2)}) collective-permute-start(f32[2,128]{1,0:T(2,128)S(1)} %broadcast_add_fusion.2), channel_id=1, source_target_pairs={{0,2},{1,3},{2,0},{3,1},{4,6},{5,7},{6,4},{7,5},{8,10},{9,11},{10,... | collective-permute-start | bytes 3080 | tf_op jit(solution)/shard_map/ppermute | solution.py:374
  87.2 0.9 collective-permute-start.19
  88.8 2.0 %collective-permute-done.19 = f32[2,128]{1,0:T(2,128)S(1)} collective-permute-done((f32[2,128]{1,0:T(2,128)S(1)}, f32[2,128]{1,0:T(2,128)S(1)}, u32[]{:S(2)}, u32[]{:S(2)}) %collective-permute-start.19) | collective-permute-done | bytes 1056 | tf_op jit(solution)/shard_map/ppermute | solution.py:374
  90.8 1.8 %collective-permute-done.20 = f32[2,128]{1,0:T(2,128)S(1)} collective-permute-done((f32[2,128]{1,0:T(2,128)S(1)}, f32[2,128]{1,0:T(2,128)S(1)}, u32[]{:S(2)}, u32[]{:S(2)}) %collective-permute-start.20) | collective-permute-done | bytes 1056 | tf_op jit(solution)/shard_map/ppermute | solution.py:374
  93.3 1.1 collective-permute-start.22
  94.4 2.7 %collective-permute-start.23 = (f32[2,128]{1,0:T(2,128)S(1)}, f32[2,128]{1,0:T(2,128)S(1)}, u32[]{:S(2)}, u32[]{:S(2)}) collective-permute-start(f32[2,128]{1,0:T(2,128)S(1)} %add_add_fusion.6), channel_id=1, source_target_pairs={{0,24},{4,28},{8,16},{12,20},{16,8},{20,12},{24,0},{28,4},{1,25},{... | collective-permute-start | bytes 3080 | tf_op jit(solution)/shard_map/ppermute | solution.py:374
  97.8 2.0 %collective-permute-done.23 = f32[2,128]{1,0:T(2,128)S(1)} collective-permute-done((f32[2,128]{1,0:T(2,128)S(1)}, f32[2,128]{1,0:T(2,128)S(1)}, u32[]{:S(2)}, u32[]{:S(2)}) %collective-permute-start.23) | collective-permute-done | bytes 1056 | tf_op jit(solution)/shard_map/ppermute | solution.py:374
  101.7 2.2 %collective-permute-start.24 = (f32[16,1,128]{2,1,0:T(1,128)S(1)}, f32[16,1,128]{2,1,0:T(1,128)S(1)}, u32[]{:S(2)}, u32[]{:S(2)}) collective-permute-start(f32[16,1,128]{2,1,0:T(1,128)S(1)} %get-tuple-element.45), channel_id=1, source_target_pairs={{0,4},{4,8},{8,12},{12,16},{16,20},{20,24},{24,28},{1,5},{5,9},{9,... | collective-permute-start | bytes 24584 | tf_op jit(solution)/shard_map/ppermute | solution.py:404
  103.9 1.3 collective-permute-start.25
  105.2 4.2 %collective-permute-done.25 = f32[16,1,128]{2,1,0:T(1,128)S(1)} collective-permute-done((f32[16,1,128]{2,1,0:T(1,128)S(1)}, f32[16,1,128]{2,1,0:T(1,128)S(1)}, u32[]{:S(2)}, u32[]{:S(2)}) %collective-permute-start.25) | collective-permute-done | bytes 8224 | tf_op jit(solution)/shard_map/ppermute | solution.py:405
  109.4 1.3 collective-permute-start.26
  110.7 3.0 %collective-permute-start.27 = (f32[1,10,128]{2,1,0:T(8,128)S(1)}, f32[1,10,128]{2,1,0:T(8,128)S(1)}, u32[]{:S(2)}, u32[]{:S(2)}) collective-permute-start(f32[1,10,128]{2,1,0:T(8,128)S(1)} %get-tuple-element.39), channel_id=1, source_target_pairs={{0,1},{1,2},{2,3},{4,5},{5,6},{6,7},{8,9},{9,10},{10,11},{12,13},{... | collective-permute-start | bytes 15368 | tf_op jit(solution)/shard_map/ppermute | solution.py:404
  115.3 1.3 pad_maximum_fusion.34
  117.9 2.1 %collective-permute-start.29 = (f32[2,128]{1,0:T(2,128)S(1)}, f32[2,128]{1,0:T(2,128)S(1)}, u32[]{:S(2)}, u32[]{:S(2)}) collective-permute-start(f32[2,128]{1,0:T(2,128)S(1)} %broadcast_add_fusion.1), channel_id=1, source_target_pairs={{0,2},{1,3},{2,0},{3,1},{4,6},{5,7},{6,4},{7,5},{8,10},{9,11},{10,... | collective-permute-start | bytes 3080 | tf_op jit(solution)/shard_map/ppermute | solution.py:374
  120.0 2.3 %collective-permute-start.30 = (f32[2,128]{1,0:T(2,128)S(1)}, f32[2,128]{1,0:T(2,128)S(1)}, u32[]{:S(2)}, u32[]{:S(2)}) collective-permute-start(f32[2,128]{1,0:T(2,128)S(1)} %broadcast_add_fusion.1), channel_id=1, source_target_pairs={{0,4},{1,5},{2,6},{3,7},{4,0},{5,1},{6,2},{7,3},{8,12},{9,13},{10,... | collective-permute-start | bytes 3080 | tf_op jit(solution)/shard_map/ppermute | solution.py:374
  122.3 1.5 collective-permute-done.30
  123.9 2.9 %collective-permute-done.31 = f32[2,128]{1,0:T(2,128)S(1)} collective-permute-done((f32[2,128]{1,0:T(2,128)S(1)}, f32[2,128]{1,0:T(2,128)S(1)}, u32[]{:S(2)}, u32[]{:S(2)}) %collective-permute-start.31) | collective-permute-done | bytes 1056 | tf_op jit(solution)/shard_map/ppermute | solution.py:374
  127.2 2.7 %collective-permute-start.33 = (f32[2,128]{1,0:T(2,128)S(1)}, f32[2,128]{1,0:T(2,128)S(1)}, u32[]{:S(2)}, u32[]{:S(2)}) collective-permute-start(f32[2,128]{1,0:T(2,128)S(1)} %add_add_fusion.4), channel_id=1, source_target_pairs={{0,16},{4,20},{8,24},{12,28},{16,0},{20,4},{24,8},{28,12},{1,17},{... | collective-permute-start | bytes 3080 | tf_op jit(solution)/shard_map/ppermute | solution.py:374
  129.9 1.5 collective-permute-start.34
  131.7 3.6 %collective-permute-done.34 = f32[2,128]{1,0:T(2,128)S(1)} collective-permute-done((f32[2,128]{1,0:T(2,128)S(1)}, f32[2,128]{1,0:T(2,128)S(1)}, u32[]{:S(2)}, u32[]{:S(2)}) %collective-permute-start.34) | collective-permute-done | bytes 1056 | tf_op jit(solution)/shard_map/ppermute | solution.py:374
  140.5 2.7 %collective-permute-start.35 = (f32[16,1,128]{2,1,0:T(1,128)S(1)}, f32[16,1,128]{2,1,0:T(1,128)S(1)}, u32[]{:S(2)}, u32[]{:S(2)}) collective-permute-start(f32[16,1,128]{2,1,0:T(1,128)S(1)} %get-tuple-element.43), channel_id=1, source_target_pairs={{0,4},{4,8},{8,12},{12,16},{16,20},{20,24},{24,28},{1,5},{5,9},{9,... | collective-permute-start | bytes 24584 | tf_op jit(solution)/shard_map/ppermute | solution.py:404
  143.2 1.3 collective-permute-start.36
  144.5 4.2 %collective-permute-done.36 = f32[16,1,128]{2,1,0:T(1,128)S(1)} collective-permute-done((f32[16,1,128]{2,1,0:T(1,128)S(1)}, f32[16,1,128]{2,1,0:T(1,128)S(1)}, u32[]{:S(2)}, u32[]{:S(2)}) %collective-permute-start.36) | collective-permute-done | bytes 8224 | tf_op jit(solution)/shard_map/ppermute | solution.py:405
  148.7 1.3 collective-permute-start.37
  150.0 3.0 %collective-permute-start.38 = (f32[1,10,128]{2,1,0:T(8,128)S(1)}, f32[1,10,128]{2,1,0:T(8,128)S(1)}, u32[]{:S(2)}, u32[]{:S(2)}) collective-permute-start(f32[1,10,128]{2,1,0:T(8,128)S(1)} %get-tuple-element.37), channel_id=1, source_target_pairs={{0,1},{1,2},{2,3},{4,5},{5,6},{6,7},{8,9},{9,10},{10,11},{12,13},{... | collective-permute-start | bytes 15368 | tf_op jit(solution)/shard_map/ppermute | solution.py:404
  154.6 1.4 pad_maximum_fusion.35
  157.3 2.1 %collective-permute-start.40 = (f32[2,128]{1,0:T(2,128)S(1)}, f32[2,128]{1,0:T(2,128)S(1)}, u32[]{:S(2)}, u32[]{:S(2)}) collective-permute-start(f32[2,128]{1,0:T(2,128)S(1)} %broadcast_add_fusion), channel_id=1, source_target_pairs={{0,2},{1,3},{2,0},{3,1},{4,6},{5,7},{6,4},{7,5},{8,10},{9,11},{10,... | collective-permute-start | bytes 3080 | tf_op jit(solution)/shard_map/ppermute | solution.py:374
  159.4 1.8 %collective-permute-start.41 = (f32[2,128]{1,0:T(2,128)S(1)}, f32[2,128]{1,0:T(2,128)S(1)}, u32[]{:S(2)}, u32[]{:S(2)}) collective-permute-start(f32[2,128]{1,0:T(2,128)S(1)} %broadcast_add_fusion), channel_id=1, source_target_pairs={{0,4},{1,5},{2,6},{3,7},{4,0},{5,1},{6,2},{7,3},{8,12},{9,13},{10,... | collective-permute-start | bytes 3080 | tf_op jit(solution)/shard_map/ppermute | solution.py:374
  161.2 1.7 collective-permute-done.41
  162.9 2.7 %collective-permute-done.42 = f32[2,128]{1,0:T(2,128)S(1)} collective-permute-done((f32[2,128]{1,0:T(2,128)S(1)}, f32[2,128]{1,0:T(2,128)S(1)}, u32[]{:S(2)}, u32[]{:S(2)}) %collective-permute-start.42) | collective-permute-done | bytes 1056 | tf_op jit(solution)/shard_map/ppermute | solution.py:374
  165.7 1.8 %collective-permute-start.44 = (f32[2,128]{1,0:T(2,128)S(1)}, f32[2,128]{1,0:T(2,128)S(1)}, u32[]{:S(2)}, u32[]{:S(2)}) collective-permute-start(f32[2,128]{1,0:T(2,128)S(1)} %add_add_fusion.2), channel_id=1, source_target_pairs={{0,16},{4,20},{8,24},{12,28},{16,0},{20,4},{24,8},{28,12},{1,17},{... | collective-permute-start | bytes 3080 | tf_op jit(solution)/shard_map/ppermute | solution.py:374
  167.5 2.6 %collective-permute-start.45 = (f32[2,128]{1,0:T(2,128)S(1)}, f32[2,128]{1,0:T(2,128)S(1)}, u32[]{:S(2)}, u32[]{:S(2)}) collective-permute-start(f32[2,128]{1,0:T(2,128)S(1)} %add_add_fusion.2), channel_id=1, source_target_pairs={{0,24},{4,28},{8,16},{12,20},{16,8},{20,12},{24,0},{28,4},{1,25},{... | collective-permute-start | bytes 3080 | tf_op jit(solution)/shard_map/ppermute | solution.py:374
  170.2 2.7 %collective-permute-done.45 = f32[2,128]{1,0:T(2,128)S(1)} collective-permute-done((f32[2,128]{1,0:T(2,128)S(1)}, f32[2,128]{1,0:T(2,128)S(1)}, u32[]{:S(2)}, u32[]{:S(2)}) %collective-permute-start.45) | collective-permute-done | bytes 1056 | tf_op jit(solution)/shard_map/ppermute | solution.py:374
  (111 shorter events, 22.2 us)
Async XLA Ops:
  0.6 1.7 copy-start
  2.3 1.3 copy-start.1
  3.6 1.3 copy-start.2
  13.5 10.5 %copy-start.3 = (f32[8,384]{1,0:T(8,128)}, f32[8,384]{1,0:T(8,128)S(1)}, u32[]{:S(2)}) copy-start(f32[8,384]{1,0:T(8,128)S(1)} %get-tuple-element.23.second_diags) | copy-start | bytes 36868
  13.5 19.3 %collective-permute-start.4 = (f32[3,384,384]{2,1,0:T(8,128)S(1)}, f32[3,384,384]{2,1,0:T(8,128)}, u32[]{:S(2)}, u32[]{:S(2)}) collective-permute-start(f32[3,384,384]{2,1,0:T(8,128)S(1)} %get-tuple-element.18.maps), channel_id=1, source_target_pairs={{0,0},{1,1},{2,3},{3,2},{4,4},{5,5},{6,7},{7,6},{8,8},{9,9},{10,11... | collective-permute-start | bytes 5308424 | tf_op jit(solution)/shard_map/ppermute | solution.py:363
  15.5 1.7 collective-permute-start.1
  15.5 7.8 %collective-permute-start = (f32[6,128,128]{2,1,0:T(8,128)S(1)}, f32[6,128,128]{2,1,0:T(8,128)S(1)}, u32[]{:S(2)}, u32[]{:S(2)}) collective-permute-start(f32[6,128,128]{2,1,0:T(8,128)S(1)} %get-tuple-element.14), channel_id=1, source_target_pairs={{0,1},{1,0},{2,3},{3,2},{4,5},{5,4},{6,7},{7,6},{8,9},{9,8},{10,11... | collective-permute-start | bytes 1179656 | tf_op jit(solution)/shard_map/ppermute | solution.py:363
  17.2 6.9 %copy-start.5 = (f32[6,128,128]{2,1,0:T(8,128)}, f32[6,128,128]{2,1,0:T(8,128)S(1)}, u32[]{:S(2)}) copy-start(f32[6,128,128]{2,1,0:T(8,128)S(1)} %collective-permute-done.1.packed.second_x) | copy-start | bytes 1179652
  18.0 0.6 copy-start.11
  18.6 14.2 %copy-start.9 = (f32[2]{0:T(128)S(1)}, f32[2]{0:T(128)}, u32[]{:S(2)}) copy-start(f32[2]{0:T(128)} %weight_ref.1) | copy-start | bytes 28
  18.6 14.2 %collective-permute-start.3 = (f32[6,128,128]{2,1,0:T(8,128)}, f32[6,128,128]{2,1,0:T(8,128)}, u32[]{:S(2)}, u32[]{:S(2)}) collective-permute-start(f32[6,128,128]{2,1,0:T(8,128)} %get-tuple-element.21), channel_id=1, source_target_pairs={{0,0},{1,3},{2,2},{3,1},{4,4},{5,7},{6,6},{7,5},{8,8},{9,11},{10,1... | collective-permute-start | bytes 1179656 | tf_op jit(solution)/shard_map/ppermute | solution.py:363
  23.2 1.5 copy-start.7
  24.1 0.6 copy-start.13
  24.7 8.2 %collective-permute-start.2 = (f32[6,128,128]{2,1,0:T(8,128)}, f32[6,128,128]{2,1,0:T(8,128)}, u32[]{:S(2)}, u32[]{:S(2)}) collective-permute-start(f32[6,128,128]{2,1,0:T(8,128)} %get-tuple-element.19), channel_id=1, source_target_pairs={{0,0},{1,2},{2,1},{3,3},{4,4},{5,6},{6,5},{7,7},{8,8},{9,10},{10,9... | collective-permute-start | bytes 1179656 | tf_op jit(solution)/shard_map/ppermute | solution.py:363
  29.9 3.0 %collective-permute-start.5 = (f32[8,384]{1,0:T(8,128)S(1)}, f32[8,384]{1,0:T(8,128)S(1)}, u32[]{:S(2)}, u32[]{:S(2)}) collective-permute-start(f32[8,384]{1,0:T(8,128)S(1)} %get-tuple-element.48), channel_id=1, source_target_pairs={{0,1},{1,0},{2,3},{3,2},{4,5},{5,4},{6,7},{7,6},{8,9},{9,8},{10,11... | collective-permute-start | bytes 36872 | tf_op jit(solution)/shard_map/ppermute | solution.py:441
  32.8 0.7 copy-start.4
  33.6 1.0 copy-start.6
  34.6 1.0 copy-start.8
  35.6 0.7 copy-start.10
  36.2 0.7 copy-start.12
  36.9 0.7 copy-start.14
  37.6 23.7 %copy-start.16 = (s32[2,48]{1,0:T(2,128)S(1)}, s32[2,48]{1,0:T(2,128)}, u32[]{:S(2)}) copy-start(s32[2,48]{1,0:T(2,128)} %param.16) | copy-start | bytes 1156
  37.6 29.0 %copy-start.17 = (f32[4]{0:T(128)S(1)}, f32[4]{0:T(128)}, u32[]{:S(2)}) copy-start(f32[4]{0:T(128)} %param.14) | copy-start | bytes 52
  37.6 30.9 %copy-start.15 = (f32[16,8,128]{2,1,0:T(8,128)S(1)}, f32[16,8,128]{2,1,0:T(8,128)}, u32[]{:S(2)}) copy-start(f32[16,8,128]{2,1,0:T(8,128)} %param.17) | copy-start | bytes 196612
  39.1 9.0 %collective-permute-start.6 = (f32[32,128]{1,0:T(8,128)S(1)}, f32[32,128]{1,0:T(8,128)S(1)}, u32[]{:S(2)}, u32[]{:S(2)}) collective-permute-start(f32[32,128]{1,0:T(8,128)S(1)} %density.1), channel_id=1, source_target_pairs={{0,1},{1,0},{2,3},{3,2},{4,5},{5,4},{6,7},{7,6},{8,9},{9,8},{10,11... | collective-permute-start | bytes 49160 | tf_op jit(solution)/shard_map/ppermute | solution.py:374
  48.1 4.4 %collective-permute-start.7 = (f32[32,128]{1,0:T(8,128)S(1)}, f32[32,128]{1,0:T(8,128)S(1)}, u32[]{:S(2)}, u32[]{:S(2)}) collective-permute-start(f32[32,128]{1,0:T(8,128)S(1)} %add.187), channel_id=1, source_target_pairs={{0,2},{1,3},{2,0},{3,1},{4,6},{5,7},{6,4},{7,5},{8,10},{9,11},{10,... | collective-permute-start | bytes 49160 | tf_op jit(solution)/shard_map/ppermute | solution.py:374
  50.8 3.8 %collective-permute-start.8 = (f32[32,128]{1,0:T(8,128)S(1)}, f32[32,128]{1,0:T(8,128)S(1)}, u32[]{:S(2)}, u32[]{:S(2)}) collective-permute-start(f32[32,128]{1,0:T(8,128)S(1)} %add.187), channel_id=1, source_target_pairs={{0,4},{1,5},{2,6},{3,7},{4,0},{5,1},{6,2},{7,3},{8,12},{9,13},{10,... | collective-permute-start | bytes 49160 | tf_op jit(solution)/shard_map/ppermute | solution.py:374
  52.3 4.6 %collective-permute-start.9 = (f32[32,128]{1,0:T(8,128)S(1)}, f32[32,128]{1,0:T(8,128)S(1)}, u32[]{:S(2)}, u32[]{:S(2)}) collective-permute-start(f32[32,128]{1,0:T(8,128)S(1)} %add.187), channel_id=1, source_target_pairs={{0,6},{1,7},{2,4},{3,5},{4,2},{5,3},{6,0},{7,1},{8,14},{9,15},{10,... | collective-permute-start | bytes 49160 | tf_op jit(solution)/shard_map/ppermute | solution.py:374
  57.0 4.6 %collective-permute-start.10 = (f32[32,128]{1,0:T(8,128)S(1)}, f32[32,128]{1,0:T(8,128)S(1)}, u32[]{:S(2)}, u32[]{:S(2)}) collective-permute-start(f32[32,128]{1,0:T(8,128)S(1)} %add_add_fusion), channel_id=1, source_target_pairs={{0,8},{4,12},{8,0},{12,4},{16,24},{20,28},{24,16},{28,20},{1,9},{5... | collective-permute-start | bytes 49160 | tf_op jit(solution)/shard_map/ppermute | solution.py:374
  58.5 4.7 %collective-permute-start.11 = (f32[32,128]{1,0:T(8,128)S(1)}, f32[32,128]{1,0:T(8,128)S(1)}, u32[]{:S(2)}, u32[]{:S(2)}) collective-permute-start(f32[32,128]{1,0:T(8,128)S(1)} %add_add_fusion), channel_id=1, source_target_pairs={{0,16},{4,20},{8,24},{12,28},{16,0},{20,4},{24,8},{28,12},{1,17},{... | collective-permute-start | bytes 49160 | tf_op jit(solution)/shard_map/ppermute | solution.py:374
  61.1 5.5 %collective-permute-start.12 = (f32[32,128]{1,0:T(8,128)S(1)}, f32[32,128]{1,0:T(8,128)S(1)}, u32[]{:S(2)}, u32[]{:S(2)}) collective-permute-start(f32[32,128]{1,0:T(8,128)S(1)} %add_add_fusion), channel_id=1, source_target_pairs={{0,24},{4,28},{8,16},{12,20},{16,8},{20,12},{24,0},{28,4},{1,25},{... | collective-permute-start | bytes 49160 | tf_op jit(solution)/shard_map/ppermute | solution.py:374
  68.6 3.8 %collective-permute-start.13 = (f32[16,1,128]{2,1,0:T(1,128)S(1)}, f32[16,1,128]{2,1,0:T(1,128)S(1)}, u32[]{:S(2)}, u32[]{:S(2)}) collective-permute-start(f32[16,1,128]{2,1,0:T(1,128)S(1)} %get-tuple-element.47), channel_id=1, source_target_pairs={{0,4},{4,8},{8,12},{12,16},{16,20},{20,24},{24,28},{1,5},{5,9},{9,... | collective-permute-start | bytes 24584 | tf_op jit(solution)/shard_map/ppermute | solution.py:404
  71.0 5.5 %collective-permute-start.14 = (f32[16,1,128]{2,1,0:T(1,128)S(1)}, f32[16,1,128]{2,1,0:T(1,128)S(1)}, u32[]{:S(2)}, u32[]{:S(2)}) collective-permute-start(f32[16,1,128]{2,1,0:T(1,128)S(1)} %get-tuple-element.46), channel_id=1, source_target_pairs={{4,0},{8,4},{12,8},{16,12},{20,16},{24,20},{28,24},{5,1},{9,5},{13... | collective-permute-start | bytes 24584 | tf_op jit(solution)/shard_map/ppermute | solution.py:405
  76.6 4.3 %collective-permute-start.15 = (f32[1,10,128]{2,1,0:T(8,128)S(1)}, f32[1,10,128]{2,1,0:T(8,128)S(1)}, u32[]{:S(2)}, u32[]{:S(2)}) collective-permute-start(f32[1,10,128]{2,1,0:T(8,128)S(1)} %get-tuple-element.40), channel_id=1, source_target_pairs={{1,0},{2,1},{3,2},{5,4},{6,5},{7,6},{9,8},{10,9},{11,10},{13,12},{... | collective-permute-start | bytes 15368 | tf_op jit(solution)/shard_map/ppermute | solution.py:405
  77.9 3.8 %collective-permute-start.16 = (f32[1,10,128]{2,1,0:T(8,128)S(1)}, f32[1,10,128]{2,1,0:T(8,128)S(1)}, u32[]{:S(2)}, u32[]{:S(2)}) collective-permute-start(f32[1,10,128]{2,1,0:T(8,128)S(1)} %get-tuple-element.41), channel_id=1, source_target_pairs={{0,1},{1,2},{2,3},{4,5},{5,6},{6,7},{8,9},{9,10},{10,11},{12,13},{... | collective-permute-start | bytes 15368 | tf_op jit(solution)/shard_map/ppermute | solution.py:404
  83.9 1.2 collective-permute-start.17
  85.1 3.7 %collective-permute-start.18 = (f32[2,128]{1,0:T(2,128)S(1)}, f32[2,128]{1,0:T(2,128)S(1)}, u32[]{:S(2)}, u32[]{:S(2)}) collective-permute-start(f32[2,128]{1,0:T(2,128)S(1)} %broadcast_add_fusion.2), channel_id=1, source_target_pairs={{0,2},{1,3},{2,0},{3,1},{4,6},{5,7},{6,4},{7,5},{8,10},{9,11},{10,... | collective-permute-start | bytes 3080 | tf_op jit(solution)/shard_map/ppermute | solution.py:374
  87.2 3.6 %collective-permute-start.19 = (f32[2,128]{1,0:T(2,128)S(1)}, f32[2,128]{1,0:T(2,128)S(1)}, u32[]{:S(2)}, u32[]{:S(2)}) collective-permute-start(f32[2,128]{1,0:T(2,128)S(1)} %broadcast_add_fusion.2), channel_id=1, source_target_pairs={{0,4},{1,5},{2,6},{3,7},{4,0},{5,1},{6,2},{7,3},{8,12},{9,13},{10,... | collective-permute-start | bytes 3080 | tf_op jit(solution)/shard_map/ppermute | solution.py:374
  88.2 4.5 %collective-permute-start.20 = (f32[2,128]{1,0:T(2,128)S(1)}, f32[2,128]{1,0:T(2,128)S(1)}, u32[]{:S(2)}, u32[]{:S(2)}) collective-permute-start(f32[2,128]{1,0:T(2,128)S(1)} %broadcast_add_fusion.2), channel_id=1, source_target_pairs={{0,6},{1,7},{2,4},{3,5},{4,2},{5,3},{6,0},{7,1},{8,14},{9,15},{10,... | collective-permute-start | bytes 3080 | tf_op jit(solution)/shard_map/ppermute | solution.py:374
  92.7 4.4 %collective-permute-start.21 = (f32[2,128]{1,0:T(2,128)S(1)}, f32[2,128]{1,0:T(2,128)S(1)}, u32[]{:S(2)}, u32[]{:S(2)}) collective-permute-start(f32[2,128]{1,0:T(2,128)S(1)} %add_add_fusion.6), channel_id=1, source_target_pairs={{0,8},{4,12},{8,0},{12,4},{16,24},{20,28},{24,16},{28,20},{1,9},{5... | collective-permute-start | bytes 3080 | tf_op jit(solution)/shard_map/ppermute | solution.py:374
  93.3 4.5 %collective-permute-start.22 = (f32[2,128]{1,0:T(2,128)S(1)}, f32[2,128]{1,0:T(2,128)S(1)}, u32[]{:S(2)}, u32[]{:S(2)}) collective-permute-start(f32[2,128]{1,0:T(2,128)S(1)} %add_add_fusion.6), channel_id=1, source_target_pairs={{0,16},{4,20},{8,24},{12,28},{16,0},{20,4},{24,8},{28,12},{1,17},{... | collective-permute-start | bytes 3080 | tf_op jit(solution)/shard_map/ppermute | solution.py:374
  94.4 5.4 %collective-permute-start.23 = (f32[2,128]{1,0:T(2,128)S(1)}, f32[2,128]{1,0:T(2,128)S(1)}, u32[]{:S(2)}, u32[]{:S(2)}) collective-permute-start(f32[2,128]{1,0:T(2,128)S(1)} %add_add_fusion.6), channel_id=1, source_target_pairs={{0,24},{4,28},{8,16},{12,20},{16,8},{20,12},{24,0},{28,4},{1,25},{... | collective-permute-start | bytes 3080 | tf_op jit(solution)/shard_map/ppermute | solution.py:374
  101.7 3.6 %collective-permute-start.24 = (f32[16,1,128]{2,1,0:T(1,128)S(1)}, f32[16,1,128]{2,1,0:T(1,128)S(1)}, u32[]{:S(2)}, u32[]{:S(2)}) collective-permute-start(f32[16,1,128]{2,1,0:T(1,128)S(1)} %get-tuple-element.45), channel_id=1, source_target_pairs={{0,4},{4,8},{8,12},{12,16},{16,20},{20,24},{24,28},{1,5},{5,9},{9,... | collective-permute-start | bytes 24584 | tf_op jit(solution)/shard_map/ppermute | solution.py:404
  103.9 5.5 %collective-permute-start.25 = (f32[16,1,128]{2,1,0:T(1,128)S(1)}, f32[16,1,128]{2,1,0:T(1,128)S(1)}, u32[]{:S(2)}, u32[]{:S(2)}) collective-permute-start(f32[16,1,128]{2,1,0:T(1,128)S(1)} %get-tuple-element.44), channel_id=1, source_target_pairs={{4,0},{8,4},{12,8},{16,12},{20,16},{24,20},{28,24},{5,1},{9,5},{13... | collective-permute-start | bytes 24584 | tf_op jit(solution)/shard_map/ppermute | solution.py:405
  109.4 4.3 %collective-permute-start.26 = (f32[1,10,128]{2,1,0:T(8,128)S(1)}, f32[1,10,128]{2,1,0:T(8,128)S(1)}, u32[]{:S(2)}, u32[]{:S(2)}) collective-permute-start(f32[1,10,128]{2,1,0:T(8,128)S(1)} %get-tuple-element.38), channel_id=1, source_target_pairs={{1,0},{2,1},{3,2},{5,4},{6,5},{7,6},{9,8},{10,9},{11,10},{13,12},{... | collective-permute-start | bytes 15368 | tf_op jit(solution)/shard_map/ppermute | solution.py:405
  110.7 3.8 %collective-permute-start.27 = (f32[1,10,128]{2,1,0:T(8,128)S(1)}, f32[1,10,128]{2,1,0:T(8,128)S(1)}, u32[]{:S(2)}, u32[]{:S(2)}) collective-permute-start(f32[1,10,128]{2,1,0:T(8,128)S(1)} %get-tuple-element.39), channel_id=1, source_target_pairs={{0,1},{1,2},{2,3},{4,5},{5,6},{6,7},{8,9},{9,10},{10,11},{12,13},{... | collective-permute-start | bytes 15368 | tf_op jit(solution)/shard_map/ppermute | solution.py:404
  116.7 1.2 collective-permute-start.28
  117.9 4.4 %collective-permute-start.29 = (f32[2,128]{1,0:T(2,128)S(1)}, f32[2,128]{1,0:T(2,128)S(1)}, u32[]{:S(2)}, u32[]{:S(2)}) collective-permute-start(f32[2,128]{1,0:T(2,128)S(1)} %broadcast_add_fusion.1), channel_id=1, source_target_pairs={{0,2},{1,3},{2,0},{3,1},{4,6},{5,7},{6,4},{7,5},{8,10},{9,11},{10,... | collective-permute-start | bytes 3080 | tf_op jit(solution)/shard_map/ppermute | solution.py:374
  120.0 3.8 %collective-permute-start.30 = (f32[2,128]{1,0:T(2,128)S(1)}, f32[2,128]{1,0:T(2,128)S(1)}, u32[]{:S(2)}, u32[]{:S(2)}) collective-permute-start(f32[2,128]{1,0:T(2,128)S(1)} %broadcast_add_fusion.1), channel_id=1, source_target_pairs={{0,4},{1,5},{2,6},{3,7},{4,0},{5,1},{6,2},{7,3},{8,12},{9,13},{10,... | collective-permute-start | bytes 3080 | tf_op jit(solution)/shard_map/ppermute | solution.py:374
  122.3 4.5 %collective-permute-start.31 = (f32[2,128]{1,0:T(2,128)S(1)}, f32[2,128]{1,0:T(2,128)S(1)}, u32[]{:S(2)}, u32[]{:S(2)}) collective-permute-start(f32[2,128]{1,0:T(2,128)S(1)} %broadcast_add_fusion.1), channel_id=1, source_target_pairs={{0,6},{1,7},{2,4},{3,5},{4,2},{5,3},{6,0},{7,1},{8,14},{9,15},{10,... | collective-permute-start | bytes 3080 | tf_op jit(solution)/shard_map/ppermute | solution.py:374
  126.9 4.5 %collective-permute-start.32 = (f32[2,128]{1,0:T(2,128)S(1)}, f32[2,128]{1,0:T(2,128)S(1)}, u32[]{:S(2)}, u32[]{:S(2)}) collective-permute-start(f32[2,128]{1,0:T(2,128)S(1)} %add_add_fusion.4), channel_id=1, source_target_pairs={{0,8},{4,12},{8,0},{12,4},{16,24},{20,28},{24,16},{28,20},{1,9},{5... | collective-permute-start | bytes 3080 | tf_op jit(solution)/shard_map/ppermute | solution.py:374
  127.2 4.5 %collective-permute-start.33 = (f32[2,128]{1,0:T(2,128)S(1)}, f32[2,128]{1,0:T(2,128)S(1)}, u32[]{:S(2)}, u32[]{:S(2)}) collective-permute-start(f32[2,128]{1,0:T(2,128)S(1)} %add_add_fusion.4), channel_id=1, source_target_pairs={{0,16},{4,20},{8,24},{12,28},{16,0},{20,4},{24,8},{28,12},{1,17},{... | collective-permute-start | bytes 3080 | tf_op jit(solution)/shard_map/ppermute | solution.py:374
  129.9 5.4 %collective-permute-start.34 = (f32[2,128]{1,0:T(2,128)S(1)}, f32[2,128]{1,0:T(2,128)S(1)}, u32[]{:S(2)}, u32[]{:S(2)}) collective-permute-start(f32[2,128]{1,0:T(2,128)S(1)} %add_add_fusion.4), channel_id=1, source_target_pairs={{0,24},{4,28},{8,16},{12,20},{16,8},{20,12},{24,0},{28,4},{1,25},{... | collective-permute-start | bytes 3080 | tf_op jit(solution)/shard_map/ppermute | solution.py:374
  140.5 4.0 %collective-permute-start.35 = (f32[16,1,128]{2,1,0:T(1,128)S(1)}, f32[16,1,128]{2,1,0:T(1,128)S(1)}, u32[]{:S(2)}, u32[]{:S(2)}) collective-permute-start(f32[16,1,128]{2,1,0:T(1,128)S(1)} %get-tuple-element.43), channel_id=1, source_target_pairs={{0,4},{4,8},{8,12},{12,16},{16,20},{20,24},{24,28},{1,5},{5,9},{9,... | collective-permute-start | bytes 24584 | tf_op jit(solution)/shard_map/ppermute | solution.py:404
  143.2 5.5 %collective-permute-start.36 = (f32[16,1,128]{2,1,0:T(1,128)S(1)}, f32[16,1,128]{2,1,0:T(1,128)S(1)}, u32[]{:S(2)}, u32[]{:S(2)}) collective-permute-start(f32[16,1,128]{2,1,0:T(1,128)S(1)} %get-tuple-element.42), channel_id=1, source_target_pairs={{4,0},{8,4},{12,8},{16,12},{20,16},{24,20},{28,24},{5,1},{9,5},{13... | collective-permute-start | bytes 24584 | tf_op jit(solution)/shard_map/ppermute | solution.py:405
  148.7 4.3 %collective-permute-start.37 = (f32[1,10,128]{2,1,0:T(8,128)S(1)}, f32[1,10,128]{2,1,0:T(8,128)S(1)}, u32[]{:S(2)}, u32[]{:S(2)}) collective-permute-start(f32[1,10,128]{2,1,0:T(8,128)S(1)} %get-tuple-element.36), channel_id=1, source_target_pairs={{1,0},{2,1},{3,2},{5,4},{6,5},{7,6},{9,8},{10,9},{11,10},{13,12},{... | collective-permute-start | bytes 15368 | tf_op jit(solution)/shard_map/ppermute | solution.py:405
  150.0 3.8 %collective-permute-start.38 = (f32[1,10,128]{2,1,0:T(8,128)S(1)}, f32[1,10,128]{2,1,0:T(8,128)S(1)}, u32[]{:S(2)}, u32[]{:S(2)}) collective-permute-start(f32[1,10,128]{2,1,0:T(8,128)S(1)} %get-tuple-element.37), channel_id=1, source_target_pairs={{0,1},{1,2},{2,3},{4,5},{5,6},{6,7},{8,9},{9,10},{10,11},{12,13},{... | collective-permute-start | bytes 15368 | tf_op jit(solution)/shard_map/ppermute | solution.py:404
  156.0 1.2 collective-permute-start.39
  157.3 3.9 %collective-permute-start.40 = (f32[2,128]{1,0:T(2,128)S(1)}, f32[2,128]{1,0:T(2,128)S(1)}, u32[]{:S(2)}, u32[]{:S(2)}) collective-permute-start(f32[2,128]{1,0:T(2,128)S(1)} %broadcast_add_fusion), channel_id=1, source_target_pairs={{0,2},{1,3},{2,0},{3,1},{4,6},{5,7},{6,4},{7,5},{8,10},{9,11},{10,... | collective-permute-start | bytes 3080 | tf_op jit(solution)/shard_map/ppermute | solution.py:374
  159.4 3.6 %collective-permute-start.41 = (f32[2,128]{1,0:T(2,128)S(1)}, f32[2,128]{1,0:T(2,128)S(1)}, u32[]{:S(2)}, u32[]{:S(2)}) collective-permute-start(f32[2,128]{1,0:T(2,128)S(1)} %broadcast_add_fusion), channel_id=1, source_target_pairs={{0,4},{1,5},{2,6},{3,7},{4,0},{5,1},{6,2},{7,3},{8,12},{9,13},{10,... | collective-permute-start | bytes 3080 | tf_op jit(solution)/shard_map/ppermute | solution.py:374
  161.2 4.5 %collective-permute-start.42 = (f32[2,128]{1,0:T(2,128)S(1)}, f32[2,128]{1,0:T(2,128)S(1)}, u32[]{:S(2)}, u32[]{:S(2)}) collective-permute-start(f32[2,128]{1,0:T(2,128)S(1)} %broadcast_add_fusion), channel_id=1, source_target_pairs={{0,6},{1,7},{2,4},{3,5},{4,2},{5,3},{6,0},{7,1},{8,14},{9,15},{10,... | collective-permute-start | bytes 3080 | tf_op jit(solution)/shard_map/ppermute | solution.py:374
  165.7 4.4 %collective-permute-start.43 = (f32[2,128]{1,0:T(2,128)S(1)}, f32[2,128]{1,0:T(2,128)S(1)}, u32[]{:S(2)}, u32[]{:S(2)}) collective-permute-start(f32[2,128]{1,0:T(2,128)S(1)} %add_add_fusion.2), channel_id=1, source_target_pairs={{0,8},{4,12},{8,0},{12,4},{16,24},{20,28},{24,16},{28,20},{1,9},{5... | collective-permute-start | bytes 3080 | tf_op jit(solution)/shard_map/ppermute | solution.py:374
  165.7 4.5 %collective-permute-start.44 = (f32[2,128]{1,0:T(2,128)S(1)}, f32[2,128]{1,0:T(2,128)S(1)}, u32[]{:S(2)}, u32[]{:S(2)}) collective-permute-start(f32[2,128]{1,0:T(2,128)S(1)} %add_add_fusion.2), channel_id=1, source_target_pairs={{0,16},{4,20},{8,24},{12,28},{16,0},{20,4},{24,8},{28,12},{1,17},{... | collective-permute-start | bytes 3080 | tf_op jit(solution)/shard_map/ppermute | solution.py:374
  167.5 5.4 %collective-permute-start.45 = (f32[2,128]{1,0:T(2,128)S(1)}, f32[2,128]{1,0:T(2,128)S(1)}, u32[]{:S(2)}, u32[]{:S(2)}) collective-permute-start(f32[2,128]{1,0:T(2,128)S(1)} %add_add_fusion.2), channel_id=1, source_target_pairs={{0,24},{4,28},{8,16},{12,20},{16,8},{20,12},{24,0},{28,4},{1,25},{... | collective-permute-start | bytes 3080 | tf_op jit(solution)/shard_map/ppermute | solution.py:374

commit v2 on v1

--- a/solution.py
+++ b/solution.py
@@ -241,7 +241,7 @@
 
 
 def density_kernel(
-    slab_total,
+    pairs,
     place_ref,
     weight_ref,
     group_ref,
@@ -258,6 +258,7 @@
     second_diags,
     first_relayed,
     second_relayed,
+    extra,
     out,
     state,
     near_buf,
@@ -323,25 +324,29 @@
         piece = rest.astype(BF16)
         folded = folded + dot(piece, member, True)
         rest = rest - piece.astype(F32)
-    slabs = lax.broadcasted_iota(jnp.int32, (slab_total, TILE), 0)
-    for group in range(out.shape[0] // slab_total):
-        block = jnp.zeros((slab_total, TILE), F32)
+    turned = pltpu.roll(folded, HALF, 1)
+    pair_rows = lax.broadcasted_iota(jnp.int32, (pairs, TILE), 0)
+    groups = (out.shape[0] - extra.shape[0]) // pairs
+    for group in range(groups):
+        block = jnp.zeros((pairs, TILE), F32)
         for row in range(4):
             energy = jnp.where(place < 2, row // 2, core)
-            slab = jnp.where(place < 2, 2 * place + row % 2, 2 * (place - core) + row)
+            pair = jnp.where(place < 2, place, place - core + row // 2)
             weight = jnp.where(group_ref[energy] == group, weight_ref[energy], 0.0)
-            block = block + jnp.where(slabs == slab, weight, 0.0) * folded[row : row + 1, :]
-        out[group * slab_total : (group + 1) * slab_total, :] = block
-
-
-def density_call(place, weight, group, orbital_atom, groups, slab_total, vectors, maps):
+            value = (turned if row % 2 else folded)[row : row + 1, :]
+            block = block + jnp.where(pair_rows == pair, weight, 0.0) * value
+        out[group * pairs : (group + 1) * pairs, :] = block
+    out[groups * pairs :, :] = extra[...]
+
+
+def density_call(place, weight, group, orbital_atom, groups, pairs, vectors, maps):
     n = orbital_atom.shape[0]
     vmem, hbm = (pl.BlockSpec(memory_space=pltpu.VMEM), pl.BlockSpec(memory_space=pl.ANY))
     smem = pl.BlockSpec(memory_space=pltpu.SMEM)
     return pl.pallas_call(
-        functools.partial(density_kernel, slab_total),
-        out_shape=jax.ShapeDtypeStruct((groups * slab_total, TILE), F32),
-        in_specs=[smem, smem, smem, vmem] + [vmem] * 4 + [hbm] * 2 + [vmem] * 6,
+        functools.partial(density_kernel, pairs),
+        out_shape=jax.ShapeDtypeStruct((groups * pairs + vectors[-1].shape[0], TILE), F32),
+        in_specs=[smem, smem, smem, vmem] + [vmem] * 4 + [hbm] * 2 + [vmem] * 7,
         out_specs=vmem,
         scratch_shapes=[
             pltpu.VMEM((n, n), F32),
@@ -372,9 +377,9 @@
     for name in axis if isinstance(axis, tuple) else (axis,):
         size *= lax.axis_size(name)
     got = [lax.ppermute(value, axis, [(i, i ^ k) for i in range(size)]) for k in strides]
-    for other in got:
-        value = value + other
-    return value
+    if len(got) == 1:
+        return value + got[0]
+    return (value + got[0]) + (got[1] + got[2])
 
 
 def total_over_all(value):
@@ -394,37 +399,468 @@
     return value
 
 
-def with_halo(x, sides, width):
-    for axis, dim in sides:
-        size, length = (lax.axis_size(axis), x.shape[dim])
-        up = [(i, (i + 1) % size) for i in range(size - 1)]
-        down = [(j, i) for i, j in up]
-        last = lax.slice_in_dim(x, length - width, length, axis=dim)
-        initial = lax.slice_in_dim(x, 0, width, axis=dim)
-        before = lax.ppermute(last, axis, up)
-        after = lax.ppermute(initial, axis, down)
-        x = jnp.concatenate([before, x, after], axis=dim)
-    return x
-
-
-def operate(field):
-    padded = with_halo(field, (("energy", 1), ("slab", 0)), 1)
-    beside = padded[2:, 1:-1] + padded[:-2, 1:-1] + padded[1:-1, 2:] + padded[1:-1, :-2]
-    deeper = jnp.pad(field, ((0, 0), (0, 0), (1, 1)))
-    beside = beside + deeper[:, :, 2:] + deeper[:, :, :-2]
-    return 6.5 * field - beside
-
-
-def two_products(residual, image):
-    pair = jnp.stack([jnp.sum(residual * residual), jnp.sum(residual * image)])
-    total = total_over_all(jnp.broadcast_to(pair[:, None], (2, TILE)))
-    return total[0, 0], total[1, 0]
-
-
-def sweep(green_iso, coupling, lead_green, energy_weight, energy_group, groups, orbital_atom):
+REACH = 5
+HALF = 64
+
+
+def edges_kernel(index_ref, cells, field, out, row):
+    place = index_ref[0]
+    atoms = cells.shape[1]
+    length = field.shape[0]
+    even = lax.rem(place, 2) == 0
+    out[:REACH] = jnp.where(even, field[length - REACH :], field[:REACH])
+    row[...] = jnp.zeros_like(row)
+    row[0:1, 0:atoms] = cells[0:1, :].astype(F32)
+    row[0:1, HALF : HALF + atoms] = cells[1:2, :].astype(F32)
+    rows = lax.broadcasted_iota(jnp.int32, out.shape[1:], 0)
+    out[REACH] = jnp.where(rows == place, row[0:1, :], 0.0)
+
+
+def mix_kernel(index_ref, field, mine, other, out):
+    length = field.shape[0]
+    even = lax.rem(index_ref[0], 2) == 0
+    out[:REACH] = jnp.where(even, field[:REACH], field[length - REACH :])
+    out[REACH] = mine[REACH] + other[REACH]
+
+
+def join_kernel(devices, index_ref, field, mixed, first, second, out, cells):
+    place = index_ref[0]
+    length = field.shape[0]
+    even = lax.rem(place, 2) == 0
+    one, two = (first[:REACH], second[:REACH])
+    out[:REACH] = jnp.where(even, jnp.where(place == 0, 0.0, two), one)
+    out[REACH : REACH + length] = field[...]
+    out[REACH + length :] = jnp.where(even, one, jnp.where(place == devices - 1, 0.0, two))
+    cells[...] = mixed[REACH] + second[REACH]
+
+
+def shifted_pair(x, axis):
+    size = x.shape[axis]
+    before, after = (pltpu.roll(x, 1, axis), pltpu.roll(x, size - 1, axis))
+    if axis == x.ndim - 1:
+        lanes = lax.broadcasted_iota(jnp.int32, x.shape, axis)
+        before = jnp.where(lanes == 0, 0.0, before)
+        after = jnp.where(lanes == size - 1, 0.0, after)
+    return before, after
+
+
+def neighbours(x):
+    centre = x[1:-1]
+    up, down = shifted_pair(centre, 1)
+    left, right = shifted_pair(centre, 2)
+    return (x[2:] + x[:-2]) + (up + down) + (left + right)
+
+
+def differences(x):
+    centre = x[1:-1]
+    up, down = shifted_pair(centre, 1)
+    left, right = shifted_pair(centre, 2)
+    along = (x[2:] - centre) + (x[:-2] - centre)
+    across = (up - centre) + (down - centre)
+    deep = (left - centre) + (right - centre)
+    return along + (across + deep)
+
+
+def grid_mask(shape, margin, length, rows, place, devices, wire, wires):
+    planes = lax.broadcasted_iota(jnp.int32, shape, 0)
+    row = lax.broadcasted_iota(jnp.int32, shape, 1)
+    low_x = jnp.where(place == 0, margin, 0)
+    high_x = jnp.where(place == devices - 1, margin + length, shape[0])
+    low_y = jnp.where(wire == 0, rows, 0)
+    high_y = jnp.where(wire == wires - 1, 2 * rows, shape[1])
+    inside = (planes >= low_x) & (planes < high_x) & (row >= low_y) & (row < high_y)
+    return inside.astype(F32)
+
+
+def three_parts(x):
+    parts = []
+    for _ in range(3):
+        parts.append(x.astype(BF16))
+        x = x - parts[-1].astype(F32)
+    return parts
+
+
+def coordinates(cell, rows_y, depth):
+    z_part = cell - depth * jnp.floor(cell * (1.0 / depth))
+    plane = jnp.floor(cell * (1.0 / depth))
+    x_part = jnp.floor(plane * (1.0 / rows_y))
+    return x_part, plane - rows_y * x_part, z_part
+
+
+WALKS = ((0, 1),), ((1, 1),), ((0, 2), (2, 1)), ((1, 3), (3, 1)), ((0, 6), (2, 4), (4, 1)), ((1, 10), (3, 5), (5, 1))
+FACTORIAL = (1.0, 1.0, 2.0, 6.0, 24.0, 120.0)
+
+
+def walk_counts(here, there, length):
+    apart = jnp.abs(here - there)
+    low = here + there + 2.0
+    high = 2.0 * length - here - there
+    at = []
+    for steps in range(6):
+        value = (apart == steps).astype(F32)
+        if steps >= 2:
+            value = value - (low == steps).astype(F32) - (high == steps).astype(F32)
+        at.append(value)
+    counts = []
+    for steps, terms in enumerate(WALKS):
+        total = None
+        for distance, count in terms:
+            term = at[distance] * (count / FACTORIAL[steps])
+            total = term if total is None else total + term
+        counts.append(total)
+    return counts
+
+
+def convolved(left, right):
+    result = []
+    for steps in range(6):
+        total = left[0] * right[steps]
+        for part in range(1, steps + 1):
+            total = total + left[part] * right[steps - part]
+        result.append(total)
+    return result
+
+
+def prepare_kernel(
+    devices, wires, width_x, atoms, index_ref, cells, left, field, right, out, walks, row_hot, deep_hot
+):
+    place, wire = (index_ref[0], index_ref[1])
+    planes, rows, depth = field.shape
+    length = planes - 2 * REACH
+    grid_y = rows * wires
+    pairs = devices
+    whole = (planes, 3 * rows, depth)
+    mask = grid_mask(whole, REACH, length, rows, place, devices, wire, wires)
+    source = jnp.concatenate([left[...], field[...], right[...]], axis=1) * mask
+
+    def inner(x):
+        extra = (x.shape[0] - length) // 2
+        return x[extra : extra + length, rows : 2 * rows]
+
+    chain = [source]
+    for step in range(1, 6):
+        chain.append(neighbours(chain[-1]) * mask[step : planes - step])
+    blocks = [inner(x) for x in chain]
+    near = source[2:-2]
+    other = [near]
+    for step in range(1, 4):
+        other.append(differences(other[-1]) * mask[2 + step : planes - 2 - step])
+    other = [inner(x) for x in other]
+    lanes = lax.broadcasted_iota(jnp.int32, (8, depth), 1)
+    sums = jnp.zeros((8, depth), F32)
+    for base, fields in enumerate((blocks, other)):
+        for steps in range(6):
+            part = jnp.sum(fields[steps // 2] * fields[(steps + 1) // 2], axis=0)
+            part = jnp.sum(jnp.sum(part, axis=1, keepdims=True), axis=0, keepdims=True)
+            sums = jnp.where(lanes == 8 * base + steps, part, sums)
+    out[...] = jnp.zeros_like(out)
+    out[6 * pairs : 6 * pairs + 8, :] = sums
+    mine = cells[pl.ds(place, 1), :]
+    lane = lax.broadcasted_iota(jnp.int32, (1, depth), 1)
+    odd = (lane >= HALF).astype(F32)
+    used = lax.rem(lane, HALF) < atoms
+    x_part, y_part, z_part = coordinates(mine, grid_y, depth)
+    start = (wire * rows).astype(F32)
+    ours = used & (y_part >= start) & (y_part < start + rows)
+    at_row = jnp.where(ours, (x_part + width_x * odd) * rows + y_part - start, -1.0)
+    cell_rows = length * rows
+    row_iota = lax.broadcasted_iota(jnp.int32, (cell_rows, depth), 0).astype(F32)
+    deep_iota = lax.broadcasted_iota(jnp.int32, (depth, depth), 0).astype(F32)
+    at_rows = (row_iota == at_row).astype(F32)
+    at_deep = (deep_iota == z_part).astype(BF16)
+    for steps, block in enumerate(blocks):
+        value = jnp.zeros((cell_rows, depth), F32)
+        for part in three_parts(block.reshape(cell_rows, depth)):
+            value = value + dot(part, at_deep, False)
+        value = jnp.sum(value * at_rows, axis=0, keepdims=True)
+        out[pl.ds(steps * pairs + place, 1), :] = value
+    row_cells = cells[...]
+    row_x, row_y, row_z = coordinates(row_cells, grid_y, depth)
+    padded = jnp.concatenate([row_cells, jnp.zeros((depth - 8, depth), F32)], axis=0)
+    column_x, column_y, column_z = coordinates(padded.T, grid_y, depth)
+    row_lane = lax.broadcasted_iota(jnp.int32, (8, depth), 1)
+    next_x, next_y, next_z = [jnp.concatenate([v[1:], v[:1]], axis=0) for v in (row_x, row_y, row_z)]
+
+    def turned(now, later, step_now, step_later):
+        value = jnp.where(row_lane >= HALF, now + step_now, later + step_later)
+        return pltpu.roll(value, HALF, 1)
+
+    even_x = row_x + width_x * (row_lane >= HALF).astype(F32)
+    odd_x, odd_y, odd_z = (
+        turned(row_x, next_x, 0.0, float(width_x)),
+        turned(row_y, next_y, 0.0, 0.0),
+        turned(row_z, next_z, 0.0, 0.0),
+    )
+    for slab in range(2 * pairs):
+        pair, side = (slab // 2, slab % 2)
+        base = float(slab * width_x)
+        if side:
+            there = (odd_x, odd_y, odd_z)
+        else:
+            there = (even_x, row_y, row_z)
+        there = [v[pair : pair + 1, :] for v in there]
+        here = [
+            v[side * HALF : side * HALF + atoms, pair : pair + 1]
+            for v in (column_x, column_y, column_z)
+        ]
+        shape = (atoms, depth)
+        sizes = (2 * pairs * width_x, grid_y, depth)
+        axes = []
+        for axis in range(3):
+            shift = base if axis == 0 else 0.0
+            axes.append(
+                walk_counts(
+                    jnp.broadcast_to(here[axis] + shift, shape),
+                    jnp.broadcast_to(there[axis] + shift, shape),
+                    float(sizes[axis]),
+                )
+            )
+        total = convolved(convolved(axes[0], axes[1]), axes[2])
+        for steps in range(6):
+            walks[steps, slab * atoms : (slab + 1) * atoms, :] = total[steps] * FACTORIAL[steps]
+    wide = length + 4
+    first_x = (place * length - 2).astype(F32)
+    first_y = start - rows
+    count = wide * 3 * rows
+    rows_iota = lax.broadcasted_iota(jnp.int32, (count, depth), 0).astype(F32)
+    used_row = lax.rem(row_lane, HALF) < atoms
+    for pair in range(pairs):
+        x_at = even_x[pair : pair + 1, :] + float(2 * pair * width_x) - first_x
+        y_at = row_y[pair : pair + 1, :] - first_y
+        good = (x_at >= 0) & (x_at < wide) & (y_at >= 0) & (y_at < 3 * rows) & used_row[0:1, :]
+        target = jnp.where(good, x_at * (3 * rows) + y_at, -1.0)
+        row_hot[:, pair * depth : (pair + 1) * depth] = (rows_iota == target).astype(BF16)
+        z_at = column_z[:, pair : pair + 1]
+        lanes_z = lax.broadcasted_iota(jnp.int32, (depth, depth), 1).astype(F32)
+        deep_hot[pair * depth : (pair + 1) * depth, :] = (lanes_z == z_at).astype(F32)
+
+
+def total_of(x):
+    return jnp.sum(jnp.sum(x, axis=1, keepdims=True), axis=0, keepdims=True)
+
+
+def quadratic_form(poly, moments, shift):
+    total = None
+    for i, one in enumerate(poly):
+        for j, two in enumerate(poly):
+            if j < i:
+                continue
+            term = one * two * moments[i + j + shift] * (1.0 if i == j else 2.0)
+            total = term if total is None else total + term
+    return total
+
+
+def finish_kernel(
+    devices,
+    wires,
+    atoms,
+    index_ref,
+    charge_ref,
+    payload,
+    walks,
+    row_hot,
+    deep_hot,
+    left,
+    field,
+    right,
+    density,
+    potential,
+):
+    place, wire = (index_ref[0], index_ref[1])
+    planes, rows, depth = field.shape
+    length = planes - 2 * REACH
+    pairs = devices
+    groups = density.shape[0]
+    charge = charge_ref[0] * payload[0:pairs, :]
+    for group in range(1, groups):
+        charge = charge + charge_ref[group] * payload[group * pairs : (group + 1) * pairs, :]
+    for group in range(groups):
+        value = payload[pl.ds(group * pairs + place, 1), :]
+        density[group, 0:1, :] = value[:, :atoms]
+        density[group, 1:2, :] = pltpu.roll(value, HALF, 1)[:, :atoms]
+    square = jnp.concatenate([charge, jnp.zeros((depth - pairs, depth), F32)], axis=0)
+    columns = square.T
+    later = jnp.concatenate([charge[1:], jnp.zeros((1, depth), F32)], axis=0)
+    lanes = lax.broadcasted_iota(jnp.int32, (pairs, depth), 1)
+    even_row = jnp.where(lanes >= HALF, 2.0 * charge, charge)
+    odd_row = pltpu.roll(jnp.where(lanes >= HALF, charge, 2.0 * later), HALF, 1)
+    totals = [None] * 6
+    for slab in range(2 * pairs):
+        pair, side = (slab // 2, slab % 2)
+        row = (odd_row if side else even_row)[pair : pair + 1, :]
+        column = columns[side * HALF : side * HALF + atoms, pair : pair + 1]
+        outer = column * row
+        for steps in range(6):
+            term = walks[steps, slab * atoms : (slab + 1) * atoms, :] * outer
+            totals[steps] = term if totals[steps] is None else totals[steps] + term
+    base = groups * pairs
+    crossed = []
+    for steps in range(6):
+        cross = 2.0 * charge * payload[base + steps * pairs : base + (steps + 1) * pairs, :]
+        crossed.append(total_of(totals[steps]) + total_of(cross))
+    sums = payload[base + 6 * pairs : base + 6 * pairs + 1, :]
+    plain = [sums[:, steps : steps + 1] + crossed[steps] for steps in range(6)]
+    moved = []
+    for steps in range(6):
+        value = sums[:, 8 + steps : 9 + steps]
+        binomial = 1
+        for part in range(steps, -1, -1):
+            value = value + (binomial * (-6.0) ** (steps - part)) * crossed[part]
+            binomial = binomial * part // (steps - part + 1)
+        moved.append(value)
+    smooth = plain[1] > 3.5 * plain[0]
+    level = jnp.where(smooth, 0.5, 6.5)
+    moments = [jnp.where(smooth, two, one) for one, two in zip(plain, moved)]
+    residual, direction = ([jnp.ones_like(level)], [jnp.ones_like(level)])
+    norm = moments[0]
+    alphas, betas = ([], [])
+    for turn in range(ITERS):
+        energy = level * quadratic_form(direction, moments, 0) - quadratic_form(direction, moments, 1)
+        alpha = norm / energy
+        alphas.append(alpha)
+        if turn + 1 == ITERS:
+            break
+        longer = residual + [jnp.zeros_like(level)]
+        for i, value in enumerate(direction):
+            longer[i] = longer[i] - alpha * level * value
+            longer[i + 1] = longer[i + 1] + alpha * value
+        residual = longer
+        following = quadratic_form(residual, moments, 0)
+        beta = following / norm
+        betas.append(beta)
+        norm = following
+        direction = [
+            value + beta * direction[i] if i < len(direction) else value
+            for i, value in enumerate(residual)
+        ]
+    pieces = [[], [], []]
+    for pair in range(pairs):
+        hot = deep_hot[pair * depth : (pair + 1) * depth, :]
+        for place_in, piece in enumerate(three_parts(columns[:, pair : pair + 1] * hot)):
+            pieces[place_in].append(piece)
+    spread = jnp.concatenate([jnp.concatenate(piece, axis=0) for piece in pieces], axis=1)
+    placed = dot(row_hot[...], spread, False)
+    placed = placed[:, :depth] + (placed[:, depth : 2 * depth] + placed[:, 2 * depth :])
+    margin = ITERS - 1
+    wide = (length + 2 * margin, 3 * rows, depth)
+    mask = grid_mask(wide, margin, length, rows, place, devices, wire, wires)
+    cut = slice(REACH - margin, REACH + length + margin)
+    source = jnp.concatenate([left[cut], field[cut], right[cut]], axis=1) * mask
+    source = source + placed.reshape(wide)
+    residual, direction = (source, source)
+    total = alphas[0] * source[margin:-margin, rows : 2 * rows]
+    for turn in range(ITERS - 1):
+        image = 6.5 * direction[1:-1] - neighbours(direction)
+        inner_mask = mask[turn + 1 : wide[0] - turn - 1]
+        residual = (residual[1:-1] - alphas[turn] * image) * inner_mask
+        direction = residual + betas[turn] * direction[1:-1]
+        extra = margin - turn - 1
+        block = direction[extra : extra + length, rows : 2 * rows]
+        total = total + alphas[turn + 1] * block
+    potential[...] = total
+
+
+def local_call(kernel, shapes, scratch, specs, name, limit, *operands):
+    vmem, smem = (pl.BlockSpec(memory_space=pltpu.VMEM), pl.BlockSpec(memory_space=pltpu.SMEM))
+    single = not isinstance(shapes, tuple)
+    return pl.pallas_call(
+        kernel,
+        out_shape=shapes,
+        in_specs=[smem if spec == "s" else vmem for spec in specs],
+        out_specs=vmem if single else (vmem,) * len(shapes),
+        scratch_shapes=scratch,
+        compiler_params=pltpu.CompilerParams(vmem_limit_bytes=limit * 2**20),
+        name=name,
+    )(*operands)
+
+
+def gather_field(index, atom_cell, doping):
+    devices, wires = (lax.axis_size("slab"), lax.axis_size("energy"))
+    length, rows, depth = doping.shape
+    edge = jax.ShapeDtypeStruct((REACH + 1, rows, depth), F32)
+    scratch = [pltpu.VMEM((8, depth), F32)]
+    mine = local_call(edges_kernel, edge, scratch, "svv", "edges", 8, index, atom_cell, doping)
+    first = lax.ppermute(mine, "slab", pairs_of(devices))
+    mixed = local_call(mix_kernel, edge, [], "svvv", "mix", 8, index, doping, mine, first)
+    turn = [(i, (i + 1) % devices if i % 2 else (i - 1) % devices) for i in range(devices)]
+    second = lax.ppermute(mixed, "slab", turn)
+    shapes = (
+        jax.ShapeDtypeStruct((length + 2 * REACH, rows, depth), F32),
+        jax.ShapeDtypeStruct((rows, depth), F32),
+    )
+    field, cells = local_call(
+        functools.partial(join_kernel, devices),
+        shapes,
+        [],
+        "svvvv",
+        "join",
+        8,
+        index,
+        doping,
+        mixed,
+        first,
+        second,
+    )
+    if devices > 4:
+        cells = lax.psum(mine[REACH], "slab")
+    right = lax.ppermute(field, "energy", [((i + 1) % wires, i) for i in range(wires)])
+    left = lax.ppermute(field, "energy", [(i, (i + 1) % wires) for i in range(wires)])
+    return cells, left, field, right
+
+
+def prepare(index, cells, left, field, right, atom_cell):
+    devices, wires = (lax.axis_size("slab"), lax.axis_size("energy"))
+    planes, rows, depth = field.shape
+    length = planes - 2 * REACH
+    atoms = atom_cell.shape[1]
+    shapes = (
+        jax.ShapeDtypeStruct((6 * devices + 8, depth), F32),
+        jax.ShapeDtypeStruct((6, 2 * devices * atoms, depth), F32),
+        jax.ShapeDtypeStruct(((length + 4) * 3 * rows, devices * depth), BF16),
+        jax.ShapeDtypeStruct((devices * depth, depth), F32),
+    )
+    kernel = functools.partial(prepare_kernel, devices, wires, length // 2, atoms)
+    return local_call(kernel, shapes, [], "svvvv", "prepare", 32, index, cells, left, field, right)
+
+
+def finish(index, group_charge, payload, prepared, left, field, right, atom_cell):
+    devices, wires = (lax.axis_size("slab"), lax.axis_size("energy"))
+    planes, rows, depth = field.shape
+    slabs, atoms = atom_cell.shape
+    shapes = (
+        jax.ShapeDtypeStruct((group_charge.shape[0], slabs, atoms), F32),
+        jax.ShapeDtypeStruct((planes - 2 * REACH, rows, depth), F32),
+    )
+    kernel = functools.partial(finish_kernel, devices, wires, atoms)
+    return local_call(
+        kernel,
+        shapes,
+        [],
+        "ssvvvvvvv",
+        "finish",
+        32,
+        index,
+        group_charge,
+        payload,
+        *prepared,
+        left,
+        field,
+        right,
+    )
+
+
+def sweep(
+    place,
+    green_iso,
+    coupling,
+    lead_green,
+    energy_weight,
+    energy_group,
+    groups,
+    orbital_atom,
+    extra,
+):
     devices = lax.axis_size("slab")
-    slab_total = devices * green_iso.shape[1]
-    place = lax.axis_index("slab").astype(jnp.int32).reshape(1)
     own, sent, packed, first_diags = first_call(0, place, green_iso, coupling, lead_green, ())
     first_x = over_slab(packed, pairs_of(devices))
     own, sent, packed, second_diags = first_call(
@@ -461,9 +897,10 @@
         second_diags,
         first_relayed,
         second_relayed,
+        extra,
     )
     return density_call(
-        place, energy_weight, energy_group, orbital_atom, groups, slab_total, vectors, (own, got)
+        place, energy_weight, energy_group, orbital_atom, groups, devices, vectors, (own, got)
     )
 
 
@@ -478,53 +915,23 @@
     atom_cell,
     doping,
 ):
-    slab_count, atom_count = atom_cell.shape
     groups = group_charge.shape[0]
-    partial = sweep(
-        green_iso, coupling, lead_green, energy_weight, energy_group, groups, orbital_atom
-    )
-    density = total_over_all(partial).reshape(groups, -1, TILE)
-    atom_density = lax.dynamic_slice(
-        density,
-        (0, lax.axis_index("slab") * slab_count, 0),
-        (groups, slab_count, atom_count),
-    )
-    charge = jnp.sum(group_charge[:, None, None] * atom_density, axis=0)
-    depth = doping.shape[2]
-    rows_y = doping.shape[1]
-    width_x = doping.shape[0] // slab_count
-    full_y = rows_y * lax.axis_size("energy")
-    y_start = lax.axis_index("energy") * rows_y
-    x_part = atom_cell // (full_y * depth)
-    y_part = atom_cell // depth % full_y
-    z_part = atom_cell % depth
-    slab_place = jnp.arange(slab_count, dtype=jnp.int32)[:, None]
-    inside = (y_part >= y_start) & (y_part < y_start + rows_y)
-    volume = doping.size
-    target = ((slab_place * width_x + x_part) * rows_y + (y_part - y_start)) * depth + z_part
-    target = jnp.where(inside, target, volume)
-    placed = jax.ops.segment_sum(charge.reshape(-1), target.reshape(-1), num_segments=volume + 1)[
-        :volume
-    ]
-    source = doping + placed.reshape(doping.shape)
-    potential = jnp.zeros_like(source)
-    residual = source
-    image = operate(residual)
-    norm_now, product_now = two_products(residual, image)
-    alpha = norm_now / product_now
-    direction, along = (residual, image)
-    for turn in range(ITERS):
-        potential = potential + alpha * direction
-        residual = residual - alpha * along
-        if turn + 1 < ITERS:
-            image = operate(residual)
-            norm_next, product_now = two_products(residual, image)
-            ratio = norm_next / norm_now
-            alpha = norm_next / (product_now - ratio * norm_next / alpha)
-            direction = residual + ratio * direction
-            along = image + ratio * along
-            norm_now = norm_next
-    return (atom_density, potential)
+    index = jnp.stack([lax.axis_index("slab"), lax.axis_index("energy")]).astype(jnp.int32)
+    cells, *fields = gather_field(index, atom_cell, doping)
+    extra, *prepared = prepare(index, cells, *fields, atom_cell)
+    payload = sweep(
+        index,
+        green_iso,
+        coupling,
+        lead_green,
+        energy_weight,
+        energy_group,
+        groups,
+        orbital_atom,
+        extra,
+    )
+    payload = total_over_all(payload)
+    return finish(index, group_charge, payload, prepared, *fields, atom_cell)
 
 
 def solution(mesh):

time: 180 us -> 85.2 us (0.47)
  starting transfers between devices: 80.9 us -> 30.9 us
  waiting for transfers between devices: 51.8 us -> 16.2 us
  Pallas kernels: 11.7 us -> 22.1 us
  between operations: 10.9 us -> 0.82 us
  other arithmetic: 9.91 us -> 0.81 us
    ppermute x28 -> x7, starting transfers between devices: 43.1 us -> 11.4 us  [total_over(): lax.ppermute(value, axis, [(i, i ^ k) for i in range(size)])]
    ppermute x28 -> x7, waiting for transfers between devices: 35.3 us -> 8.72 us  [total_over(): lax.ppermute(value, axis, [(i, i ^ k) for i in range(size)])]
    ppermute x12 -> x4, starting transfers between devices: 24.2 us -> 7.98 us  [the longest x1 3.22 us: gather_field(): lax.ppermute(field, 'energy', [((i + 1) % wires, i) for i in range(wires)])]
    ppermute x12 -> x4, waiting for transfers between devices: 15.1 us -> 6.26 us  [the longest x1 2.95 us: gather_field(): second = lax.ppermute(mixed, 'slab', turn)]
    pallas_call x1 -> x6, Pallas kernels: 1.43 us -> 9.5 us  [the longest x5 8.03 us: local_call(): pl.pallas_call(kernel, out_shape=shapes, in_specs=[smem if spec == 's' el...]
    another operation x3 -> x1, other arithmetic: 4.01 us -> 0.08 us  [on_device(): jnp.stack([lax.axis_index('slab'), lax.axis_index('energy')])]
    reduce_sum x4 -> x0, other arithmetic: 2.78 us -> none  [the longest x3 2.17 us: two_products(): pair = jnp.stack([jnp.sum(residual * residual), jnp.sum(residual * image)])]
    unnamed x36 -> x42, local copies, waits for them, and re-layouts: 10.2 us -> 12.6 us
  transfers between devices with their start and end apart: 46 -> 17, of which waited for: 30 -> 9; matrix products, arithmetic and copies ran while one was open for 1% -> 2% of each run, Pallas kernels for 1% -> 11%
where the time goes in v2:
time: 85.2 us; the launch traced here: 84 us
  starting transfers between devices  30.9 us (36%)
  Pallas kernels  22.1 us (26%)
  waiting for transfers between devices  16.2 us (19%)
  local copies, waits for them, and re-layouts  13.2 us (15%)
    unnamed x42, local copies, waits for them, and re-layouts  12.6 us
    ppermute x5, starting transfers between devices, over_slab(): return lax.ppermute(value, 'slab', moves)  11.5 us
    ppermute x7, starting transfers between devices, total_over(): lax.ppermute(value, axis, [(i, i ^ k) for i in range(size)])  11.4 us
    pallas_call x2, Pallas kernels, first_call(): pl.pallas_call(functools.partial(first_kernel, energy), out_shape=(map_sh...  9.74 us
    ppermute x7, waiting for transfers between devices, total_over(): lax.ppermute(value, axis, [(i, i ^ k) for i in range(size)])  8.72 us
    pallas_call x5, Pallas kernels, local_call(): pl.pallas_call(kernel, out_shape=shapes, in_specs=[smem if spec == 's' el...  8.03 us
    ppermute x1, starting transfers between devices, gather_field(): lax.ppermute(field, 'energy', [((i + 1) % wires, i) for i in range(wires)])  3.22 us
    ppermute x1, waiting for transfers between devices, gather_field(): second = lax.ppermute(mixed, 'slab', turn)  2.95 us
  transfers between devices with their start and end apart: 17, of which 9 were waited for; matrix products, arithmetic and copies ran while one was open for 2% of the time, Pallas kernels for 11%

profile of v2, /device:TPU:0, one launch (start us, length us, event | category | flops | bytes accessed | tf_op | source)
XLA Modules:
  0.0 84.0 jit_solution(16736453113415981878)
XLA Ops:
  0.6 0.1 pad_add_fusion.place_ref.index_ref
  0.7 1.7 %copy-done = f32[2,2,384,384]{3,2,1,0:T(8,128)S(1)} copy-done((f32[2,2,384,384]{3,2,1,0:T(8,128)S(1)}, f32[2,2,384,384]{3,2,1,0:T(8,128)}, u32[]{:S(2)}) %copy-start) | copy-done | bytes 2359320
  2.4 1.3 %copy-done.1 = f32[2,384,384]{2,1,0:T(8,128)S(1)} copy-done((f32[2,384,384]{2,1,0:T(8,128)S(1)}, f32[2,384,384]{2,1,0:T(8,128)}, u32[]{:S(2)}) %copy-start.1) | copy-done | bytes 1179672
  3.6 1.3 %copy-done.2 = f32[2,384,384]{2,1,0:T(8,128)S(1)} copy-done((f32[2,384,384]{2,1,0:T(8,128)S(1)}, f32[2,384,384]{2,1,0:T(8,128)}, u32[]{:S(2)}) %copy-start.2) | copy-done | bytes 1179672
  4.9 4.9 %slabs_0.1 = (f32[3,384,384]{2,1,0:T(8,128)S(1)}, f32[3,384,384]{2,1,0:T(8,128)S(1)}, f32[6,128,128]{2,1,0:T(8,128)S(1)}, f32[8,384]{1,0:T(8,128)S(1)}) custom-call(s32[2]{0:T(128)S(1)} %pad_add_fusion.place_ref.index_ref, f32[2,2,384,384]{3,2,1,0:T(8,128)S(1)} %copy-done, f32[2,384,384]{2,1,0:T(8,128)S(1)} %copy-done.1, f32[2,384,384]{2,1,0:T(8,128)S(1)} %copy-done.2), custom_call_target="tpu_custom_call" | custom-call | flops 2038431744 | bytes 3538944 | tf_op jit(solution)/shard_map/slabs_0/pallas_call | solution.py:131
  9.8 4.9 %slabs_1.1 = (f32[3,384,384]{2,1,0:T(8,128)S(1)}, f32[3,384,384]{2,1,0:T(8,128)S(1)}, f32[6,128,128]{2,1,0:T(8,128)S(1)}, f32[8,384]{1,0:T(8,128)S(1)}) custom-call(s32[2]{0:T(128)S(1)} %pad_add_fusion.place_ref.index_ref, f32[2,2,384,384]{3,2,1,0:T(8,128)S(1)} %copy-done, ...), custom_call_target="tpu_custom_call", output_to_operand_aliasing={{0}: (4, {}), {1}: (5, {})} | custom-call | flops 2038431744 | bytes 3538944 | tf_op jit(solution)/shard_map/slabs_1/pallas_call | solution.py:131
  14.7 1.9 %collective-permute-start.4 = (f32[3,384,384]{2,1,0:T(8,128)S(1)}, f32[3,384,384]{2,1,0:T(8,128)}, u32[]{:S(2)}, u32[]{:S(2)}) collective-permute-start(f32[3,384,384]{2,1,0:T(8,128)S(1)} %get-tuple-element.24.maps), channel_id=1, source_target_pairs={{0,0},{1,1},{2,3},{3,2},{4,4},{5,5},{6,7},{7,6},{8,8},{9,9},{10,11... | collective-permute-start | bytes 5308424 | tf_op jit(solution)/shard_map/ppermute | solution.py:368
  16.6 0.0 collective-permute-start
  16.6 0.5 collective-permute-start.1
  17.1 1.2 %collective-permute-done.packed.first_x = f32[6,128,128]{2,1,0:T(8,128)S(1)} collective-permute-done((f32[6,128,128]{2,1,0:T(8,128)S(1)}, f32[6,128,128]{2,1,0:T(8,128)S(1)}, u32[]{:S(2)}, u32[]{:S(2)}) %collective-permute-start) | collective-permute-done | bytes 393248 | tf_op jit(solution)/shard_map/ppermute | solution.py:368
  18.3 1.3 %relay.2 = (f32[6,128,128]{2,1,0:T(8,128)}, f32[8,384]{1,0:T(8,128)S(1)}) custom-call(s32[2]{0:T(128)S(1)} %pad_add_fusion.place_ref.index_ref, f32[6,128,128]{2,1,0:T(8,128)S(1)} %collective-permute-done.packed.first_x, f32[3,384,384]{2,1,0:T(8,128)S(1)} %get-tuple-element.24.maps), custom_call_target="tpu_custom_call" | custom-call | flops 679477248 | bytes 1769472 | tf_op jit(solution)/shard_map/relay/pallas_call | solution.py:174
  19.6 0.7 copy-done.11
  20.4 0.6 copy-done.17
  21.0 4.6 %collective-permute-start.2 = (f32[6,128,128]{2,1,0:T(8,128)}, f32[6,128,128]{2,1,0:T(8,128)}, u32[]{:S(2)}, u32[]{:S(2)}) collective-permute-start(f32[6,128,128]{2,1,0:T(8,128)} %get-tuple-element.25), channel_id=1, source_target_pairs={{0,0},{1,2},{2,1},{3,3},{4,4},{5,6},{6,5},{7,7},{8,8},{9,10},{10,9... | collective-permute-start | bytes 1179656 | tf_op jit(solution)/shard_map/ppermute | solution.py:368
  25.6 0.0 collective-permute-done.1.packed.second_x
  25.6 1.5 %relay.3 = (f32[6,128,128]{2,1,0:T(8,128)}, f32[8,384]{1,0:T(8,128)S(1)}) custom-call(s32[2]{0:T(128)S(1)} %pad_add_fusion.place_ref.index_ref, f32[6,128,128]{2,1,0:T(8,128)S(1)} %collective-permute-done.1.packed.second_x, f32[3,384,384]{2,1,0:T(8,128)S(1)} %get-tuple-element.26.maps.own), custom_call_target="tpu_custom_call" | custom-call | flops 679477248 | bytes 1769472 | tf_op jit(solution)/shard_map/relay/pallas_call | solution.py:174
  27.1 4.5 %collective-permute-start.3 = (f32[6,128,128]{2,1,0:T(8,128)}, f32[6,128,128]{2,1,0:T(8,128)}, u32[]{:S(2)}, u32[]{:S(2)}) collective-permute-start(f32[6,128,128]{2,1,0:T(8,128)} %get-tuple-element.27), channel_id=1, source_target_pairs={{0,0},{1,3},{2,2},{3,1},{4,4},{5,7},{6,6},{7,5},{8,8},{9,11},{10,1... | collective-permute-start | bytes 1179656 | tf_op jit(solution)/shard_map/ppermute | solution.py:368
  31.6 0.0 copy-done.9
  31.6 0.6 edges.1.mine
  32.3 2.2 %collective-permute-start.6 = (f32[6,8,128]{2,1,0:T(8,128)S(1)}, f32[6,8,128]{2,1,0:T(8,128)S(1)}, u32[]{:S(2)}, u32[]{:S(2)}) collective-permute-start(f32[6,8,128]{2,1,0:T(8,128)S(1)} %edges.1.mine), channel_id=1, source_target_pairs={{0,1},{1,0},{2,3},{3,2},{4,5},{5,4},{6,7},{7,6},{8,9},{9,8},{10,11... | collective-permute-start | bytes 73736 | tf_op jit(solution)/shard_map/ppermute | solution.py:783
  34.4 0.8 %collective-permute-done.6.other.first = f32[6,8,128]{2,1,0:T(8,128)S(1)} collective-permute-done((f32[6,8,128]{2,1,0:T(8,128)S(1)}, f32[6,8,128]{2,1,0:T(8,128)S(1)}, u32[]{:S(2)}, u32[]{:S(2)}) %collective-permute-start.6) | collective-permute-done | bytes 24608 | tf_op jit(solution)/shard_map/ppermute | solution.py:783
  35.3 1.2 %mix.1.mixed = f32[6,8,128]{2,1,0:T(8,128)} custom-call(s32[2]{0:T(128)S(1)} %pad_add_fusion.place_ref.index_ref, f32[16,8,128]{2,1,0:T(8,128)S(1)} %copy-done.3, f32[6,8,128]{2,1,0:T(8,128)S(1)} %edges.1.mine, f32[6,8,128]{2,1,0:T(8,128)S(1)} %collective-permute-done.6.other.first), custom_call_target="tpu_custom_call" | custom-call | tf_op jit(solution)/shard_map/mix/pallas_call | solution.py:766
  36.4 0.0 copy-done.13
  36.4 0.0 copy-done.5
  36.4 1.1 %collective-permute-start.7 = (f32[6,8,128]{2,1,0:T(8,128)}, f32[6,8,128]{2,1,0:T(8,128)}, u32[]{:S(2)}, u32[]{:S(2)}) collective-permute-start(f32[6,8,128]{2,1,0:T(8,128)} %mix.1.mixed), channel_id=1, source_target_pairs={{0,3},{1,2},{2,1},{3,0},{4,7},{5,6},{6,5},{7,4},{8,11},{9,10},{10,... | collective-permute-start | bytes 73736 | tf_op jit(solution)/shard_map/ppermute | solution.py:786
  37.5 2.9 %collective-permute-done.7.second = f32[6,8,128]{2,1,0:T(8,128)} collective-permute-done((f32[6,8,128]{2,1,0:T(8,128)}, f32[6,8,128]{2,1,0:T(8,128)}, u32[]{:S(2)}, u32[]{:S(2)}) %collective-permute-start.7) | collective-permute-done | bytes 24608 | tf_op jit(solution)/shard_map/ppermute | solution.py:786
  40.4 0.8 copy-done.4
  41.3 0.7 copy-done.6
  42.0 0.8 join.1
  42.8 1.6 %collective-permute-start.8 = (f32[26,8,128]{2,1,0:T(8,128)S(1)}, f32[26,8,128]{2,1,0:T(8,128)S(1)}, u32[]{:S(2)}, u32[]{:S(2)}) collective-permute-start(f32[26,8,128]{2,1,0:T(8,128)S(1)} %get-tuple-element.33.field), channel_id=1, source_target_pairs={{0,4},{4,8},{8,12},{12,16},{16,20},{20,24},{24,28},{28,0},{1,5},{5... | collective-permute-start | bytes 319496 | tf_op jit(solution)/shard_map/ppermute | solution.py:807
  44.3 3.2 %collective-permute-start.9 = (f32[26,8,128]{2,1,0:T(8,128)S(1)}, f32[26,8,128]{2,1,0:T(8,128)S(1)}, u32[]{:S(2)}, u32[]{:S(2)}) collective-permute-start(f32[26,8,128]{2,1,0:T(8,128)S(1)} %get-tuple-element.33.field), channel_id=1, source_target_pairs={{4,0},{8,4},{12,8},{16,12},{20,16},{24,20},{28,24},{0,28},{5,1},{9... | collective-permute-start | bytes 319496 | tf_op jit(solution)/shard_map/ppermute | solution.py:806
  47.6 0.7 broadcast_select_fusion
  48.3 2.5 %collective-permute-done.8.left = f32[26,8,128]{2,1,0:T(8,128)S(1)} collective-permute-done((f32[26,8,128]{2,1,0:T(8,128)S(1)}, f32[26,8,128]{2,1,0:T(8,128)S(1)}, u32[]{:S(2)}, u32[]{:S(2)}) %collective-permute-start.8) | collective-permute-done | bytes 106528 | tf_op jit(solution)/shard_map/ppermute | solution.py:807
  50.7 0.0 collective-permute-start.5
  50.8 0.7 reshape.7.orbital_atom
  51.4 0.0 collective-permute-done.9.right
  51.4 3.5 %prepare.1 = (f32[32,128]{1,0:T(8,128)S(1)}, f32[6,384,128]{2,1,0:T(8,128)S(1)}, bf16[480,512]{1,0:T(8,128)(2,1)S(1)}, f32[512,128]{1,0:T(8,128)S(1)}) custom-call(s32[2]{0:T(128)S(1)} %pad_add_fusion.place_ref.index_ref, f32[8,128]{1,0:T(8,128)S(1)} %get-tuple-element.32.cells, f32[26,8,128]{2,1,0:T(8,128)S(1)} %collective-permute-done.8.left, ...), custom_call_target="tpu_custom_call" | custom-call | tf_op jit(solution)/shard_map/prepare/pallas_call | solution.py:766
  54.9 0.0 collective-permute-done.5.got_diags
  54.9 0.0 collective-permute-done.2.first_y
  54.9 0.0 collective-permute-done.3.second_y
  54.9 0.0 collective-permute-done.4.got
  55.0 0.7 copy-done.8
  55.7 1.0 %copy-done.12 = f32[6,128,128]{2,1,0:T(8,128)S(1)} copy-done((f32[6,128,128]{2,1,0:T(8,128)S(1)}, f32[6,128,128]{2,1,0:T(8,128)}, u32[]{:S(2)}) %copy-start.12) | copy-done | bytes 393240
  56.6 1.0 %copy-done.14 = f32[6,128,128]{2,1,0:T(8,128)S(1)} copy-done((f32[6,128,128]{2,1,0:T(8,128)S(1)}, f32[6,128,128]{2,1,0:T(8,128)}, u32[]{:S(2)}) %copy-start.14) | copy-done | bytes 393240
  57.6 0.7 copy-done.15
  58.3 0.7 copy-done.16
  59.0 0.7 copy-done.18
  59.7 0.7 copy-done.20
  60.4 1.5 %density.1 = f32[48,128]{1,0:T(8,128)S(1)} custom-call(s32[2]{0:T(128)S(1)} %pad_add_fusion.place_ref.index_ref, f32[2]{0:T(128)S(1)} %copy-done.15, s32[2]{0:T(128)S(1)} %copy-done.16, s32[1,384]{1,0:T(1,128)S(1)} %reshape.7.orbital_atom, f32[6,128,128]{2,1,0:T(8,128)S(1)} %copy-done.12, f32[6,128,128]{2,1,0:T(8,128)S(1)} %copy-done.14, ...), custom_call_target="tpu_custom_call" | custom-call | flops 1698693120 | bytes 3538944 | tf_op jit(solution)/shard_map/density/pallas_call | solution.py:346
  61.8 3.4 %collective-permute-start.10 = (f32[48,128]{1,0:T(8,128)S(1)}, f32[48,128]{1,0:T(8,128)S(1)}, u32[]{:S(2)}, u32[]{:S(2)}) collective-permute-start(f32[48,128]{1,0:T(8,128)S(1)} %density.1), channel_id=1, source_target_pairs={{0,1},{1,0},{2,3},{3,2},{4,5},{5,4},{6,7},{7,6},{8,9},{9,8},{10,11... | collective-permute-start | bytes 73736 | tf_op jit(solution)/shard_map/ppermute | solution.py:379
  65.2 0.8 %collective-permute-done.10 = f32[48,128]{1,0:T(8,128)S(1)} collective-permute-done((f32[48,128]{1,0:T(8,128)S(1)}, f32[48,128]{1,0:T(8,128)S(1)}, u32[]{:S(2)}, u32[]{:S(2)}) %collective-permute-start.10) | collective-permute-done | bytes 24608 | tf_op jit(solution)/shard_map/ppermute | solution.py:379
  66.1 0.9 %collective-permute-start.12 = (f32[48,128]{1,0:T(8,128)S(1)}, f32[48,128]{1,0:T(8,128)S(1)}, u32[]{:S(2)}, u32[]{:S(2)}) collective-permute-start(f32[48,128]{1,0:T(8,128)S(1)} %add.21), channel_id=1, source_target_pairs={{0,4},{1,5},{2,6},{3,7},{4,0},{5,1},{6,2},{7,3},{8,12},{9,13},{10,... | collective-permute-start | bytes 73736 | tf_op jit(solution)/shard_map/ppermute | solution.py:379
  66.9 3.3 %collective-permute-start.13 = (f32[48,128]{1,0:T(8,128)S(1)}, f32[48,128]{1,0:T(8,128)S(1)}, u32[]{:S(2)}, u32[]{:S(2)}) collective-permute-start(f32[48,128]{1,0:T(8,128)S(1)} %add.21), channel_id=1, source_target_pairs={{0,6},{1,7},{2,4},{3,5},{4,2},{5,3},{6,0},{7,1},{8,14},{9,15},{10,... | collective-permute-start | bytes 73736 | tf_op jit(solution)/shard_map/ppermute | solution.py:379
  70.2 0.0 collective-permute-start.11
  70.2 0.0 collective-permute-done.12
  70.2 2.1 %collective-permute-done.13 = f32[48,128]{1,0:T(8,128)S(1)} collective-permute-done((f32[48,128]{1,0:T(8,128)S(1)}, f32[48,128]{1,0:T(8,128)S(1)}, u32[]{:S(2)}, u32[]{:S(2)}) %collective-permute-start.13) | collective-permute-done | bytes 24608 | tf_op jit(solution)/shard_map/ppermute | solution.py:379
  72.3 1.8 %collective-permute-done.11 = f32[48,128]{1,0:T(8,128)S(1)} collective-permute-done((f32[48,128]{1,0:T(8,128)S(1)}, f32[48,128]{1,0:T(8,128)S(1)}, u32[]{:S(2)}, u32[]{:S(2)}) %collective-permute-start.11) | collective-permute-done | bytes 24608 | tf_op jit(solution)/shard_map/ppermute | solution.py:379
  74.1 2.2 %collective-permute-start.15 = (f32[48,128]{1,0:T(8,128)S(1)}, f32[48,128]{1,0:T(8,128)S(1)}, u32[]{:S(2)}, u32[]{:S(2)}) collective-permute-start(f32[48,128]{1,0:T(8,128)S(1)} %add_add_fusion.1), channel_id=1, source_target_pairs={{0,16},{4,20},{8,24},{12,28},{16,0},{20,4},{24,8},{28,12},{1,17},{... | collective-permute-start | bytes 73736 | tf_op jit(solution)/shard_map/ppermute | solution.py:379
  76.3 1.3 %collective-permute-start.16 = (f32[48,128]{1,0:T(8,128)S(1)}, f32[48,128]{1,0:T(8,128)S(1)}, u32[]{:S(2)}, u32[]{:S(2)}) collective-permute-start(f32[48,128]{1,0:T(8,128)S(1)} %add_add_fusion.1), channel_id=1, source_target_pairs={{0,24},{4,28},{8,16},{12,20},{16,8},{20,12},{24,0},{28,4},{1,25},{... | collective-permute-start | bytes 73736 | tf_op jit(solution)/shard_map/ppermute | solution.py:379
  77.7 0.2 collective-permute-start.14
  77.9 1.0 %collective-permute-done.15 = f32[48,128]{1,0:T(8,128)S(1)} collective-permute-done((f32[48,128]{1,0:T(8,128)S(1)}, f32[48,128]{1,0:T(8,128)S(1)}, u32[]{:S(2)}, u32[]{:S(2)}) %collective-permute-start.15) | collective-permute-done | bytes 24608 | tf_op jit(solution)/shard_map/ppermute | solution.py:379
  78.9 3.1 %collective-permute-done.16 = f32[48,128]{1,0:T(8,128)S(1)} collective-permute-done((f32[48,128]{1,0:T(8,128)S(1)}, f32[48,128]{1,0:T(8,128)S(1)}, u32[]{:S(2)}, u32[]{:S(2)}) %collective-permute-start.16) | collective-permute-done | bytes 24608 | tf_op jit(solution)/shard_map/ppermute | solution.py:379
  81.9 0.0 collective-permute-done.14
  82.0 2.0 %finish.1 = (f32[4,2,48]{2,1,0:T(2,128)}, f32[16,8,128]{2,1,0:T(8,128)}) custom-call(s32[2]{0:T(128)S(1)} %pad_add_fusion.place_ref.index_ref, f32[4]{0:T(128)S(1)} %copy-done.10, f32[48,128]{1,0:T(8,128)S(1)} %add_add_fusion.payload, f32[6,384,128]{2,1,0:T(8,128)S(1)} %get-tuple-element.35.walks, bf16[480,512]{1,0:T(8,128)(2,1)S(1)} %get-tuple-element.36.row_hot, ...), custom_call_target="tpu_custom_call" | custom-call | tf_op jit(solution)/shard_map/finish/pallas_call | solution.py:766
  (28 shorter events, 0.1 us)
Async XLA Ops:
  0.7 1.7 %copy-start = (f32[2,2,384,384]{3,2,1,0:T(8,128)S(1)}, f32[2,2,384,384]{3,2,1,0:T(8,128)}, u32[]{:S(2)}) copy-start(f32[2,2,384,384]{3,2,1,0:T(8,128)} %iso.3) | copy-start | bytes 7077892
  2.4 1.3 %copy-start.1 = (f32[2,384,384]{2,1,0:T(8,128)S(1)}, f32[2,384,384]{2,1,0:T(8,128)}, u32[]{:S(2)}) copy-start(f32[2,384,384]{2,1,0:T(8,128)} %coupling.3) | copy-start | bytes 3538948
  3.6 1.3 %copy-start.2 = (f32[2,384,384]{2,1,0:T(8,128)S(1)}, f32[2,384,384]{2,1,0:T(8,128)}, u32[]{:S(2)}) copy-start(f32[2,384,384]{2,1,0:T(8,128)} %lead.3) | copy-start | bytes 3538948
  14.7 12.5 %copy-start.7 = (f32[8,384]{1,0:T(8,128)}, f32[8,384]{1,0:T(8,128)S(1)}, u32[]{:S(2)}) copy-start(f32[8,384]{1,0:T(8,128)S(1)} %get-tuple-element.29.second_diags) | copy-start | bytes 36868
  14.7 40.2 %collective-permute-start.4 = (f32[3,384,384]{2,1,0:T(8,128)S(1)}, f32[3,384,384]{2,1,0:T(8,128)}, u32[]{:S(2)}, u32[]{:S(2)}) collective-permute-start(f32[3,384,384]{2,1,0:T(8,128)S(1)} %get-tuple-element.24.maps), channel_id=1, source_target_pairs={{0,0},{1,1},{2,3},{3,2},{4,4},{5,5},{6,7},{7,6},{8,8},{9,9},{10,11... | collective-permute-start | bytes 5308424 | tf_op jit(solution)/shard_map/ppermute | solution.py:368
  16.6 1.7 %collective-permute-start = (f32[6,128,128]{2,1,0:T(8,128)S(1)}, f32[6,128,128]{2,1,0:T(8,128)S(1)}, u32[]{:S(2)}, u32[]{:S(2)}) collective-permute-start(f32[6,128,128]{2,1,0:T(8,128)S(1)} %get-tuple-element.20), channel_id=1, source_target_pairs={{0,1},{1,0},{2,3},{3,2},{4,5},{5,4},{6,7},{7,6},{8,9},{9,8},{10,11... | collective-permute-start | bytes 1179656 | tf_op jit(solution)/shard_map/ppermute | solution.py:368
  16.6 9.0 %collective-permute-start.1 = (f32[6,128,128]{2,1,0:T(8,128)S(1)}, f32[6,128,128]{2,1,0:T(8,128)S(1)}, u32[]{:S(2)}, u32[]{:S(2)}) collective-permute-start(f32[6,128,128]{2,1,0:T(8,128)S(1)} %get-tuple-element.23), channel_id=1, source_target_pairs={{0,1},{1,0},{2,3},{3,2},{4,5},{5,4},{6,7},{7,6},{8,9},{9,8},{10,11... | collective-permute-start | bytes 1179656 | tf_op jit(solution)/shard_map/ppermute | solution.py:368
  19.6 0.8 copy-start.11
  20.4 0.6 copy-start.17
  21.0 10.7 %copy-start.3 = (f32[16,8,128]{2,1,0:T(8,128)S(1)}, f32[16,8,128]{2,1,0:T(8,128)}, u32[]{:S(2)}) copy-start(f32[16,8,128]{2,1,0:T(8,128)} %field.5) | copy-start | bytes 196612
  21.0 10.7 %copy-start.9 = (s32[2,48]{1,0:T(2,128)S(1)}, s32[2,48]{1,0:T(2,128)}, u32[]{:S(2)}) copy-start(s32[2,48]{1,0:T(2,128)} %cells.1) | copy-start | bytes 1156
  21.0 33.9 %collective-permute-start.2 = (f32[6,128,128]{2,1,0:T(8,128)}, f32[6,128,128]{2,1,0:T(8,128)}, u32[]{:S(2)}, u32[]{:S(2)}) collective-permute-start(f32[6,128,128]{2,1,0:T(8,128)} %get-tuple-element.25), channel_id=1, source_target_pairs={{0,0},{1,2},{2,1},{3,3},{4,4},{5,6},{6,5},{7,7},{8,8},{9,10},{10,9... | collective-permute-start | bytes 1179656 | tf_op jit(solution)/shard_map/ppermute | solution.py:368
  25.6 10.8 %copy-start.13 = (f32[6,128,128]{2,1,0:T(8,128)}, f32[6,128,128]{2,1,0:T(8,128)S(1)}, u32[]{:S(2)}) copy-start(f32[6,128,128]{2,1,0:T(8,128)S(1)} %collective-permute-done.1.packed.second_x) | copy-start | bytes 1179652
  27.1 9.3 %copy-start.19 = (f32[8,384]{1,0:T(8,128)}, f32[8,384]{1,0:T(8,128)S(1)}, u32[]{:S(2)}) copy-start(f32[8,384]{1,0:T(8,128)S(1)} %get-tuple-element.31.second_relayed) | copy-start | bytes 36868
  27.1 27.8 %collective-permute-start.3 = (f32[6,128,128]{2,1,0:T(8,128)}, f32[6,128,128]{2,1,0:T(8,128)}, u32[]{:S(2)}, u32[]{:S(2)}) collective-permute-start(f32[6,128,128]{2,1,0:T(8,128)} %get-tuple-element.27), channel_id=1, source_target_pairs={{0,0},{1,3},{2,2},{3,1},{4,4},{5,7},{6,6},{7,5},{8,8},{9,11},{10,1... | collective-permute-start | bytes 1179656 | tf_op jit(solution)/shard_map/ppermute | solution.py:368
  32.3 3.0 %collective-permute-start.6 = (f32[6,8,128]{2,1,0:T(8,128)S(1)}, f32[6,8,128]{2,1,0:T(8,128)S(1)}, u32[]{:S(2)}, u32[]{:S(2)}) collective-permute-start(f32[6,8,128]{2,1,0:T(8,128)S(1)} %edges.1.mine), channel_id=1, source_target_pairs={{0,1},{1,0},{2,3},{3,2},{4,5},{5,4},{6,7},{7,6},{8,9},{9,8},{10,11... | collective-permute-start | bytes 73736 | tf_op jit(solution)/shard_map/ppermute | solution.py:783
  35.3 1.2 %copy-start.5 = (f32[6,8,128]{2,1,0:T(8,128)}, f32[6,8,128]{2,1,0:T(8,128)S(1)}, u32[]{:S(2)}) copy-start(f32[6,8,128]{2,1,0:T(8,128)S(1)} %collective-permute-done.6.other.first) | copy-start | bytes 73732
  36.4 4.0 %collective-permute-start.7 = (f32[6,8,128]{2,1,0:T(8,128)}, f32[6,8,128]{2,1,0:T(8,128)}, u32[]{:S(2)}, u32[]{:S(2)}) collective-permute-start(f32[6,8,128]{2,1,0:T(8,128)} %mix.1.mixed), channel_id=1, source_target_pairs={{0,3},{1,2},{2,1},{3,0},{4,7},{5,6},{6,5},{7,4},{8,11},{9,10},{10,... | collective-permute-start | bytes 73736 | tf_op jit(solution)/shard_map/ppermute | solution.py:786
  40.4 0.8 %copy-start.4 = (f32[16,8,128]{2,1,0:T(8,128)S(1)}, f32[16,8,128]{2,1,0:T(8,128)}, u32[]{:S(2)}) copy-start(f32[16,8,128]{2,1,0:T(8,128)} %field.5) | copy-start | bytes 196612
  41.3 0.7 copy-start.6
  42.8 8.0 %collective-permute-start.8 = (f32[26,8,128]{2,1,0:T(8,128)S(1)}, f32[26,8,128]{2,1,0:T(8,128)S(1)}, u32[]{:S(2)}, u32[]{:S(2)}) collective-permute-start(f32[26,8,128]{2,1,0:T(8,128)S(1)} %get-tuple-element.33.field), channel_id=1, source_target_pairs={{0,4},{4,8},{8,12},{12,16},{16,20},{20,24},{24,28},{28,0},{1,5},{5... | collective-permute-start | bytes 319496 | tf_op jit(solution)/shard_map/ppermute | solution.py:807
  44.3 7.1 %collective-permute-start.9 = (f32[26,8,128]{2,1,0:T(8,128)S(1)}, f32[26,8,128]{2,1,0:T(8,128)S(1)}, u32[]{:S(2)}, u32[]{:S(2)}) collective-permute-start(f32[26,8,128]{2,1,0:T(8,128)S(1)} %get-tuple-element.33.field), channel_id=1, source_target_pairs={{4,0},{8,4},{12,8},{16,12},{20,16},{24,20},{28,24},{0,28},{5,1},{9... | collective-permute-start | bytes 319496 | tf_op jit(solution)/shard_map/ppermute | solution.py:806
  50.7 4.2 %collective-permute-start.5 = (f32[8,384]{1,0:T(8,128)S(1)}, f32[8,384]{1,0:T(8,128)S(1)}, u32[]{:S(2)}, u32[]{:S(2)}) collective-permute-start(f32[8,384]{1,0:T(8,128)S(1)} %get-tuple-element.38), channel_id=1, source_target_pairs={{0,1},{1,0},{2,3},{3,2},{4,5},{5,4},{6,7},{7,6},{8,9},{9,8},{10,11... | collective-permute-start | bytes 36872 | tf_op jit(solution)/shard_map/ppermute | solution.py:877
  54.9 0.7 copy-start.8
  55.6 1.0 %copy-start.12 = (f32[6,128,128]{2,1,0:T(8,128)S(1)}, f32[6,128,128]{2,1,0:T(8,128)}, u32[]{:S(2)}) copy-start(f32[6,128,128]{2,1,0:T(8,128)} %copy-done.11) | copy-start | bytes 1179652
  56.6 1.0 %copy-start.14 = (f32[6,128,128]{2,1,0:T(8,128)S(1)}, f32[6,128,128]{2,1,0:T(8,128)}, u32[]{:S(2)}) copy-start(f32[6,128,128]{2,1,0:T(8,128)} %copy-done.13) | copy-start | bytes 1179652
  57.6 0.7 copy-start.15
  58.3 0.7 copy-start.16
  59.0 0.7 copy-start.18
  59.7 0.7 copy-start.20
  60.4 21.6 %copy-start.10 = (f32[4]{0:T(128)S(1)}, f32[4]{0:T(128)}, u32[]{:S(2)}) copy-start(f32[4]{0:T(128)} %charge_ref.1) | copy-start | bytes 52
  61.8 4.2 %collective-permute-start.10 = (f32[48,128]{1,0:T(8,128)S(1)}, f32[48,128]{1,0:T(8,128)S(1)}, u32[]{:S(2)}, u32[]{:S(2)}) collective-permute-start(f32[48,128]{1,0:T(8,128)S(1)} %density.1), channel_id=1, source_target_pairs={{0,1},{1,0},{2,3},{3,2},{4,5},{5,4},{6,7},{7,6},{8,9},{9,8},{10,11... | collective-permute-start | bytes 73736 | tf_op jit(solution)/shard_map/ppermute | solution.py:379
  66.1 4.2 %collective-permute-start.12 = (f32[48,128]{1,0:T(8,128)S(1)}, f32[48,128]{1,0:T(8,128)S(1)}, u32[]{:S(2)}, u32[]{:S(2)}) collective-permute-start(f32[48,128]{1,0:T(8,128)S(1)} %add.21), channel_id=1, source_target_pairs={{0,4},{1,5},{2,6},{3,7},{4,0},{5,1},{6,2},{7,3},{8,12},{9,13},{10,... | collective-permute-start | bytes 73736 | tf_op jit(solution)/shard_map/ppermute | solution.py:379
  66.9 5.4 %collective-permute-start.13 = (f32[48,128]{1,0:T(8,128)S(1)}, f32[48,128]{1,0:T(8,128)S(1)}, u32[]{:S(2)}, u32[]{:S(2)}) collective-permute-start(f32[48,128]{1,0:T(8,128)S(1)} %add.21), channel_id=1, source_target_pairs={{0,6},{1,7},{2,4},{3,5},{4,2},{5,3},{6,0},{7,1},{8,14},{9,15},{10,... | collective-permute-start | bytes 73736 | tf_op jit(solution)/shard_map/ppermute | solution.py:379
  70.2 3.8 %collective-permute-start.11 = (f32[48,128]{1,0:T(8,128)S(1)}, f32[48,128]{1,0:T(8,128)S(1)}, u32[]{:S(2)}, u32[]{:S(2)}) collective-permute-start(f32[48,128]{1,0:T(8,128)S(1)} %add.21), channel_id=1, source_target_pairs={{0,2},{1,3},{2,0},{3,1},{4,6},{5,7},{6,4},{7,5},{8,10},{9,11},{10,... | collective-permute-start | bytes 73736 | tf_op jit(solution)/shard_map/ppermute | solution.py:379
  74.1 4.8 %collective-permute-start.15 = (f32[48,128]{1,0:T(8,128)S(1)}, f32[48,128]{1,0:T(8,128)S(1)}, u32[]{:S(2)}, u32[]{:S(2)}) collective-permute-start(f32[48,128]{1,0:T(8,128)S(1)} %add_add_fusion.1), channel_id=1, source_target_pairs={{0,16},{4,20},{8,24},{12,28},{16,0},{20,4},{24,8},{28,12},{1,17},{... | collective-permute-start | bytes 73736 | tf_op jit(solution)/shard_map/ppermute | solution.py:379
  76.3 5.6 %collective-permute-start.16 = (f32[48,128]{1,0:T(8,128)S(1)}, f32[48,128]{1,0:T(8,128)S(1)}, u32[]{:S(2)}, u32[]{:S(2)}) collective-permute-start(f32[48,128]{1,0:T(8,128)S(1)} %add_add_fusion.1), channel_id=1, source_target_pairs={{0,24},{4,28},{8,16},{12,20},{16,8},{20,12},{24,0},{28,4},{1,25},{... | collective-permute-start | bytes 73736 | tf_op jit(solution)/shard_map/ppermute | solution.py:379
  77.7 4.3 %collective-permute-start.14 = (f32[48,128]{1,0:T(8,128)S(1)}, f32[48,128]{1,0:T(8,128)S(1)}, u32[]{:S(2)}, u32[]{:S(2)}) collective-permute-start(f32[48,128]{1,0:T(8,128)S(1)} %add_add_fusion.1), channel_id=1, source_target_pairs={{0,8},{4,12},{8,0},{12,4},{16,24},{20,28},{24,16},{28,20},{1,9},{5... | collective-permute-start | bytes 73736 | tf_op jit(solution)/shard_map/ppermute | solution.py:379

commit v3 on v0

v3 whole, which is shorter than its diff:
```python
import functools

import jax
import jax.numpy as jnp
from jax import lax
from jax.experimental import pallas as pl
from jax.experimental.pallas import tpu as pltpu
from jax.sharding import PartitionSpec as P

ITERS = 3
F32 = jnp.float32
BF16 = jnp.bfloat16
TILE = 128
BOTH = ("energy", "slab")
REACH = 5
HALF = 64


def split(a):
    high = a.astype(BF16)
    return high, (a - high.astype(F32)).astype(BF16)


def dot(a, b, transposed):
    dims = (((1,), (1 if transposed else 0,)), ((), ()))
    return lax.dot_general(a, b, dims, preferred_element_type=F32)


def product(left, right, transposed=False):
    n = right[0].shape[0 if transposed else 1]
    wide = dot(left[0], jnp.concatenate(right, 0 if transposed else 1), transposed)
    return wide[:, :n] + (wide[:, n:] + dot(left[1], right[0], transposed))


def diagonal_row(matrix):
    rows = lax.broadcasted_iota(jnp.int32, (TILE, TILE), 0)
    columns = lax.broadcasted_iota(jnp.int32, (TILE, TILE), 1)
    parts = []
    for start in range(0, matrix.shape[0], TILE):
        block = matrix[start : start + TILE, start : start + TILE]
        parts.append(jnp.sum(jnp.where(rows == columns, block, 0.0), axis=0, keepdims=True))
    return jnp.concatenate(parts, axis=1)


PACKED_ROWS = 5 * TILE + 8


def pack(matrix, out):
    def block(i, j):
        return matrix[i * TILE : (i + 1) * TILE, j * TILE : (j + 1) * TILE]

    rows = lax.broadcasted_iota(jnp.int32, (TILE, TILE), 0)
    columns = lax.broadcasted_iota(jnp.int32, (TILE, TILE), 1)
    for place, (i, j) in enumerate(((0, 1), (0, 2), (1, 2))):
        out[place * TILE : (place + 1) * TILE, :] = block(i, j) + block(j, i).T
    one, two = (block(0, 0), block(1, 1))
    merged = jnp.where(rows < columns, one + one.T, jnp.where(rows > columns, two + two.T, one))
    out[3 * TILE : 4 * TILE, :] = merged
    out[4 * TILE : 5 * TILE, :] = block(2, 2)
    row = jnp.sum(jnp.where(rows == columns, two, 0.0), axis=0, keepdims=True)
    out[5 * TILE :, :] = jnp.broadcast_to(row, (8, TILE))


def unpack(packed, out):
    rows = lax.broadcasted_iota(jnp.int32, (TILE, TILE), 0)
    columns = lax.broadcasted_iota(jnp.int32, (TILE, TILE), 1)
    out[...] = jnp.zeros_like(out)
    for place, (i, j) in enumerate(((0, 1), (0, 2), (1, 2))):
        value = packed[place * TILE : (place + 1) * TILE, :]
        out[i * TILE : (i + 1) * TILE, j * TILE : (j + 1) * TILE] = value
    merged = packed[3 * TILE : 4 * TILE, :]
    row = packed[5 * TILE : 5 * TILE + 1, :]
    out[:TILE, :TILE] = jnp.where(rows <= columns, merged, 0.0)
    out[TILE : 2 * TILE, TILE : 2 * TILE] = jnp.where(
        rows > columns, merged, jnp.where(rows == columns, row, 0.0)
    )
    out[2 * TILE :, 2 * TILE :] = packed[4 * TILE : 5 * TILE, :]


def pair_kernel(index_ref, iso, coupling, lead, cells, own, near, first, sent, c_buf, g_buf, lead_buf, row, sems):
    place = index_ref[0]
    core = lax.rem(place, 2)
    n = lead_buf.shape[1]
    sources = []
    for slab in range(2):
        sources.append((coupling.at[slab], c_buf.at[slab]))
        for turn, energy in enumerate((core, 1 - core)):
            sources.append((iso.at[energy, slab], g_buf.at[turn, slab]))
    for turn, energy in enumerate((core, 1 - core)):
        sources.append((lead.at[energy], lead_buf.at[turn]))
    copies = [pltpu.make_async_copy(src, dst, sems.at[i]) for i, (src, dst) in enumerate(sources)]
    for copy in copies:
        copy.start()
    atoms = cells.shape[1]
    row[...] = jnp.zeros_like(row)
    row[0:1, 0:atoms] = cells[0:1, :].astype(F32)
    row[0:1, HALF : HALF + atoms] = cells[1:2, :].astype(F32)
    rows = lax.broadcasted_iota(jnp.int32, (8, TILE), 0)
    for ref in (own, sent):
        ref[2 * n + 8 :, 0:TILE] = jnp.where(rows == place, row[0:1, :], 0.0)
        ref[2 * n + 8 :, TILE:] = jnp.zeros((8, n - TILE), F32)
    steps = []
    for slab in range(2):
        for copy in copies[3 * slab : 3 * slab + 3]:
            copy.wait()
        parts = split(c_buf[slab])
        steps.append([product(split(g_buf[turn, slab]), parts) for turn in range(2)])
    for copy in copies[6:]:
        copy.wait()
    outputs = (own, sent)

    @pl.when(place == 0)
    def _():
        parts = [[split(steps[slab][turn]) for turn in range(2)] for slab in range(2)]
        states = [lead_buf[turn] for turn in range(2)]
        for slab in range(2):
            states = [product(parts[slab][turn], split(states[turn])) for turn in range(2)]
            states = [
                product(split(states[turn]), parts[slab][turn], True) + g_buf[turn, slab]
                for turn in range(2)
            ]
            for turn in range(2):
                outputs[turn][2 * n + slab : 2 * n + slab + 1, :] = diagonal_row(states[turn])
        for turn in range(2):
            outputs[turn][n : 2 * n, :] = states[turn]

    @pl.when(place != 0)
    def _():
        early = [split(steps[0][turn]) for turn in range(2)]
        later = [split(steps[1][turn]) for turn in range(2)]
        terms = [product(later[turn], split(g_buf[turn, 0])) for turn in range(2)]
        maps = [product(later[turn], early[turn]) for turn in range(2)]
        terms = [product(split(terms[turn]), later[turn], True) + g_buf[turn, 1] for turn in range(2)]
        for turn in range(2):
            outputs[turn][0:n, :] = maps[turn]
            outputs[turn][n : 2 * n, :] = terms[turn]
            outputs[turn][2 * n : 2 * n + 1, :] = diagonal_row(g_buf[turn, 0])
            outputs[turn][2 * n + 1 : 2 * n + 2, :] = diagonal_row(terms[turn])
        near[...] = steps[0][0]
        first[...] = steps[0][1]


def advance(map_ref, state):
    n = map_ref.shape[1]
    composed = split(map_ref[0:n, :])
    term = product(composed, split(state))
    return product(split(term), composed, True) + map_ref[n : 2 * n, :]


def relay_kernel(index_ref, own, got, field, left, right, out, first, second):
    place = index_ref[0]
    n = own.shape[1]
    length, rows, depth = field.shape
    even = lax.rem(place, 2) == 0
    for part, block in enumerate((left, field, right)):
        low = block[:REACH].reshape(REACH * rows, depth)
        high = block[length - REACH :].reshape(REACH * rows, depth)
        first[:, part * depth : (part + 1) * depth] = jnp.where(even, high, low)
        second[: REACH * rows, part * depth : (part + 1) * depth] = jnp.where(even, low, high)
    second[REACH * rows :, :] = jnp.zeros((8, n), F32)
    second[REACH * rows :, :TILE] = own[2 * n + 8 :, :TILE] + got[2 * n + 8 :, :TILE]

    @pl.when(place == 0)
    def _():
        pack(advance(got, own[n : 2 * n, :]), out)

    @pl.when(place == 1)
    def _():
        pack(advance(own, got[n : 2 * n, :]), out)


def pass_kernel(turn, index_ref, packed, own, got, out, state):
    place = index_ref[0]
    for core, (near, far) in enumerate(((own, got), (got, own))):

        @pl.when(place == 2 * turn + core)
        def _():
            unpack(packed, state)
            state[...] = advance(near, state[...])
            pack(advance(far, state[...]), out)


def density_kernel(
    pairs,
    index_ref,
    weight_ref,
    group_ref,
    orbital_atom,
    member,
    packed,
    own,
    got,
    own_step,
    got_step,
    extra,
    out,
    state,
    fold,
):
    place = index_ref[0]
    core = lax.rem(place, 2)
    n = state.shape[0]
    atoms = lax.broadcasted_iota(jnp.int32, (TILE, n), 0)
    spots = (atoms == orbital_atom[...]).astype(BF16)

    def folded(matrix, parts):
        both = matrix * product(split(matrix), parts)
        return jnp.sum(jnp.sum(both, axis=1, keepdims=True) * member[...], axis=0, keepdims=True)

    for number, (near, near_step, far, far_step) in enumerate(
        ((own, own_step, got, got_step), (got, got_step, own, own_step))
    ):

        @pl.when(core == number)
        def _():
            rest = jnp.concatenate(
                [near[2 * n : 2 * n + 2, :], far[2 * n : 2 * n + 2, :], jnp.zeros((4, n), F32)],
                axis=0,
            )
            total = jnp.zeros((8, TILE), F32)
            for _ in range(3):
                piece = rest.astype(BF16)
                total = total + dot(piece, spots, True)
                rest = rest - piece.astype(F32)
            fold[...] = total

            @pl.when(place < 2)
            def _():
                state[...] = near[n : 2 * n, :]

            @pl.when(place >= 2)
            def _():
                unpack(packed, state)
                parts = split(state[...])
                fold[0:1, :] += folded(near_step[...], parts)
                matrix = near[0:n, :]
                composed = split(matrix)
                term = product(composed, parts)
                value = jnp.sum(matrix * term, axis=1, keepdims=True) * member[...]
                fold[1:2, :] += jnp.sum(value, axis=0, keepdims=True)
                state[...] = product(split(term), composed, True) + near[n : 2 * n, :]

            parts = split(state[...])
            fold[2:3, :] += folded(far_step[...], parts)
            fold[3:4, :] += folded(far[0:n, :], parts)

    plain = fold[...]
    turned = pltpu.roll(plain, HALF, 1)
    pair_rows = lax.broadcasted_iota(jnp.int32, (pairs, TILE), 0)
    groups = (out.shape[0] - extra.shape[0]) // pairs
    for group in range(groups):
        weight = jnp.where(group_ref[core] == group, weight_ref[core], 0.0)
        block = jnp.zeros((pairs, TILE), F32)
        for half in range(2):
            value = plain[2 * half : 2 * half + 1, :] + turned[2 * half + 1 : 2 * half + 2, :]
            block = block + jnp.where(pair_rows == place - core + half, weight, 0.0) * value
        out[group * pairs : (group + 1) * pairs, :] = block
    out[groups * pairs :, :] = extra[...]


def local_call(kernel, shapes, scratch, specs, name, limit, flops, *operands):
    spaces = {"v": pltpu.VMEM, "s": pltpu.SMEM, "h": pltpu.HBM}
    single = not isinstance(shapes, tuple)
    vmem = pl.BlockSpec(memory_space=pltpu.VMEM)
    return pl.pallas_call(
        kernel,
        out_shape=shapes,
        in_specs=[pl.BlockSpec(memory_space=spaces[spec]) for spec in specs],
        out_specs=vmem if single else (vmem,) * len(shapes),
        scratch_shapes=scratch,
        compiler_params=pltpu.CompilerParams(vmem_limit_bytes=limit * 2**20),
        cost_estimate=pl.CostEstimate(flops=flops, bytes_accessed=2**20, transcendentals=0),
        name=name,
    )(*operands)


def shifted_pair(x, axis):
    size = x.shape[axis]
    before, after = (pltpu.roll(x, 1, axis), pltpu.roll(x, size - 1, axis))
    if axis == x.ndim - 1:
        lanes = lax.broadcasted_iota(jnp.int32, x.shape, axis)
        before = jnp.where(lanes == 0, 0.0, before)
        after = jnp.where(lanes == size - 1, 0.0, after)
    return before, after


def neighbours(x):
    centre = x[1:-1]
    up, down = shifted_pair(centre, 1)
    left, right = shifted_pair(centre, 2)
    return (x[2:] + x[:-2]) + (up + down) + (left + right)


def differences(x):
    centre = x[1:-1]
    up, down = shifted_pair(centre, 1)
    left, right = shifted_pair(centre, 2)
    along = (x[2:] - centre) + (x[:-2] - centre)
    across = (up - centre) + (down - centre)
    deep = (left - centre) + (right - centre)
    return along + (across + deep)


def grid_mask(shape, margin, length, rows, place, devices, wire, wires):
    planes = lax.broadcasted_iota(jnp.int32, shape, 0)
    row = lax.broadcasted_iota(jnp.int32, shape, 1)
    low_x = jnp.where(place == 0, margin, 0)
    high_x = jnp.where(place == devices - 1, margin + length, shape[0])
    low_y = jnp.where(wire == 0, rows, 0)
    high_y = jnp.where(wire == wires - 1, 2 * rows, shape[1])
    inside = (planes >= low_x) & (planes < high_x) & (row >= low_y) & (row < high_y)
    return inside.astype(F32)


def three_parts(x):
    parts = []
    for _ in range(3):
        parts.append(x.astype(BF16))
        x = x - parts[-1].astype(F32)
    return parts


def coordinates(cell, rows_y, depth):
    z_part = cell - depth * jnp.floor(cell * (1.0 / depth))
    plane = jnp.floor(cell * (1.0 / depth))
    x_part = jnp.floor(plane * (1.0 / rows_y))
    return x_part, plane - rows_y * x_part, z_part


WALKS = ((0, 1),), ((1, 1),), ((0, 2), (2, 1)), ((1, 3), (3, 1)), ((0, 6), (2, 4), (4, 1)), ((1, 10), (3, 5), (5, 1))
FACTORIAL = (1.0, 1.0, 2.0, 6.0, 24.0, 120.0)


def walk_counts(here, there, length):
    apart = jnp.abs(here - there)
    low = here + there + 2.0
    high = 2.0 * length - here - there
    at = []
    for steps in range(6):
        value = (apart == steps).astype(F32)
        if steps >= 2:
            value = value - (low == steps).astype(F32) - (high == steps).astype(F32)
        at.append(value)
    counts = []
    for steps, terms in enumerate(WALKS):
        total = None
        for distance, count in terms:
            term = at[distance] * (count / FACTORIAL[steps])
            total = term if total is None else total + term
        counts.append(total)
    return counts


def convolved(left, right):
    result = []
    for steps in range(6):
        total = left[0] * right[steps]
        for part in range(1, steps + 1):
            total = total + left[part] * right[steps - part]
        result.append(total)
    return result


def prepare_kernel(
    devices,
    wires,
    index_ref,
    orbital_atom,
    own,
    field,
    left,
    right,
    first,
    second,
    all_cells,
    out,
    walks,
    row_hot,
    deep_hot,
    member,
    wide_field,
):
    place, wire = (index_ref[0], index_ref[1])
    length, rows, depth = field.shape
    planes = length + 2 * REACH
    width_x = length // 2
    atoms = walks.shape[1] // (2 * devices)
    grid_y = rows * wires
    pairs = devices
    n = orbital_atom.shape[1]
    even = lax.rem(place, 2) == 0
    edges = REACH * rows
    before = jnp.where(even, second[:edges, :], first[...])
    after = jnp.where(even, first[...], second[:edges, :])

    def block_of(x, part):
        return x[:, part * depth : (part + 1) * depth].reshape(REACH, rows, depth)

    columns = [
        jnp.concatenate([block_of(before, part), block[...], block_of(after, part)], axis=0)
        for part, block in enumerate((left, field, right))
    ]
    whole = (planes, 3 * rows, depth)
    mask = grid_mask(whole, REACH, length, rows, place, devices, wire, wires)
    source = jnp.concatenate(columns, axis=1) * mask
    margin = ITERS - 1
    wide_field[...] = source[REACH - margin : REACH + length + margin]
    spots = lax.broadcasted_iota(jnp.int32, (TILE, n), 0) == orbital_atom[...]
    spots = spots.astype(F32)
    for start in range(0, n, TILE):
        member[start : start + TILE, :] = spots[:, start : start + TILE].T
    if devices > 4:
        cells = all_cells[...]
    else:
        cells = second[edges:, :depth] + all_cells[...]

    def inner(x):
        extra = (x.shape[0] - length) // 2
        return x[extra : extra + length, rows : 2 * rows]

    chain = [source]
    for step in range(1, 6):
        chain.append(neighbours(chain[-1]) * mask[step : planes - step])
    blocks = [inner(x) for x in chain]
    near = source[2:-2]
    other = [near]
    for step in range(1, 4):
        other.append(differences(other[-1]) * mask[2 + step : planes - 2 - step])
    other = [inner(x) for x in other]
    lanes = lax.broadcasted_iota(jnp.int32, (8, depth), 1)
    sums = jnp.zeros((8, depth), F32)
    for base, fields in enumerate((blocks, other)):
        for steps in range(6):
            part = jnp.sum(fields[steps // 2] * fields[(steps + 1) // 2], axis=0)
            part = jnp.sum(jnp.sum(part, axis=1, keepdims=True), axis=0, keepdims=True)
            sums = jnp.where(lanes == 8 * base + steps, part, sums)
    out[...] = jnp.zeros_like(out)
    out[6 * pairs : 6 * pairs + 8, :] = sums
    mine = own[2 * n + 8 :, :depth]
    mine = jnp.sum(mine, axis=0, keepdims=True)
    lane = lax.broadcasted_iota(jnp.int32, (1, depth), 1)
    odd = (lane >= HALF).astype(F32)
    used = lax.rem(lane, HALF) < atoms
    x_part, y_part, z_part = coordinates(mine, grid_y, depth)
    start = (wire * rows).astype(F32)
    ours = used & (y_part >= start) & (y_part < start + rows)
    at_row = jnp.where(ours, (x_part + width_x * odd) * rows + y_part - start, -1.0)
    cell_rows = length * rows
    row_iota = lax.broadcasted_iota(jnp.int32, (cell_rows, depth), 0).astype(F32)
    deep_iota = lax.broadcasted_iota(jnp.int32, (depth, depth), 0).astype(F32)
    at_rows = (row_iota == at_row).astype(F32)
    at_deep = (deep_iota == z_part).astype(BF16)
    for steps, block in enumerate(blocks):
        value = jnp.zeros((cell_rows, depth), F32)
        for part in three_parts(block.reshape(cell_rows, depth)):
            value = value + dot(part, at_deep, False)
        value = jnp.sum(value * at_rows, axis=0, keepdims=True)
        out[pl.ds(steps * pairs + place, 1), :] = value
    row_cells = cells
    row_x, row_y, row_z = coordinates(row_cells, grid_y, depth)
    padded = jnp.concatenate([row_cells, jnp.zeros((depth - 8, depth), F32)], axis=0)
    column_x, column_y, column_z = coordinates(padded.T, grid_y, depth)
    row_lane = lax.broadcasted_iota(jnp.int32, (8, depth), 1)
    next_x, next_y, next_z = [jnp.concatenate([v[1:], v[:1]], axis=0) for v in (row_x, row_y, row_z)]

    def turned(now, later, step_now, step_later):
        value = jnp.where(row_lane >= HALF, now + step_now, later + step_later)
        return pltpu.roll(value, HALF, 1)

    even_x = row_x + width_x * (row_lane >= HALF).astype(F32)
    odd_x, odd_y, odd_z = (
        turned(row_x, next_x, 0.0, float(width_x)),
        turned(row_y, next_y, 0.0, 0.0),
        turned(row_z, next_z, 0.0, 0.0),
    )
    for slab in range(2 * pairs):
        pair, side = (slab // 2, slab % 2)
        base = float(slab * width_x)
        if side:
            there = (odd_x, odd_y, odd_z)
        else:
            there = (even_x, row_y, row_z)
        there = [v[pair : pair + 1, :] for v in there]
        here = [
            v[side * HALF : side * HALF + atoms, pair : pair + 1]
            for v in (column_x, column_y, column_z)
        ]
        shape = (atoms, depth)
        sizes = (2 * pairs * width_x, grid_y, depth)
        axes = []
        for axis in range(3):
            shift = base if axis == 0 else 0.0
            axes.append(
                walk_counts(
                    jnp.broadcast_to(here[axis] + shift, shape),
                    jnp.broadcast_to(there[axis] + shift, shape),
                    float(sizes[axis]),
                )
            )
        total = convolved(convolved(axes[0], axes[1]), axes[2])
        for steps in range(6):
            walks[steps, slab * atoms : (slab + 1) * atoms, :] = total[steps] * FACTORIAL[steps]
    wide = length + 4
    first_x = (place * length - 2).astype(F32)
    first_y = start - rows
    count = wide * 3 * rows
    rows_iota = lax.broadcasted_iota(jnp.int32, (count, depth), 0).astype(F32)
    used_row = lax.rem(row_lane, HALF) < atoms
    for pair in range(pairs):
        x_at = even_x[pair : pair + 1, :] + float(2 * pair * width_x) - first_x
        y_at = row_y[pair : pair + 1, :] - first_y
        good = (x_at >= 0) & (x_at < wide) & (y_at >= 0) & (y_at < 3 * rows) & used_row[0:1, :]
        target = jnp.where(good, x_at * (3 * rows) + y_at, -1.0)
        row_hot[:, pair * depth : (pair + 1) * depth] = (rows_iota == target).astype(BF16)
        z_at = column_z[:, pair : pair + 1]
        lanes_z = lax.broadcasted_iota(jnp.int32, (depth, depth), 1).astype(F32)
        deep_hot[pair * depth : (pair + 1) * depth, :] = (lanes_z == z_at).astype(F32)


def total_of(x):
    return jnp.sum(jnp.sum(x, axis=1, keepdims=True), axis=0, keepdims=True)


def quadratic_form(poly, moments, shift):
    total = None
    for i, one in enumerate(poly):
        for j, two in enumerate(poly):
            if j < i:
                continue
            term = one * two * moments[i + j + shift] * (1.0 if i == j else 2.0)
            total = term if total is None else total + term
    return total


def finish_kernel(
    devices,
    wires,
    atoms,
    index_ref,
    charge_ref,
    payload,
    walks,
    row_hot,
    deep_hot,
    field,
    density,
    potential,
):
    place, wire = (index_ref[0], index_ref[1])
    length, rows, depth = potential.shape
    pairs = devices
    groups = density.shape[0]
    charge = charge_ref[0] * payload[0:pairs, :]
    for group in range(1, groups):
        charge = charge + charge_ref[group] * payload[group * pairs : (group + 1) * pairs, :]
    for group in range(groups):
        value = payload[pl.ds(group * pairs + place, 1), :]
        density[group, 0:1, :] = value[:, :atoms]
        density[group, 1:2, :] = pltpu.roll(value, HALF, 1)[:, :atoms]
    square = jnp.concatenate([charge, jnp.zeros((depth - pairs, depth), F32)], axis=0)
    columns = square.T
    later = jnp.concatenate([charge[1:], jnp.zeros((1, depth), F32)], axis=0)
    lanes = lax.broadcasted_iota(jnp.int32, (pairs, depth), 1)
    even_row = jnp.where(lanes >= HALF, 2.0 * charge, charge)
    odd_row = pltpu.roll(jnp.where(lanes >= HALF, charge, 2.0 * later), HALF, 1)
    totals = [None] * 6
    for slab in range(2 * pairs):
        pair, side = (slab // 2, slab % 2)
        row = (odd_row if side else even_row)[pair : pair + 1, :]
        column = columns[side * HALF : side * HALF + atoms, pair : pair + 1]
        outer = column * row
        for steps in range(6):
            term = walks[steps, slab * atoms : (slab + 1) * atoms, :] * outer
            totals[steps] = term if totals[steps] is None else totals[steps] + term
    base = groups * pairs
    crossed = []
    for steps in range(6):
        cross = 2.0 * charge * payload[base + steps * pairs : base + (steps + 1) * pairs, :]
        crossed.append(total_of(totals[steps]) + total_of(cross))
    sums = payload[base + 6 * pairs : base + 6 * pairs + 1, :]
    plain = [sums[:, steps : steps + 1] + crossed[steps] for steps in range(6)]
    moved = []
    for steps in range(6):
        value = sums[:, 8 + steps : 9 + steps]
        binomial = 1
        for part in range(steps, -1, -1):
            value = value + (binomial * (-6.0) ** (steps - part)) * crossed[part]
            binomial = binomial * part // (steps - part + 1)
        moved.append(value)
    smooth = plain[1] > 3.5 * plain[0]
    level = jnp.where(smooth, 0.5, 6.5)
    moments = [jnp.where(smooth, two, one) for one, two in zip(plain, moved)]
    residual, direction = ([jnp.ones_like(level)], [jnp.ones_like(level)])
    norm = moments[0]
    alphas, betas = ([], [])
    for turn in range(ITERS):
        energy = level * quadratic_form(direction, moments, 0) - quadratic_form(direction, moments, 1)
        alpha = norm / energy
        alphas.append(alpha)
        if turn + 1 == ITERS:
            break
        longer = residual + [jnp.zeros_like(level)]
        for i, value in enumerate(direction):
            longer[i] = longer[i] - alpha * level * value
            longer[i + 1] = longer[i + 1] + alpha * value
        residual = longer
        following = quadratic_form(residual, moments, 0)
        beta = following / norm
        betas.append(beta)
        norm = following
        direction = [
            value + beta * direction[i] if i < len(direction) else value
            for i, value in enumerate(residual)
        ]
    pieces = [[], [], []]
    for pair in range(pairs):
        hot = deep_hot[pair * depth : (pair + 1) * depth, :]
        for place_in, piece in enumerate(three_parts(columns[:, pair : pair + 1] * hot)):
            pieces[place_in].append(piece)
    spread = jnp.concatenate([jnp.concatenate(piece, axis=0) for piece in pieces], axis=1)
    placed = dot(row_hot[...], spread, False)
    placed = placed[:, :depth] + (placed[:, depth : 2 * depth] + placed[:, 2 * depth :])
    margin = ITERS - 1
    wide = (length + 2 * margin, 3 * rows, depth)
    mask = grid_mask(wide, margin, length, rows, place, devices, wire, wires)
    source = field[...] + placed.reshape(wide)
    residual, direction = (source, source)
    total = alphas[0] * source[margin:-margin, rows : 2 * rows]
    for turn in range(ITERS - 1):
        image = 6.5 * direction[1:-1] - neighbours(direction)
        inner_mask = mask[turn + 1 : wide[0] - turn - 1]
        residual = (residual[1:-1] - alphas[turn] * image) * inner_mask
        direction = residual + betas[turn] * direction[1:-1]
        extra = margin - turn - 1
        block = direction[extra : extra + length, rows : 2 * rows]
        total = total + alphas[turn + 1] * block
    potential[...] = total


def hop(count, turn):
    moves = {i: i for i in range(count)}
    for core in range(2):
        here, there = (2 * turn - 2 + core, 2 * turn + core)
        moves[here], moves[there] = (there, here)
    return sorted(moves.items())


def pairs_of(count):
    return [(i, i ^ 1) for i in range(count)]


def total_over(value, axis, strides):
    size = 1
    for name in axis if isinstance(axis, tuple) else (axis,):
        size *= lax.axis_size(name)
    got = [lax.ppermute(value, axis, [(i, i ^ k) for i in range(size)]) for k in strides]
    if len(got) == 1:
        return value + got[0]
    return (value + got[0]) + (got[1] + got[2])


def total_over_all(value):
    wires, slabs = (lax.axis_size("energy"), lax.axis_size("slab"))
    value = total_over(value, "slab", (1,))
    stride = 2
    while stride * 2 < slabs:
        value = total_over(value, "slab", (stride,))
        stride *= 2
    value = total_over(value, BOTH, (stride, slabs, stride + slabs))
    stride = 2
    while stride * 4 <= wires:
        value = total_over(value, "energy", (stride, 2 * stride, 3 * stride))
        stride *= 4
    if stride < wires:
        value = total_over(value, "energy", (stride,))
    return value


def neighbour_turn(count):
    return [(i, (i + 1) % count if i % 2 else (i - 1) % count) for i in range(count)]


def on_device(
    green_iso,
    coupling,
    lead_green,
    energy_weight,
    energy_group,
    group_charge,
    orbital_atom,
    atom_cell,
    doping,
):
    devices, wires = (lax.axis_size("slab"), lax.axis_size("energy"))
    groups = group_charge.shape[0]
    atoms = atom_cell.shape[1]
    n = lead_green.shape[-1]
    length, rows, depth = doping.shape
    shape = jax.ShapeDtypeStruct
    index = jnp.stack([lax.axis_index("slab"), lax.axis_index("energy")]).astype(jnp.int32)
    orbital_row = orbital_atom.reshape(1, n)
    maps = shape((2 * n + 16, n), F32)
    own, own_step, sent_step, sent = local_call(
        pair_kernel,
        (maps, shape((n, n), F32), shape((n, n), F32), maps),
        [
            pltpu.VMEM((2, n, n), F32),
            pltpu.VMEM((2, 2, n, n), F32),
            pltpu.VMEM((2, n, n), F32),
            pltpu.VMEM((8, TILE), F32),
            pltpu.SemaphoreType.DMA((8,)),
        ],
        "shhhv",
        "pair",
        28,
        72 * n**3,
        index,
        green_iso,
        coupling,
        lead_green,
        atom_cell,
    )
    got = lax.ppermute(sent, "slab", pairs_of(devices))
    left = lax.ppermute(doping, "energy", [(i, (i + 1) % wires) for i in range(wires)])
    right = lax.ppermute(doping, "energy", [((i + 1) % wires, i) for i in range(wires)])
    planes = REACH * rows
    passed, first, second = local_call(
        relay_kernel,
        (shape((PACKED_ROWS, TILE), F32), shape((planes, n), F32), shape((planes + 8, n), F32)),
        [],
        "svvvvv",
        "relay",
        20,
        12 * n**3,
        index,
        own,
        got,
        doping,
        left,
        right,
    )
    second_in = lax.ppermute(second, "slab", neighbour_turn(devices))
    packed = lax.ppermute(passed, "slab", hop(devices, 1))
    first_in = lax.ppermute(first, "slab", pairs_of(devices))
    got_step = lax.ppermute(sent_step, "slab", pairs_of(devices))
    cells = second[planes:, :depth]
    if devices > 4:
        cells = lax.psum(own[2 * n + 8 :, :depth], "slab")
    wide = (length + 2 * ITERS - 2, 3 * rows, depth)
    extra, walks, row_hot, deep_hot, member, wide_field = local_call(
        functools.partial(prepare_kernel, devices, wires),
        (
            shape((6 * devices + 8, depth), F32),
            shape((6, 2 * devices * atoms, depth), F32),
            shape((wide[0] * wide[1], devices * depth), BF16),
            shape((devices * depth, depth), F32),
            shape((n, TILE), F32),
            shape(wide, F32),
        ),
        [],
        "svvvvvvvv",
        "prepare",
        28,
        2**30,
        index,
        orbital_row,
        own,
        doping,
        left,
        right,
        first_in,
        second_in,
        cells,
    )
    for turn in range(1, devices // 2 - 1):
        passed = local_call(
            functools.partial(pass_kernel, turn),
            shape((PACKED_ROWS, TILE), F32),
            [pltpu.VMEM((n, n), F32)],
            "svvv",
            "pass_on",
            20,
            24 * n**3,
            index,
            packed,
            own,
            got,
        )
        arrived = lax.ppermute(passed, "slab", hop(devices, turn + 1))
        packed = jnp.where(index[0] // 2 == turn + 1, arrived, packed)
    payload = local_call(
        functools.partial(density_kernel, devices),
        shape(((groups + 6) * devices + 8, TILE), F32),
        [pltpu.VMEM((n, n), F32), pltpu.VMEM((8, TILE), F32)],
        "sssvvvvvvvv",
        "density",
        20,
        30 * n**3,
        index,
        energy_weight,
        energy_group,
        orbital_row,
        member,
        packed,
        own,
        got,
        own_step,
        got_step,
        extra,
    )
    payload = total_over_all(payload)
    return local_call(
        functools.partial(finish_kernel, devices, wires, atoms),
        (shape((groups, 2, atoms), F32), shape(doping.shape, F32)),
        [],
        "ssvvvvv",
        "finish",
        28,
        2**29,
        index,
        group_charge,
        payload,
        walks,
        row_hot,
        deep_hot,
        wide_field,
    )


def solution(mesh):
    in_specs = (
        P("energy", "slab", None, None),
        P("slab", None, None),
        P("energy", None, None),
        P("energy"),
        P("energy"),
        P(),
        P(),
        P("slab", None),
        P("slab", "energy", None),
    )
    out_specs = (P(None, "slab", None), P("slab", "energy", None))
    return jax.shard_map(
        on_device, mesh=mesh, in_specs=in_specs, out_specs=out_specs, check_vma=False
    )
```

time: 403 us -> 61.5 us (0.15)
  blocking collectives: 155 us -> 0 us
  local copies, waits for them, and re-layouts: 91.9 us -> 4.91 us
  starting transfers between devices: 69.1 us -> 18.7 us
  matrix products: 47.3 us -> 0 us
  Pallas kernels: 0 us -> 17.7 us
  between operations: 10.7 us -> 0.78 us
  other arithmetic: 9.83 us -> 0.1 us
    psum x4 -> x0, blocking collectives: 155 us -> none  [the longest x3 134 us: two_products(): lax.psum((jnp.sum(residual * residual), jnp.sum(residual * image)), ('ene...]
    add x2 -> x0, local copies, waits for them, and re-layouts: 71 us -> none  [affine(): matprod(matprod(propagator, state), jnp.swapaxes(propagator, -1, -2))]
    ppermute x15 -> x14, starting transfers between devices: 69.1 us -> 18.7 us  [the longest x7 9.95 us: total_over(): lax.ppermute(value, axis, [(i, i ^ k) for i in range(size)])]
    dot_general x17 -> x0, matrix products: 47.3 us -> none  [the longest x14 46.7 us: matprod(): return jnp.matmul(left, right, precision=lax.Precision.HIGHEST)]
    pallas_call x0 -> x5, Pallas kernels: none -> 17.7 us  [local_call(): pl.pallas_call(kernel, out_shape=shapes, in_specs=[pl.BlockSpec(memory_sp...]
    gather x2 -> x0, local copies, waits for them, and re-layouts: 16.6 us -> none  [on_device(): diagonals.append(jnp.diagonal(state, axis1=1, axis2=2))]
    select_n x5 -> x0, other arithmetic: 5.6 us -> none  [the longest x3 4.17 us: relay_turn(): return jnp.where(leftmost, lead_green, arrived)]
    ppermute x15 -> x14, waiting for transfers between devices: 16.4 us -> 19 us  [the longest x7 6.47 us: total_over(): lax.ppermute(value, axis, [(i, i ^ k) for i in range(size)])]
  transfers between devices with their start and end apart: 15 -> 14, of which waited for: 9 -> 10; matrix products, arithmetic and copies ran while one was open for 0% -> 0% of each run, Pallas kernels for 0% -> 9%
where the time goes in v3:
time: 61.5 us; the launch traced here: 61.2 us
  waiting for transfers between devices  19 us (31%)
  starting transfers between devices  18.7 us (30%)
  Pallas kernels  17.7 us (29%)
  local copies, waits for them, and re-layouts  4.91 us (8%)
  between operations  0.78 us (1%)
    pallas_call x5, Pallas kernels, local_call(): pl.pallas_call(kernel, out_shape=shapes, in_specs=[pl.BlockSpec(memory_sp...  17.7 us
    ppermute x7, starting transfers between devices, total_over(): lax.ppermute(value, axis, [(i, i ^ k) for i in range(size)])  9.95 us
    ppermute x7, waiting for transfers between devices, total_over(): lax.ppermute(value, axis, [(i, i ^ k) for i in range(size)])  6.47 us
    ppermute x1, starting transfers between devices, on_device(): lax.ppermute(doping, 'energy', [((i + 1) % wires, i) for i in range(wires)])  5.98 us
    ppermute x1, waiting for transfers between devices, on_device(): lax.ppermute(doping, 'energy', [(i, (i + 1) % wires) for i in range(wires)])  5.06 us
    unnamed x18, local copies, waits for them, and re-layouts  4.91 us
    ppermute x1, waiting for transfers between devices, on_device(): second_in = lax.ppermute(second, 'slab', neighbour_turn(devices))  4.69 us
    ppermute x1, starting transfers between devices, on_device(): first_in = lax.ppermute(first, 'slab', pairs_of(devices))  2.05 us
  transfers between devices with their start and end apart: 14, of which 10 were waited for; matrix products, arithmetic and copies ran while one was open for 0% of the time, Pallas kernels for 9%

profile of v3, /device:TPU:0, one launch (start us, length us, event | category | flops | bytes accessed | tf_op | source)
XLA Modules:
  0.0 61.2 jit_solution(4521387429077560315)
XLA Ops:
  0.6 0.1 pad_add_fusion.index_ref
  0.7 0.0 copy-start.2
  0.7 1.7 %copy-done.2 = f32[2,2,384,384]{3,2,1,0:T(8,128)S(1)} copy-done((f32[2,2,384,384]{3,2,1,0:T(8,128)S(1)}, f32[2,2,384,384]{3,2,1,0:T(8,128)}, u32[]{:S(2)}) %copy-start.2) | copy-done | bytes 2359320
  2.4 0.0 copy-start.3
  2.4 1.3 %copy-done.3 = f32[2,384,384]{2,1,0:T(8,128)S(1)} copy-done((f32[2,384,384]{2,1,0:T(8,128)S(1)}, f32[2,384,384]{2,1,0:T(8,128)}, u32[]{:S(2)}) %copy-start.3) | copy-done | bytes 1179672
  3.6 0.0 copy-start.4
  3.6 1.3 %copy-done.4 = f32[2,384,384]{2,1,0:T(8,128)S(1)} copy-done((f32[2,384,384]{2,1,0:T(8,128)S(1)}, f32[2,384,384]{2,1,0:T(8,128)}, u32[]{:S(2)}) %copy-start.4) | copy-done | bytes 1179672
  4.9 0.0 copy-start.5
  4.9 0.7 %copy-done.5 = s32[2,48]{1,0:T(2,128)S(1)} copy-done((s32[2,48]{1,0:T(2,128)S(1)}, s32[2,48]{1,0:T(2,128)}, u32[]{:S(2)}) %copy-start.5) | copy-done | bytes 408
  5.6 0.0 copy-start
  5.6 8.1 %pair.1 = (f32[784,384]{1,0:T(8,128)S(1)}, f32[384,384]{1,0:T(8,128)S(1)}, f32[384,384]{1,0:T(8,128)S(1)}, f32[784,384]{1,0:T(8,128)S(1)}) custom-call(s32[2]{0:T(128)S(1)} %pad_add_fusion.index_ref, f32[2,2,384,384]{3,2,1,0:T(8,128)S(1)} %copy-done.2, f32[2,384,384]{2,1,0:T(8,128)S(1)} %copy-done.3, f32[2,384,384]{2,1,0:T(8,128)S(1)} %copy-done.4, ...), custom_call_target="tpu_custom_call" | custom-call | flops 4076863488 | bytes 1048576 | tf_op jit(solution)/shard_map/pair/pallas_call | solution.py:265
  13.7 0.1 collective-permute-start.2
  13.8 0.5 collective-permute-start.6
  14.3 0.0 copy-done
  14.3 6.0 %collective-permute-start.1 = (f32[16,8,128]{2,1,0:T(8,128)S(1)}, f32[16,8,128]{2,1,0:T(8,128)S(1)}, u32[]{:S(2)}, u32[]{:S(2)}) collective-permute-start(f32[16,8,128]{2,1,0:T(8,128)S(1)} %copy-done), channel_id=1, source_target_pairs={{4,0},{8,4},{12,8},{16,12},{20,16},{24,20},{28,24},{0,28},{5,1},{9... | collective-permute-start | bytes 196616 | tf_op jit(solution)/shard_map/ppermute | solution.py:725
  20.2 0.0 collective-permute-start
  20.2 1.9 %collective-permute-done.1.right = f32[16,8,128]{2,1,0:T(8,128)S(1)} collective-permute-done((f32[16,8,128]{2,1,0:T(8,128)S(1)}, f32[16,8,128]{2,1,0:T(8,128)S(1)}, u32[]{:S(2)}, u32[]{:S(2)}) %collective-permute-start.1) | collective-permute-done | bytes 65568 | tf_op jit(solution)/shard_map/ppermute | solution.py:725
  22.1 5.1 %collective-permute-done.left = f32[16,8,128]{2,1,0:T(8,128)S(1)} collective-permute-done((f32[16,8,128]{2,1,0:T(8,128)S(1)}, f32[16,8,128]{2,1,0:T(8,128)S(1)}, u32[]{:S(2)}, u32[]{:S(2)}) %collective-permute-start) | collective-permute-done | bytes 65568 | tf_op jit(solution)/shard_map/ppermute | solution.py:724
  27.2 0.0 collective-permute-done.2.got
  27.2 0.0 copy-start.8
  27.2 2.0 %relay.1 = (f32[648,128]{1,0:T(8,128)S(1)}, f32[40,384]{1,0:T(8,128)S(1)}, f32[48,384]{1,0:T(8,128)S(1)}) custom-call(s32[2]{0:T(128)S(1)} %pad_add_fusion.index_ref, f32[784,384]{1,0:T(8,128)S(1)} %get-tuple-element.15.own, f32[784,384]{1,0:T(8,128)S(1)} %collective-permute-done.2.got, f32[16,8,128]{2,1,0:T(8,128)S(1)} %copy-done, ...), custom_call_target="tpu_custom_call" | custom-call | flops 679477248 | bytes 1048576 | tf_op jit(solution)/shard_map/relay/pallas_call | solution.py:265
  29.2 0.1 collective-permute-start.5
  29.3 0.1 collective-permute-start.4
  29.3 2.0 %collective-permute-start.3 = (f32[40,384]{1,0:T(8,128)S(1)}, f32[40,384]{1,0:T(8,128)S(1)}, u32[]{:S(2)}, u32[]{:S(2)}) collective-permute-start(f32[40,384]{1,0:T(8,128)S(1)} %get-tuple-element.17), channel_id=1, source_target_pairs={{0,1},{1,0},{2,3},{3,2},{4,5},{5,4},{6,7},{7,6},{8,9},{9,8},{10,11... | collective-permute-start | bytes 184328 | tf_op jit(solution)/shard_map/ppermute | solution.py:744
  31.4 0.0 copy-done.8
  31.4 0.0 copy-start.6
  31.4 0.0 copy-start.7
  31.4 0.9 %collective-permute-done.3.first = f32[40,384]{1,0:T(8,128)S(1)} collective-permute-done((f32[40,384]{1,0:T(8,128)S(1)}, f32[40,384]{1,0:T(8,128)S(1)}, u32[]{:S(2)}, u32[]{:S(2)}) %collective-permute-start.3) | collective-permute-done | bytes 61472 | tf_op jit(solution)/shard_map/ppermute | solution.py:744
  32.3 4.7 %collective-permute-done.4.second = f32[48,384]{1,0:T(8,128)S(1)} collective-permute-done((f32[48,384]{1,0:T(8,128)S(1)}, f32[48,384]{1,0:T(8,128)S(1)}, u32[]{:S(2)}, u32[]{:S(2)}) %collective-permute-start.4) | collective-permute-done | bytes 73760 | tf_op jit(solution)/shard_map/ppermute | solution.py:742
  37.0 3.5 %prepare.1 = (f32[32,128]{1,0:T(8,128)S(1)}, f32[6,384,128]{2,1,0:T(8,128)S(1)}, bf16[480,512]{1,0:T(8,128)(2,1)S(1)}, f32[512,128]{1,0:T(8,128)S(1)}, f32[384,1...) custom-call(s32[2]{0:T(128)S(1)} %pad_add_fusion.index_ref, s32[1,384]{1,0:T(1,128)S(1)} %reshape.7.orbital_atom, ...), custom_call_target="tpu_custom_call" | custom-call | flops 1073741824 | bytes 1048576 | tf_op jit(solution)/shard_map/prepare/pallas_call | solution.py:265
  40.4 0.0 collective-permute-done.6.got_step
  40.5 0.0 collective-permute-done.5.packed
  40.5 0.0 copy-done.6
  40.5 0.0 copy-done.7
  40.5 0.0 copy-start.1
  40.5 2.2 %density.1 = f32[48,128]{1,0:T(8,128)S(1)} custom-call(s32[2]{0:T(128)S(1)} %pad_add_fusion.index_ref, f32[2]{0:T(128)S(1)} %copy-done.6, s32[2]{0:T(128)S(1)} %copy-done.7, s32[1,384]{1,0:T(1,128)S(1)} %reshape.7.orbital_atom, f32[384,128]{1,0:T(8,128)S(1)} %get-tuple-element.19.member, f32[648,128]{1,0:T(8,128)S(1)} %collective-permute-done.5.packed, ...), custom_call_target="tpu_custom_call" | custom-call | flops 1698693120 | bytes 1048576 | tf_op jit(solution)/shard_map/density/pallas_call | solution.py:265
  42.7 2.0 %collective-permute-start.7 = (f32[48,128]{1,0:T(8,128)S(1)}, f32[48,128]{1,0:T(8,128)S(1)}, u32[]{:S(2)}, u32[]{:S(2)}) collective-permute-start(f32[48,128]{1,0:T(8,128)S(1)} %density.1), channel_id=1, source_target_pairs={{0,1},{1,0},{2,3},{3,2},{4,5},{5,4},{6,7},{7,6},{8,9},{9,8},{10,11... | collective-permute-start | bytes 73736 | tf_op jit(solution)/shard_map/ppermute | solution.py:656
  44.7 0.8 %collective-permute-done.7 = f32[48,128]{1,0:T(8,128)S(1)} collective-permute-done((f32[48,128]{1,0:T(8,128)S(1)}, f32[48,128]{1,0:T(8,128)S(1)}, u32[]{:S(2)}, u32[]{:S(2)}) %collective-permute-start.7) | collective-permute-done | bytes 24608 | tf_op jit(solution)/shard_map/ppermute | solution.py:656
  45.6 0.0 collective-permute-start.10
  45.6 3.5 %collective-permute-start.9 = (f32[48,128]{1,0:T(8,128)S(1)}, f32[48,128]{1,0:T(8,128)S(1)}, u32[]{:S(2)}, u32[]{:S(2)}) collective-permute-start(f32[48,128]{1,0:T(8,128)S(1)} %add.21), channel_id=1, source_target_pairs={{0,4},{1,5},{2,6},{3,7},{4,0},{5,1},{6,2},{7,3},{8,12},{9,13},{10,... | collective-permute-start | bytes 73736 | tf_op jit(solution)/shard_map/ppermute | solution.py:656
  49.1 0.0 collective-permute-start.8
  49.1 1.5 %collective-permute-done.10 = f32[48,128]{1,0:T(8,128)S(1)} collective-permute-done((f32[48,128]{1,0:T(8,128)S(1)}, f32[48,128]{1,0:T(8,128)S(1)}, u32[]{:S(2)}, u32[]{:S(2)}) %collective-permute-start.10) | collective-permute-done | bytes 24608 | tf_op jit(solution)/shard_map/ppermute | solution.py:656
  50.6 0.6 collective-permute-done.9
  51.1 1.8 %collective-permute-done.8 = f32[48,128]{1,0:T(8,128)S(1)} collective-permute-done((f32[48,128]{1,0:T(8,128)S(1)}, f32[48,128]{1,0:T(8,128)S(1)}, u32[]{:S(2)}, u32[]{:S(2)}) %collective-permute-start.8) | collective-permute-done | bytes 24608 | tf_op jit(solution)/shard_map/ppermute | solution.py:656
  52.9 0.1 collective-permute-start.13
  53.0 0.1 collective-permute-start.12
  53.1 4.3 %collective-permute-start.11 = (f32[48,128]{1,0:T(8,128)S(1)}, f32[48,128]{1,0:T(8,128)S(1)}, u32[]{:S(2)}, u32[]{:S(2)}) collective-permute-start(f32[48,128]{1,0:T(8,128)S(1)} %add_add_fusion.1), channel_id=1, source_target_pairs={{0,8},{4,12},{8,0},{12,4},{16,24},{20,28},{24,16},{28,20},{1,9},{5... | collective-permute-start | bytes 73736 | tf_op jit(solution)/shard_map/ppermute | solution.py:656
  57.4 1.2 %collective-permute-done.13 = f32[48,128]{1,0:T(8,128)S(1)} collective-permute-done((f32[48,128]{1,0:T(8,128)S(1)}, f32[48,128]{1,0:T(8,128)S(1)}, u32[]{:S(2)}, u32[]{:S(2)}) %collective-permute-start.13) | collective-permute-done | bytes 24608 | tf_op jit(solution)/shard_map/ppermute | solution.py:656
  58.6 0.0 collective-permute-done.12
  58.6 0.6 collective-permute-done.11
  59.2 0.0 copy-done.1
  59.2 2.0 %finish.1 = (f32[4,2,48]{2,1,0:T(2,128)}, f32[16,8,128]{2,1,0:T(8,128)}) custom-call(s32[2]{0:T(128)S(1)} %pad_add_fusion.index_ref, f32[4]{0:T(128)S(1)} %copy-done.1, f32[48,128]{1,0:T(8,128)S(1)} %add_add_fusion.payload, f32[6,384,128]{2,1,0:T(8,128)S(1)} %get-tuple-element.24.walks, bf16[480,512]{1,0:T(8,128)(2,1)S(1)} %get-tuple-element.25.row_hot, ...), custom_call_target="tpu_custom_call" | custom-call | flops 536870912 | bytes 1048576 | tf_op jit(solution)/shard_map/finish/pallas_call | solution.py:265
  (5 shorter events, 0.0 us)
Async XLA Ops:
  0.7 1.7 %copy-start.2 = (f32[2,2,384,384]{3,2,1,0:T(8,128)S(1)}, f32[2,2,384,384]{3,2,1,0:T(8,128)}, u32[]{:S(2)}) copy-start(f32[2,2,384,384]{3,2,1,0:T(8,128)} %iso.1) | copy-start | bytes 7077892
  2.4 1.3 %copy-start.3 = (f32[2,384,384]{2,1,0:T(8,128)S(1)}, f32[2,384,384]{2,1,0:T(8,128)}, u32[]{:S(2)}) copy-start(f32[2,384,384]{2,1,0:T(8,128)} %coupling.1) | copy-start | bytes 3538948
  3.6 1.3 %copy-start.4 = (f32[2,384,384]{2,1,0:T(8,128)S(1)}, f32[2,384,384]{2,1,0:T(8,128)}, u32[]{:S(2)}) copy-start(f32[2,384,384]{2,1,0:T(8,128)} %lead.1) | copy-start | bytes 3538948
  4.9 0.7 %copy-start.5 = (s32[2,48]{1,0:T(2,128)S(1)}, s32[2,48]{1,0:T(2,128)}, u32[]{:S(2)}) copy-start(s32[2,48]{1,0:T(2,128)} %cells.1) | copy-start | bytes 1156
  5.6 8.7 %copy-start = (f32[16,8,128]{2,1,0:T(8,128)S(1)}, f32[16,8,128]{2,1,0:T(8,128)}, u32[]{:S(2)}) copy-start(f32[16,8,128]{2,1,0:T(8,128)} %field.3) | copy-start | bytes 196612
  13.7 13.5 %collective-permute-start.2 = (f32[784,384]{1,0:T(8,128)S(1)}, f32[784,384]{1,0:T(8,128)S(1)}, u32[]{:S(2)}, u32[]{:S(2)}) collective-permute-start(f32[784,384]{1,0:T(8,128)S(1)} %get-tuple-element.16), channel_id=1, source_target_pairs={{0,1},{1,0},{2,3},{3,2},{4,5},{5,4},{6,7},{7,6},{8,9},{9,8},{10,11... | collective-permute-start | bytes 3612680 | tf_op jit(solution)/shard_map/ppermute | solution.py:723
  13.8 26.7 %collective-permute-start.6 = (f32[384,384]{1,0:T(8,128)S(1)}, f32[384,384]{1,0:T(8,128)S(1)}, u32[]{:S(2)}, u32[]{:S(2)}) collective-permute-start(f32[384,384]{1,0:T(8,128)S(1)} %get-tuple-element.22), channel_id=1, source_target_pairs={{0,1},{1,0},{2,3},{3,2},{4,5},{5,4},{6,7},{7,6},{8,9},{9,8},{10,11... | collective-permute-start | bytes 1769480 | tf_op jit(solution)/shard_map/ppermute | solution.py:745
  14.3 7.9 %collective-permute-start.1 = (f32[16,8,128]{2,1,0:T(8,128)S(1)}, f32[16,8,128]{2,1,0:T(8,128)S(1)}, u32[]{:S(2)}, u32[]{:S(2)}) collective-permute-start(f32[16,8,128]{2,1,0:T(8,128)S(1)} %copy-done), channel_id=1, source_target_pairs={{4,0},{8,4},{12,8},{16,12},{20,16},{24,20},{28,24},{0,28},{5,1},{9... | collective-permute-start | bytes 196616 | tf_op jit(solution)/shard_map/ppermute | solution.py:725
  20.2 7.0 %collective-permute-start = (f32[16,8,128]{2,1,0:T(8,128)S(1)}, f32[16,8,128]{2,1,0:T(8,128)S(1)}, u32[]{:S(2)}, u32[]{:S(2)}) collective-permute-start(f32[16,8,128]{2,1,0:T(8,128)S(1)} %copy-done), channel_id=1, source_target_pairs={{0,4},{4,8},{8,12},{12,16},{16,20},{20,24},{24,28},{28,0},{1,5},{5... | collective-permute-start | bytes 196616 | tf_op jit(solution)/shard_map/ppermute | solution.py:724
  27.2 4.2 %copy-start.8 = (s32[384]{0:T(512)S(1)}, s32[384]{0:T(512)}, u32[]{:S(2)}) copy-start(s32[384]{0:T(512)} %param.15) | copy-start | bytes 4612
  29.2 11.3 %collective-permute-start.5 = (f32[648,128]{1,0:T(8,128)S(1)}, f32[648,128]{1,0:T(8,128)S(1)}, u32[]{:S(2)}, u32[]{:S(2)}) collective-permute-start(f32[648,128]{1,0:T(8,128)S(1)} %get-tuple-element.20), channel_id=1, source_target_pairs={{0,2},{1,3},{2,0},{3,1},{4,6},{5,7},{6,4},{7,5},{8,10},{9,11},{10,... | collective-permute-start | bytes 995336 | tf_op jit(solution)/shard_map/ppermute | solution.py:743
  29.3 7.7 %collective-permute-start.4 = (f32[48,384]{1,0:T(8,128)S(1)}, f32[48,384]{1,0:T(8,128)S(1)}, u32[]{:S(2)}, u32[]{:S(2)}) collective-permute-start(f32[48,384]{1,0:T(8,128)S(1)} %get-tuple-element.18), channel_id=1, source_target_pairs={{0,3},{1,2},{2,1},{3,0},{4,7},{5,6},{6,5},{7,4},{8,11},{9,10},{10,... | collective-permute-start | bytes 221192 | tf_op jit(solution)/shard_map/ppermute | solution.py:742
  29.3 2.9 %collective-permute-start.3 = (f32[40,384]{1,0:T(8,128)S(1)}, f32[40,384]{1,0:T(8,128)S(1)}, u32[]{:S(2)}, u32[]{:S(2)}) collective-permute-start(f32[40,384]{1,0:T(8,128)S(1)} %get-tuple-element.17), channel_id=1, source_target_pairs={{0,1},{1,0},{2,3},{3,2},{4,5},{5,4},{6,7},{7,6},{8,9},{9,8},{10,11... | collective-permute-start | bytes 184328 | tf_op jit(solution)/shard_map/ppermute | solution.py:744
  31.4 9.1 %copy-start.6 = (f32[2]{0:T(128)S(1)}, f32[2]{0:T(128)}, u32[]{:S(2)}) copy-start(f32[2]{0:T(128)} %weight_ref.1) | copy-start | bytes 28
  31.4 9.1 %copy-start.7 = (s32[2]{0:T(128)S(1)}, s32[2]{0:T(128)}, u32[]{:S(2)}) copy-start(s32[2]{0:T(128)} %group_ref.1) | copy-start | bytes 28
  40.5 18.7 %copy-start.1 = (f32[4]{0:T(128)S(1)}, f32[4]{0:T(128)}, u32[]{:S(2)}) copy-start(f32[4]{0:T(128)} %charge_ref.1) | copy-start | bytes 52
  42.7 2.9 %collective-permute-start.7 = (f32[48,128]{1,0:T(8,128)S(1)}, f32[48,128]{1,0:T(8,128)S(1)}, u32[]{:S(2)}, u32[]{:S(2)}) collective-permute-start(f32[48,128]{1,0:T(8,128)S(1)} %density.1), channel_id=1, source_target_pairs={{0,1},{1,0},{2,3},{3,2},{4,5},{5,4},{6,7},{7,6},{8,9},{9,8},{10,11... | collective-permute-start | bytes 73736 | tf_op jit(solution)/shard_map/ppermute | solution.py:656
  45.6 5.0 %collective-permute-start.10 = (f32[48,128]{1,0:T(8,128)S(1)}, f32[48,128]{1,0:T(8,128)S(1)}, u32[]{:S(2)}, u32[]{:S(2)}) collective-permute-start(f32[48,128]{1,0:T(8,128)S(1)} %add.21), channel_id=1, source_target_pairs={{0,6},{1,7},{2,4},{3,5},{4,2},{5,3},{6,0},{7,1},{8,14},{9,15},{10,... | collective-permute-start | bytes 73736 | tf_op jit(solution)/shard_map/ppermute | solution.py:656
  45.6 5.6 %collective-permute-start.9 = (f32[48,128]{1,0:T(8,128)S(1)}, f32[48,128]{1,0:T(8,128)S(1)}, u32[]{:S(2)}, u32[]{:S(2)}) collective-permute-start(f32[48,128]{1,0:T(8,128)S(1)} %add.21), channel_id=1, source_target_pairs={{0,4},{1,5},{2,6},{3,7},{4,0},{5,1},{6,2},{7,3},{8,12},{9,13},{10,... | collective-permute-start | bytes 73736 | tf_op jit(solution)/shard_map/ppermute | solution.py:656
  49.1 3.8 %collective-permute-start.8 = (f32[48,128]{1,0:T(8,128)S(1)}, f32[48,128]{1,0:T(8,128)S(1)}, u32[]{:S(2)}, u32[]{:S(2)}) collective-permute-start(f32[48,128]{1,0:T(8,128)S(1)} %add.21), channel_id=1, source_target_pairs={{0,2},{1,3},{2,0},{3,1},{4,6},{5,7},{6,4},{7,5},{8,10},{9,11},{10,... | collective-permute-start | bytes 73736 | tf_op jit(solution)/shard_map/ppermute | solution.py:656
  52.9 5.7 %collective-permute-start.13 = (f32[48,128]{1,0:T(8,128)S(1)}, f32[48,128]{1,0:T(8,128)S(1)}, u32[]{:S(2)}, u32[]{:S(2)}) collective-permute-start(f32[48,128]{1,0:T(8,128)S(1)} %add_add_fusion.1), channel_id=1, source_target_pairs={{0,24},{4,28},{8,16},{12,20},{16,8},{20,12},{24,0},{28,4},{1,25},{... | collective-permute-start | bytes 73736 | tf_op jit(solution)/shard_map/ppermute | solution.py:656
  53.0 5.6 %collective-permute-start.12 = (f32[48,128]{1,0:T(8,128)S(1)}, f32[48,128]{1,0:T(8,128)S(1)}, u32[]{:S(2)}, u32[]{:S(2)}) collective-permute-start(f32[48,128]{1,0:T(8,128)S(1)} %add_add_fusion.1), channel_id=1, source_target_pairs={{0,16},{4,20},{8,24},{12,28},{16,0},{20,4},{24,8},{28,12},{1,17},{... | collective-permute-start | bytes 73736 | tf_op jit(solution)/shard_map/ppermute | solution.py:656
  53.1 6.1 %collective-permute-start.11 = (f32[48,128]{1,0:T(8,128)S(1)}, f32[48,128]{1,0:T(8,128)S(1)}, u32[]{:S(2)}, u32[]{:S(2)}) collective-permute-start(f32[48,128]{1,0:T(8,128)S(1)} %add_add_fusion.1), channel_id=1, source_target_pairs={{0,8},{4,12},{8,0},{12,4},{16,24},{20,28},{24,16},{28,20},{1,9},{5... | collective-permute-start | bytes 73736 | tf_op jit(solution)/shard_map/ppermute | solution.py:656

commit v4 on v3

--- a/solution.py
+++ b/solution.py
@@ -77,8 +77,35 @@
     out[2 * TILE :, 2 * TILE :] = packed[4 * TILE : 5 * TILE, :]
 
 
-def pair_kernel(index_ref, iso, coupling, lead, cells, own, near, first, sent, c_buf, g_buf, lead_buf, row, sems):
-    place = index_ref[0]
+def plane_rows(n, plane):
+    start = 2 * n + 16 + 8 * (plane // 3)
+    return slice(start, start + 8)
+
+
+def plane_lanes(plane):
+    return slice((plane % 3) * TILE, (plane % 3 + 1) * TILE)
+
+
+def pair_kernel(
+    iso,
+    coupling,
+    lead,
+    cells_in,
+    field_in,
+    own,
+    near,
+    first,
+    sent,
+    planes,
+    c_buf,
+    g_buf,
+    lead_buf,
+    row,
+    cells,
+    field,
+    sems,
+):
+    place = lax.axis_index("slab")
     core = lax.rem(place, 2)
     n = lead_buf.shape[1]
     sources = []
@@ -88,25 +115,35 @@
             sources.append((iso.at[energy, slab], g_buf.at[turn, slab]))
     for turn, energy in enumerate((core, 1 - core)):
         sources.append((lead.at[energy], lead_buf.at[turn]))
+    sources += [(cells_in, cells), (field_in, field)]
     copies = [pltpu.make_async_copy(src, dst, sems.at[i]) for i, (src, dst) in enumerate(sources)]
     for copy in copies:
         copy.start()
-    atoms = cells.shape[1]
-    row[...] = jnp.zeros_like(row)
-    row[0:1, 0:atoms] = cells[0:1, :].astype(F32)
-    row[0:1, HALF : HALF + atoms] = cells[1:2, :].astype(F32)
-    rows = lax.broadcasted_iota(jnp.int32, (8, TILE), 0)
-    for ref in (own, sent):
-        ref[2 * n + 8 :, 0:TILE] = jnp.where(rows == place, row[0:1, :], 0.0)
-        ref[2 * n + 8 :, TILE:] = jnp.zeros((8, n - TILE), F32)
     steps = []
     for slab in range(2):
         for copy in copies[3 * slab : 3 * slab + 3]:
             copy.wait()
         parts = split(c_buf[slab])
         steps.append([product(split(g_buf[turn, slab]), parts) for turn in range(2)])
-    for copy in copies[6:]:
+    for copy in copies[6:8]:
         copy.wait()
+    for copy in copies[8:]:
+        copy.wait()
+    atoms = cells.shape[1]
+    row[...] = jnp.zeros_like(row)
+    row[0:1, 0:atoms] = cells[0:1, :].astype(F32)
+    row[0:1, HALF : HALF + atoms] = cells[1:2, :].astype(F32)
+    rows = lax.broadcasted_iota(jnp.int32, (8, TILE), 0)
+    mine = jnp.where(rows == place, row[0:1, :], 0.0)
+    own[2 * n + 8 : 2 * n + 16, 0:TILE] = mine
+    sent[2 * n + 8 : 2 * n + 16, 0:TILE] = mine
+    planes[REACH * 8 :, :] = mine
+    length = field.shape[0]
+    even = core == 0
+    for plane in range(REACH):
+        low, high = (field[plane], field[length - REACH + plane])
+        planes[plane * 8 : plane * 8 + 8, :] = jnp.where(even, low, high)
+        sent[plane_rows(n, plane), plane_lanes(plane)] = jnp.where(even, high, low)
     outputs = (own, sent)
 
     @pl.when(place == 0)
@@ -147,18 +184,19 @@
     return product(split(term), composed, True) + map_ref[n : 2 * n, :]
 
 
-def relay_kernel(index_ref, own, got, field, left, right, out, first, second):
-    place = index_ref[0]
+def relay_kernel(own, got, field, second, out, wide, cells):
+    place = lax.axis_index("slab")
     n = own.shape[1]
-    length, rows, depth = field.shape
+    length = field.shape[0]
     even = lax.rem(place, 2) == 0
-    for part, block in enumerate((left, field, right)):
-        low = block[:REACH].reshape(REACH * rows, depth)
-        high = block[length - REACH :].reshape(REACH * rows, depth)
-        first[:, part * depth : (part + 1) * depth] = jnp.where(even, high, low)
-        second[: REACH * rows, part * depth : (part + 1) * depth] = jnp.where(even, low, high)
-    second[REACH * rows :, :] = jnp.zeros((8, n), F32)
-    second[REACH * rows :, :TILE] = own[2 * n + 8 :, :TILE] + got[2 * n + 8 :, :TILE]
+    wide[REACH : REACH + length] = field[...]
+    for plane in range(REACH):
+        one = got[plane_rows(n, plane), plane_lanes(plane)]
+        two = second[plane * 8 : plane * 8 + 8, :]
+        wide[plane] = jnp.where(even, two, one)
+        wide[REACH + length + plane] = jnp.where(even, one, two)
+    spot = slice(2 * n + 8, 2 * n + 16)
+    cells[...] = own[spot, :TILE] + got[spot, :TILE] + second[REACH * 8 :, :]
 
     @pl.when(place == 0)
     def _():
@@ -169,8 +207,8 @@
         pack(advance(own, got[n : 2 * n, :]), out)
 
 
-def pass_kernel(turn, index_ref, packed, own, got, out, state):
-    place = index_ref[0]
+def pass_kernel(turn, packed, own, got, out, state):
+    place = lax.axis_index("slab")
     for core, (near, far) in enumerate(((own, got), (got, own))):
 
         @pl.when(place == 2 * turn + core)
@@ -182,7 +220,6 @@
 
 def density_kernel(
     pairs,
-    index_ref,
     weight_ref,
     group_ref,
     orbital_atom,
@@ -197,7 +234,7 @@
     state,
     fold,
 ):
-    place = index_ref[0]
+    place = lax.axis_index("slab")
     core = lax.rem(place, 2)
     n = state.shape[0]
     atoms = lax.broadcasted_iota(jnp.int32, (TILE, n), 0)
@@ -361,58 +398,24 @@
     return result
 
 
-def prepare_kernel(
-    devices,
-    wires,
-    index_ref,
-    orbital_atom,
-    own,
-    field,
-    left,
-    right,
-    first,
-    second,
-    all_cells,
-    out,
-    walks,
-    row_hot,
-    deep_hot,
-    member,
-    wide_field,
-):
-    place, wire = (index_ref[0], index_ref[1])
-    length, rows, depth = field.shape
-    planes = length + 2 * REACH
+def moments_kernel(devices, wires, own, field, one_beside, two_beside, cells, out, wide_field):
+    place, wire = (lax.axis_index("slab"), lax.axis_index("energy"))
+    planes, rows, depth = field.shape
+    length = planes - 2 * REACH
     width_x = length // 2
-    atoms = walks.shape[1] // (2 * devices)
+    atoms = cells.shape[1]
     grid_y = rows * wires
     pairs = devices
-    n = orbital_atom.shape[1]
-    even = lax.rem(place, 2) == 0
-    edges = REACH * rows
-    before = jnp.where(even, second[:edges, :], first[...])
-    after = jnp.where(even, first[...], second[:edges, :])
-
-    def block_of(x, part):
-        return x[:, part * depth : (part + 1) * depth].reshape(REACH, rows, depth)
-
-    columns = [
-        jnp.concatenate([block_of(before, part), block[...], block_of(after, part)], axis=0)
-        for part, block in enumerate((left, field, right))
-    ]
+    n = own.shape[1]
+    even = lax.rem(wire, 2) == 0
+    left = jnp.where(even, two_beside[...], one_beside[...])
+    right = jnp.where(even, one_beside[...], two_beside[...])
     whole = (planes, 3 * rows, depth)
     mask = grid_mask(whole, REACH, length, rows, place, devices, wire, wires)
-    source = jnp.concatenate(columns, axis=1) * mask
+    source = jnp.concatenate([left, field[...], right], axis=1)
+    source = jnp.where(mask > 0, source, 0.0)
     margin = ITERS - 1
     wide_field[...] = source[REACH - margin : REACH + length + margin]
-    spots = lax.broadcasted_iota(jnp.int32, (TILE, n), 0) == orbital_atom[...]
-    spots = spots.astype(F32)
-    for start in range(0, n, TILE):
-        member[start : start + TILE, :] = spots[:, start : start + TILE].T
-    if devices > 4:
-        cells = all_cells[...]
-    else:
-        cells = second[edges:, :depth] + all_cells[...]
 
     def inner(x):
         extra = (x.shape[0] - length) // 2
@@ -436,7 +439,7 @@
             sums = jnp.where(lanes == 8 * base + steps, part, sums)
     out[...] = jnp.zeros_like(out)
     out[6 * pairs : 6 * pairs + 8, :] = sums
-    mine = own[2 * n + 8 :, :depth]
+    mine = own[2 * n + 8 : 2 * n + 16, :depth]
     mine = jnp.sum(mine, axis=0, keepdims=True)
     lane = lax.broadcasted_iota(jnp.int32, (1, depth), 1)
     odd = (lane >= HALF).astype(F32)
@@ -456,6 +459,33 @@
             value = value + dot(part, at_deep, False)
         value = jnp.sum(value * at_rows, axis=0, keepdims=True)
         out[pl.ds(steps * pairs + place, 1), :] = value
+
+
+def atoms_kernel(
+    devices,
+    wires,
+    length,
+    orbital_atom,
+    some_cells,
+    other_cells,
+    walks,
+    row_hot,
+    deep_hot,
+    member,
+):
+    place, wire = (lax.axis_index("slab"), lax.axis_index("energy"))
+    rows, depth = some_cells.shape
+    width_x = length // 2
+    atoms = walks.shape[1] // (2 * devices)
+    grid_y = rows * wires
+    pairs = devices
+    n = orbital_atom.shape[1]
+    start = (wire * rows).astype(F32)
+    cells = jnp.maximum(some_cells[...], other_cells[...])
+    spots = lax.broadcasted_iota(jnp.int32, (TILE, n), 0) == orbital_atom[...]
+    spots = spots.astype(F32)
+    for first in range(0, n, TILE):
+        member[first : first + TILE, :] = spots[:, first : first + TILE].T
     row_cells = cells
     row_x, row_y, row_z = coordinates(row_cells, grid_y, depth)
     padded = jnp.concatenate([row_cells, jnp.zeros((depth - 8, depth), F32)], axis=0)
@@ -536,7 +566,6 @@
     devices,
     wires,
     atoms,
-    index_ref,
     charge_ref,
     payload,
     walks,
@@ -546,7 +575,7 @@
     density,
     potential,
 ):
-    place, wire = (index_ref[0], index_ref[1])
+    place, wire = (lax.axis_index("slab"), lax.axis_index("energy"))
     length, rows, depth = potential.shape
     pairs = devices
     groups = density.shape[0]
@@ -676,6 +705,10 @@
     return value
 
 
+def inner_pairs(count):
+    return [(i, i + 1 if i % 2 else i - 1) for i in range(1, count - 1)]
+
+
 def neighbour_turn(count):
     return [(i, (i + 1) % count if i % 2 else (i - 1) % count) for i in range(count)]
 
@@ -697,106 +730,111 @@
     n = lead_green.shape[-1]
     length, rows, depth = doping.shape
     shape = jax.ShapeDtypeStruct
-    index = jnp.stack([lax.axis_index("slab"), lax.axis_index("energy")]).astype(jnp.int32)
     orbital_row = orbital_atom.reshape(1, n)
-    maps = shape((2 * n + 16, n), F32)
-    own, own_step, sent_step, sent = local_call(
+    maps = shape((2 * n + 32, n), F32)
+    edge_rows = REACH * rows + 8
+    own, own_step, sent_step, sent, edge = local_call(
         pair_kernel,
-        (maps, shape((n, n), F32), shape((n, n), F32), maps),
+        (maps, shape((n, n), F32), shape((n, n), F32), maps, shape((edge_rows, depth), F32)),
         [
             pltpu.VMEM((2, n, n), F32),
             pltpu.VMEM((2, 2, n, n), F32),
             pltpu.VMEM((2, n, n), F32),
             pltpu.VMEM((8, TILE), F32),
-            pltpu.SemaphoreType.DMA((8,)),
+            pltpu.VMEM(atom_cell.shape, jnp.int32),
+            pltpu.VMEM(doping.shape, F32),
+            pltpu.SemaphoreType.DMA((10,)),
         ],
-        "shhhv",
+        "hhhhh",
         "pair",
-        28,
+        30,
         72 * n**3,
-        index,
-        green_iso,
-        coupling,
-        lead_green,
-        atom_cell,
+        *[
+            pltpu.with_memory_space_constraint(x, pltpu.HBM)
+            for x in (green_iso, coupling, lead_green, atom_cell, doping)
+        ],
     )
     got = lax.ppermute(sent, "slab", pairs_of(devices))
-    left = lax.ppermute(doping, "energy", [(i, (i + 1) % wires) for i in range(wires)])
-    right = lax.ppermute(doping, "energy", [((i + 1) % wires, i) for i in range(wires)])
-    planes = REACH * rows
-    passed, first, second = local_call(
+    second = lax.ppermute(edge, "slab", neighbour_turn(devices))
+    passed, wide_block, cells = local_call(
         relay_kernel,
-        (shape((PACKED_ROWS, TILE), F32), shape((planes, n), F32), shape((planes + 8, n), F32)),
+        (
+            shape((PACKED_ROWS, TILE), F32),
+            shape((length + 2 * REACH, rows, depth), F32),
+            shape((8, depth), F32),
+        ),
         [],
-        "svvvvv",
+        "vvvv",
         "relay",
         20,
         12 * n**3,
-        index,
         own,
         got,
         doping,
-        left,
-        right,
-    )
-    second_in = lax.ppermute(second, "slab", neighbour_turn(devices))
+        second,
+    )
     packed = lax.ppermute(passed, "slab", hop(devices, 1))
-    first_in = lax.ppermute(first, "slab", pairs_of(devices))
+    one_beside = lax.ppermute(wide_block, "energy", pairs_of(wires))
+    two_beside = lax.ppermute(wide_block, "energy", inner_pairs(wires))
+    other_cells = lax.ppermute(cells, "slab", pairs_of(devices))
+    if devices > 4:
+        other_cells = lax.psum(own[2 * n + 8 : 2 * n + 16, :depth], "slab")
     got_step = lax.ppermute(sent_step, "slab", pairs_of(devices))
-    cells = second[planes:, :depth]
-    if devices > 4:
-        cells = lax.psum(own[2 * n + 8 :, :depth], "slab")
     wide = (length + 2 * ITERS - 2, 3 * rows, depth)
-    extra, walks, row_hot, deep_hot, member, wide_field = local_call(
-        functools.partial(prepare_kernel, devices, wires),
+    walks, row_hot, deep_hot, member = local_call(
+        functools.partial(atoms_kernel, devices, wires, length),
         (
-            shape((6 * devices + 8, depth), F32),
             shape((6, 2 * devices * atoms, depth), F32),
             shape((wide[0] * wide[1], devices * depth), BF16),
             shape((devices * depth, depth), F32),
             shape((n, TILE), F32),
-            shape(wide, F32),
         ),
         [],
-        "svvvvvvvv",
-        "prepare",
+        "vvv",
+        "atoms",
         28,
+        2 * 2**30,
+        orbital_row,
+        cells,
+        other_cells,
+    )
+    extra, wide_field = local_call(
+        functools.partial(moments_kernel, devices, wires),
+        (shape((6 * devices + 8, depth), F32), shape(wide, F32)),
+        [],
+        "vvvvv",
+        "moments",
+        20,
         2**30,
-        index,
-        orbital_row,
         own,
-        doping,
-        left,
-        right,
-        first_in,
-        second_in,
-        cells,
+        wide_block,
+        one_beside,
+        two_beside,
+        atom_cell,
     )
     for turn in range(1, devices // 2 - 1):
         passed = local_call(
             functools.partial(pass_kernel, turn),
             shape((PACKED_ROWS, TILE), F32),
             [pltpu.VMEM((n, n), F32)],
-            "svvv",
+            "vvv",
             "pass_on",
             20,
             24 * n**3,
-            index,
-            packed,
+                packed,
             own,
             got,
         )
         arrived = lax.ppermute(passed, "slab", hop(devices, turn + 1))
-        packed = jnp.where(index[0] // 2 == turn + 1, arrived, packed)
+        packed = jnp.where(lax.axis_index("slab") // 2 == turn + 1, arrived, packed)
     payload = local_call(
         functools.partial(density_kernel, devices),
         shape(((groups + 6) * devices + 8, TILE), F32),
         [pltpu.VMEM((n, n), F32), pltpu.VMEM((8, TILE), F32)],
-        "sssvvvvvvvv",
+        "ssvvvvvvvv",
         "density",
         20,
         30 * n**3,
-        index,
         energy_weight,
         energy_group,
         orbital_row,
@@ -813,11 +851,10 @@
         functools.partial(finish_kernel, devices, wires, atoms),
         (shape((groups, 2, atoms), F32), shape(doping.shape, F32)),
         [],
-        "ssvvvvv",
+        "svvvvv",
         "finish",
         28,
         2**29,
-        index,
         group_charge,
         payload,
         walks,

time: 61.5 us -> 50.2 us (0.82)
  waiting for transfers between devices: 19 us -> 12.3 us
  local copies, waits for them, and re-layouts: 4.91 us -> 0.04 us
  starting transfers between devices: 18.7 us -> 20.4 us
  Pallas kernels: 17.7 us -> 16.5 us
    ppermute x4, waiting for transfers between devices: 12.5 us -> 3.87 us  [the longest x1 2.34 us: on_device(): one_beside = lax.ppermute(wide_block, 'energy', pairs_of(wires))]
    unnamed x18 -> x12, local copies, waits for them, and re-layouts: 4.91 us -> 0.03 us
    ppermute x7, waiting for transfers between devices: 6.47 us -> 8.44 us  [total_over(): lax.ppermute(value, axis, [(i, i ^ k) for i in range(size)])]
    pallas_call x5 -> x6, Pallas kernels: 17.7 us -> 16.5 us  [local_call(): pl.pallas_call(kernel, out_shape=shapes, in_specs=[pl.BlockSpec(memory_sp...]
    ppermute x7, starting transfers between devices: 9.95 us -> 11.1 us  [total_over(): lax.ppermute(value, axis, [(i, i ^ k) for i in range(size)])]
    ppermute x1, starting transfers between devices: 0.07 us -> 0.91 us  [on_device(): packed = lax.ppermute(passed, 'slab', hop(devices, 1))]
  transfers between devices with their start and end apart: 14 -> 14, of which waited for: 10 -> 7; matrix products, arithmetic and copies ran while one was open for 0% -> 0% of each run, Pallas kernels for 9% -> 8%
where the time goes in v4:
time: 50.2 us; the launch traced here: 50 us
  starting transfers between devices  20.4 us (41%)
  Pallas kernels  16.5 us (33%)
  waiting for transfers between devices  12.3 us (25%)
  between operations  0.77 us (2%)
    pallas_call x6, Pallas kernels, local_call(): pl.pallas_call(kernel, out_shape=shapes, in_specs=[pl.BlockSpec(memory_sp...  16.5 us
    ppermute x7, starting transfers between devices, total_over(): lax.ppermute(value, axis, [(i, i ^ k) for i in range(size)])  11.1 us
    ppermute x7, waiting for transfers between devices, total_over(): lax.ppermute(value, axis, [(i, i ^ k) for i in range(size)])  8.44 us
    ppermute x1, starting transfers between devices, on_device(): one_beside = lax.ppermute(wide_block, 'energy', pairs_of(wires))  5.2 us
    ppermute x1, waiting for transfers between devices, on_device(): one_beside = lax.ppermute(wide_block, 'energy', pairs_of(wires))  2.34 us
    ppermute x1, starting transfers between devices, on_device(): second = lax.ppermute(edge, 'slab', neighbour_turn(devices))  1.78 us
    ppermute x1, waiting for transfers between devices, on_device(): second = lax.ppermute(edge, 'slab', neighbour_turn(devices))  1.52 us
  transfers between devices with their start and end apart: 14, of which 7 were waited for; matrix products, arithmetic and copies ran while one was open for 0% of the time, Pallas kernels for 8%

profile of v4, /device:TPU:0, one launch (start us, length us, event | category | flops | bytes accessed | tf_op | source)
XLA Modules:
  0.0 50.0 jit_solution(9371389806573063932)
XLA Ops:
  0.6 0.0 copy-start
  0.6 8.0 %pair.1 = (f32[800,384]{1,0:T(8,128)S(1)}, f32[384,384]{1,0:T(8,128)S(1)}, f32[384,384]{1,0:T(8,128)S(1)}, f32[800,384]{1,0:T(8,128)S(1)}, f32[48,128]{1,0:T(8,128)S(1)}) custom-call(f32[2,2,384,384]{3,2,1,0:T(8,128)} %iso.1, f32[2,384,384]{2,1,0:T(8,128)} %coupling.1, f32[2,384,384]{2,1,0:T(8,128)} %lead.1, s32[2,48]{1,0:T(2,128)} %cells.1, f32[16,8,128]{2,1,0:T(8,128)} %field.1), custom_call_target="tpu_custom_call" | custom-call | flops 4076863488 | bytes 1048576 | tf_op jit(solution)/shard_map/pair/pallas_call | solution.py:302
  8.7 0.1 collective-permute-start
  8.8 0.5 collective-permute-start.4
  9.3 1.8 %collective-permute-start.1 = (f32[48,128]{1,0:T(8,128)S(1)}, f32[48,128]{1,0:T(8,128)S(1)}, u32[]{:S(2)}, u32[]{:S(2)}) collective-permute-start(f32[48,128]{1,0:T(8,128)S(1)} %get-tuple-element.18), channel_id=1, source_target_pairs={{0,3},{1,2},{2,1},{3,0},{4,7},{5,6},{6,5},{7,4},{8,11},{9,10},{10,... | collective-permute-start | bytes 73736 | tf_op jit(solution)/shard_map/ppermute | solution.py:758
  11.0 1.5 %collective-permute-done.1.second = f32[48,128]{1,0:T(8,128)S(1)} collective-permute-done((f32[48,128]{1,0:T(8,128)S(1)}, f32[48,128]{1,0:T(8,128)S(1)}, u32[]{:S(2)}, u32[]{:S(2)}) %collective-permute-start.1) | collective-permute-done | bytes 24608 | tf_op jit(solution)/shard_map/ppermute | solution.py:758
  12.6 0.0 collective-permute-done.got
  12.6 0.0 copy-done
  12.6 0.0 copy-start.5
  12.6 1.2 %relay.1 = (f32[648,128]{1,0:T(8,128)S(1)}, f32[26,8,128]{2,1,0:T(8,128)S(1)}, f32[8,128]{1,0:T(8,128)S(1)}) custom-call(f32[800,384]{1,0:T(8,128)S(1)} %get-tuple-element.16.own, f32[800,384]{1,0:T(8,128)S(1)} %collective-permute-done.got, f32[16,8,128]{2,1,0:T(8,128)S(1)} %copy-done, f32[48,128]{1,0:T(8,128)S(1)} %collective-permute-done.1.second), custom_call_target="tpu_custom_call" | custom-call | flops 679477248 | bytes 1048576 | tf_op jit(solution)/shard_map/relay/pallas_call | solution.py:302
  13.8 0.9 %collective-permute-start.3 = (f32[648,128]{1,0:T(8,128)S(1)}, f32[648,128]{1,0:T(8,128)S(1)}, u32[]{:S(2)}, u32[]{:S(2)}) collective-permute-start(f32[648,128]{1,0:T(8,128)S(1)} %get-tuple-element.21), channel_id=1, source_target_pairs={{0,2},{1,3},{2,0},{3,1},{4,6},{5,7},{6,4},{7,5},{8,10},{9,11},{10,... | collective-permute-start | bytes 995336 | tf_op jit(solution)/shard_map/ppermute | solution.py:776
  14.7 0.0 collective-permute-start.2
  14.7 0.0 copy-done.5
  14.7 0.0 copy-start.2
  14.7 0.8 %collective-permute-start.6 = (f32[26,8,128]{2,1,0:T(8,128)S(1)}, f32[26,8,128]{2,1,0:T(8,128)S(1)}, u32[]{:S(2)}, u32[]{:S(2)}) collective-permute-start(f32[26,8,128]{2,1,0:T(8,128)S(1)} %get-tuple-element.24.field), channel_id=1, source_target_pairs={{4,8},{8,4},{12,16},{16,12},{20,24},{24,20},{5,9},{9,5},{13,17},{1... | collective-permute-start | bytes 319496 | tf_op jit(solution)/shard_map/ppermute | solution.py:778
  15.6 5.2 %collective-permute-start.5 = (f32[26,8,128]{2,1,0:T(8,128)S(1)}, f32[26,8,128]{2,1,0:T(8,128)S(1)}, u32[]{:S(2)}, u32[]{:S(2)}) collective-permute-start(f32[26,8,128]{2,1,0:T(8,128)S(1)} %get-tuple-element.24.field), channel_id=1, source_target_pairs={{0,4},{4,0},{8,12},{12,8},{16,20},{20,16},{24,28},{28,24},{1,5},{5... | collective-permute-start | bytes 319496 | tf_op jit(solution)/shard_map/ppermute | solution.py:777
  20.8 0.0 collective-permute-done.2.other_cells
  20.8 1.8 %atoms.1 = (f32[6,384,128]{2,1,0:T(8,128)S(1)}, bf16[480,512]{1,0:T(8,128)(2,1)S(1)}, f32[512,128]{1,0:T(8,128)S(1)}, f32[384,128]{1,0:T(8,128)S(1)}) custom-call(s32[1,384]{1,0:T(1,128)S(1)} %reshape.7.orbital_atom, f32[8,128]{1,0:T(8,128)S(1)} %get-tuple-element.19.some_cells, f32[8,128]{1,0:T(8,128)S(1)} %collective-permute-done.2.other_cells), custom_call_target="tpu_custom_call" | custom-call | flops 2147483648 | bytes 1048576 | tf_op jit(solution)/shard_map/atoms/pallas_call | solution.py:302
  22.6 0.0 copy-start.3
  22.6 0.0 copy-start.4
  22.7 0.0 collective-permute-done.6.two_beside
  22.7 2.3 %collective-permute-done.5.one_beside = f32[26,8,128]{2,1,0:T(8,128)S(1)} collective-permute-done((f32[26,8,128]{2,1,0:T(8,128)S(1)}, f32[26,8,128]{2,1,0:T(8,128)S(1)}, u32[]{:S(2)}, u32[]{:S(2)}) %collective-permute-start.5) | collective-permute-done | bytes 106528 | tf_op jit(solution)/shard_map/ppermute | solution.py:777
  25.0 0.0 copy-done.2
  25.0 1.2 %moments.1 = (f32[32,128]{1,0:T(8,128)S(1)}, f32[20,24,128]{2,1,0:T(8,128)S(1)}) custom-call(f32[800,384]{1,0:T(8,128)S(1)} %get-tuple-element.16.own, f32[26,8,128]{2,1,0:T(8,128)S(1)} %get-tuple-element.24.field, f32[26,8,128]{2,1,0:T(8,128)S(1)} %collective-permute-done.5.one_beside, f32[26,8,128]{2,1,0:T(8,128)S(1)} %collective-permute-done.6.two_beside, ...), custom_call_target="tpu_custom_call" | custom-call | flops 1073741824 | bytes 1048576 | tf_op jit(solution)/shard_map/moments/pallas_call | solution.py:302
  26.2 0.0 collective-permute-done.4.got_step
  26.2 0.0 collective-permute-done.3.packed
  26.2 0.0 copy-done.3
  26.2 0.0 copy-done.4
  26.2 0.0 copy-start.1
  26.2 2.2 %density.1 = f32[48,128]{1,0:T(8,128)S(1)} custom-call(f32[2]{0:T(128)S(1)} %copy-done.3, s32[2]{0:T(128)S(1)} %copy-done.4, s32[1,384]{1,0:T(1,128)S(1)} %reshape.7.orbital_atom, f32[384,128]{1,0:T(8,128)S(1)} %get-tuple-element.20.member, f32[648,128]{1,0:T(8,128)S(1)} %collective-permute-done.3.packed, f32[800,384]{1,0:T(8,128)S(1)} %get-tuple-element.16.own, ...), custom_call_target="tpu_custom_call" | custom-call | flops 1698693120 | bytes 1048576 | tf_op jit(solution)/shard_map/density/pallas_call | solution.py:302
  28.4 0.0 collective-permute-start.7
  28.5 1.2 %collective-permute-done.7 = f32[48,128]{1,0:T(8,128)S(1)} collective-permute-done((f32[48,128]{1,0:T(8,128)S(1)}, f32[48,128]{1,0:T(8,128)S(1)}, u32[]{:S(2)}, u32[]{:S(2)}) %collective-permute-start.7) | collective-permute-done | bytes 24608 | tf_op jit(solution)/shard_map/ppermute | solution.py:685
  29.6 5.6 %collective-permute-start.10 = (f32[48,128]{1,0:T(8,128)S(1)}, f32[48,128]{1,0:T(8,128)S(1)}, u32[]{:S(2)}, u32[]{:S(2)}) collective-permute-start(f32[48,128]{1,0:T(8,128)S(1)} %add.21), channel_id=1, source_target_pairs={{0,6},{1,7},{2,4},{3,5},{4,2},{5,3},{6,0},{7,1},{8,14},{9,15},{10,... | collective-permute-start | bytes 73736 | tf_op jit(solution)/shard_map/ppermute | solution.py:685
  35.2 0.0 collective-permute-start.9
  35.2 0.6 %collective-permute-start.8 = (f32[48,128]{1,0:T(8,128)S(1)}, f32[48,128]{1,0:T(8,128)S(1)}, u32[]{:S(2)}, u32[]{:S(2)}) collective-permute-start(f32[48,128]{1,0:T(8,128)S(1)} %add.21), channel_id=1, source_target_pairs={{0,2},{1,3},{2,0},{3,1},{4,6},{5,7},{6,4},{7,5},{8,10},{9,11},{10,... | collective-permute-start | bytes 73736 | tf_op jit(solution)/shard_map/ppermute | solution.py:685
  35.8 1.2 %collective-permute-done.10 = f32[48,128]{1,0:T(8,128)S(1)} collective-permute-done((f32[48,128]{1,0:T(8,128)S(1)}, f32[48,128]{1,0:T(8,128)S(1)}, u32[]{:S(2)}, u32[]{:S(2)}) %collective-permute-start.10) | collective-permute-done | bytes 24608 | tf_op jit(solution)/shard_map/ppermute | solution.py:685
  37.0 2.0 %collective-permute-done.9 = f32[48,128]{1,0:T(8,128)S(1)} collective-permute-done((f32[48,128]{1,0:T(8,128)S(1)}, f32[48,128]{1,0:T(8,128)S(1)}, u32[]{:S(2)}, u32[]{:S(2)}) %collective-permute-start.9) | collective-permute-done | bytes 24608 | tf_op jit(solution)/shard_map/ppermute | solution.py:685
  39.0 0.0 collective-permute-done.8
  39.0 4.2 %collective-permute-start.13 = (f32[48,128]{1,0:T(8,128)S(1)}, f32[48,128]{1,0:T(8,128)S(1)}, u32[]{:S(2)}, u32[]{:S(2)}) collective-permute-start(f32[48,128]{1,0:T(8,128)S(1)} %add_add_fusion.1), channel_id=1, source_target_pairs={{0,24},{4,28},{8,16},{12,20},{16,8},{20,12},{24,0},{28,4},{1,25},{... | collective-permute-start | bytes 73736 | tf_op jit(solution)/shard_map/ppermute | solution.py:685
  43.2 0.0 collective-permute-start.12
  43.2 0.6 %collective-permute-start.11 = (f32[48,128]{1,0:T(8,128)S(1)}, f32[48,128]{1,0:T(8,128)S(1)}, u32[]{:S(2)}, u32[]{:S(2)}) collective-permute-start(f32[48,128]{1,0:T(8,128)S(1)} %add_add_fusion.1), channel_id=1, source_target_pairs={{0,8},{4,12},{8,0},{12,4},{16,24},{20,28},{24,16},{28,20},{1,9},{5... | collective-permute-start | bytes 73736 | tf_op jit(solution)/shard_map/ppermute | solution.py:685
  43.9 1.2 %collective-permute-done.13 = f32[48,128]{1,0:T(8,128)S(1)} collective-permute-done((f32[48,128]{1,0:T(8,128)S(1)}, f32[48,128]{1,0:T(8,128)S(1)}, u32[]{:S(2)}, u32[]{:S(2)}) %collective-permute-start.13) | collective-permute-done | bytes 24608 | tf_op jit(solution)/shard_map/ppermute | solution.py:685
  45.0 2.9 %collective-permute-done.12 = f32[48,128]{1,0:T(8,128)S(1)} collective-permute-done((f32[48,128]{1,0:T(8,128)S(1)}, f32[48,128]{1,0:T(8,128)S(1)}, u32[]{:S(2)}, u32[]{:S(2)}) %collective-permute-start.12) | collective-permute-done | bytes 24608 | tf_op jit(solution)/shard_map/ppermute | solution.py:685
  47.9 0.0 collective-permute-done.11
  48.0 0.0 copy-done.1
  48.0 2.0 %finish.1 = (f32[4,2,48]{2,1,0:T(2,128)}, f32[16,8,128]{2,1,0:T(8,128)}) custom-call(f32[4]{0:T(128)S(1)} %copy-done.1, f32[48,128]{1,0:T(8,128)S(1)} %add_add_fusion.payload, f32[6,384,128]{2,1,0:T(8,128)S(1)} %get-tuple-element.26.walks, bf16[480,512]{1,0:T(8,128)(2,1)S(1)} %get-tuple-element.27.row_hot, f32[512,128]{1,0:T(8,128)S(1)} %get-tuple-element.28.deep_hot, ...), custom_call_target="tpu_custom_call" | custom-call | flops 536870912 | bytes 1048576 | tf_op jit(solution)/shard_map/finish/pallas_call | solution.py:302
  (4 shorter events, 0.0 us)
Async XLA Ops:
  0.6 11.9 %copy-start = (f32[16,8,128]{2,1,0:T(8,128)S(1)}, f32[16,8,128]{2,1,0:T(8,128)}, u32[]{:S(2)}) copy-start(f32[16,8,128]{2,1,0:T(8,128)} %field.1) | copy-start | bytes 196612
  8.7 3.9 %collective-permute-start = (f32[800,384]{1,0:T(8,128)S(1)}, f32[800,384]{1,0:T(8,128)S(1)}, u32[]{:S(2)}, u32[]{:S(2)}) collective-permute-start(f32[800,384]{1,0:T(8,128)S(1)} %get-tuple-element.17), channel_id=1, source_target_pairs={{0,1},{1,0},{2,3},{3,2},{4,5},{5,4},{6,7},{7,6},{8,9},{9,8},{10,11... | collective-permute-start | bytes 3686408 | tf_op jit(solution)/shard_map/ppermute | solution.py:757
  8.8 17.4 %collective-permute-start.4 = (f32[384,384]{1,0:T(8,128)S(1)}, f32[384,384]{1,0:T(8,128)S(1)}, u32[]{:S(2)}, u32[]{:S(2)}) collective-permute-start(f32[384,384]{1,0:T(8,128)S(1)} %get-tuple-element.23), channel_id=1, source_target_pairs={{0,1},{1,0},{2,3},{3,2},{4,5},{5,4},{6,7},{7,6},{8,9},{9,8},{10,11... | collective-permute-start | bytes 1769480 | tf_op jit(solution)/shard_map/ppermute | solution.py:782
  9.3 3.3 %collective-permute-start.1 = (f32[48,128]{1,0:T(8,128)S(1)}, f32[48,128]{1,0:T(8,128)S(1)}, u32[]{:S(2)}, u32[]{:S(2)}) collective-permute-start(f32[48,128]{1,0:T(8,128)S(1)} %get-tuple-element.18), channel_id=1, source_target_pairs={{0,3},{1,2},{2,1},{3,0},{4,7},{5,6},{6,5},{7,4},{8,11},{9,10},{10,... | collective-permute-start | bytes 73736 | tf_op jit(solution)/shard_map/ppermute | solution.py:758
  12.6 2.2 %copy-start.5 = (s32[384]{0:T(512)S(1)}, s32[384]{0:T(512)}, u32[]{:S(2)}) copy-start(s32[384]{0:T(512)} %param.15) | copy-start | bytes 4612
  13.8 12.4 %collective-permute-start.3 = (f32[648,128]{1,0:T(8,128)S(1)}, f32[648,128]{1,0:T(8,128)S(1)}, u32[]{:S(2)}, u32[]{:S(2)}) collective-permute-start(f32[648,128]{1,0:T(8,128)S(1)} %get-tuple-element.21), channel_id=1, source_target_pairs={{0,2},{1,3},{2,0},{3,1},{4,6},{5,7},{6,4},{7,5},{8,10},{9,11},{10,... | collective-permute-start | bytes 995336 | tf_op jit(solution)/shard_map/ppermute | solution.py:776
  14.7 6.1 %collective-permute-start.2 = (f32[8,128]{1,0:T(8,128)S(1)}, f32[8,128]{1,0:T(8,128)S(1)}, u32[]{:S(2)}, u32[]{:S(2)}) collective-permute-start(f32[8,128]{1,0:T(8,128)S(1)} %get-tuple-element.19.some_cells), channel_id=1, source_target_pairs={{0,1},{1,0},{2,3},{3,2},{4,5},{5,4},{6,7},{7,6},{8,9},{9,8},{10,11... | collective-permute-start | bytes 12296 | tf_op jit(solution)/shard_map/ppermute | solution.py:779
  14.7 10.3 %copy-start.2 = (s32[2,48]{1,0:T(2,128)S(1)}, s32[2,48]{1,0:T(2,128)}, u32[]{:S(2)}) copy-start(s32[2,48]{1,0:T(2,128)} %cells.1) | copy-start | bytes 1156
  14.7 7.9 %collective-permute-start.6 = (f32[26,8,128]{2,1,0:T(8,128)S(1)}, f32[26,8,128]{2,1,0:T(8,128)S(1)}, u32[]{:S(2)}, u32[]{:S(2)}) collective-permute-start(f32[26,8,128]{2,1,0:T(8,128)S(1)} %get-tuple-element.24.field), channel_id=1, source_target_pairs={{4,8},{8,4},{12,16},{16,12},{20,24},{24,20},{5,9},{9,5},{13,17},{1... | collective-permute-start | bytes 319496 | tf_op jit(solution)/shard_map/ppermute | solution.py:778
  15.6 9.4 %collective-permute-start.5 = (f32[26,8,128]{2,1,0:T(8,128)S(1)}, f32[26,8,128]{2,1,0:T(8,128)S(1)}, u32[]{:S(2)}, u32[]{:S(2)}) collective-permute-start(f32[26,8,128]{2,1,0:T(8,128)S(1)} %get-tuple-element.24.field), channel_id=1, source_target_pairs={{0,4},{4,0},{8,12},{12,8},{16,20},{20,16},{24,28},{28,24},{1,5},{5... | collective-permute-start | bytes 319496 | tf_op jit(solution)/shard_map/ppermute | solution.py:777
  22.6 3.6 %copy-start.3 = (f32[2]{0:T(128)S(1)}, f32[2]{0:T(128)}, u32[]{:S(2)}) copy-start(f32[2]{0:T(128)} %weight_ref.1) | copy-start | bytes 28
  22.6 3.6 %copy-start.4 = (s32[2]{0:T(128)S(1)}, s32[2]{0:T(128)}, u32[]{:S(2)}) copy-start(s32[2]{0:T(128)} %group_ref.1) | copy-start | bytes 28
  26.2 21.8 %copy-start.1 = (f32[4]{0:T(128)S(1)}, f32[4]{0:T(128)}, u32[]{:S(2)}) copy-start(f32[4]{0:T(128)} %charge_ref.1) | copy-start | bytes 52
  28.4 1.2 %collective-permute-start.7 = (f32[48,128]{1,0:T(8,128)S(1)}, f32[48,128]{1,0:T(8,128)S(1)}, u32[]{:S(2)}, u32[]{:S(2)}) collective-permute-start(f32[48,128]{1,0:T(8,128)S(1)} %density.1), channel_id=1, source_target_pairs={{0,1},{1,0},{2,3},{3,2},{4,5},{5,4},{6,7},{7,6},{8,9},{9,8},{10,11... | collective-permute-start | bytes 73736 | tf_op jit(solution)/shard_map/ppermute | solution.py:685
  29.6 7.4 %collective-permute-start.10 = (f32[48,128]{1,0:T(8,128)S(1)}, f32[48,128]{1,0:T(8,128)S(1)}, u32[]{:S(2)}, u32[]{:S(2)}) collective-permute-start(f32[48,128]{1,0:T(8,128)S(1)} %add.21), channel_id=1, source_target_pairs={{0,6},{1,7},{2,4},{3,5},{4,2},{5,3},{6,0},{7,1},{8,14},{9,15},{10,... | collective-permute-start | bytes 73736 | tf_op jit(solution)/shard_map/ppermute | solution.py:685
  35.2 3.8 %collective-permute-start.9 = (f32[48,128]{1,0:T(8,128)S(1)}, f32[48,128]{1,0:T(8,128)S(1)}, u32[]{:S(2)}, u32[]{:S(2)}) collective-permute-start(f32[48,128]{1,0:T(8,128)S(1)} %add.21), channel_id=1, source_target_pairs={{0,4},{1,5},{2,6},{3,7},{4,0},{5,1},{6,2},{7,3},{8,12},{9,13},{10,... | collective-permute-start | bytes 73736 | tf_op jit(solution)/shard_map/ppermute | solution.py:685
  35.2 3.8 %collective-permute-start.8 = (f32[48,128]{1,0:T(8,128)S(1)}, f32[48,128]{1,0:T(8,128)S(1)}, u32[]{:S(2)}, u32[]{:S(2)}) collective-permute-start(f32[48,128]{1,0:T(8,128)S(1)} %add.21), channel_id=1, source_target_pairs={{0,2},{1,3},{2,0},{3,1},{4,6},{5,7},{6,4},{7,5},{8,10},{9,11},{10,... | collective-permute-start | bytes 73736 | tf_op jit(solution)/shard_map/ppermute | solution.py:685
  39.0 6.0 %collective-permute-start.13 = (f32[48,128]{1,0:T(8,128)S(1)}, f32[48,128]{1,0:T(8,128)S(1)}, u32[]{:S(2)}, u32[]{:S(2)}) collective-permute-start(f32[48,128]{1,0:T(8,128)S(1)} %add_add_fusion.1), channel_id=1, source_target_pairs={{0,24},{4,28},{8,16},{12,20},{16,8},{20,12},{24,0},{28,4},{1,25},{... | collective-permute-start | bytes 73736 | tf_op jit(solution)/shard_map/ppermute | solution.py:685
  43.2 4.7 %collective-permute-start.12 = (f32[48,128]{1,0:T(8,128)S(1)}, f32[48,128]{1,0:T(8,128)S(1)}, u32[]{:S(2)}, u32[]{:S(2)}) collective-permute-start(f32[48,128]{1,0:T(8,128)S(1)} %add_add_fusion.1), channel_id=1, source_target_pairs={{0,16},{4,20},{8,24},{12,28},{16,0},{20,4},{24,8},{28,12},{1,17},{... | collective-permute-start | bytes 73736 | tf_op jit(solution)/shard_map/ppermute | solution.py:685
  43.2 4.7 %collective-permute-start.11 = (f32[48,128]{1,0:T(8,128)S(1)}, f32[48,128]{1,0:T(8,128)S(1)}, u32[]{:S(2)}, u32[]{:S(2)}) collective-permute-start(f32[48,128]{1,0:T(8,128)S(1)} %add_add_fusion.1), channel_id=1, source_target_pairs={{0,8},{4,12},{8,0},{12,4},{16,24},{20,28},{24,16},{28,20},{1,9},{5... | collective-permute-start | bytes 73736 | tf_op jit(solution)/shard_map/ppermute | solution.py:685

commit v5 on v4

--- a/solution.py
+++ b/solution.py
@@ -30,6 +30,30 @@
     n = right[0].shape[0 if transposed else 1]
     wide = dot(left[0], jnp.concatenate(right, 0 if transposed else 1), transposed)
     return wide[:, :n] + (wide[:, n:] + dot(left[1], right[0], transposed))
+
+
+def joined(left):
+    return jnp.concatenate([left[0], left[1], left[0]], axis=1)
+
+
+def product_joined(wide, right, transposed=False):
+    high, low = right
+    axis = 0 if transposed else 1
+    n = high.shape[axis]
+    cut = n - TILE
+
+    def part(x, start, stop):
+        return lax.slice_in_dim(x, start, stop, axis=axis)
+
+    first = [part(x, 0, cut) for x in (high, high, low)]
+    last_high, last_low = (part(high, cut, n), part(low, cut, n))
+    last = [
+        jnp.concatenate([last_high, last_low], axis),
+        jnp.concatenate([last_high, jnp.zeros_like(last_high)], axis),
+    ]
+    one = dot(wide, jnp.concatenate(first, 1 - axis), transposed)
+    two = dot(wide[:, : 2 * high.shape[1 - axis]], jnp.concatenate(last, 1 - axis), transposed)
+    return jnp.concatenate([one, two[:, :TILE] + two[:, TILE:]], axis=1)
 
 
 def diagonal_row(matrix):
@@ -124,7 +148,7 @@
         for copy in copies[3 * slab : 3 * slab + 3]:
             copy.wait()
         parts = split(c_buf[slab])
-        steps.append([product(split(g_buf[turn, slab]), parts) for turn in range(2)])
+        steps.append([product_joined(joined(split(g_buf[turn, slab])), parts) for turn in range(2)])
     for copy in copies[6:8]:
         copy.wait()
     for copy in copies[8:]:
@@ -151,9 +175,12 @@
         parts = [[split(steps[slab][turn]) for turn in range(2)] for slab in range(2)]
         states = [lead_buf[turn] for turn in range(2)]
         for slab in range(2):
-            states = [product(parts[slab][turn], split(states[turn])) for turn in range(2)]
             states = [
-                product(split(states[turn]), parts[slab][turn], True) + g_buf[turn, slab]
+                product_joined(joined(parts[slab][turn]), split(states[turn])) for turn in range(2)
+            ]
+            states = [
+                product_joined(joined(split(states[turn])), parts[slab][turn], True)
+                + g_buf[turn, slab]
                 for turn in range(2)
             ]
             for turn in range(2):
@@ -165,9 +192,13 @@
     def _():
         early = [split(steps[0][turn]) for turn in range(2)]
         later = [split(steps[1][turn]) for turn in range(2)]
-        terms = [product(later[turn], split(g_buf[turn, 0])) for turn in range(2)]
-        maps = [product(later[turn], early[turn]) for turn in range(2)]
-        terms = [product(split(terms[turn]), later[turn], True) + g_buf[turn, 1] for turn in range(2)]
+        wide = [joined(later[turn]) for turn in range(2)]
+        terms = [product_joined(wide[turn], split(g_buf[turn, 0])) for turn in range(2)]
+        maps = [product_joined(wide[turn], early[turn]) for turn in range(2)]
+        terms = [
+            product_joined(joined(split(terms[turn])), later[turn], True) + g_buf[turn, 1]
+            for turn in range(2)
+        ]
         for turn in range(2):
             outputs[turn][0:n, :] = maps[turn]
             outputs[turn][n : 2 * n, :] = terms[turn]
@@ -184,10 +215,10 @@
     return product(split(term), composed, True) + map_ref[n : 2 * n, :]
 
 
-def relay_kernel(own, got, field, second, out, wide, cells):
-    place = lax.axis_index("slab")
+def relay_kernel(own, got, field, second, out, wide, cells, one_side, two_side):
+    place, wire = (lax.axis_index("slab"), lax.axis_index("energy"))
     n = own.shape[1]
-    length = field.shape[0]
+    length, rows, _ = field.shape
     even = lax.rem(place, 2) == 0
     wide[REACH : REACH + length] = field[...]
     for plane in range(REACH):
@@ -197,6 +228,12 @@
         wide[REACH + length + plane] = jnp.where(even, one, two)
     spot = slice(2 * n + 8, 2 * n + 16)
     cells[...] = own[spot, :TILE] + got[spot, :TILE] + second[REACH * 8 :, :]
+    even = lax.rem(wire, 2) == 0
+    for plane in range(length + 2 * REACH):
+        low, high = (wide[plane, :REACH, :], wide[plane, rows - REACH :, :])
+        spot = slice(plane * REACH, (plane + 1) * REACH)
+        one_side[spot, :] = jnp.where(even, high, low)
+        two_side[spot, :] = jnp.where(even, low, high)
 
     @pl.when(place == 0)
     def _():
@@ -218,17 +255,48 @@
             pack(advance(far, state[...]), out)
 
 
+def compose_kernel(orbital_atom, member, own, got, own_step, got_step, stack, wide, fold):
+    core = lax.rem(lax.axis_index("slab"), 2)
+    n = own.shape[1]
+    atoms = lax.broadcasted_iota(jnp.int32, (TILE, n), 0)
+    spots = (atoms == orbital_atom[...]).astype(BF16)
+
+    def near_far(mine, other):
+        return jnp.where(core == 0, mine, other), jnp.where(core == 0, other, mine)
+
+    near_step, far_step = near_far(own_step[...], got_step[...])
+    near_map, far_map = near_far(own[0:n, :], got[0:n, :])
+    near_source = jnp.where(core == 0, own[n : 2 * n, :], got[n : 2 * n, :])
+    far = jnp.concatenate([far_step, far_map], axis=0)
+    high, low = split(jnp.concatenate([near_map, near_source], axis=1))
+    both = dot(joined(split(far)), jnp.concatenate([high, high, low], axis=0), False)
+    maps = (near_step, near_map, both[:n, :n], both[n:, :n])
+    for number, value in enumerate(maps):
+        stack[number * n : (number + 1) * n, :] = value
+        wide[number * n : (number + 1) * n, :] = joined(split(value))
+    near_rows, far_rows = near_far(own[2 * n : 2 * n + 2, :], got[2 * n : 2 * n + 2, :])
+    rest = jnp.concatenate([near_rows, far_rows, jnp.zeros((4, n), F32)], axis=0)
+    total = jnp.zeros((8, TILE), F32)
+    for _ in range(3):
+        piece = rest.astype(BF16)
+        total = total + dot(piece, spots, True)
+        rest = rest - piece.astype(F32)
+    fold[...] = total
+    for number in range(2):
+        rows = slice(number * n, (number + 1) * n)
+        value = jnp.sum(far[rows] * both[rows, n:], axis=1, keepdims=True) * member[...]
+        fold[2 + number : 3 + number, :] += jnp.sum(value, axis=0, keepdims=True)
+
+
 def density_kernel(
     pairs,
     weight_ref,
     group_ref,
-    orbital_atom,
     member,
     packed,
-    own,
-    got,
-    own_step,
-    got_step,
+    stack,
+    wide,
+    known,
     extra,
     out,
     state,
@@ -237,49 +305,16 @@
     place = lax.axis_index("slab")
     core = lax.rem(place, 2)
     n = state.shape[0]
-    atoms = lax.broadcasted_iota(jnp.int32, (TILE, n), 0)
-    spots = (atoms == orbital_atom[...]).astype(BF16)
-
-    def folded(matrix, parts):
-        both = matrix * product(split(matrix), parts)
-        return jnp.sum(jnp.sum(both, axis=1, keepdims=True) * member[...], axis=0, keepdims=True)
-
-    for number, (near, near_step, far, far_step) in enumerate(
-        ((own, own_step, got, got_step), (got, got_step, own, own_step))
-    ):
-
-        @pl.when(core == number)
-        def _():
-            rest = jnp.concatenate(
-                [near[2 * n : 2 * n + 2, :], far[2 * n : 2 * n + 2, :], jnp.zeros((4, n), F32)],
-                axis=0,
-            )
-            total = jnp.zeros((8, TILE), F32)
-            for _ in range(3):
-                piece = rest.astype(BF16)
-                total = total + dot(piece, spots, True)
-                rest = rest - piece.astype(F32)
-            fold[...] = total
-
-            @pl.when(place < 2)
-            def _():
-                state[...] = near[n : 2 * n, :]
-
-            @pl.when(place >= 2)
-            def _():
-                unpack(packed, state)
-                parts = split(state[...])
-                fold[0:1, :] += folded(near_step[...], parts)
-                matrix = near[0:n, :]
-                composed = split(matrix)
-                term = product(composed, parts)
-                value = jnp.sum(matrix * term, axis=1, keepdims=True) * member[...]
-                fold[1:2, :] += jnp.sum(value, axis=0, keepdims=True)
-                state[...] = product(split(term), composed, True) + near[n : 2 * n, :]
-
-            parts = split(state[...])
-            fold[2:3, :] += folded(far_step[...], parts)
-            fold[3:4, :] += folded(far[0:n, :], parts)
+    fold[...] = known[...]
+
+    @pl.when(place >= 2)
+    def _():
+        unpack(packed, state)
+        both = product_joined(wide[...], split(state[...]))
+        for number in range(4):
+            rows = slice(number * n, (number + 1) * n)
+            value = jnp.sum(stack[rows, :] * both[rows], axis=1, keepdims=True) * member[...]
+            fold[number : number + 1, :] += jnp.sum(value, axis=0, keepdims=True)
 
     plain = fold[...]
     turned = pltpu.roll(plain, HALF, 1)
@@ -398,7 +433,7 @@
     return result
 
 
-def moments_kernel(devices, wires, own, field, one_beside, two_beside, cells, out, wide_field):
+def moments_kernel(devices, wires, own, field, one_beside, two_beside, cells, out, wide_field, whole_field):
     place, wire = (lax.axis_index("slab"), lax.axis_index("energy"))
     planes, rows, depth = field.shape
     length = planes - 2 * REACH
@@ -408,12 +443,16 @@
     pairs = devices
     n = own.shape[1]
     even = lax.rem(wire, 2) == 0
-    left = jnp.where(even, two_beside[...], one_beside[...])
-    right = jnp.where(even, one_beside[...], two_beside[...])
+    whole_field[...] = jnp.zeros_like(whole_field)
+    whole_field[:, rows : 2 * rows, :] = field[...]
+    for plane in range(planes):
+        spot = slice(plane * REACH, (plane + 1) * REACH)
+        one, two = (one_beside[spot, :], two_beside[spot, :])
+        whole_field[plane, rows - REACH : rows, :] = jnp.where(even, two, one)
+        whole_field[plane, 2 * rows : 2 * rows + REACH, :] = jnp.where(even, one, two)
     whole = (planes, 3 * rows, depth)
     mask = grid_mask(whole, REACH, length, rows, place, devices, wire, wires)
-    source = jnp.concatenate([left, field[...], right], axis=1)
-    source = jnp.where(mask > 0, source, 0.0)
+    source = jnp.where(mask > 0, whole_field[...], 0.0)
     margin = ITERS - 1
     wide_field[...] = source[REACH - margin : REACH + length + margin]
 
@@ -706,7 +745,7 @@
 
 
 def inner_pairs(count):
-    return [(i, i + 1 if i % 2 else i - 1) for i in range(1, count - 1)]
+    return [(i, (i + 1) % count if i % 2 else (i - 1) % count) for i in range(count)]
 
 
 def neighbour_turn(count):
@@ -756,12 +795,15 @@
     )
     got = lax.ppermute(sent, "slab", pairs_of(devices))
     second = lax.ppermute(edge, "slab", neighbour_turn(devices))
-    passed, wide_block, cells = local_call(
+    side = shape((-(-REACH * (length + 2 * REACH) // 8) * 8, depth), F32)
+    passed, wide_block, cells, one_side, two_side = local_call(
         relay_kernel,
         (
             shape((PACKED_ROWS, TILE), F32),
             shape((length + 2 * REACH, rows, depth), F32),
             shape((8, depth), F32),
+            side,
+            side,
         ),
         [],
         "vvvv",
@@ -774,8 +816,8 @@
         second,
     )
     packed = lax.ppermute(passed, "slab", hop(devices, 1))
-    one_beside = lax.ppermute(wide_block, "energy", pairs_of(wires))
-    two_beside = lax.ppermute(wide_block, "energy", inner_pairs(wires))
+    one_beside = lax.ppermute(one_side, "energy", pairs_of(wires))
+    two_beside = lax.ppermute(two_side, "energy", inner_pairs(wires))
     other_cells = lax.ppermute(cells, "slab", pairs_of(devices))
     if devices > 4:
         other_cells = lax.psum(own[2 * n + 8 : 2 * n + 16, :depth], "slab")
@@ -793,7 +835,7 @@
         "vvv",
         "atoms",
         28,
-        2 * 2**30,
+        2**29,
         orbital_row,
         cells,
         other_cells,
@@ -801,16 +843,31 @@
     extra, wide_field = local_call(
         functools.partial(moments_kernel, devices, wires),
         (shape((6 * devices + 8, depth), F32), shape(wide, F32)),
-        [],
+        [pltpu.VMEM((length + 2 * REACH, 3 * rows, depth), F32)],
         "vvvvv",
         "moments",
         20,
-        2**30,
+        2**26,
         own,
         wide_block,
         one_beside,
         two_beside,
         atom_cell,
+    )
+    stack, stack_parts, known = local_call(
+        compose_kernel,
+        (shape((4 * n, n), F32), shape((4 * n, 3 * n), BF16), shape((8, TILE), F32)),
+        [],
+        "vvvvvv",
+        "compose",
+        28,
+        2**28,
+        orbital_row,
+        member,
+        own,
+        got,
+        own_step,
+        got_step,
     )
     for turn in range(1, devices // 2 - 1):
         passed = local_call(
@@ -831,19 +888,17 @@
         functools.partial(density_kernel, devices),
         shape(((groups + 6) * devices + 8, TILE), F32),
         [pltpu.VMEM((n, n), F32), pltpu.VMEM((8, TILE), F32)],
-        "ssvvvvvvvv",
+        "ssvvvvvv",
         "density",
         20,
-        30 * n**3,
+        24 * n**3,
         energy_weight,
         energy_group,
-        orbital_row,
         member,
         packed,
-        own,
-        got,
-        own_step,
-        got_step,
+        stack,
+        stack_parts,
+        known,
         extra,
     )
     payload = total_over_all(payload)

time: 50.2 us -> 46 us (0.916)
  waiting for transfers between devices: 12.3 us -> 9.91 us
  starting transfers between devices: 20.4 us -> 18.9 us
    ppermute x2, waiting for transfers between devices: 2.35 us -> 0.01 us  [the longest x1 0.01 us: on_device(): one_beside = lax.ppermute(one_side, 'energy', pairs_of(wires))]
    ppermute x7, starting transfers between devices: 11.1 us -> 9.84 us  [total_over(): lax.ppermute(value, axis, [(i, i ^ k) for i in range(size)])]
    pallas_call x6 -> x7, Pallas kernels: 16.5 us -> 16.2 us  [local_call(): pl.pallas_call(kernel, out_shape=shapes, in_specs=[pl.BlockSpec(memory_sp...]
  transfers between devices with their start and end apart: 14 -> 14, of which waited for: 7 -> 6; matrix products, arithmetic and copies ran while one was open for 0% -> 0% of each run, Pallas kernels for 8% -> 14%
where the time goes in v5:
time: 46 us; the launch traced here: 45.9 us
  starting transfers between devices  18.9 us (41%)
  Pallas kernels  16.2 us (35%)
  waiting for transfers between devices  9.91 us (22%)
  between operations  0.79 us (2%)
    pallas_call x7, Pallas kernels, local_call(): pl.pallas_call(kernel, out_shape=shapes, in_specs=[pl.BlockSpec(memory_sp...  16.2 us
    ppermute x7, starting transfers between devices, total_over(): lax.ppermute(value, axis, [(i, i ^ k) for i in range(size)])  9.84 us
    ppermute x7, waiting for transfers between devices, total_over(): lax.ppermute(value, axis, [(i, i ^ k) for i in range(size)])  8.37 us
    ppermute x1, starting transfers between devices, on_device(): two_beside = lax.ppermute(two_side, 'energy', inner_pairs(wires))  3.57 us
    ppermute x1, starting transfers between devices, on_device(): one_beside = lax.ppermute(one_side, 'energy', pairs_of(wires))  2.07 us
    ppermute x1, starting transfers between devices, on_device(): second = lax.ppermute(edge, 'slab', neighbour_turn(devices))  1.94 us
    ppermute x1, waiting for transfers between devices, on_device(): second = lax.ppermute(edge, 'slab', neighbour_turn(devices))  1.52 us
  transfers between devices with their start and end apart: 14, of which 6 were waited for; matrix products, arithmetic and copies ran while one was open for 0% of the time, Pallas kernels for 14%

profile of v5, /device:TPU:0, one launch (start us, length us, event | category | flops | bytes accessed | tf_op | source)
XLA Modules:
  0.0 45.9 jit_solution(6731698874680918976)
XLA Ops:
  0.6 0.0 copy-start
  0.6 7.0 %pair.1 = (f32[800,384]{1,0:T(8,128)S(1)}, f32[384,384]{1,0:T(8,128)S(1)}, f32[384,384]{1,0:T(8,128)S(1)}, f32[800,384]{1,0:T(8,128)S(1)}, f32[48,128]{1,0:T(8,128)S(1)}) custom-call(f32[2,2,384,384]{3,2,1,0:T(8,128)} %iso.1, f32[2,384,384]{2,1,0:T(8,128)} %coupling.1, f32[2,384,384]{2,1,0:T(8,128)} %lead.1, s32[2,48]{1,0:T(2,128)} %cells.1, f32[16,8,128]{2,1,0:T(8,128)} %field.1), custom_call_target="tpu_custom_call" | custom-call | flops 4076863488 | bytes 1048576 | tf_op jit(solution)/shard_map/pair/pallas_call | solution.py:337
  7.7 0.1 collective-permute-start
  7.8 0.5 %collective-permute-start.4 = (f32[384,384]{1,0:T(8,128)S(1)}, f32[384,384]{1,0:T(8,128)S(1)}, u32[]{:S(2)}, u32[]{:S(2)}) collective-permute-start(f32[384,384]{1,0:T(8,128)S(1)} %get-tuple-element.28), channel_id=1, source_target_pairs={{0,1},{1,0},{2,3},{3,2},{4,5},{5,4},{6,7},{7,6},{8,9},{9,8},{10,11... | collective-permute-start | bytes 1769480 | tf_op jit(solution)/shard_map/ppermute | solution.py:824
  8.3 1.9 %collective-permute-start.1 = (f32[48,128]{1,0:T(8,128)S(1)}, f32[48,128]{1,0:T(8,128)S(1)}, u32[]{:S(2)}, u32[]{:S(2)}) collective-permute-start(f32[48,128]{1,0:T(8,128)S(1)} %get-tuple-element.23), channel_id=1, source_target_pairs={{0,3},{1,2},{2,1},{3,0},{4,7},{5,6},{6,5},{7,4},{8,11},{9,10},{10,... | collective-permute-start | bytes 73736 | tf_op jit(solution)/shard_map/ppermute | solution.py:797
  10.2 1.5 %collective-permute-done.1.second = f32[48,128]{1,0:T(8,128)S(1)} collective-permute-done((f32[48,128]{1,0:T(8,128)S(1)}, f32[48,128]{1,0:T(8,128)S(1)}, u32[]{:S(2)}, u32[]{:S(2)}) %collective-permute-start.1) | collective-permute-done | bytes 24608 | tf_op jit(solution)/shard_map/ppermute | solution.py:797
  11.7 0.0 collective-permute-done.got
  11.7 0.0 copy-done
  11.7 0.0 copy-start.5
  11.7 1.4 %relay.1 = (f32[648,128]{1,0:T(8,128)S(1)}, f32[26,8,128]{2,1,0:T(8,128)S(1)}, f32[8,128]{1,0:T(8,128)S(1)}, f32[136,128]{1,0:T(8,128)S(1)}, f32[136,128]{1,0:T(8,128)S(1)}) custom-call(f32[800,384]{1,0:T(8,128)S(1)} %get-tuple-element.21.own, f32[800,384]{1,0:T(8,128)S(1)} %collective-permute-done.got, f32[16,8,128]{2,1,0:T(8,128)S(1)} %copy-done, ...), custom_call_target="tpu_custom_call" | custom-call | flops 679477248 | bytes 1048576 | tf_op jit(solution)/shard_map/relay/pallas_call | solution.py:337
  13.2 0.9 %collective-permute-start.3 = (f32[648,128]{1,0:T(8,128)S(1)}, f32[648,128]{1,0:T(8,128)S(1)}, u32[]{:S(2)}, u32[]{:S(2)}) collective-permute-start(f32[648,128]{1,0:T(8,128)S(1)} %get-tuple-element.26), channel_id=1, source_target_pairs={{0,2},{1,3},{2,0},{3,1},{4,6},{5,7},{6,4},{7,5},{8,10},{9,11},{10,... | collective-permute-start | bytes 995336 | tf_op jit(solution)/shard_map/ppermute | solution.py:818
  14.1 0.0 collective-permute-start.2
  14.1 0.0 copy-done.5
  14.1 2.1 %collective-permute-start.5 = (f32[136,128]{1,0:T(8,128)S(1)}, f32[136,128]{1,0:T(8,128)S(1)}, u32[]{:S(2)}, u32[]{:S(2)}) collective-permute-start(f32[136,128]{1,0:T(8,128)S(1)} %get-tuple-element.33), channel_id=1, source_target_pairs={{0,4},{4,0},{8,12},{12,8},{16,20},{20,16},{24,28},{28,24},{1,5},{5... | collective-permute-start | bytes 208904 | tf_op jit(solution)/shard_map/ppermute | solution.py:819
  16.2 3.6 %collective-permute-start.6 = (f32[136,128]{1,0:T(8,128)S(1)}, f32[136,128]{1,0:T(8,128)S(1)}, u32[]{:S(2)}, u32[]{:S(2)}) collective-permute-start(f32[136,128]{1,0:T(8,128)S(1)} %get-tuple-element.34), channel_id=1, source_target_pairs={{0,28},{4,8},{8,4},{12,16},{16,12},{20,24},{24,20},{28,0},{1,29},{... | collective-permute-start | bytes 208904 | tf_op jit(solution)/shard_map/ppermute | solution.py:820
  19.7 0.0 collective-permute-done.2.other_cells
  19.7 1.8 %atoms.1 = (f32[6,384,128]{2,1,0:T(8,128)S(1)}, bf16[480,512]{1,0:T(8,128)(2,1)S(1)}, f32[512,128]{1,0:T(8,128)S(1)}, f32[384,128]{1,0:T(8,128)S(1)}) custom-call(s32[1,384]{1,0:T(1,128)S(1)} %reshape.7.orbital_atom, f32[8,128]{1,0:T(8,128)S(1)} %get-tuple-element.24.some_cells, f32[8,128]{1,0:T(8,128)S(1)} %collective-permute-done.2.other_cells), custom_call_target="tpu_custom_call" | custom-call | flops 536870912 | bytes 1048576 | tf_op jit(solution)/shard_map/atoms/pallas_call | solution.py:337
  21.6 0.0 collective-permute-done.4.got_step
  21.6 0.0 copy-start.1
  21.6 2.1 %compose.1 = (f32[1536,384]{1,0:T(8,128)S(1)}, bf16[1536,1152]{1,0:T(8,128)(2,1)S(1)}, f32[8,128]{1,0:T(8,128)S(1)}) custom-call(s32[1,384]{1,0:T(1,128)S(1)} %reshape.7.orbital_atom, f32[384,128]{1,0:T(8,128)S(1)} %get-tuple-element.25.member, f32[800,384]{1,0:T(8,128)S(1)} %get-tuple-element.21.own, f32[800,384]{1,0:T(8,128)S(1)} %collective-permute-done.got, ...), custom_call_target="tpu_custom_call" | custom-call | flops 268435456 | bytes 1048576 | tf_op jit(solution)/shard_map/compose/pallas_call | solution.py:337
  23.7 0.0 copy-start.3
  23.7 0.0 copy-start.4
  23.7 0.0 collective-permute-done.5.one_beside
  23.7 0.0 collective-permute-done.6.two_beside
  23.7 0.0 copy-done.1
  23.7 1.2 %moments.1 = (f32[32,128]{1,0:T(8,128)S(1)}, f32[20,24,128]{2,1,0:T(8,128)S(1)}) custom-call(f32[800,384]{1,0:T(8,128)S(1)} %get-tuple-element.21.own, f32[26,8,128]{2,1,0:T(8,128)S(1)} %get-tuple-element.32.field, f32[136,128]{1,0:T(8,128)S(1)} %collective-permute-done.5.one_beside, f32[136,128]{1,0:T(8,128)S(1)} %collective-permute-done.6.two_beside, ...), custom_call_target="tpu_custom_call" | custom-call | flops 67108864 | bytes 1048576 | tf_op jit(solution)/shard_map/moments/pallas_call | solution.py:337
  24.9 0.0 collective-permute-done.3.packed
  24.9 0.0 copy-done.3
  24.9 0.0 copy-done.4
  24.9 0.0 copy-start.2
  24.9 0.6 %density.1 = f32[48,128]{1,0:T(8,128)S(1)} custom-call(f32[2]{0:T(128)S(1)} %copy-done.3, s32[2]{0:T(128)S(1)} %copy-done.4, f32[384,128]{1,0:T(8,128)S(1)} %get-tuple-element.25.member, f32[648,128]{1,0:T(8,128)S(1)} %collective-permute-done.3.packed, f32[1536,384]{1,0:T(8,128)S(1)} %get-tuple-element.29.stack, ...), custom_call_target="tpu_custom_call" | custom-call | flops 1358954496 | bytes 1048576 | tf_op jit(solution)/shard_map/density/pallas_call | solution.py:337
  25.6 0.0 collective-permute-start.7
  25.6 1.2 %collective-permute-done.7 = f32[48,128]{1,0:T(8,128)S(1)} collective-permute-done((f32[48,128]{1,0:T(8,128)S(1)}, f32[48,128]{1,0:T(8,128)S(1)}, u32[]{:S(2)}, u32[]{:S(2)}) %collective-permute-start.7) | collective-permute-done | bytes 24608 | tf_op jit(solution)/shard_map/ppermute | solution.py:724
  26.8 2.8 %collective-permute-start.10 = (f32[48,128]{1,0:T(8,128)S(1)}, f32[48,128]{1,0:T(8,128)S(1)}, u32[]{:S(2)}, u32[]{:S(2)}) collective-permute-start(f32[48,128]{1,0:T(8,128)S(1)} %add.21), channel_id=1, source_target_pairs={{0,6},{1,7},{2,4},{3,5},{4,2},{5,3},{6,0},{7,1},{8,14},{9,15},{10,... | collective-permute-start | bytes 73736 | tf_op jit(solution)/shard_map/ppermute | solution.py:724
  29.6 1.2 %collective-permute-start.8 = (f32[48,128]{1,0:T(8,128)S(1)}, f32[48,128]{1,0:T(8,128)S(1)}, u32[]{:S(2)}, u32[]{:S(2)}) collective-permute-start(f32[48,128]{1,0:T(8,128)S(1)} %add.21), channel_id=1, source_target_pairs={{0,2},{1,3},{2,0},{3,1},{4,6},{5,7},{6,4},{7,5},{8,10},{9,11},{10,... | collective-permute-start | bytes 73736 | tf_op jit(solution)/shard_map/ppermute | solution.py:724
  30.8 1.4 %collective-permute-start.9 = (f32[48,128]{1,0:T(8,128)S(1)}, f32[48,128]{1,0:T(8,128)S(1)}, u32[]{:S(2)}, u32[]{:S(2)}) collective-permute-start(f32[48,128]{1,0:T(8,128)S(1)} %add.21), channel_id=1, source_target_pairs={{0,4},{1,5},{2,6},{3,7},{4,0},{5,1},{6,2},{7,3},{8,12},{9,13},{10,... | collective-permute-start | bytes 73736 | tf_op jit(solution)/shard_map/ppermute | solution.py:724
  32.2 0.0 collective-permute-done.10
  32.2 1.3 %collective-permute-done.8 = f32[48,128]{1,0:T(8,128)S(1)} collective-permute-done((f32[48,128]{1,0:T(8,128)S(1)}, f32[48,128]{1,0:T(8,128)S(1)}, u32[]{:S(2)}, u32[]{:S(2)}) %collective-permute-start.8) | collective-permute-done | bytes 24608 | tf_op jit(solution)/shard_map/ppermute | solution.py:724
  33.4 1.2 %collective-permute-done.9 = f32[48,128]{1,0:T(8,128)S(1)} collective-permute-done((f32[48,128]{1,0:T(8,128)S(1)}, f32[48,128]{1,0:T(8,128)S(1)}, u32[]{:S(2)}, u32[]{:S(2)}) %collective-permute-start.9) | collective-permute-done | bytes 24608 | tf_op jit(solution)/shard_map/ppermute | solution.py:724
  34.6 0.5 %collective-permute-start.11 = (f32[48,128]{1,0:T(8,128)S(1)}, f32[48,128]{1,0:T(8,128)S(1)}, u32[]{:S(2)}, u32[]{:S(2)}) collective-permute-start(f32[48,128]{1,0:T(8,128)S(1)} %add_add_fusion.1), channel_id=1, source_target_pairs={{0,8},{4,12},{8,0},{12,4},{16,24},{20,28},{24,16},{28,20},{1,9},{5... | collective-permute-start | bytes 73736 | tf_op jit(solution)/shard_map/ppermute | solution.py:724
  35.1 3.1 %collective-permute-start.12 = (f32[48,128]{1,0:T(8,128)S(1)}, f32[48,128]{1,0:T(8,128)S(1)}, u32[]{:S(2)}, u32[]{:S(2)}) collective-permute-start(f32[48,128]{1,0:T(8,128)S(1)} %add_add_fusion.1), channel_id=1, source_target_pairs={{0,16},{4,20},{8,24},{12,28},{16,0},{20,4},{24,8},{28,12},{1,17},{... | collective-permute-start | bytes 73736 | tf_op jit(solution)/shard_map/ppermute | solution.py:724
  38.2 0.9 %collective-permute-start.13 = (f32[48,128]{1,0:T(8,128)S(1)}, f32[48,128]{1,0:T(8,128)S(1)}, u32[]{:S(2)}, u32[]{:S(2)}) collective-permute-start(f32[48,128]{1,0:T(8,128)S(1)} %add_add_fusion.1), channel_id=1, source_target_pairs={{0,24},{4,28},{8,16},{12,20},{16,8},{20,12},{24,0},{28,4},{1,25},{... | collective-permute-start | bytes 73736 | tf_op jit(solution)/shard_map/ppermute | solution.py:724
  39.1 0.0 collective-permute-done.11
  39.1 0.9 %collective-permute-done.12 = f32[48,128]{1,0:T(8,128)S(1)} collective-permute-done((f32[48,128]{1,0:T(8,128)S(1)}, f32[48,128]{1,0:T(8,128)S(1)}, u32[]{:S(2)}, u32[]{:S(2)}) %collective-permute-start.12) | collective-permute-done | bytes 24608 | tf_op jit(solution)/shard_map/ppermute | solution.py:724
  40.0 3.8 %collective-permute-done.13 = f32[48,128]{1,0:T(8,128)S(1)} collective-permute-done((f32[48,128]{1,0:T(8,128)S(1)}, f32[48,128]{1,0:T(8,128)S(1)}, u32[]{:S(2)}, u32[]{:S(2)}) %collective-permute-start.13) | collective-permute-done | bytes 24608 | tf_op jit(solution)/shard_map/ppermute | solution.py:724
  43.8 0.0 copy-done.2
  43.8 2.1 %finish.1 = (f32[4,2,48]{2,1,0:T(2,128)}, f32[16,8,128]{2,1,0:T(8,128)}) custom-call(f32[4]{0:T(128)S(1)} %copy-done.2, f32[48,128]{1,0:T(8,128)S(1)} %add_add_fusion.payload, f32[6,384,128]{2,1,0:T(8,128)S(1)} %get-tuple-element.36.walks, bf16[480,512]{1,0:T(8,128)(2,1)S(1)} %get-tuple-element.37.row_hot, f32[512,128]{1,0:T(8,128)S(1)} %get-tuple-element.38.deep_hot, ...), custom_call_target="tpu_custom_call" | custom-call | flops 536870912 | bytes 1048576 | tf_op jit(solution)/shard_map/finish/pallas_call | solution.py:337
  (4 shorter events, 0.0 us)
Async XLA Ops:
  0.6 11.1 %copy-start = (f32[16,8,128]{2,1,0:T(8,128)S(1)}, f32[16,8,128]{2,1,0:T(8,128)}, u32[]{:S(2)}) copy-start(f32[16,8,128]{2,1,0:T(8,128)} %field.1) | copy-start | bytes 196612
  7.7 4.0 %collective-permute-start = (f32[800,384]{1,0:T(8,128)S(1)}, f32[800,384]{1,0:T(8,128)S(1)}, u32[]{:S(2)}, u32[]{:S(2)}) collective-permute-start(f32[800,384]{1,0:T(8,128)S(1)} %get-tuple-element.22), channel_id=1, source_target_pairs={{0,1},{1,0},{2,3},{3,2},{4,5},{5,4},{6,7},{7,6},{8,9},{9,8},{10,11... | collective-permute-start | bytes 3686408 | tf_op jit(solution)/shard_map/ppermute | solution.py:796
  7.8 13.8 %collective-permute-start.4 = (f32[384,384]{1,0:T(8,128)S(1)}, f32[384,384]{1,0:T(8,128)S(1)}, u32[]{:S(2)}, u32[]{:S(2)}) collective-permute-start(f32[384,384]{1,0:T(8,128)S(1)} %get-tuple-element.28), channel_id=1, source_target_pairs={{0,1},{1,0},{2,3},{3,2},{4,5},{5,4},{6,7},{7,6},{8,9},{9,8},{10,11... | collective-permute-start | bytes 1769480 | tf_op jit(solution)/shard_map/ppermute | solution.py:824
  8.3 3.5 %collective-permute-start.1 = (f32[48,128]{1,0:T(8,128)S(1)}, f32[48,128]{1,0:T(8,128)S(1)}, u32[]{:S(2)}, u32[]{:S(2)}) collective-permute-start(f32[48,128]{1,0:T(8,128)S(1)} %get-tuple-element.23), channel_id=1, source_target_pairs={{0,3},{1,2},{2,1},{3,0},{4,7},{5,6},{6,5},{7,4},{8,11},{9,10},{10,... | collective-permute-start | bytes 73736 | tf_op jit(solution)/shard_map/ppermute | solution.py:797
  11.7 2.4 %copy-start.5 = (s32[384]{0:T(512)S(1)}, s32[384]{0:T(512)}, u32[]{:S(2)}) copy-start(s32[384]{0:T(512)} %param.15) | copy-start | bytes 4612
  13.2 11.7 %collective-permute-start.3 = (f32[648,128]{1,0:T(8,128)S(1)}, f32[648,128]{1,0:T(8,128)S(1)}, u32[]{:S(2)}, u32[]{:S(2)}) collective-permute-start(f32[648,128]{1,0:T(8,128)S(1)} %get-tuple-element.26), channel_id=1, source_target_pairs={{0,2},{1,3},{2,0},{3,1},{4,6},{5,7},{6,4},{7,5},{8,10},{9,11},{10,... | collective-permute-start | bytes 995336 | tf_op jit(solution)/shard_map/ppermute | solution.py:818
  14.1 5.7 %collective-permute-start.2 = (f32[8,128]{1,0:T(8,128)S(1)}, f32[8,128]{1,0:T(8,128)S(1)}, u32[]{:S(2)}, u32[]{:S(2)}) collective-permute-start(f32[8,128]{1,0:T(8,128)S(1)} %get-tuple-element.24.some_cells), channel_id=1, source_target_pairs={{0,1},{1,0},{2,3},{3,2},{4,5},{5,4},{6,7},{7,6},{8,9},{9,8},{10,11... | collective-permute-start | bytes 12296 | tf_op jit(solution)/shard_map/ppermute | solution.py:821
  14.1 9.6 %collective-permute-start.5 = (f32[136,128]{1,0:T(8,128)S(1)}, f32[136,128]{1,0:T(8,128)S(1)}, u32[]{:S(2)}, u32[]{:S(2)}) collective-permute-start(f32[136,128]{1,0:T(8,128)S(1)} %get-tuple-element.33), channel_id=1, source_target_pairs={{0,4},{4,0},{8,12},{12,8},{16,20},{20,16},{24,28},{28,24},{1,5},{5... | collective-permute-start | bytes 208904 | tf_op jit(solution)/shard_map/ppermute | solution.py:819
  16.2 7.5 %collective-permute-start.6 = (f32[136,128]{1,0:T(8,128)S(1)}, f32[136,128]{1,0:T(8,128)S(1)}, u32[]{:S(2)}, u32[]{:S(2)}) collective-permute-start(f32[136,128]{1,0:T(8,128)S(1)} %get-tuple-element.34), channel_id=1, source_target_pairs={{0,28},{4,8},{8,4},{12,16},{16,12},{20,24},{24,20},{28,0},{1,29},{... | collective-permute-start | bytes 208904 | tf_op jit(solution)/shard_map/ppermute | solution.py:820
  21.6 2.1 %copy-start.1 = (s32[2,48]{1,0:T(2,128)S(1)}, s32[2,48]{1,0:T(2,128)}, u32[]{:S(2)}) copy-start(s32[2,48]{1,0:T(2,128)} %cells.1) | copy-start | bytes 1156
  23.7 1.3 %copy-start.3 = (f32[2]{0:T(128)S(1)}, f32[2]{0:T(128)}, u32[]{:S(2)}) copy-start(f32[2]{0:T(128)} %weight_ref.1) | copy-start | bytes 28
  23.7 1.2 %copy-start.4 = (s32[2]{0:T(128)S(1)}, s32[2]{0:T(128)}, u32[]{:S(2)}) copy-start(s32[2]{0:T(128)} %group_ref.1) | copy-start | bytes 28
  24.9 18.9 %copy-start.2 = (f32[4]{0:T(128)S(1)}, f32[4]{0:T(128)}, u32[]{:S(2)}) copy-start(f32[4]{0:T(128)} %charge_ref.1) | copy-start | bytes 52
  25.6 1.2 %collective-permute-start.7 = (f32[48,128]{1,0:T(8,128)S(1)}, f32[48,128]{1,0:T(8,128)S(1)}, u32[]{:S(2)}, u32[]{:S(2)}) collective-permute-start(f32[48,128]{1,0:T(8,128)S(1)} %density.1), channel_id=1, source_target_pairs={{0,1},{1,0},{2,3},{3,2},{4,5},{5,4},{6,7},{7,6},{8,9},{9,8},{10,11... | collective-permute-start | bytes 73736 | tf_op jit(solution)/shard_map/ppermute | solution.py:724
  26.8 5.4 %collective-permute-start.10 = (f32[48,128]{1,0:T(8,128)S(1)}, f32[48,128]{1,0:T(8,128)S(1)}, u32[]{:S(2)}, u32[]{:S(2)}) collective-permute-start(f32[48,128]{1,0:T(8,128)S(1)} %add.21), channel_id=1, source_target_pairs={{0,6},{1,7},{2,4},{3,5},{4,2},{5,3},{6,0},{7,1},{8,14},{9,15},{10,... | collective-permute-start | bytes 73736 | tf_op jit(solution)/shard_map/ppermute | solution.py:724
  29.6 3.8 %collective-permute-start.8 = (f32[48,128]{1,0:T(8,128)S(1)}, f32[48,128]{1,0:T(8,128)S(1)}, u32[]{:S(2)}, u32[]{:S(2)}) collective-permute-start(f32[48,128]{1,0:T(8,128)S(1)} %add.21), channel_id=1, source_target_pairs={{0,2},{1,3},{2,0},{3,1},{4,6},{5,7},{6,4},{7,5},{8,10},{9,11},{10,... | collective-permute-start | bytes 73736 | tf_op jit(solution)/shard_map/ppermute | solution.py:724
  30.8 3.8 %collective-permute-start.9 = (f32[48,128]{1,0:T(8,128)S(1)}, f32[48,128]{1,0:T(8,128)S(1)}, u32[]{:S(2)}, u32[]{:S(2)}) collective-permute-start(f32[48,128]{1,0:T(8,128)S(1)} %add.21), channel_id=1, source_target_pairs={{0,4},{1,5},{2,6},{3,7},{4,0},{5,1},{6,2},{7,3},{8,12},{9,13},{10,... | collective-permute-start | bytes 73736 | tf_op jit(solution)/shard_map/ppermute | solution.py:724
  34.6 4.5 %collective-permute-start.11 = (f32[48,128]{1,0:T(8,128)S(1)}, f32[48,128]{1,0:T(8,128)S(1)}, u32[]{:S(2)}, u32[]{:S(2)}) collective-permute-start(f32[48,128]{1,0:T(8,128)S(1)} %add_add_fusion.1), channel_id=1, source_target_pairs={{0,8},{4,12},{8,0},{12,4},{16,24},{20,28},{24,16},{28,20},{1,9},{5... | collective-permute-start | bytes 73736 | tf_op jit(solution)/shard_map/ppermute | solution.py:724
  35.1 4.9 %collective-permute-start.12 = (f32[48,128]{1,0:T(8,128)S(1)}, f32[48,128]{1,0:T(8,128)S(1)}, u32[]{:S(2)}, u32[]{:S(2)}) collective-permute-start(f32[48,128]{1,0:T(8,128)S(1)} %add_add_fusion.1), channel_id=1, source_target_pairs={{0,16},{4,20},{8,24},{12,28},{16,0},{20,4},{24,8},{28,12},{1,17},{... | collective-permute-start | bytes 73736 | tf_op jit(solution)/shard_map/ppermute | solution.py:724
  38.2 5.6 %collective-permute-start.13 = (f32[48,128]{1,0:T(8,128)S(1)}, f32[48,128]{1,0:T(8,128)S(1)}, u32[]{:S(2)}, u32[]{:S(2)}) collective-permute-start(f32[48,128]{1,0:T(8,128)S(1)} %add_add_fusion.1), channel_id=1, source_target_pairs={{0,24},{4,28},{8,16},{12,20},{16,8},{20,12},{24,0},{28,4},{1,25},{... | collective-permute-start | bytes 73736 | tf_op jit(solution)/shard_map/ppermute | solution.py:724

commit v6 on v5

--- a/solution.py
+++ b/solution.py
@@ -110,24 +110,62 @@
     return slice((plane % 3) * TILE, (plane % 3 + 1) * TILE)
 
 
-def pair_kernel(
+def copy_all(pairs, sems):
+    copies = [pltpu.make_async_copy(src, dst, sems.at[i]) for i, (src, dst) in enumerate(pairs)]
+    for copy in copies:
+        copy.start()
+    return copies
+
+
+def slabs(early, late, isos, lead, maps, step):
+    place = lax.axis_index("slab")
+    n = early.shape[0]
+
+    @pl.when(place == 0)
+    def _():
+        state = lead[...]
+        for slab, value in enumerate((early, late)):
+            parts = split(value)
+            state = product(parts, split(state))
+            state = product(split(state), parts, True) + isos[slab]
+            maps[2 * n + slab : 2 * n + slab + 1, :] = diagonal_row(state)
+        maps[n : 2 * n, :] = state
+
+    @pl.when(place != 0)
+    def _():
+        later = split(late)
+        wide = joined(later)
+        term = product_joined(wide, split(isos[0]))
+        maps[0:n, :] = product_joined(wide, split(early))
+        term = product(split(term), later, True) + isos[1]
+        maps[n : 2 * n, :] = term
+        maps[2 * n : 2 * n + 1, :] = diagonal_row(isos[0])
+        maps[2 * n + 1 : 2 * n + 2, :] = diagonal_row(term)
+        if step is not None:
+            step[...] = early
+
+
+def other_kernel(
     iso,
     coupling,
     lead,
     cells_in,
     field_in,
-    own,
-    near,
-    first,
+    step,
     sent,
     planes,
+    own_early,
+    own_late,
+    own_iso,
+    own_lead,
     c_buf,
     g_buf,
     lead_buf,
+    sems,
     row,
     cells,
     field,
-    sems,
+    more_sems,
 ):
     place = lax.axis_index("slab")
     core = lax.rem(place, 2)
@@ -135,23 +173,25 @@
     sources = []
     for slab in range(2):
         sources.append((coupling.at[slab], c_buf.at[slab]))
-        for turn, energy in enumerate((core, 1 - core)):
-            sources.append((iso.at[energy, slab], g_buf.at[turn, slab]))
-    for turn, energy in enumerate((core, 1 - core)):
-        sources.append((lead.at[energy], lead_buf.at[turn]))
-    sources += [(cells_in, cells), (field_in, field)]
-    copies = [pltpu.make_async_copy(src, dst, sems.at[i]) for i, (src, dst) in enumerate(sources)]
-    for copy in copies:
-        copy.start()
+        sources.append((iso.at[1 - core, slab], g_buf.at[slab]))
+        sources.append((iso.at[core, slab], own_iso.at[slab]))
+    sources.append((lead.at[1 - core], lead_buf))
+    sources.append((lead.at[core], own_lead))
+    waits = copy_all(sources, sems)
+    copies = copy_all([(cells_in, cells), (field_in, field)], more_sems)
     steps = []
     for slab in range(2):
-        for copy in copies[3 * slab : 3 * slab + 3]:
+        for copy in waits[3 * slab : 3 * slab + 3]:
             copy.wait()
         parts = split(c_buf[slab])
-        steps.append([product_joined(joined(split(g_buf[turn, slab])), parts) for turn in range(2)])
-    for copy in copies[6:8]:
-        copy.wait()
-    for copy in copies[8:]:
+        for buf in (g_buf, own_iso):
+            steps.append(product_joined(joined(split(buf[slab])), parts))
+    waits[6].wait()
+    own_early[...] = steps[1]
+    own_late[...] = steps[3]
+    slabs(steps[0], steps[2], g_buf, lead_buf, sent, step)
+    waits[7].wait()
+    for copy in copies:
         copy.wait()
     atoms = cells.shape[1]
     row[...] = jnp.zeros_like(row)
@@ -159,7 +199,6 @@
     row[0:1, HALF : HALF + atoms] = cells[1:2, :].astype(F32)
     rows = lax.broadcasted_iota(jnp.int32, (8, TILE), 0)
     mine = jnp.where(rows == place, row[0:1, :], 0.0)
-    own[2 * n + 8 : 2 * n + 16, 0:TILE] = mine
     sent[2 * n + 8 : 2 * n + 16, 0:TILE] = mine
     planes[REACH * 8 :, :] = mine
     length = field.shape[0]
@@ -168,44 +207,12 @@
         low, high = (field[plane], field[length - REACH + plane])
         planes[plane * 8 : plane * 8 + 8, :] = jnp.where(even, low, high)
         sent[plane_rows(n, plane), plane_lanes(plane)] = jnp.where(even, high, low)
-    outputs = (own, sent)
-
-    @pl.when(place == 0)
-    def _():
-        parts = [[split(steps[slab][turn]) for turn in range(2)] for slab in range(2)]
-        states = [lead_buf[turn] for turn in range(2)]
-        for slab in range(2):
-            states = [
-                product_joined(joined(parts[slab][turn]), split(states[turn])) for turn in range(2)
-            ]
-            states = [
-                product_joined(joined(split(states[turn])), parts[slab][turn], True)
-                + g_buf[turn, slab]
-                for turn in range(2)
-            ]
-            for turn in range(2):
-                outputs[turn][2 * n + slab : 2 * n + slab + 1, :] = diagonal_row(states[turn])
-        for turn in range(2):
-            outputs[turn][n : 2 * n, :] = states[turn]
-
-    @pl.when(place != 0)
-    def _():
-        early = [split(steps[0][turn]) for turn in range(2)]
-        later = [split(steps[1][turn]) for turn in range(2)]
-        wide = [joined(later[turn]) for turn in range(2)]
-        terms = [product_joined(wide[turn], split(g_buf[turn, 0])) for turn in range(2)]
-        maps = [product_joined(wide[turn], early[turn]) for turn in range(2)]
-        terms = [
-            product_joined(joined(split(terms[turn])), later[turn], True) + g_buf[turn, 1]
-            for turn in range(2)
-        ]
-        for turn in range(2):
-            outputs[turn][0:n, :] = maps[turn]
-            outputs[turn][n : 2 * n, :] = terms[turn]
-            outputs[turn][2 * n : 2 * n + 1, :] = diagonal_row(g_buf[turn, 0])
-            outputs[turn][2 * n + 1 : 2 * n + 2, :] = diagonal_row(terms[turn])
-        near[...] = steps[0][0]
-        first[...] = steps[0][1]
+
+
+def own_kernel(planes, early, late, isos, lead, own):
+    n = lead.shape[0]
+    own[2 * n + 8 : 2 * n + 16, 0:TILE] = planes[REACH * 8 :, :]
+    slabs(early[...], late[...], isos, lead, own, None)
 
 
 def advance(map_ref, state):
@@ -215,10 +222,17 @@
     return product(split(term), composed, True) + map_ref[n : 2 * n, :]
 
 
-def relay_kernel(own, got, field, second, out, wide, cells, one_side, two_side):
+def near_far(mine, other):
+    core = lax.rem(lax.axis_index("slab"), 2)
+    return jnp.where(core == 0, mine, other), jnp.where(core == 0, other, mine)
+
+
+def relay_kernel(
+    own, got, own_step, got_step, field, second, out, stack, parts, wide, cells, one_side, two_side
+):
     place, wire = (lax.axis_index("slab"), lax.axis_index("energy"))
     n = own.shape[1]
-    length, rows, _ = field.shape
+    length, height, _ = field.shape
     even = lax.rem(place, 2) == 0
     wide[REACH : REACH + length] = field[...]
     for plane in range(REACH):
@@ -230,7 +244,7 @@
     cells[...] = own[spot, :TILE] + got[spot, :TILE] + second[REACH * 8 :, :]
     even = lax.rem(wire, 2) == 0
     for plane in range(length + 2 * REACH):
-        low, high = (wide[plane, :REACH, :], wide[plane, rows - REACH :, :])
+        low, high = (wide[plane, :REACH, :], wide[plane, height - REACH :, :])
         spot = slice(plane * REACH, (plane + 1) * REACH)
         one_side[spot, :] = jnp.where(even, high, low)
         two_side[spot, :] = jnp.where(even, low, high)
@@ -242,6 +256,20 @@
     @pl.when(place == 1)
     def _():
         pack(advance(own, got[n : 2 * n, :]), out)
+
+    @pl.when(place >= 2)
+    def _():
+        near_step, far_step = near_far(own_step[...], got_step[...])
+        near_map, far_map = near_far(own[0:n, :], got[0:n, :])
+        far = jnp.concatenate([far_step, far_map], axis=0)
+        both = product_joined(joined(split(far)), split(near_map))
+        for number, value in enumerate((near_step, near_map, both[:n], both[n:])):
+            rows = slice(number * n, (number + 1) * n)
+            stack[rows, :] = value
+            high, low = split(value)
+            parts[rows, :] = jnp.concatenate(
+                [high, low, high[:, : n - TILE], low[:, : n - TILE], high[:, : n - TILE]], axis=1
+            )
 
 
 def pass_kernel(turn, packed, own, got, out, state):
@@ -255,25 +283,15 @@
             pack(advance(far, state[...]), out)
 
 
-def compose_kernel(orbital_atom, member, own, got, own_step, got_step, stack, wide, fold):
-    core = lax.rem(lax.axis_index("slab"), 2)
+def known_kernel(orbital_atom, member, own, got, own_step, got_step, fold):
     n = own.shape[1]
     atoms = lax.broadcasted_iota(jnp.int32, (TILE, n), 0)
     spots = (atoms == orbital_atom[...]).astype(BF16)
-
-    def near_far(mine, other):
-        return jnp.where(core == 0, mine, other), jnp.where(core == 0, other, mine)
-
-    near_step, far_step = near_far(own_step[...], got_step[...])
-    near_map, far_map = near_far(own[0:n, :], got[0:n, :])
-    near_source = jnp.where(core == 0, own[n : 2 * n, :], got[n : 2 * n, :])
+    _, far_step = near_far(own_step[...], got_step[...])
+    _, far_map = near_far(own[0:n, :], got[0:n, :])
+    near_source, _ = near_far(own[n : 2 * n, :], got[n : 2 * n, :])
     far = jnp.concatenate([far_step, far_map], axis=0)
-    high, low = split(jnp.concatenate([near_map, near_source], axis=1))
-    both = dot(joined(split(far)), jnp.concatenate([high, high, low], axis=0), False)
-    maps = (near_step, near_map, both[:n, :n], both[n:, :n])
-    for number, value in enumerate(maps):
-        stack[number * n : (number + 1) * n, :] = value
-        wide[number * n : (number + 1) * n, :] = joined(split(value))
+    both = product_joined(joined(split(far)), split(near_source))
     near_rows, far_rows = near_far(own[2 * n : 2 * n + 2, :], got[2 * n : 2 * n + 2, :])
     rest = jnp.concatenate([near_rows, far_rows, jnp.zeros((4, n), F32)], axis=0)
     total = jnp.zeros((8, TILE), F32)
@@ -284,7 +302,7 @@
     fold[...] = total
     for number in range(2):
         rows = slice(number * n, (number + 1) * n)
-        value = jnp.sum(far[rows] * both[rows, n:], axis=1, keepdims=True) * member[...]
+        value = jnp.sum(far[rows] * both[rows], axis=1, keepdims=True) * member[...]
         fold[2 + number : 3 + number, :] += jnp.sum(value, axis=0, keepdims=True)
 
 
@@ -310,7 +328,17 @@
     @pl.when(place >= 2)
     def _():
         unpack(packed, state)
-        both = product_joined(wide[...], split(state[...]))
+        high, low = split(state[...])
+        cut = n - TILE
+        corner = [x[:cut, :cut] for x in (high, high, low)]
+        one = dot(wide[:, 2 * n :], jnp.concatenate(corner, axis=0), False)
+        last_high, last_low = (high[:, cut:], low[:, cut:])
+        last = [
+            jnp.concatenate([last_high, last_low], axis=1),
+            jnp.concatenate([last_high, jnp.zeros_like(last_high)], axis=1),
+        ]
+        two = dot(wide[:, : 2 * n], jnp.concatenate(last, axis=0), False)
+        both = jnp.concatenate([one, two[:, :TILE] + two[:, TILE:]], axis=1)
         for number in range(4):
             rows = slice(number * n, (number + 1) * n)
             value = jnp.sum(stack[rows, :] * both[rows], axis=1, keepdims=True) * member[...]
@@ -772,46 +800,69 @@
     orbital_row = orbital_atom.reshape(1, n)
     maps = shape((2 * n + 32, n), F32)
     edge_rows = REACH * rows + 8
-    own, own_step, sent_step, sent, edge = local_call(
-        pair_kernel,
-        (maps, shape((n, n), F32), shape((n, n), F32), maps, shape((edge_rows, depth), F32)),
+    held = [
+        pltpu.with_memory_space_constraint(x, pltpu.HBM)
+        for x in (green_iso, coupling, lead_green, atom_cell, doping)
+    ]
+    matrix = shape((n, n), F32)
+    two = shape((2, n, n), F32)
+    sent_step, sent, edge, own_step, own_late, own_iso, own_lead = local_call(
+        other_kernel,
+        (matrix, maps, shape((edge_rows, depth), F32), matrix, matrix, two, matrix),
         [
             pltpu.VMEM((2, n, n), F32),
-            pltpu.VMEM((2, 2, n, n), F32),
             pltpu.VMEM((2, n, n), F32),
+            pltpu.VMEM((n, n), F32),
+            pltpu.SemaphoreType.DMA((8,)),
             pltpu.VMEM((8, TILE), F32),
             pltpu.VMEM(atom_cell.shape, jnp.int32),
             pltpu.VMEM(doping.shape, F32),
-            pltpu.SemaphoreType.DMA((10,)),
+            pltpu.SemaphoreType.DMA((2,)),
         ],
         "hhhhh",
-        "pair",
-        30,
-        72 * n**3,
-        *[
-            pltpu.with_memory_space_constraint(x, pltpu.HBM)
-            for x in (green_iso, coupling, lead_green, atom_cell, doping)
-        ],
+        "other",
+        28,
+        48 * n**3,
+        *held,
     )
     got = lax.ppermute(sent, "slab", pairs_of(devices))
     second = lax.ppermute(edge, "slab", neighbour_turn(devices))
+    own = local_call(
+        own_kernel,
+        maps,
+        [],
+        "vvvvv",
+        "own",
+        24,
+        2**31,
+        edge,
+        own_step,
+        own_late,
+        own_iso,
+        own_lead,
+    )
     side = shape((-(-REACH * (length + 2 * REACH) // 8) * 8, depth), F32)
-    passed, wide_block, cells, one_side, two_side = local_call(
+    got_step = lax.ppermute(sent_step, "slab", pairs_of(devices))
+    passed, stack, stack_parts, wide_block, cells, one_side, two_side = local_call(
         relay_kernel,
         (
             shape((PACKED_ROWS, TILE), F32),
+            shape((4 * n, n), F32),
+            shape((4 * n, 5 * n - 3 * TILE), BF16),
             shape((length + 2 * REACH, rows, depth), F32),
             shape((8, depth), F32),
             side,
             side,
         ),
         [],
-        "vvvv",
+        "vvvvvv",
         "relay",
-        20,
+        28,
         12 * n**3,
         own,
         got,
+        own_step,
+        got_step,
         doping,
         second,
     )
@@ -821,7 +872,6 @@
     other_cells = lax.ppermute(cells, "slab", pairs_of(devices))
     if devices > 4:
         other_cells = lax.psum(own[2 * n + 8 : 2 * n + 16, :depth], "slab")
-    got_step = lax.ppermute(sent_step, "slab", pairs_of(devices))
     wide = (length + 2 * ITERS - 2, 3 * rows, depth)
     walks, row_hot, deep_hot, member = local_call(
         functools.partial(atoms_kernel, devices, wires, length),
@@ -854,13 +904,13 @@
         two_beside,
         atom_cell,
     )
-    stack, stack_parts, known = local_call(
-        compose_kernel,
-        (shape((4 * n, n), F32), shape((4 * n, 3 * n), BF16), shape((8, TILE), F32)),
+    known = local_call(
+        known_kernel,
+        shape((8, TILE), F32),
         [],
         "vvvvvv",
-        "compose",
-        28,
+        "known",
+        24,
         2**28,
         orbital_row,
         member,

time: 46 us -> 43.3 us (0.941)
  waiting for transfers between devices: 9.91 us -> 8.08 us
  starting transfers between devices: 18.9 us -> 17.6 us
    ppermute x1, waiting for transfers between devices: 1.52 us -> 0.01 us  [on_device(): second = lax.ppermute(edge, 'slab', neighbour_turn(devices))]
    ppermute x7, starting transfers between devices: 9.84 us -> 8.82 us  [total_over(): lax.ppermute(value, axis, [(i, i ^ k) for i in range(size)])]
    ppermute x7, waiting for transfers between devices: 8.37 us -> 7.69 us  [total_over(): lax.ppermute(value, axis, [(i, i ^ k) for i in range(size)])]
    ppermute x1, starting transfers between devices: 2.07 us -> 1.55 us  [on_device(): one_beside = lax.ppermute(one_side, 'energy', pairs_of(wires))]
    pallas_call x7 -> x8, Pallas kernels: 16.2 us -> 16.6 us  [local_call(): pl.pallas_call(kernel, out_shape=shapes, in_specs=[pl.BlockSpec(memory_sp...]
  transfers between devices with their start and end apart: 14 -> 14, of which waited for: 6 -> 7; matrix products, arithmetic and copies ran while one was open for 0% -> 0% of each run, Pallas kernels for 14% -> 15%
where the time goes in v6:
time: 43.3 us; the launch traced here: 43.1 us
  starting transfers between devices  17.6 us (41%)
  Pallas kernels  16.6 us (38%)
  waiting for transfers between devices  8.08 us (19%)
  between operations  0.8 us (2%)
    pallas_call x8, Pallas kernels, local_call(): pl.pallas_call(kernel, out_shape=shapes, in_specs=[pl.BlockSpec(memory_sp...  16.6 us
    ppermute x7, starting transfers between devices, total_over(): lax.ppermute(value, axis, [(i, i ^ k) for i in range(size)])  8.82 us
    ppermute x7, waiting for transfers between devices, total_over(): lax.ppermute(value, axis, [(i, i ^ k) for i in range(size)])  7.69 us
    ppermute x1, starting transfers between devices, on_device(): two_beside = lax.ppermute(two_side, 'energy', inner_pairs(wires))  3.57 us
    ppermute x1, starting transfers between devices, on_device(): second = lax.ppermute(edge, 'slab', neighbour_turn(devices))  1.92 us
    ppermute x1, starting transfers between devices, on_device(): one_beside = lax.ppermute(one_side, 'energy', pairs_of(wires))  1.55 us
    ppermute x1, starting transfers between devices, on_device(): packed = lax.ppermute(passed, 'slab', hop(devices, 1))  1.17 us
  transfers between devices with their start and end apart: 14, of which 7 were waited for; matrix products, arithmetic and copies ran while one was open for 0% of the time, Pallas kernels for 15%

profile of v6, /device:TPU:0, one launch (start us, length us, event | category | flops | bytes accessed | tf_op | source)
XLA Modules:
  0.0 43.1 jit_solution(11552045193770740531)
XLA Ops:
  0.6 5.9 %other.1 = (f32[384,384]{1,0:T(8,128)S(1)}, f32[800,384]{1,0:T(8,128)S(1)}, f32[48,128]{1,0:T(8,128)S(1)}, f32[384,384]{1,0:T(8,128)S(1)}, f32[384,384]{1,0:T(8,...) custom-call(f32[2,2,384,384]{3,2,1,0:T(8,128)} %iso.1, f32[2,384,384]{2,1,0:T(8,128)} %coupling.1, ...), custom_call_target="tpu_custom_call" | custom-call | flops 2717908992 | bytes 1048576 | tf_op jit(solution)/shard_map/other/pallas_call | solution.py:365
  6.6 0.1 collective-permute-start
  6.7 0.5 %collective-permute-start.1 = (f32[384,384]{1,0:T(8,128)S(1)}, f32[384,384]{1,0:T(8,128)S(1)}, u32[]{:S(2)}, u32[]{:S(2)}) collective-permute-start(f32[384,384]{1,0:T(8,128)S(1)} %get-tuple-element.28), channel_id=1, source_target_pairs={{0,1},{1,0},{2,3},{3,2},{4,5},{5,4},{6,7},{7,6},{8,9},{9,8},{10,11... | collective-permute-start | bytes 1769480 | tf_op jit(solution)/shard_map/ppermute | solution.py:845
  7.2 1.9 %collective-permute-start.2 = (f32[48,128]{1,0:T(8,128)S(1)}, f32[48,128]{1,0:T(8,128)S(1)}, u32[]{:S(2)}, u32[]{:S(2)}) collective-permute-start(f32[48,128]{1,0:T(8,128)S(1)} %get-tuple-element.22.planes), channel_id=1, source_target_pairs={{0,3},{1,2},{2,1},{3,0},{4,7},{5,6},{6,5},{7,4},{8,11},{9,10},{10,... | collective-permute-start | bytes 73736 | tf_op jit(solution)/shard_map/ppermute | solution.py:829
  9.1 0.0 copy-start
  9.1 2.4 %own.1 = f32[800,384]{1,0:T(8,128)S(1)} custom-call(f32[48,128]{1,0:T(8,128)S(1)} %get-tuple-element.22.planes, f32[384,384]{1,0:T(8,128)S(1)} %get-tuple-element.23.early.own_step, f32[384,384]{1,0:T(8,128)S(1)} %get-tuple-element.24.late, f32[2,384,384]{2,1,0:T(8,128)S(1)} %get-tuple-element.25.isos, f32[384,384]{1,0:T(8,128)S(1)} %get-tuple-element.26.lead), custom_call_target="tpu_custom_call" | custom-call | flops 2147483648 | bytes 1048576 | tf_op jit(solution)/shard_map/own/pallas_call | solution.py:365
  11.5 0.0 copy-start.5
  11.5 0.0 collective-permute-done.2.second
  11.5 0.0 collective-permute-done.1.got_step
  11.5 0.0 collective-permute-done.got
  11.5 0.0 copy-done
  11.5 1.4 %relay.1 = (f32[648,128]{1,0:T(8,128)S(1)}, f32[1536,384]{1,0:T(8,128)S(1)}, bf16[1536,1536]{1,0:T(8,128)(2,1)S(1)}, f32[26,8,128]{2,1,0:T(8,128)S(1)}, f32[8,12...) custom-call(f32[800,384]{1,0:T(8,128)S(1)} %own.1, f32[800,384]{1,0:T(8,128)S(1)} %collective-permute-done.got, ...), custom_call_target="tpu_custom_call" | custom-call | flops 679477248 | bytes 1048576 | tf_op jit(solution)/shard_map/relay/pallas_call | solution.py:365
  12.9 1.2 %collective-permute-start.4 = (f32[648,128]{1,0:T(8,128)S(1)}, f32[648,128]{1,0:T(8,128)S(1)}, u32[]{:S(2)}, u32[]{:S(2)}) collective-permute-start(f32[648,128]{1,0:T(8,128)S(1)} %get-tuple-element.31), channel_id=1, source_target_pairs={{0,2},{1,3},{2,0},{3,1},{4,6},{5,7},{6,4},{7,5},{8,10},{9,11},{10,... | collective-permute-start | bytes 995336 | tf_op jit(solution)/shard_map/ppermute | solution.py:869
  14.1 0.0 collective-permute-start.3
  14.1 0.0 copy-done.5
  14.1 1.6 %collective-permute-start.5 = (f32[136,128]{1,0:T(8,128)S(1)}, f32[136,128]{1,0:T(8,128)S(1)}, u32[]{:S(2)}, u32[]{:S(2)}) collective-permute-start(f32[136,128]{1,0:T(8,128)S(1)} %get-tuple-element.35), channel_id=1, source_target_pairs={{0,4},{4,0},{8,12},{12,8},{16,20},{20,16},{24,28},{28,24},{1,5},{5... | collective-permute-start | bytes 208904 | tf_op jit(solution)/shard_map/ppermute | solution.py:870
  15.7 3.6 %collective-permute-start.6 = (f32[136,128]{1,0:T(8,128)S(1)}, f32[136,128]{1,0:T(8,128)S(1)}, u32[]{:S(2)}, u32[]{:S(2)}) collective-permute-start(f32[136,128]{1,0:T(8,128)S(1)} %get-tuple-element.36), channel_id=1, source_target_pairs={{0,28},{4,8},{8,4},{12,16},{16,12},{20,24},{24,20},{28,0},{1,29},{... | collective-permute-start | bytes 208904 | tf_op jit(solution)/shard_map/ppermute | solution.py:871
  19.2 0.0 collective-permute-done.3.other_cells
  19.2 1.8 %atoms.1 = (f32[6,384,128]{2,1,0:T(8,128)S(1)}, bf16[480,512]{1,0:T(8,128)(2,1)S(1)}, f32[512,128]{1,0:T(8,128)S(1)}, f32[384,128]{1,0:T(8,128)S(1)}) custom-call(s32[1,384]{1,0:T(1,128)S(1)} %reshape.7.orbital_atom, f32[8,128]{1,0:T(8,128)S(1)} %get-tuple-element.29.some_cells, f32[8,128]{1,0:T(8,128)S(1)} %collective-permute-done.3.other_cells), custom_call_target="tpu_custom_call" | custom-call | flops 536870912 | bytes 1048576 | tf_op jit(solution)/shard_map/atoms/pallas_call | solution.py:365
  21.1 0.0 copy-start.1
  21.1 1.2 %known.1 = f32[8,128]{1,0:T(8,128)S(1)} custom-call(s32[1,384]{1,0:T(1,128)S(1)} %reshape.7.orbital_atom, f32[384,128]{1,0:T(8,128)S(1)} %get-tuple-element.30.member, f32[800,384]{1,0:T(8,128)S(1)} %own.1, f32[800,384]{1,0:T(8,128)S(1)} %collective-permute-done.got, f32[384,384]{1,0:T(8,128)S(1)} %get-tuple-element.23.early.own_step, ...), custom_call_target="tpu_custom_call" | custom-call | flops 268435456 | bytes 1048576 | tf_op jit(solution)/shard_map/known/pallas_call | solution.py:365
  22.3 0.0 copy-start.2
  22.3 0.0 copy-start.3
  22.3 0.0 collective-permute-done.5.one_beside
  22.3 0.4 collective-permute-done.6.two_beside
  22.7 0.0 copy-done.1
  22.7 1.2 %moments.1 = (f32[32,128]{1,0:T(8,128)S(1)}, f32[20,24,128]{2,1,0:T(8,128)S(1)}) custom-call(f32[800,384]{1,0:T(8,128)S(1)} %own.1, f32[26,8,128]{2,1,0:T(8,128)S(1)} %get-tuple-element.34.field, f32[136,128]{1,0:T(8,128)S(1)} %collective-permute-done.5.one_beside, f32[136,128]{1,0:T(8,128)S(1)} %collective-permute-done.6.two_beside, s32[2,48]{1,0:T(2,128)S(1)} %copy-done.1), custom_call_target="tpu_custom_call" | custom-call | flops 67108864 | bytes 1048576 | tf_op jit(solution)/shard_map/moments/pallas_call | solution.py:365
  23.9 0.0 collective-permute-done.4.packed
  23.9 0.0 copy-done.2
  23.9 0.0 copy-done.3
  23.9 0.0 copy-start.4
  23.9 0.6 %density.1 = f32[48,128]{1,0:T(8,128)S(1)} custom-call(f32[2]{0:T(128)S(1)} %copy-done.2, s32[2]{0:T(128)S(1)} %copy-done.3, f32[384,128]{1,0:T(8,128)S(1)} %get-tuple-element.30.member, f32[648,128]{1,0:T(8,128)S(1)} %collective-permute-done.4.packed, f32[1536,384]{1,0:T(8,128)S(1)} %get-tuple-element.32.stack, ...), custom_call_target="tpu_custom_call" | custom-call | flops 1358954496 | bytes 1048576 | tf_op jit(solution)/shard_map/density/pallas_call | solution.py:365
  24.5 0.0 collective-permute-start.7
  24.6 1.2 %collective-permute-done.7 = f32[48,128]{1,0:T(8,128)S(1)} collective-permute-done((f32[48,128]{1,0:T(8,128)S(1)}, f32[48,128]{1,0:T(8,128)S(1)}, u32[]{:S(2)}, u32[]{:S(2)}) %collective-permute-start.7) | collective-permute-done | bytes 24608 | tf_op jit(solution)/shard_map/ppermute | solution.py:752
  25.7 2.6 %collective-permute-start.10 = (f32[48,128]{1,0:T(8,128)S(1)}, f32[48,128]{1,0:T(8,128)S(1)}, u32[]{:S(2)}, u32[]{:S(2)}) collective-permute-start(f32[48,128]{1,0:T(8,128)S(1)} %add.21), channel_id=1, source_target_pairs={{0,6},{1,7},{2,4},{3,5},{4,2},{5,3},{6,0},{7,1},{8,14},{9,15},{10,... | collective-permute-start | bytes 73736 | tf_op jit(solution)/shard_map/ppermute | solution.py:752
  28.3 1.8 %collective-permute-start.9 = (f32[48,128]{1,0:T(8,128)S(1)}, f32[48,128]{1,0:T(8,128)S(1)}, u32[]{:S(2)}, u32[]{:S(2)}) collective-permute-start(f32[48,128]{1,0:T(8,128)S(1)} %add.21), channel_id=1, source_target_pairs={{0,4},{1,5},{2,6},{3,7},{4,0},{5,1},{6,2},{7,3},{8,12},{9,13},{10,... | collective-permute-start | bytes 73736 | tf_op jit(solution)/shard_map/ppermute | solution.py:752
  30.1 0.0 collective-permute-start.8
  30.1 0.4 collective-permute-done.10
  30.5 1.7 %collective-permute-done.9 = f32[48,128]{1,0:T(8,128)S(1)} collective-permute-done((f32[48,128]{1,0:T(8,128)S(1)}, f32[48,128]{1,0:T(8,128)S(1)}, u32[]{:S(2)}, u32[]{:S(2)}) %collective-permute-start.9) | collective-permute-done | bytes 24608 | tf_op jit(solution)/shard_map/ppermute | solution.py:752
  32.2 1.8 %collective-permute-done.8 = f32[48,128]{1,0:T(8,128)S(1)} collective-permute-done((f32[48,128]{1,0:T(8,128)S(1)}, f32[48,128]{1,0:T(8,128)S(1)}, u32[]{:S(2)}, u32[]{:S(2)}) %collective-permute-start.8) | collective-permute-done | bytes 24608 | tf_op jit(solution)/shard_map/ppermute | solution.py:752
  33.9 2.4 %collective-permute-start.13 = (f32[48,128]{1,0:T(8,128)S(1)}, f32[48,128]{1,0:T(8,128)S(1)}, u32[]{:S(2)}, u32[]{:S(2)}) collective-permute-start(f32[48,128]{1,0:T(8,128)S(1)} %add_add_fusion.1), channel_id=1, source_target_pairs={{0,24},{4,28},{8,16},{12,20},{16,8},{20,12},{24,0},{28,4},{1,25},{... | collective-permute-start | bytes 73736 | tf_op jit(solution)/shard_map/ppermute | solution.py:752
  36.3 0.0 collective-permute-start.12
  36.3 2.0 %collective-permute-start.11 = (f32[48,128]{1,0:T(8,128)S(1)}, f32[48,128]{1,0:T(8,128)S(1)}, u32[]{:S(2)}, u32[]{:S(2)}) collective-permute-start(f32[48,128]{1,0:T(8,128)S(1)} %add_add_fusion.1), channel_id=1, source_target_pairs={{0,8},{4,12},{8,0},{12,4},{16,24},{20,28},{24,16},{28,20},{1,9},{5... | collective-permute-start | bytes 73736 | tf_op jit(solution)/shard_map/ppermute | solution.py:752
  38.4 1.4 %collective-permute-done.13 = f32[48,128]{1,0:T(8,128)S(1)} collective-permute-done((f32[48,128]{1,0:T(8,128)S(1)}, f32[48,128]{1,0:T(8,128)S(1)}, u32[]{:S(2)}, u32[]{:S(2)}) %collective-permute-start.13) | collective-permute-done | bytes 24608 | tf_op jit(solution)/shard_map/ppermute | solution.py:752
  39.8 1.3 %collective-permute-done.12 = f32[48,128]{1,0:T(8,128)S(1)} collective-permute-done((f32[48,128]{1,0:T(8,128)S(1)}, f32[48,128]{1,0:T(8,128)S(1)}, u32[]{:S(2)}, u32[]{:S(2)}) %collective-permute-start.12) | collective-permute-done | bytes 24608 | tf_op jit(solution)/shard_map/ppermute | solution.py:752
  41.1 0.0 collective-permute-done.11
  41.1 0.0 copy-done.4
  41.1 2.0 %finish.1 = (f32[4,2,48]{2,1,0:T(2,128)}, f32[16,8,128]{2,1,0:T(8,128)}) custom-call(f32[4]{0:T(128)S(1)} %copy-done.4, f32[48,128]{1,0:T(8,128)S(1)} %add_add_fusion.payload, f32[6,384,128]{2,1,0:T(8,128)S(1)} %get-tuple-element.38.walks, bf16[480,512]{1,0:T(8,128)(2,1)S(1)} %get-tuple-element.39.row_hot, f32[512,128]{1,0:T(8,128)S(1)} %get-tuple-element.40.deep_hot, ...), custom_call_target="tpu_custom_call" | custom-call | flops 536870912 | bytes 1048576 | tf_op jit(solution)/shard_map/finish/pallas_call | solution.py:365
  (4 shorter events, 0.0 us)
Async XLA Ops:
  6.6 4.9 %collective-permute-start = (f32[800,384]{1,0:T(8,128)S(1)}, f32[800,384]{1,0:T(8,128)S(1)}, u32[]{:S(2)}, u32[]{:S(2)}) collective-permute-start(f32[800,384]{1,0:T(8,128)S(1)} %get-tuple-element.27), channel_id=1, source_target_pairs={{0,1},{1,0},{2,3},{3,2},{4,5},{5,4},{6,7},{7,6},{8,9},{9,8},{10,11... | collective-permute-start | bytes 3686408 | tf_op jit(solution)/shard_map/ppermute | solution.py:828
  6.7 4.8 %collective-permute-start.1 = (f32[384,384]{1,0:T(8,128)S(1)}, f32[384,384]{1,0:T(8,128)S(1)}, u32[]{:S(2)}, u32[]{:S(2)}) collective-permute-start(f32[384,384]{1,0:T(8,128)S(1)} %get-tuple-element.28), channel_id=1, source_target_pairs={{0,1},{1,0},{2,3},{3,2},{4,5},{5,4},{6,7},{7,6},{8,9},{9,8},{10,11... | collective-permute-start | bytes 1769480 | tf_op jit(solution)/shard_map/ppermute | solution.py:845
  7.2 4.3 %collective-permute-start.2 = (f32[48,128]{1,0:T(8,128)S(1)}, f32[48,128]{1,0:T(8,128)S(1)}, u32[]{:S(2)}, u32[]{:S(2)}) collective-permute-start(f32[48,128]{1,0:T(8,128)S(1)} %get-tuple-element.22.planes), channel_id=1, source_target_pairs={{0,3},{1,2},{2,1},{3,0},{4,7},{5,6},{6,5},{7,4},{8,11},{9,10},{10,... | collective-permute-start | bytes 73736 | tf_op jit(solution)/shard_map/ppermute | solution.py:829
  9.1 2.4 %copy-start = (f32[16,8,128]{2,1,0:T(8,128)S(1)}, f32[16,8,128]{2,1,0:T(8,128)}, u32[]{:S(2)}) copy-start(f32[16,8,128]{2,1,0:T(8,128)} %field.1) | copy-start | bytes 196612
  11.5 2.7 %copy-start.5 = (s32[384]{0:T(512)S(1)}, s32[384]{0:T(512)}, u32[]{:S(2)}) copy-start(s32[384]{0:T(512)} %param.15) | copy-start | bytes 4612
  12.9 10.9 %collective-permute-start.4 = (f32[648,128]{1,0:T(8,128)S(1)}, f32[648,128]{1,0:T(8,128)S(1)}, u32[]{:S(2)}, u32[]{:S(2)}) collective-permute-start(f32[648,128]{1,0:T(8,128)S(1)} %get-tuple-element.31), channel_id=1, source_target_pairs={{0,2},{1,3},{2,0},{3,1},{4,6},{5,7},{6,4},{7,5},{8,10},{9,11},{10,... | collective-permute-start | bytes 995336 | tf_op jit(solution)/shard_map/ppermute | solution.py:869
  14.1 5.1 %collective-permute-start.3 = (f32[8,128]{1,0:T(8,128)S(1)}, f32[8,128]{1,0:T(8,128)S(1)}, u32[]{:S(2)}, u32[]{:S(2)}) collective-permute-start(f32[8,128]{1,0:T(8,128)S(1)} %get-tuple-element.29.some_cells), channel_id=1, source_target_pairs={{0,1},{1,0},{2,3},{3,2},{4,5},{5,4},{6,7},{7,6},{8,9},{9,8},{10,11... | collective-permute-start | bytes 12296 | tf_op jit(solution)/shard_map/ppermute | solution.py:872
  14.1 8.2 %collective-permute-start.5 = (f32[136,128]{1,0:T(8,128)S(1)}, f32[136,128]{1,0:T(8,128)S(1)}, u32[]{:S(2)}, u32[]{:S(2)}) collective-permute-start(f32[136,128]{1,0:T(8,128)S(1)} %get-tuple-element.35), channel_id=1, source_target_pairs={{0,4},{4,0},{8,12},{12,8},{16,20},{20,16},{24,28},{28,24},{1,5},{5... | collective-permute-start | bytes 208904 | tf_op jit(solution)/shard_map/ppermute | solution.py:870
  15.7 7.0 %collective-permute-start.6 = (f32[136,128]{1,0:T(8,128)S(1)}, f32[136,128]{1,0:T(8,128)S(1)}, u32[]{:S(2)}, u32[]{:S(2)}) collective-permute-start(f32[136,128]{1,0:T(8,128)S(1)} %get-tuple-element.36), channel_id=1, source_target_pairs={{0,28},{4,8},{8,4},{12,16},{16,12},{20,24},{24,20},{28,0},{1,29},{... | collective-permute-start | bytes 208904 | tf_op jit(solution)/shard_map/ppermute | solution.py:871
  21.1 1.6 %copy-start.1 = (s32[2,48]{1,0:T(2,128)S(1)}, s32[2,48]{1,0:T(2,128)}, u32[]{:S(2)}) copy-start(s32[2,48]{1,0:T(2,128)} %cells.1) | copy-start | bytes 1156
  22.3 1.6 %copy-start.2 = (f32[2]{0:T(128)S(1)}, f32[2]{0:T(128)}, u32[]{:S(2)}) copy-start(f32[2]{0:T(128)} %weight_ref.1) | copy-start | bytes 28
  22.3 1.6 %copy-start.3 = (s32[2]{0:T(128)S(1)}, s32[2]{0:T(128)}, u32[]{:S(2)}) copy-start(s32[2]{0:T(128)} %group_ref.1) | copy-start | bytes 28
  23.9 17.2 %copy-start.4 = (f32[4]{0:T(128)S(1)}, f32[4]{0:T(128)}, u32[]{:S(2)}) copy-start(f32[4]{0:T(128)} %charge_ref.1) | copy-start | bytes 52
  24.5 1.2 %collective-permute-start.7 = (f32[48,128]{1,0:T(8,128)S(1)}, f32[48,128]{1,0:T(8,128)S(1)}, u32[]{:S(2)}, u32[]{:S(2)}) collective-permute-start(f32[48,128]{1,0:T(8,128)S(1)} %density.1), channel_id=1, source_target_pairs={{0,1},{1,0},{2,3},{3,2},{4,5},{5,4},{6,7},{7,6},{8,9},{9,8},{10,11... | collective-permute-start | bytes 73736 | tf_op jit(solution)/shard_map/ppermute | solution.py:752
  25.7 4.7 %collective-permute-start.10 = (f32[48,128]{1,0:T(8,128)S(1)}, f32[48,128]{1,0:T(8,128)S(1)}, u32[]{:S(2)}, u32[]{:S(2)}) collective-permute-start(f32[48,128]{1,0:T(8,128)S(1)} %add.21), channel_id=1, source_target_pairs={{0,6},{1,7},{2,4},{3,5},{4,2},{5,3},{6,0},{7,1},{8,14},{9,15},{10,... | collective-permute-start | bytes 73736 | tf_op jit(solution)/shard_map/ppermute | solution.py:752
  28.3 3.9 %collective-permute-start.9 = (f32[48,128]{1,0:T(8,128)S(1)}, f32[48,128]{1,0:T(8,128)S(1)}, u32[]{:S(2)}, u32[]{:S(2)}) collective-permute-start(f32[48,128]{1,0:T(8,128)S(1)} %add.21), channel_id=1, source_target_pairs={{0,4},{1,5},{2,6},{3,7},{4,0},{5,1},{6,2},{7,3},{8,12},{9,13},{10,... | collective-permute-start | bytes 73736 | tf_op jit(solution)/shard_map/ppermute | solution.py:752
  30.1 3.8 %collective-permute-start.8 = (f32[48,128]{1,0:T(8,128)S(1)}, f32[48,128]{1,0:T(8,128)S(1)}, u32[]{:S(2)}, u32[]{:S(2)}) collective-permute-start(f32[48,128]{1,0:T(8,128)S(1)} %add.21), channel_id=1, source_target_pairs={{0,2},{1,3},{2,0},{3,1},{4,6},{5,7},{6,4},{7,5},{8,10},{9,11},{10,... | collective-permute-start | bytes 73736 | tf_op jit(solution)/shard_map/ppermute | solution.py:752
  33.9 5.8 %collective-permute-start.13 = (f32[48,128]{1,0:T(8,128)S(1)}, f32[48,128]{1,0:T(8,128)S(1)}, u32[]{:S(2)}, u32[]{:S(2)}) collective-permute-start(f32[48,128]{1,0:T(8,128)S(1)} %add_add_fusion.1), channel_id=1, source_target_pairs={{0,24},{4,28},{8,16},{12,20},{16,8},{20,12},{24,0},{28,4},{1,25},{... | collective-permute-start | bytes 73736 | tf_op jit(solution)/shard_map/ppermute | solution.py:752
  36.3 4.7 %collective-permute-start.12 = (f32[48,128]{1,0:T(8,128)S(1)}, f32[48,128]{1,0:T(8,128)S(1)}, u32[]{:S(2)}, u32[]{:S(2)}) collective-permute-start(f32[48,128]{1,0:T(8,128)S(1)} %add_add_fusion.1), channel_id=1, source_target_pairs={{0,16},{4,20},{8,24},{12,28},{16,0},{20,4},{24,8},{28,12},{1,17},{... | collective-permute-start | bytes 73736 | tf_op jit(solution)/shard_map/ppermute | solution.py:752
  36.3 4.7 %collective-permute-start.11 = (f32[48,128]{1,0:T(8,128)S(1)}, f32[48,128]{1,0:T(8,128)S(1)}, u32[]{:S(2)}, u32[]{:S(2)}) collective-permute-start(f32[48,128]{1,0:T(8,128)S(1)} %add_add_fusion.1), channel_id=1, source_target_pairs={{0,8},{4,12},{8,0},{12,4},{16,24},{20,28},{24,16},{28,20},{1,9},{5... | collective-permute-start | bytes 73736 | tf_op jit(solution)/shard_map/ppermute | solution.py:752

commit v7 on v6

--- a/solution.py
+++ b/solution.py
@@ -283,7 +283,22 @@
             pack(advance(far, state[...]), out)
 
 
-def known_kernel(orbital_atom, member, own, got, own_step, got_step, fold):
+def known_kernel(
+    pairs, weight_ref, group_ref, orbital_atom, member, own, got, own_step, got_step, fold, weights
+):
+    place = lax.axis_index("slab")
+    core = lax.rem(place, 2)
+    pair_rows = lax.broadcasted_iota(jnp.int32, (pairs, TILE), 0)
+    mine_weight = jnp.where(core == 0, weight_ref[:, 0:1], weight_ref[:, 1:2])
+    mine_group = jnp.where(core == 0, group_ref[:, 0:1], group_ref[:, 1:2])
+    groups = weights.shape[0] // (2 * pairs)
+    for half in range(2):
+        for group in range(groups):
+            weight = jnp.where(mine_group == group, mine_weight, 0.0)
+            start = (half * groups + group) * pairs
+            weights[start : start + pairs, :] = jnp.where(
+                pair_rows == place - core + half, jnp.broadcast_to(weight, (pairs, TILE)), 0.0
+            )
     n = own.shape[1]
     atoms = lax.broadcasted_iota(jnp.int32, (TILE, n), 0)
     spots = (atoms == orbital_atom[...]).astype(BF16)
@@ -308,20 +323,18 @@
 
 def density_kernel(
     pairs,
-    weight_ref,
-    group_ref,
     member,
     packed,
     stack,
     wide,
     known,
+    weights,
     extra,
     out,
     state,
     fold,
 ):
     place = lax.axis_index("slab")
-    core = lax.rem(place, 2)
     n = state.shape[0]
     fold[...] = known[...]
 
@@ -346,16 +359,10 @@
 
     plain = fold[...]
     turned = pltpu.roll(plain, HALF, 1)
-    pair_rows = lax.broadcasted_iota(jnp.int32, (pairs, TILE), 0)
-    groups = (out.shape[0] - extra.shape[0]) // pairs
-    for group in range(groups):
-        weight = jnp.where(group_ref[core] == group, weight_ref[core], 0.0)
-        block = jnp.zeros((pairs, TILE), F32)
-        for half in range(2):
-            value = plain[2 * half : 2 * half + 1, :] + turned[2 * half + 1 : 2 * half + 2, :]
-            block = block + jnp.where(pair_rows == place - core + half, weight, 0.0) * value
-        out[group * pairs : (group + 1) * pairs, :] = block
-    out[groups * pairs :, :] = extra[...]
+    rows = out.shape[0] - extra.shape[0]
+    values = [plain[2 * i : 2 * i + 1, :] + turned[2 * i + 1 : 2 * i + 2, :] for i in range(2)]
+    out[:rows, :] = weights[:rows, :] * values[0] + weights[rows:, :] * values[1]
+    out[rows:, :] = extra[...]
 
 
 def local_call(kernel, shapes, scratch, specs, name, limit, flops, *operands):
@@ -497,15 +504,14 @@
     for step in range(1, 4):
         other.append(differences(other[-1]) * mask[2 + step : planes - 2 - step])
     other = [inner(x) for x in other]
-    lanes = lax.broadcasted_iota(jnp.int32, (8, depth), 1)
-    sums = jnp.zeros((8, depth), F32)
+    lanes = lax.broadcasted_iota(jnp.int32, (1, depth), 1)
+    sums = jnp.zeros((1, depth), F32)
     for base, fields in enumerate((blocks, other)):
         for steps in range(6):
             part = jnp.sum(fields[steps // 2] * fields[(steps + 1) // 2], axis=0)
             part = jnp.sum(jnp.sum(part, axis=1, keepdims=True), axis=0, keepdims=True)
-            sums = jnp.where(lanes == 8 * base + steps, part, sums)
+            sums = jnp.where(lanes == atoms + 6 * base + steps, part, sums)
     out[...] = jnp.zeros_like(out)
-    out[6 * pairs : 6 * pairs + 8, :] = sums
     mine = own[2 * n + 8 : 2 * n + 16, :depth]
     mine = jnp.sum(mine, axis=0, keepdims=True)
     lane = lax.broadcasted_iota(jnp.int32, (1, depth), 1)
@@ -526,12 +532,14 @@
             value = value + dot(part, at_deep, False)
         value = jnp.sum(value * at_rows, axis=0, keepdims=True)
         out[pl.ds(steps * pairs + place, 1), :] = value
+    out[0:1, :] += sums
 
 
 def atoms_kernel(
     devices,
     wires,
     length,
+    charge_ref,
     orbital_atom,
     some_cells,
     other_cells,
@@ -539,6 +547,7 @@
     row_hot,
     deep_hot,
     member,
+    charges,
 ):
     place, wire = (lax.axis_index("slab"), lax.axis_index("energy"))
     rows, depth = some_cells.shape
@@ -548,6 +557,10 @@
     pairs = devices
     n = orbital_atom.shape[1]
     start = (wire * rows).astype(F32)
+    for group in range(charges.shape[0] // pairs):
+        charges[group * pairs : (group + 1) * pairs, :] = jnp.broadcast_to(
+            charge_ref[:, group : group + 1], (pairs, depth)
+        )
     cells = jnp.maximum(some_cells[...], other_cells[...])
     spots = lax.broadcasted_iota(jnp.int32, (TILE, n), 0) == orbital_atom[...]
     spots = spots.astype(F32)
@@ -633,11 +646,11 @@
     devices,
     wires,
     atoms,
-    charge_ref,
     payload,
     walks,
     row_hot,
     deep_hot,
+    charges,
     field,
     density,
     potential,
@@ -646,9 +659,10 @@
     length, rows, depth = potential.shape
     pairs = devices
     groups = density.shape[0]
-    charge = charge_ref[0] * payload[0:pairs, :]
+    held = charges[...] * payload[: groups * pairs, :]
+    charge = held[:pairs]
     for group in range(1, groups):
-        charge = charge + charge_ref[group] * payload[group * pairs : (group + 1) * pairs, :]
+        charge = charge + held[group * pairs : (group + 1) * pairs]
     for group in range(groups):
         value = payload[pl.ds(group * pairs + place, 1), :]
         density[group, 0:1, :] = value[:, :atoms]
@@ -672,12 +686,22 @@
     crossed = []
     for steps in range(6):
         cross = 2.0 * charge * payload[base + steps * pairs : base + (steps + 1) * pairs, :]
-        crossed.append(total_of(totals[steps]) + total_of(cross))
-    sums = payload[base + 6 * pairs : base + 6 * pairs + 1, :]
-    plain = [sums[:, steps : steps + 1] + crossed[steps] for steps in range(6)]
+        parts = [totals[steps][i : i + 8] for i in range(0, atoms, 8)]
+        if pairs < 8:
+            cross = jnp.concatenate([cross, jnp.zeros((8 - pairs, depth), F32)], axis=0)
+        parts.append(cross)
+        while len(parts) > 1:
+            parts = [sum(parts[i : i + 2][1:], parts[i]) for i in range(0, len(parts), 2)]
+        crossed.append(total_of(parts[0]))
+    lane = lax.broadcasted_iota(jnp.int32, (1, depth), 1)
+    row = payload[base : base + 1, :]
+    sums = [
+        jnp.sum(jnp.where(lane == atoms + i, row, 0.0), axis=1, keepdims=True) for i in range(12)
+    ]
+    plain = [sums[steps] + crossed[steps] for steps in range(6)]
     moved = []
     for steps in range(6):
-        value = sums[:, 8 + steps : 9 + steps]
+        value = sums[6 + steps]
         binomial = 1
         for part in range(steps, -1, -1):
             value = value + (binomial * (-6.0) ** (steps - part)) * crossed[part]
@@ -873,26 +897,28 @@
     if devices > 4:
         other_cells = lax.psum(own[2 * n + 8 : 2 * n + 16, :depth], "slab")
     wide = (length + 2 * ITERS - 2, 3 * rows, depth)
-    walks, row_hot, deep_hot, member = local_call(
+    walks, row_hot, deep_hot, member, charges = local_call(
         functools.partial(atoms_kernel, devices, wires, length),
         (
             shape((6, 2 * devices * atoms, depth), F32),
             shape((wide[0] * wide[1], devices * depth), BF16),
             shape((devices * depth, depth), F32),
             shape((n, TILE), F32),
+            shape((groups * devices, depth), F32),
         ),
         [],
-        "vvv",
+        "vvvv",
         "atoms",
         28,
         2**29,
+        group_charge.reshape(1, groups),
         orbital_row,
         cells,
         other_cells,
     )
     extra, wide_field = local_call(
         functools.partial(moments_kernel, devices, wires),
-        (shape((6 * devices + 8, depth), F32), shape(wide, F32)),
+        (shape((6 * devices, depth), F32), shape(wide, F32)),
         [pltpu.VMEM((length + 2 * REACH, 3 * rows, depth), F32)],
         "vvvvv",
         "moments",
@@ -904,14 +930,16 @@
         two_beside,
         atom_cell,
     )
-    known = local_call(
-        known_kernel,
-        shape((8, TILE), F32),
+    known, weights = local_call(
+        functools.partial(known_kernel, devices),
+        (shape((8, TILE), F32), shape((2 * groups * devices, TILE), F32)),
         [],
-        "vvvvvv",
+        "vvvvvvvv",
         "known",
         24,
         2**28,
+        energy_weight.reshape(1, -1),
+        energy_group.reshape(1, -1),
         orbital_row,
         member,
         own,
@@ -936,19 +964,18 @@
         packed = jnp.where(lax.axis_index("slab") // 2 == turn + 1, arrived, packed)
     payload = local_call(
         functools.partial(density_kernel, devices),
-        shape(((groups + 6) * devices + 8, TILE), F32),
+        shape(((groups + 6) * devices, TILE), F32),
         [pltpu.VMEM((n, n), F32), pltpu.VMEM((8, TILE), F32)],
-        "ssvvvvvv",
+        "vvvvvvv",
         "density",
         20,
         24 * n**3,
-        energy_weight,
-        energy_group,
         member,
         packed,
         stack,
         stack_parts,
         known,
+        weights,
         extra,
     )
     payload = total_over_all(payload)
@@ -956,15 +983,15 @@
         functools.partial(finish_kernel, devices, wires, atoms),
         (shape((groups, 2, atoms), F32), shape(doping.shape, F32)),
         [],
-        "svvvvv",
+        "vvvvvv",
         "finish",
         28,
         2**29,
-        group_charge,
         payload,
         walks,
         row_hot,
         deep_hot,
+        charges,
         wide_field,
     )
 

time: 43.3 us -> 42 us (0.970)
  Pallas kernels: 16.6 us -> 15.5 us
    pallas_call x8, Pallas kernels: 16.6 us -> 15.5 us  [local_call(): pl.pallas_call(kernel, out_shape=shapes, in_specs=[pl.BlockSpec(memory_sp...]
  transfers between devices with their start and end apart: 14 -> 14, of which waited for: 7 -> 7; matrix products, arithmetic and copies ran while one was open for 0% -> 0% of each run, Pallas kernels for 15% -> 16%
where the time goes in v7:
time: 42 us; the launch traced here: 41.9 us
  starting transfers between devices  17.6 us (42%)
  Pallas kernels  15.5 us (37%)
  waiting for transfers between devices  7.99 us (19%)
  between operations  0.8 us (2%)
    pallas_call x8, Pallas kernels, local_call(): pl.pallas_call(kernel, out_shape=shapes, in_specs=[pl.BlockSpec(memory_sp...  15.5 us
    ppermute x7, starting transfers between devices, total_over(): lax.ppermute(value, axis, [(i, i ^ k) for i in range(size)])  8.83 us
    ppermute x7, waiting for transfers between devices, total_over(): lax.ppermute(value, axis, [(i, i ^ k) for i in range(size)])  7.61 us
    ppermute x1, starting transfers between devices, on_device(): two_beside = lax.ppermute(two_side, 'energy', inner_pairs(wires))  3.57 us
    ppermute x1, starting transfers between devices, on_device(): second = lax.ppermute(edge, 'slab', neighbour_turn(devices))  1.92 us
    ppermute x1, starting transfers between devices, on_device(): one_beside = lax.ppermute(one_side, 'energy', pairs_of(wires))  1.55 us
    ppermute x1, starting transfers between devices, on_device(): packed = lax.ppermute(passed, 'slab', hop(devices, 1))  1.15 us
  transfers between devices with their start and end apart: 14, of which 7 were waited for; matrix products, arithmetic and copies ran while one was open for 0% of the time, Pallas kernels for 16%

profile of v7, /device:TPU:0, one launch (start us, length us, event | category | flops | bytes accessed | tf_op | source)
XLA Modules:
  0.0 41.9 jit_solution(10035817155062602298)
XLA Ops:
  0.6 5.9 %other.1 = (f32[384,384]{1,0:T(8,128)S(1)}, f32[800,384]{1,0:T(8,128)S(1)}, f32[48,128]{1,0:T(8,128)S(1)}, f32[384,384]{1,0:T(8,128)S(1)}, f32[384,384]{1,0:T(8,...) custom-call(f32[2,2,384,384]{3,2,1,0:T(8,128)} %iso.1, f32[2,384,384]{2,1,0:T(8,128)} %coupling.1, ...), custom_call_target="tpu_custom_call" | custom-call | flops 2717908992 | bytes 1048576 | tf_op jit(solution)/shard_map/other/pallas_call | solution.py:372
  6.6 0.1 collective-permute-start
  6.7 0.5 %collective-permute-start.1 = (f32[384,384]{1,0:T(8,128)S(1)}, f32[384,384]{1,0:T(8,128)S(1)}, u32[]{:S(2)}, u32[]{:S(2)}) collective-permute-start(f32[384,384]{1,0:T(8,128)S(1)} %get-tuple-element.31), channel_id=1, source_target_pairs={{0,1},{1,0},{2,3},{3,2},{4,5},{5,4},{6,7},{7,6},{8,9},{9,8},{10,11... | collective-permute-start | bytes 1769480 | tf_op jit(solution)/shard_map/ppermute | solution.py:869
  7.2 1.9 %collective-permute-start.2 = (f32[48,128]{1,0:T(8,128)S(1)}, f32[48,128]{1,0:T(8,128)S(1)}, u32[]{:S(2)}, u32[]{:S(2)}) collective-permute-start(f32[48,128]{1,0:T(8,128)S(1)} %get-tuple-element.25.planes), channel_id=1, source_target_pairs={{0,3},{1,2},{2,1},{3,0},{4,7},{5,6},{6,5},{7,4},{8,11},{9,10},{10,... | collective-permute-start | bytes 73736 | tf_op jit(solution)/shard_map/ppermute | solution.py:853
  9.1 0.0 copy-start
  9.1 2.4 %own.1 = f32[800,384]{1,0:T(8,128)S(1)} custom-call(f32[48,128]{1,0:T(8,128)S(1)} %get-tuple-element.25.planes, f32[384,384]{1,0:T(8,128)S(1)} %get-tuple-element.26.early.own_step, f32[384,384]{1,0:T(8,128)S(1)} %get-tuple-element.27.late, f32[2,384,384]{2,1,0:T(8,128)S(1)} %get-tuple-element.28.isos, f32[384,384]{1,0:T(8,128)S(1)} %get-tuple-element.29.lead), custom_call_target="tpu_custom_call" | custom-call | flops 2147483648 | bytes 1048576 | tf_op jit(solution)/shard_map/own/pallas_call | solution.py:372
  11.5 0.0 copy-start.5
  11.5 0.0 copy-start.4
  11.5 0.0 collective-permute-done.2.second
  11.5 0.0 collective-permute-done.1.got_step
  11.5 0.0 collective-permute-done.got
  11.5 0.0 copy-done
  11.5 1.4 %relay.1 = (f32[648,128]{1,0:T(8,128)S(1)}, f32[1536,384]{1,0:T(8,128)S(1)}, bf16[1536,1536]{1,0:T(8,128)(2,1)S(1)}, f32[26,8,128]{2,1,0:T(8,128)S(1)}, f32[8,12...) custom-call(f32[800,384]{1,0:T(8,128)S(1)} %own.1, f32[800,384]{1,0:T(8,128)S(1)} %collective-permute-done.got, ...), custom_call_target="tpu_custom_call" | custom-call | flops 679477248 | bytes 1048576 | tf_op jit(solution)/shard_map/relay/pallas_call | solution.py:372
  12.9 0.0 copy-start.2
  13.0 0.0 copy-start.3
  13.0 1.1 %collective-permute-start.4 = (f32[648,128]{1,0:T(8,128)S(1)}, f32[648,128]{1,0:T(8,128)S(1)}, u32[]{:S(2)}, u32[]{:S(2)}) collective-permute-start(f32[648,128]{1,0:T(8,128)S(1)} %get-tuple-element.34), channel_id=1, source_target_pairs={{0,2},{1,3},{2,0},{3,1},{4,6},{5,7},{6,4},{7,5},{8,10},{9,11},{10,... | collective-permute-start | bytes 995336 | tf_op jit(solution)/shard_map/ppermute | solution.py:893
  14.1 0.0 collective-permute-start.3
  14.1 0.0 copy-done.5
  14.1 1.6 %collective-permute-start.5 = (f32[136,128]{1,0:T(8,128)S(1)}, f32[136,128]{1,0:T(8,128)S(1)}, u32[]{:S(2)}, u32[]{:S(2)}) collective-permute-start(f32[136,128]{1,0:T(8,128)S(1)} %get-tuple-element.40), channel_id=1, source_target_pairs={{0,4},{4,0},{8,12},{12,8},{16,20},{20,16},{24,28},{28,24},{1,5},{5... | collective-permute-start | bytes 208904 | tf_op jit(solution)/shard_map/ppermute | solution.py:894
  15.7 3.6 %collective-permute-start.6 = (f32[136,128]{1,0:T(8,128)S(1)}, f32[136,128]{1,0:T(8,128)S(1)}, u32[]{:S(2)}, u32[]{:S(2)}) collective-permute-start(f32[136,128]{1,0:T(8,128)S(1)} %get-tuple-element.41), channel_id=1, source_target_pairs={{0,28},{4,8},{8,4},{12,16},{16,12},{20,24},{24,20},{28,0},{1,29},{... | collective-permute-start | bytes 208904 | tf_op jit(solution)/shard_map/ppermute | solution.py:895
  19.3 0.0 collective-permute-done.3.other_cells
  19.3 0.0 copy-done.4
  19.3 1.8 %atoms.1 = (f32[6,384,128]{2,1,0:T(8,128)S(1)}, bf16[480,512]{1,0:T(8,128)(2,1)S(1)}, f32[512,128]{1,0:T(8,128)S(1)}, f32[384,128]{1,0:T(8,128)S(1)}, f32[16,128]{1,0:T(8,128)S(1)}) custom-call(f32[1,4]{1,0:T(1,128)S(1)} %bitcast.5, s32[1,384]{1,0:T(1,128)S(1)} %reshape.17.orbital_atom, f32[8,128]{1,0:T(8,128)S(1)} %get-tuple-element.32.some_cells, ...), custom_call_target="tpu_custom_call" | custom-call | flops 536870912 | bytes 1048576 | tf_op jit(solution)/shard_map/atoms/pallas_call | solution.py:372
  21.1 0.0 copy-done.2
  21.1 0.0 copy-done.3
  21.1 0.0 copy-start.1
  21.1 1.2 %known.1 = (f32[8,128]{1,0:T(8,128)S(1)}, f32[32,128]{1,0:T(8,128)S(1)}) custom-call(f32[1,2]{1,0:T(1,128)S(1)} %bitcast.3, s32[1,2]{1,0:T(1,128)S(1)} %bitcast.4, s32[1,384]{1,0:T(1,128)S(1)} %reshape.17.orbital_atom, f32[384,128]{1,0:T(8,128)S(1)} %get-tuple-element.33.member, f32[800,384]{1,0:T(8,128)S(1)} %own.1, ...), custom_call_target="tpu_custom_call" | custom-call | flops 268435456 | bytes 1048576 | tf_op jit(solution)/shard_map/known/pallas_call | solution.py:372
  22.3 0.0 collective-permute-done.5.one_beside
  22.3 0.4 collective-permute-done.6.two_beside
  22.7 0.0 copy-done.1
  22.7 1.2 %moments.1 = (f32[24,128]{1,0:T(8,128)S(1)}, f32[20,24,128]{2,1,0:T(8,128)S(1)}) custom-call(f32[800,384]{1,0:T(8,128)S(1)} %own.1, f32[26,8,128]{2,1,0:T(8,128)S(1)} %get-tuple-element.39.field, f32[136,128]{1,0:T(8,128)S(1)} %collective-permute-done.5.one_beside, f32[136,128]{1,0:T(8,128)S(1)} %collective-permute-done.6.two_beside, s32[2,48]{1,0:T(2,128)S(1)} %copy-done.1), custom_call_target="tpu_custom_call" | custom-call | flops 67108864 | bytes 1048576 | tf_op jit(solution)/shard_map/moments/pallas_call | solution.py:372
  23.9 0.0 collective-permute-done.4.packed
  23.9 0.1 density.1
  24.0 0.0 collective-permute-start.7
  24.0 1.2 %collective-permute-done.7 = f32[40,128]{1,0:T(8,128)S(1)} collective-permute-done((f32[40,128]{1,0:T(8,128)S(1)}, f32[40,128]{1,0:T(8,128)S(1)}, u32[]{:S(2)}, u32[]{:S(2)}) %collective-permute-start.7) | collective-permute-done | bytes 20512 | tf_op jit(solution)/shard_map/ppermute | solution.py:776
  25.2 2.6 %collective-permute-start.10 = (f32[40,128]{1,0:T(8,128)S(1)}, f32[40,128]{1,0:T(8,128)S(1)}, u32[]{:S(2)}, u32[]{:S(2)}) collective-permute-start(f32[40,128]{1,0:T(8,128)S(1)} %add.21), channel_id=1, source_target_pairs={{0,6},{1,7},{2,4},{3,5},{4,2},{5,3},{6,0},{7,1},{8,14},{9,15},{10,... | collective-permute-start | bytes 61448 | tf_op jit(solution)/shard_map/ppermute | solution.py:776
  27.8 1.8 %collective-permute-start.9 = (f32[40,128]{1,0:T(8,128)S(1)}, f32[40,128]{1,0:T(8,128)S(1)}, u32[]{:S(2)}, u32[]{:S(2)}) collective-permute-start(f32[40,128]{1,0:T(8,128)S(1)} %add.21), channel_id=1, source_target_pairs={{0,4},{1,5},{2,6},{3,7},{4,0},{5,1},{6,2},{7,3},{8,12},{9,13},{10,... | collective-permute-start | bytes 61448 | tf_op jit(solution)/shard_map/ppermute | solution.py:776
  29.5 0.0 collective-permute-start.8
  29.5 0.3 collective-permute-done.10
  29.9 1.7 %collective-permute-done.9 = f32[40,128]{1,0:T(8,128)S(1)} collective-permute-done((f32[40,128]{1,0:T(8,128)S(1)}, f32[40,128]{1,0:T(8,128)S(1)}, u32[]{:S(2)}, u32[]{:S(2)}) %collective-permute-start.9) | collective-permute-done | bytes 20512 | tf_op jit(solution)/shard_map/ppermute | solution.py:776
  31.6 1.8 %collective-permute-done.8 = f32[40,128]{1,0:T(8,128)S(1)} collective-permute-done((f32[40,128]{1,0:T(8,128)S(1)}, f32[40,128]{1,0:T(8,128)S(1)}, u32[]{:S(2)}, u32[]{:S(2)}) %collective-permute-start.8) | collective-permute-done | bytes 20512 | tf_op jit(solution)/shard_map/ppermute | solution.py:776
  33.3 2.4 %collective-permute-start.13 = (f32[40,128]{1,0:T(8,128)S(1)}, f32[40,128]{1,0:T(8,128)S(1)}, u32[]{:S(2)}, u32[]{:S(2)}) collective-permute-start(f32[40,128]{1,0:T(8,128)S(1)} %add_add_fusion.1), channel_id=1, source_target_pairs={{0,24},{4,28},{8,16},{12,20},{16,8},{20,12},{24,0},{28,4},{1,25},{... | collective-permute-start | bytes 61448 | tf_op jit(solution)/shard_map/ppermute | solution.py:776
  35.8 0.0 collective-permute-start.12
  35.8 2.0 %collective-permute-start.11 = (f32[40,128]{1,0:T(8,128)S(1)}, f32[40,128]{1,0:T(8,128)S(1)}, u32[]{:S(2)}, u32[]{:S(2)}) collective-permute-start(f32[40,128]{1,0:T(8,128)S(1)} %add_add_fusion.1), channel_id=1, source_target_pairs={{0,8},{4,12},{8,0},{12,4},{16,24},{20,28},{24,16},{28,20},{1,9},{5... | collective-permute-start | bytes 61448 | tf_op jit(solution)/shard_map/ppermute | solution.py:776
  37.8 1.3 %collective-permute-done.13 = f32[40,128]{1,0:T(8,128)S(1)} collective-permute-done((f32[40,128]{1,0:T(8,128)S(1)}, f32[40,128]{1,0:T(8,128)S(1)}, u32[]{:S(2)}, u32[]{:S(2)}) %collective-permute-start.13) | collective-permute-done | bytes 20512 | tf_op jit(solution)/shard_map/ppermute | solution.py:776
  39.1 1.3 %collective-permute-done.12 = f32[40,128]{1,0:T(8,128)S(1)} collective-permute-done((f32[40,128]{1,0:T(8,128)S(1)}, f32[40,128]{1,0:T(8,128)S(1)}, u32[]{:S(2)}, u32[]{:S(2)}) %collective-permute-start.12) | collective-permute-done | bytes 20512 | tf_op jit(solution)/shard_map/ppermute | solution.py:776
  40.4 0.0 collective-permute-done.11
  40.5 1.4 %finish.1 = (f32[4,2,48]{2,1,0:T(2,128)}, f32[16,8,128]{2,1,0:T(8,128)}) custom-call(f32[40,128]{1,0:T(8,128)S(1)} %add_add_fusion.payload, f32[6,384,128]{2,1,0:T(8,128)S(1)} %get-tuple-element.43.walks, bf16[480,512]{1,0:T(8,128)(2,1)S(1)} %get-tuple-element.44.row_hot, f32[512,128]{1,0:T(8,128)S(1)} %get-tuple-element.45.deep_hot, ...), custom_call_target="tpu_custom_call" | custom-call | flops 536870912 | bytes 1048576 | tf_op jit(solution)/shard_map/finish/pallas_call | solution.py:372
  (4 shorter events, 0.0 us)
Async XLA Ops:
  6.6 4.9 %collective-permute-start = (f32[800,384]{1,0:T(8,128)S(1)}, f32[800,384]{1,0:T(8,128)S(1)}, u32[]{:S(2)}, u32[]{:S(2)}) collective-permute-start(f32[800,384]{1,0:T(8,128)S(1)} %get-tuple-element.30), channel_id=1, source_target_pairs={{0,1},{1,0},{2,3},{3,2},{4,5},{5,4},{6,7},{7,6},{8,9},{9,8},{10,11... | collective-permute-start | bytes 3686408 | tf_op jit(solution)/shard_map/ppermute | solution.py:852
  6.7 4.8 %collective-permute-start.1 = (f32[384,384]{1,0:T(8,128)S(1)}, f32[384,384]{1,0:T(8,128)S(1)}, u32[]{:S(2)}, u32[]{:S(2)}) collective-permute-start(f32[384,384]{1,0:T(8,128)S(1)} %get-tuple-element.31), channel_id=1, source_target_pairs={{0,1},{1,0},{2,3},{3,2},{4,5},{5,4},{6,7},{7,6},{8,9},{9,8},{10,11... | collective-permute-start | bytes 1769480 | tf_op jit(solution)/shard_map/ppermute | solution.py:869
  7.2 4.3 %collective-permute-start.2 = (f32[48,128]{1,0:T(8,128)S(1)}, f32[48,128]{1,0:T(8,128)S(1)}, u32[]{:S(2)}, u32[]{:S(2)}) collective-permute-start(f32[48,128]{1,0:T(8,128)S(1)} %get-tuple-element.25.planes), channel_id=1, source_target_pairs={{0,3},{1,2},{2,1},{3,0},{4,7},{5,6},{6,5},{7,4},{8,11},{9,10},{10,... | collective-permute-start | bytes 73736 | tf_op jit(solution)/shard_map/ppermute | solution.py:853
  9.1 2.4 %copy-start = (f32[16,8,128]{2,1,0:T(8,128)S(1)}, f32[16,8,128]{2,1,0:T(8,128)}, u32[]{:S(2)}) copy-start(f32[16,8,128]{2,1,0:T(8,128)} %field.1) | copy-start | bytes 196612
  11.5 2.7 %copy-start.5 = (s32[384]{0:T(512)S(1)}, s32[384]{0:T(512)}, u32[]{:S(2)}) copy-start(s32[384]{0:T(512)} %param.15) | copy-start | bytes 4612
  11.5 7.8 %copy-start.4 = (f32[4]{0:T(128)S(1)}, f32[4]{0:T(128)}, u32[]{:S(2)}) copy-start(f32[4]{0:T(128)} %param.14) | copy-start | bytes 52
  12.9 8.1 %copy-start.2 = (f32[2]{0:T(128)S(1)}, f32[2]{0:T(128)}, u32[]{:S(2)}) copy-start(f32[2]{0:T(128)} %param.12) | copy-start | bytes 28
  13.0 8.1 %copy-start.3 = (s32[2]{0:T(128)S(1)}, s32[2]{0:T(128)}, u32[]{:S(2)}) copy-start(s32[2]{0:T(128)} %param.13) | copy-start | bytes 28
  13.0 10.9 %collective-permute-start.4 = (f32[648,128]{1,0:T(8,128)S(1)}, f32[648,128]{1,0:T(8,128)S(1)}, u32[]{:S(2)}, u32[]{:S(2)}) collective-permute-start(f32[648,128]{1,0:T(8,128)S(1)} %get-tuple-element.34), channel_id=1, source_target_pairs={{0,2},{1,3},{2,0},{3,1},{4,6},{5,7},{6,4},{7,5},{8,10},{9,11},{10,... | collective-permute-start | bytes 995336 | tf_op jit(solution)/shard_map/ppermute | solution.py:893
  14.1 5.1 %collective-permute-start.3 = (f32[8,128]{1,0:T(8,128)S(1)}, f32[8,128]{1,0:T(8,128)S(1)}, u32[]{:S(2)}, u32[]{:S(2)}) collective-permute-start(f32[8,128]{1,0:T(8,128)S(1)} %get-tuple-element.32.some_cells), channel_id=1, source_target_pairs={{0,1},{1,0},{2,3},{3,2},{4,5},{5,4},{6,7},{7,6},{8,9},{9,8},{10,11... | collective-permute-start | bytes 12296 | tf_op jit(solution)/shard_map/ppermute | solution.py:896
  14.1 8.2 %collective-permute-start.5 = (f32[136,128]{1,0:T(8,128)S(1)}, f32[136,128]{1,0:T(8,128)S(1)}, u32[]{:S(2)}, u32[]{:S(2)}) collective-permute-start(f32[136,128]{1,0:T(8,128)S(1)} %get-tuple-element.40), channel_id=1, source_target_pairs={{0,4},{4,0},{8,12},{12,8},{16,20},{20,16},{24,28},{28,24},{1,5},{5... | collective-permute-start | bytes 208904 | tf_op jit(solution)/shard_map/ppermute | solution.py:894
  15.7 7.0 %collective-permute-start.6 = (f32[136,128]{1,0:T(8,128)S(1)}, f32[136,128]{1,0:T(8,128)S(1)}, u32[]{:S(2)}, u32[]{:S(2)}) collective-permute-start(f32[136,128]{1,0:T(8,128)S(1)} %get-tuple-element.41), channel_id=1, source_target_pairs={{0,28},{4,8},{8,4},{12,16},{16,12},{20,24},{24,20},{28,0},{1,29},{... | collective-permute-start | bytes 208904 | tf_op jit(solution)/shard_map/ppermute | solution.py:895
  21.1 1.6 %copy-start.1 = (s32[2,48]{1,0:T(2,128)S(1)}, s32[2,48]{1,0:T(2,128)}, u32[]{:S(2)}) copy-start(s32[2,48]{1,0:T(2,128)} %cells.1) | copy-start | bytes 1156
  24.0 1.2 %collective-permute-start.7 = (f32[40,128]{1,0:T(8,128)S(1)}, f32[40,128]{1,0:T(8,128)S(1)}, u32[]{:S(2)}, u32[]{:S(2)}) collective-permute-start(f32[40,128]{1,0:T(8,128)S(1)} %density.1), channel_id=1, source_target_pairs={{0,1},{1,0},{2,3},{3,2},{4,5},{5,4},{6,7},{7,6},{8,9},{9,8},{10,11... | collective-permute-start | bytes 61448 | tf_op jit(solution)/shard_map/ppermute | solution.py:776
  25.2 4.7 %collective-permute-start.10 = (f32[40,128]{1,0:T(8,128)S(1)}, f32[40,128]{1,0:T(8,128)S(1)}, u32[]{:S(2)}, u32[]{:S(2)}) collective-permute-start(f32[40,128]{1,0:T(8,128)S(1)} %add.21), channel_id=1, source_target_pairs={{0,6},{1,7},{2,4},{3,5},{4,2},{5,3},{6,0},{7,1},{8,14},{9,15},{10,... | collective-permute-start | bytes 61448 | tf_op jit(solution)/shard_map/ppermute | solution.py:776
  27.8 3.8 %collective-permute-start.9 = (f32[40,128]{1,0:T(8,128)S(1)}, f32[40,128]{1,0:T(8,128)S(1)}, u32[]{:S(2)}, u32[]{:S(2)}) collective-permute-start(f32[40,128]{1,0:T(8,128)S(1)} %add.21), channel_id=1, source_target_pairs={{0,4},{1,5},{2,6},{3,7},{4,0},{5,1},{6,2},{7,3},{8,12},{9,13},{10,... | collective-permute-start | bytes 61448 | tf_op jit(solution)/shard_map/ppermute | solution.py:776
  29.5 3.8 %collective-permute-start.8 = (f32[40,128]{1,0:T(8,128)S(1)}, f32[40,128]{1,0:T(8,128)S(1)}, u32[]{:S(2)}, u32[]{:S(2)}) collective-permute-start(f32[40,128]{1,0:T(8,128)S(1)} %add.21), channel_id=1, source_target_pairs={{0,2},{1,3},{2,0},{3,1},{4,6},{5,7},{6,4},{7,5},{8,10},{9,11},{10,... | collective-permute-start | bytes 61448 | tf_op jit(solution)/shard_map/ppermute | solution.py:776
  33.3 5.8 %collective-permute-start.13 = (f32[40,128]{1,0:T(8,128)S(1)}, f32[40,128]{1,0:T(8,128)S(1)}, u32[]{:S(2)}, u32[]{:S(2)}) collective-permute-start(f32[40,128]{1,0:T(8,128)S(1)} %add_add_fusion.1), channel_id=1, source_target_pairs={{0,24},{4,28},{8,16},{12,20},{16,8},{20,12},{24,0},{28,4},{1,25},{... | collective-permute-start | bytes 61448 | tf_op jit(solution)/shard_map/ppermute | solution.py:776
  35.8 4.7 %collective-permute-start.12 = (f32[40,128]{1,0:T(8,128)S(1)}, f32[40,128]{1,0:T(8,128)S(1)}, u32[]{:S(2)}, u32[]{:S(2)}) collective-permute-start(f32[40,128]{1,0:T(8,128)S(1)} %add_add_fusion.1), channel_id=1, source_target_pairs={{0,16},{4,20},{8,24},{12,28},{16,0},{20,4},{24,8},{28,12},{1,17},{... | collective-permute-start | bytes 61448 | tf_op jit(solution)/shard_map/ppermute | solution.py:776
  35.8 4.7 %collective-permute-start.11 = (f32[40,128]{1,0:T(8,128)S(1)}, f32[40,128]{1,0:T(8,128)S(1)}, u32[]{:S(2)}, u32[]{:S(2)}) collective-permute-start(f32[40,128]{1,0:T(8,128)S(1)} %add_add_fusion.1), channel_id=1, source_target_pairs={{0,8},{4,12},{8,0},{12,4},{16,24},{20,28},{24,16},{28,20},{1,9},{5... | collective-permute-start | bytes 61448 | tf_op jit(solution)/shard_map/ppermute | solution.py:776

commit v8 on v7

--- a/solution.py
+++ b/solution.py
@@ -66,7 +66,8 @@
     return jnp.concatenate(parts, axis=1)
 
 
-PACKED_ROWS = 5 * TILE + 8
+SMALL = TILE // 2
+PACKED_ROWS = 4 * TILE + SMALL + 8
 
 
 def pack(matrix, out):
@@ -77,12 +78,17 @@
     columns = lax.broadcasted_iota(jnp.int32, (TILE, TILE), 1)
     for place, (i, j) in enumerate(((0, 1), (0, 2), (1, 2))):
         out[place * TILE : (place + 1) * TILE, :] = block(i, j) + block(j, i).T
-    one, two = (block(0, 0), block(1, 1))
+    one, two, three = (block(i, i) for i in range(3))
     merged = jnp.where(rows < columns, one + one.T, jnp.where(rows > columns, two + two.T, one))
     out[3 * TILE : 4 * TILE, :] = merged
-    out[4 * TILE : 5 * TILE, :] = block(2, 2)
+    whole = jnp.where(rows == columns, three, three + three.T)
+    turned = pltpu.roll(whole[SMALL:], SMALL, 1)
+    low = (rows > columns)[:SMALL]
+    out[4 * TILE : 4 * TILE + SMALL, :] = jnp.where(low, turned, whole[:SMALL])
     row = jnp.sum(jnp.where(rows == columns, two, 0.0), axis=0, keepdims=True)
-    out[5 * TILE :, :] = jnp.broadcast_to(row, (8, TILE))
+    last = jnp.sum(jnp.where(rows == columns, three, 0.0), axis=0, keepdims=True)
+    first = lax.broadcasted_iota(jnp.int32, (8, TILE), 0) == 0
+    out[4 * TILE + SMALL :, :] = jnp.where(first, row, last)
 
 
 def unpack(packed, out):
@@ -93,12 +99,18 @@
         value = packed[place * TILE : (place + 1) * TILE, :]
         out[i * TILE : (i + 1) * TILE, j * TILE : (j + 1) * TILE] = value
     merged = packed[3 * TILE : 4 * TILE, :]
-    row = packed[5 * TILE : 5 * TILE + 1, :]
+    start = 4 * TILE + SMALL
+    row, last = (packed[start : start + 1, :], packed[start + 1 : start + 2, :])
     out[:TILE, :TILE] = jnp.where(rows <= columns, merged, 0.0)
     out[TILE : 2 * TILE, TILE : 2 * TILE] = jnp.where(
         rows > columns, merged, jnp.where(rows == columns, row, 0.0)
     )
-    out[2 * TILE :, 2 * TILE :] = packed[4 * TILE : 5 * TILE, :]
+    half = packed[4 * TILE : start, :]
+    out[2 * TILE : 2 * TILE + SMALL, 2 * TILE :] = jnp.where((rows <= columns)[:SMALL], half, 0.0)
+    turned = pltpu.roll(half, SMALL, 1)
+    inside = (columns >= SMALL) & (rows > columns)
+    value = jnp.where(rows[SMALL:] == columns[SMALL:], last, 0.0)
+    out[2 * TILE + SMALL :, 2 * TILE :] = jnp.where(inside[SMALL:], turned, value)
 
 
 def plane_rows(n, plane):
@@ -796,8 +808,15 @@
     return value
 
 
-def inner_pairs(count):
-    return [(i, (i + 1) % count if i % 2 else (i - 1) % count) for i in range(count)]
+def inner_pairs(count, slabs):
+    moves = []
+    for i in range(count * slabs):
+        wire, place = divmod(i, slabs)
+        if wire in (0, count - 1):
+            moves.append((i, i ^ 1))
+        else:
+            moves.append((i, (wire + 1 if wire % 2 else wire - 1) * slabs + place))
+    return moves
 
 
 def neighbour_turn(count):
@@ -892,7 +911,7 @@
     )
     packed = lax.ppermute(passed, "slab", hop(devices, 1))
     one_beside = lax.ppermute(one_side, "energy", pairs_of(wires))
-    two_beside = lax.ppermute(two_side, "energy", inner_pairs(wires))
+    two_beside = lax.ppermute(two_side, BOTH, inner_pairs(wires, devices))
     other_cells = lax.ppermute(cells, "slab", pairs_of(devices))
     if devices > 4:
         other_cells = lax.psum(own[2 * n + 8 : 2 * n + 16, :depth], "slab")

time: 42 us -> 41.6 us (level)
  starting transfers between devices: 17.6 us -> 14.4 us
  waiting for transfers between devices: 7.99 us -> 10.6 us
    ppermute x1, starting transfers between devices: 3.57 us -> 0.16 us  [on_device(): two_beside = lax.ppermute(two_side, BOTH, inner_pairs(wires, devices))]
    ppermute x1, waiting for transfers between devices: 0.01 us -> 1.32 us  [on_device(): packed = lax.ppermute(passed, 'slab', hop(devices, 1))]
    ppermute x7, waiting for transfers between devices: 7.61 us -> 8.91 us  [total_over(): lax.ppermute(value, axis, [(i, i ^ k) for i in range(size)])]
  transfers between devices with their start and end apart: 14 -> 14, of which waited for: 7 -> 8; matrix products, arithmetic and copies ran while one was open for 0% -> 0% of each run, Pallas kernels for 16% -> 16%
where the time goes in v8:
time: 41.6 us; the launch traced here: 41.4 us
  Pallas kernels  15.6 us (38%)
  starting transfers between devices  14.4 us (35%)
  waiting for transfers between devices  10.6 us (25%)
  between operations  0.79 us (2%)
    pallas_call x8, Pallas kernels, local_call(): pl.pallas_call(kernel, out_shape=shapes, in_specs=[pl.BlockSpec(memory_sp...  15.6 us
    ppermute x7, starting transfers between devices, total_over(): lax.ppermute(value, axis, [(i, i ^ k) for i in range(size)])  9.2 us
    ppermute x7, waiting for transfers between devices, total_over(): lax.ppermute(value, axis, [(i, i ^ k) for i in range(size)])  8.91 us
    ppermute x1, starting transfers between devices, on_device(): second = lax.ppermute(edge, 'slab', neighbour_turn(devices))  1.92 us
    ppermute x1, starting transfers between devices, on_device(): one_beside = lax.ppermute(one_side, 'energy', pairs_of(wires))  1.55 us
    ppermute x1, waiting for transfers between devices, on_device(): packed = lax.ppermute(passed, 'slab', hop(devices, 1))  1.32 us
    ppermute x1, starting transfers between devices, on_device(): packed = lax.ppermute(passed, 'slab', hop(devices, 1))  1.04 us
  transfers between devices with their start and end apart: 14, of which 8 were waited for; matrix products, arithmetic and copies ran while one was open for 0% of the time, Pallas kernels for 16%

profile of v8, /device:TPU:0, one launch (start us, length us, event | category | flops | bytes accessed | tf_op | source)
XLA Modules:
  0.0 41.4 jit_solution(9359337199867545942)
XLA Ops:
  0.6 5.9 %other.1 = (f32[384,384]{1,0:T(8,128)S(1)}, f32[800,384]{1,0:T(8,128)S(1)}, f32[48,128]{1,0:T(8,128)S(1)}, f32[384,384]{1,0:T(8,128)S(1)}, f32[384,384]{1,0:T(8,...) custom-call(f32[2,2,384,384]{3,2,1,0:T(8,128)} %iso.1, f32[2,384,384]{2,1,0:T(8,128)} %coupling.1, ...), custom_call_target="tpu_custom_call" | custom-call | flops 2717908992 | bytes 1048576 | tf_op jit(solution)/shard_map/other/pallas_call | solution.py:384
  6.6 0.1 collective-permute-start
  6.7 0.5 %collective-permute-start.1 = (f32[384,384]{1,0:T(8,128)S(1)}, f32[384,384]{1,0:T(8,128)S(1)}, u32[]{:S(2)}, u32[]{:S(2)}) collective-permute-start(f32[384,384]{1,0:T(8,128)S(1)} %get-tuple-element.31), channel_id=1, source_target_pairs={{0,1},{1,0},{2,3},{3,2},{4,5},{5,4},{6,7},{7,6},{8,9},{9,8},{10,11... | collective-permute-start | bytes 1769480 | tf_op jit(solution)/shard_map/ppermute | solution.py:888
  7.2 1.9 %collective-permute-start.2 = (f32[48,128]{1,0:T(8,128)S(1)}, f32[48,128]{1,0:T(8,128)S(1)}, u32[]{:S(2)}, u32[]{:S(2)}) collective-permute-start(f32[48,128]{1,0:T(8,128)S(1)} %get-tuple-element.25.planes), channel_id=1, source_target_pairs={{0,3},{1,2},{2,1},{3,0},{4,7},{5,6},{6,5},{7,4},{8,11},{9,10},{10,... | collective-permute-start | bytes 73736 | tf_op jit(solution)/shard_map/ppermute | solution.py:872
  9.1 0.0 copy-start
  9.1 2.4 %own.1 = f32[800,384]{1,0:T(8,128)S(1)} custom-call(f32[48,128]{1,0:T(8,128)S(1)} %get-tuple-element.25.planes, f32[384,384]{1,0:T(8,128)S(1)} %get-tuple-element.26.early.own_step, f32[384,384]{1,0:T(8,128)S(1)} %get-tuple-element.27.late, f32[2,384,384]{2,1,0:T(8,128)S(1)} %get-tuple-element.28.isos, f32[384,384]{1,0:T(8,128)S(1)} %get-tuple-element.29.lead), custom_call_target="tpu_custom_call" | custom-call | flops 2147483648 | bytes 1048576 | tf_op jit(solution)/shard_map/own/pallas_call | solution.py:384
  11.5 0.0 copy-start.5
  11.5 0.0 copy-start.4
  11.5 0.0 collective-permute-done.2.second
  11.5 0.0 collective-permute-done.1.got_step
  11.5 0.0 collective-permute-done.got
  11.5 0.0 copy-done
  11.5 1.5 %relay.1 = (f32[584,128]{1,0:T(8,128)S(1)}, f32[1536,384]{1,0:T(8,128)S(1)}, bf16[1536,1536]{1,0:T(8,128)(2,1)S(1)}, f32[26,8,128]{2,1,0:T(8,128)S(1)}, f32[8,12...) custom-call(f32[800,384]{1,0:T(8,128)S(1)} %own.1, f32[800,384]{1,0:T(8,128)S(1)} %collective-permute-done.got, ...), custom_call_target="tpu_custom_call" | custom-call | flops 679477248 | bytes 1048576 | tf_op jit(solution)/shard_map/relay/pallas_call | solution.py:384
  13.1 0.0 copy-start.2
  13.1 0.0 copy-start.3
  13.1 1.0 %collective-permute-start.4 = (f32[584,128]{1,0:T(8,128)S(1)}, f32[584,128]{1,0:T(8,128)S(1)}, u32[]{:S(2)}, u32[]{:S(2)}) collective-permute-start(f32[584,128]{1,0:T(8,128)S(1)} %get-tuple-element.34), channel_id=1, source_target_pairs={{0,2},{1,3},{2,0},{3,1},{4,6},{5,7},{6,4},{7,5},{8,10},{9,11},{10,... | collective-permute-start | bytes 897032 | tf_op jit(solution)/shard_map/ppermute | solution.py:912
  14.1 0.0 collective-permute-start.3
  14.1 0.0 copy-done.5
  14.1 1.6 %collective-permute-start.5 = (f32[136,128]{1,0:T(8,128)S(1)}, f32[136,128]{1,0:T(8,128)S(1)}, u32[]{:S(2)}, u32[]{:S(2)}) collective-permute-start(f32[136,128]{1,0:T(8,128)S(1)} %get-tuple-element.40), channel_id=1, source_target_pairs={{0,4},{4,0},{8,12},{12,8},{16,20},{20,16},{24,28},{28,24},{1,5},{5... | collective-permute-start | bytes 208904 | tf_op jit(solution)/shard_map/ppermute | solution.py:913
  15.7 0.2 collective-permute-start.6
  15.8 0.0 collective-permute-done.3.other_cells
  15.8 0.0 copy-done.4
  15.9 1.8 %atoms.1 = (f32[6,384,128]{2,1,0:T(8,128)S(1)}, bf16[480,512]{1,0:T(8,128)(2,1)S(1)}, f32[512,128]{1,0:T(8,128)S(1)}, f32[384,128]{1,0:T(8,128)S(1)}, f32[16,128]{1,0:T(8,128)S(1)}) custom-call(f32[1,4]{1,0:T(1,128)S(1)} %bitcast.5, s32[1,384]{1,0:T(1,128)S(1)} %reshape.17.orbital_atom, f32[8,128]{1,0:T(8,128)S(1)} %get-tuple-element.32.some_cells, ...), custom_call_target="tpu_custom_call" | custom-call | flops 536870912 | bytes 1048576 | tf_op jit(solution)/shard_map/atoms/pallas_call | solution.py:384
  17.7 0.0 copy-done.2
  17.7 0.0 copy-done.3
  17.7 0.0 copy-start.1
  17.7 1.2 %known.1 = (f32[8,128]{1,0:T(8,128)S(1)}, f32[32,128]{1,0:T(8,128)S(1)}) custom-call(f32[1,2]{1,0:T(1,128)S(1)} %bitcast.3, s32[1,2]{1,0:T(1,128)S(1)} %bitcast.4, s32[1,384]{1,0:T(1,128)S(1)} %reshape.17.orbital_atom, f32[384,128]{1,0:T(8,128)S(1)} %get-tuple-element.33.member, f32[800,384]{1,0:T(8,128)S(1)} %own.1, ...), custom_call_target="tpu_custom_call" | custom-call | flops 268435456 | bytes 1048576 | tf_op jit(solution)/shard_map/known/pallas_call | solution.py:384
  18.9 0.4 collective-permute-done.5.one_beside
  19.3 0.0 collective-permute-done.6.two_beside
  19.3 0.0 copy-done.1
  19.3 1.2 %moments.1 = (f32[24,128]{1,0:T(8,128)S(1)}, f32[20,24,128]{2,1,0:T(8,128)S(1)}) custom-call(f32[800,384]{1,0:T(8,128)S(1)} %own.1, f32[26,8,128]{2,1,0:T(8,128)S(1)} %get-tuple-element.39.field, f32[136,128]{1,0:T(8,128)S(1)} %collective-permute-done.5.one_beside, f32[136,128]{1,0:T(8,128)S(1)} %collective-permute-done.6.two_beside, s32[2,48]{1,0:T(2,128)S(1)} %copy-done.1), custom_call_target="tpu_custom_call" | custom-call | flops 67108864 | bytes 1048576 | tf_op jit(solution)/shard_map/moments/pallas_call | solution.py:384
  20.5 1.3 %collective-permute-done.4.packed = f32[584,128]{1,0:T(8,128)S(1)} collective-permute-done((f32[584,128]{1,0:T(8,128)S(1)}, f32[584,128]{1,0:T(8,128)S(1)}, u32[]{:S(2)}, u32[]{:S(2)}) %collective-permute-start.4) | collective-permute-done | bytes 299040 | tf_op jit(solution)/shard_map/ppermute | solution.py:912
  21.8 0.1 density.1
  21.9 0.0 collective-permute-start.7
  21.9 1.2 %collective-permute-done.7 = f32[40,128]{1,0:T(8,128)S(1)} collective-permute-done((f32[40,128]{1,0:T(8,128)S(1)}, f32[40,128]{1,0:T(8,128)S(1)}, u32[]{:S(2)}, u32[]{:S(2)}) %collective-permute-start.7) | collective-permute-done | bytes 20512 | tf_op jit(solution)/shard_map/ppermute | solution.py:788
  23.1 4.0 %collective-permute-start.10 = (f32[40,128]{1,0:T(8,128)S(1)}, f32[40,128]{1,0:T(8,128)S(1)}, u32[]{:S(2)}, u32[]{:S(2)}) collective-permute-start(f32[40,128]{1,0:T(8,128)S(1)} %add.21), channel_id=1, source_target_pairs={{0,6},{1,7},{2,4},{3,5},{4,2},{5,3},{6,0},{7,1},{8,14},{9,15},{10,... | collective-permute-start | bytes 61448 | tf_op jit(solution)/shard_map/ppermute | solution.py:788
  27.1 0.5 %collective-permute-start.9 = (f32[40,128]{1,0:T(8,128)S(1)}, f32[40,128]{1,0:T(8,128)S(1)}, u32[]{:S(2)}, u32[]{:S(2)}) collective-permute-start(f32[40,128]{1,0:T(8,128)S(1)} %add.21), channel_id=1, source_target_pairs={{0,4},{1,5},{2,6},{3,7},{4,0},{5,1},{6,2},{7,3},{8,12},{9,13},{10,... | collective-permute-start | bytes 61448 | tf_op jit(solution)/shard_map/ppermute | solution.py:788
  27.6 0.1 collective-permute-start.8
  27.7 1.2 %collective-permute-done.10 = f32[40,128]{1,0:T(8,128)S(1)} collective-permute-done((f32[40,128]{1,0:T(8,128)S(1)}, f32[40,128]{1,0:T(8,128)S(1)}, u32[]{:S(2)}, u32[]{:S(2)}) %collective-permute-start.10) | collective-permute-done | bytes 20512 | tf_op jit(solution)/shard_map/ppermute | solution.py:788
  28.9 2.0 %collective-permute-done.9 = f32[40,128]{1,0:T(8,128)S(1)} collective-permute-done((f32[40,128]{1,0:T(8,128)S(1)}, f32[40,128]{1,0:T(8,128)S(1)}, u32[]{:S(2)}, u32[]{:S(2)}) %collective-permute-start.9) | collective-permute-done | bytes 20512 | tf_op jit(solution)/shard_map/ppermute | solution.py:788
  30.9 0.5 %collective-permute-done.8 = f32[40,128]{1,0:T(8,128)S(1)} collective-permute-done((f32[40,128]{1,0:T(8,128)S(1)}, f32[40,128]{1,0:T(8,128)S(1)}, u32[]{:S(2)}, u32[]{:S(2)}) %collective-permute-start.8) | collective-permute-done | bytes 20512 | tf_op jit(solution)/shard_map/ppermute | solution.py:788
  31.4 3.9 %collective-permute-start.13 = (f32[40,128]{1,0:T(8,128)S(1)}, f32[40,128]{1,0:T(8,128)S(1)}, u32[]{:S(2)}, u32[]{:S(2)}) collective-permute-start(f32[40,128]{1,0:T(8,128)S(1)} %add_add_fusion.1), channel_id=1, source_target_pairs={{0,24},{4,28},{8,16},{12,20},{16,8},{20,12},{24,0},{28,4},{1,25},{... | collective-permute-start | bytes 61448 | tf_op jit(solution)/shard_map/ppermute | solution.py:788
  35.3 0.0 collective-permute-start.12
  35.3 0.6 %collective-permute-start.11 = (f32[40,128]{1,0:T(8,128)S(1)}, f32[40,128]{1,0:T(8,128)S(1)}, u32[]{:S(2)}, u32[]{:S(2)}) collective-permute-start(f32[40,128]{1,0:T(8,128)S(1)} %add_add_fusion.1), channel_id=1, source_target_pairs={{0,8},{4,12},{8,0},{12,4},{16,24},{20,28},{24,16},{28,20},{1,9},{5... | collective-permute-start | bytes 61448 | tf_op jit(solution)/shard_map/ppermute | solution.py:788
  35.9 1.1 %collective-permute-done.13 = f32[40,128]{1,0:T(8,128)S(1)} collective-permute-done((f32[40,128]{1,0:T(8,128)S(1)}, f32[40,128]{1,0:T(8,128)S(1)}, u32[]{:S(2)}, u32[]{:S(2)}) %collective-permute-start.13) | collective-permute-done | bytes 20512 | tf_op jit(solution)/shard_map/ppermute | solution.py:788
  37.1 2.9 %collective-permute-done.12 = f32[40,128]{1,0:T(8,128)S(1)} collective-permute-done((f32[40,128]{1,0:T(8,128)S(1)}, f32[40,128]{1,0:T(8,128)S(1)}, u32[]{:S(2)}, u32[]{:S(2)}) %collective-permute-start.12) | collective-permute-done | bytes 20512 | tf_op jit(solution)/shard_map/ppermute | solution.py:788
  40.0 0.0 collective-permute-done.11
  40.0 1.4 %finish.1 = (f32[4,2,48]{2,1,0:T(2,128)}, f32[16,8,128]{2,1,0:T(8,128)}) custom-call(f32[40,128]{1,0:T(8,128)S(1)} %add_add_fusion.payload, f32[6,384,128]{2,1,0:T(8,128)S(1)} %get-tuple-element.43.walks, bf16[480,512]{1,0:T(8,128)(2,1)S(1)} %get-tuple-element.44.row_hot, f32[512,128]{1,0:T(8,128)S(1)} %get-tuple-element.45.deep_hot, ...), custom_call_target="tpu_custom_call" | custom-call | flops 536870912 | bytes 1048576 | tf_op jit(solution)/shard_map/finish/pallas_call | solution.py:384
  (4 shorter events, 0.0 us)
Async XLA Ops:
  6.6 4.9 %collective-permute-start = (f32[800,384]{1,0:T(8,128)S(1)}, f32[800,384]{1,0:T(8,128)S(1)}, u32[]{:S(2)}, u32[]{:S(2)}) collective-permute-start(f32[800,384]{1,0:T(8,128)S(1)} %get-tuple-element.30), channel_id=1, source_target_pairs={{0,1},{1,0},{2,3},{3,2},{4,5},{5,4},{6,7},{7,6},{8,9},{9,8},{10,11... | collective-permute-start | bytes 3686408 | tf_op jit(solution)/shard_map/ppermute | solution.py:871
  6.7 4.8 %collective-permute-start.1 = (f32[384,384]{1,0:T(8,128)S(1)}, f32[384,384]{1,0:T(8,128)S(1)}, u32[]{:S(2)}, u32[]{:S(2)}) collective-permute-start(f32[384,384]{1,0:T(8,128)S(1)} %get-tuple-element.31), channel_id=1, source_target_pairs={{0,1},{1,0},{2,3},{3,2},{4,5},{5,4},{6,7},{7,6},{8,9},{9,8},{10,11... | collective-permute-start | bytes 1769480 | tf_op jit(solution)/shard_map/ppermute | solution.py:888
  7.2 4.3 %collective-permute-start.2 = (f32[48,128]{1,0:T(8,128)S(1)}, f32[48,128]{1,0:T(8,128)S(1)}, u32[]{:S(2)}, u32[]{:S(2)}) collective-permute-start(f32[48,128]{1,0:T(8,128)S(1)} %get-tuple-element.25.planes), channel_id=1, source_target_pairs={{0,3},{1,2},{2,1},{3,0},{4,7},{5,6},{6,5},{7,4},{8,11},{9,10},{10,... | collective-permute-start | bytes 73736 | tf_op jit(solution)/shard_map/ppermute | solution.py:872
  9.1 2.4 %copy-start = (f32[16,8,128]{2,1,0:T(8,128)S(1)}, f32[16,8,128]{2,1,0:T(8,128)}, u32[]{:S(2)}) copy-start(f32[16,8,128]{2,1,0:T(8,128)} %field.1) | copy-start | bytes 196612
  11.5 2.7 %copy-start.5 = (s32[384]{0:T(512)S(1)}, s32[384]{0:T(512)}, u32[]{:S(2)}) copy-start(s32[384]{0:T(512)} %param.15) | copy-start | bytes 4612
  11.5 4.4 %copy-start.4 = (f32[4]{0:T(128)S(1)}, f32[4]{0:T(128)}, u32[]{:S(2)}) copy-start(f32[4]{0:T(128)} %param.14) | copy-start | bytes 52
  13.1 4.6 %copy-start.2 = (f32[2]{0:T(128)S(1)}, f32[2]{0:T(128)}, u32[]{:S(2)}) copy-start(f32[2]{0:T(128)} %param.12) | copy-start | bytes 28
  13.1 4.6 %copy-start.3 = (s32[2]{0:T(128)S(1)}, s32[2]{0:T(128)}, u32[]{:S(2)}) copy-start(s32[2]{0:T(128)} %param.13) | copy-start | bytes 28
  13.1 8.7 %collective-permute-start.4 = (f32[584,128]{1,0:T(8,128)S(1)}, f32[584,128]{1,0:T(8,128)S(1)}, u32[]{:S(2)}, u32[]{:S(2)}) collective-permute-start(f32[584,128]{1,0:T(8,128)S(1)} %get-tuple-element.34), channel_id=1, source_target_pairs={{0,2},{1,3},{2,0},{3,1},{4,6},{5,7},{6,4},{7,5},{8,10},{9,11},{10,... | collective-permute-start | bytes 897032 | tf_op jit(solution)/shard_map/ppermute | solution.py:912
  14.1 1.7 %collective-permute-start.3 = (f32[8,128]{1,0:T(8,128)S(1)}, f32[8,128]{1,0:T(8,128)S(1)}, u32[]{:S(2)}, u32[]{:S(2)}) collective-permute-start(f32[8,128]{1,0:T(8,128)S(1)} %get-tuple-element.32.some_cells), channel_id=1, source_target_pairs={{0,1},{1,0},{2,3},{3,2},{4,5},{5,4},{6,7},{7,6},{8,9},{9,8},{10,11... | collective-permute-start | bytes 12296 | tf_op jit(solution)/shard_map/ppermute | solution.py:915
  14.1 5.1 %collective-permute-start.5 = (f32[136,128]{1,0:T(8,128)S(1)}, f32[136,128]{1,0:T(8,128)S(1)}, u32[]{:S(2)}, u32[]{:S(2)}) collective-permute-start(f32[136,128]{1,0:T(8,128)S(1)} %get-tuple-element.40), channel_id=1, source_target_pairs={{0,4},{4,0},{8,12},{12,8},{16,20},{20,16},{24,28},{28,24},{1,5},{5... | collective-permute-start | bytes 208904 | tf_op jit(solution)/shard_map/ppermute | solution.py:913
  15.7 3.6 %collective-permute-start.6 = (f32[136,128]{1,0:T(8,128)S(1)}, f32[136,128]{1,0:T(8,128)S(1)}, u32[]{:S(2)}, u32[]{:S(2)}) collective-permute-start(f32[136,128]{1,0:T(8,128)S(1)} %get-tuple-element.41), channel_id=1, source_target_pairs={{0,1},{1,0},{2,3},{3,2},{4,8},{5,9},{6,10},{7,11},{8,4},{9,5},{10,... | collective-permute-start | bytes 208904 | tf_op jit(solution)/shard_map/ppermute | solution.py:914
  17.7 1.6 %copy-start.1 = (s32[2,48]{1,0:T(2,128)S(1)}, s32[2,48]{1,0:T(2,128)}, u32[]{:S(2)}) copy-start(s32[2,48]{1,0:T(2,128)} %cells.1) | copy-start | bytes 1156
  21.9 1.2 %collective-permute-start.7 = (f32[40,128]{1,0:T(8,128)S(1)}, f32[40,128]{1,0:T(8,128)S(1)}, u32[]{:S(2)}, u32[]{:S(2)}) collective-permute-start(f32[40,128]{1,0:T(8,128)S(1)} %density.1), channel_id=1, source_target_pairs={{0,1},{1,0},{2,3},{3,2},{4,5},{5,4},{6,7},{7,6},{8,9},{9,8},{10,11... | collective-permute-start | bytes 61448 | tf_op jit(solution)/shard_map/ppermute | solution.py:788
  23.1 5.8 %collective-permute-start.10 = (f32[40,128]{1,0:T(8,128)S(1)}, f32[40,128]{1,0:T(8,128)S(1)}, u32[]{:S(2)}, u32[]{:S(2)}) collective-permute-start(f32[40,128]{1,0:T(8,128)S(1)} %add.21), channel_id=1, source_target_pairs={{0,6},{1,7},{2,4},{3,5},{4,2},{5,3},{6,0},{7,1},{8,14},{9,15},{10,... | collective-permute-start | bytes 61448 | tf_op jit(solution)/shard_map/ppermute | solution.py:788
  27.1 3.8 %collective-permute-start.9 = (f32[40,128]{1,0:T(8,128)S(1)}, f32[40,128]{1,0:T(8,128)S(1)}, u32[]{:S(2)}, u32[]{:S(2)}) collective-permute-start(f32[40,128]{1,0:T(8,128)S(1)} %add.21), channel_id=1, source_target_pairs={{0,4},{1,5},{2,6},{3,7},{4,0},{5,1},{6,2},{7,3},{8,12},{9,13},{10,... | collective-permute-start | bytes 61448 | tf_op jit(solution)/shard_map/ppermute | solution.py:788
  27.6 3.8 %collective-permute-start.8 = (f32[40,128]{1,0:T(8,128)S(1)}, f32[40,128]{1,0:T(8,128)S(1)}, u32[]{:S(2)}, u32[]{:S(2)}) collective-permute-start(f32[40,128]{1,0:T(8,128)S(1)} %add.21), channel_id=1, source_target_pairs={{0,2},{1,3},{2,0},{3,1},{4,6},{5,7},{6,4},{7,5},{8,10},{9,11},{10,... | collective-permute-start | bytes 61448 | tf_op jit(solution)/shard_map/ppermute | solution.py:788
  31.4 5.7 %collective-permute-start.13 = (f32[40,128]{1,0:T(8,128)S(1)}, f32[40,128]{1,0:T(8,128)S(1)}, u32[]{:S(2)}, u32[]{:S(2)}) collective-permute-start(f32[40,128]{1,0:T(8,128)S(1)} %add_add_fusion.1), channel_id=1, source_target_pairs={{0,24},{4,28},{8,16},{12,20},{16,8},{20,12},{24,0},{28,4},{1,25},{... | collective-permute-start | bytes 61448 | tf_op jit(solution)/shard_map/ppermute | solution.py:788
  35.3 4.7 %collective-permute-start.12 = (f32[40,128]{1,0:T(8,128)S(1)}, f32[40,128]{1,0:T(8,128)S(1)}, u32[]{:S(2)}, u32[]{:S(2)}) collective-permute-start(f32[40,128]{1,0:T(8,128)S(1)} %add_add_fusion.1), channel_id=1, source_target_pairs={{0,16},{4,20},{8,24},{12,28},{16,0},{20,4},{24,8},{28,12},{1,17},{... | collective-permute-start | bytes 61448 | tf_op jit(solution)/shard_map/ppermute | solution.py:788
  35.3 4.7 %collective-permute-start.11 = (f32[40,128]{1,0:T(8,128)S(1)}, f32[40,128]{1,0:T(8,128)S(1)}, u32[]{:S(2)}, u32[]{:S(2)}) collective-permute-start(f32[40,128]{1,0:T(8,128)S(1)} %add_add_fusion.1), channel_id=1, source_target_pairs={{0,8},{4,12},{8,0},{12,4},{16,24},{20,28},{24,16},{28,20},{1,9},{5... | collective-permute-start | bytes 61448 | tf_op jit(solution)/shard_map/ppermute | solution.py:788

commit v9 on v8

--- a/solution.py
+++ b/solution.py
@@ -727,7 +727,7 @@
     alphas, betas = ([], [])
     for turn in range(ITERS):
         energy = level * quadratic_form(direction, moments, 0) - quadratic_form(direction, moments, 1)
-        alpha = norm / energy
+        alpha = jnp.clip(norm / energy, 1.0 / 12.5, 2.0)
         alphas.append(alpha)
         if turn + 1 == ITERS:
             break
@@ -737,7 +737,7 @@
             longer[i + 1] = longer[i + 1] + alpha * value
         residual = longer
         following = quadratic_form(residual, moments, 0)
-        beta = following / norm
+        beta = jnp.clip(following / norm, 0.0, 25.0)
         betas.append(beta)
         norm = following
         direction = [

time: 41.6 us -> 41.6 us (level)
  no operation moved by 1% of the time
where the time goes in v9:
time: 41.6 us; the launch traced here: 41.4 us
  Pallas kernels  15.6 us (38%)
  starting transfers between devices  14.4 us (35%)
  waiting for transfers between devices  10.6 us (25%)
  between operations  0.79 us (2%)
    pallas_call x8, Pallas kernels, local_call(): pl.pallas_call(kernel, out_shape=shapes, in_specs=[pl.BlockSpec(memory_sp...  15.6 us
    ppermute x7, starting transfers between devices, total_over(): lax.ppermute(value, axis, [(i, i ^ k) for i in range(size)])  9.2 us
    ppermute x7, waiting for transfers between devices, total_over(): lax.ppermute(value, axis, [(i, i ^ k) for i in range(size)])  8.91 us
    ppermute x1, starting transfers between devices, on_device(): second = lax.ppermute(edge, 'slab', neighbour_turn(devices))  1.92 us
    ppermute x1, starting transfers between devices, on_device(): one_beside = lax.ppermute(one_side, 'energy', pairs_of(wires))  1.55 us
    ppermute x1, waiting for transfers between devices, on_device(): packed = lax.ppermute(passed, 'slab', hop(devices, 1))  1.32 us
    ppermute x1, starting transfers between devices, on_device(): packed = lax.ppermute(passed, 'slab', hop(devices, 1))  1.04 us
  transfers between devices with their start and end apart: 14, of which 8 were waited for; matrix products, arithmetic and copies ran while one was open for 0% of the time, Pallas kernels for 16%

profile of v9, /device:TPU:0, one launch (start us, length us, event | category | flops | bytes accessed | tf_op | source)
XLA Modules:
  0.0 41.4 jit_solution(13709844860815575145)
XLA Ops:
  0.6 5.9 %other.1 = (f32[384,384]{1,0:T(8,128)S(1)}, f32[800,384]{1,0:T(8,128)S(1)}, f32[48,128]{1,0:T(8,128)S(1)}, f32[384,384]{1,0:T(8,128)S(1)}, f32[384,384]{1,0:T(8,...) custom-call(f32[2,2,384,384]{3,2,1,0:T(8,128)} %iso.1, f32[2,384,384]{2,1,0:T(8,128)} %coupling.1, ...), custom_call_target="tpu_custom_call" | custom-call | flops 2717908992 | bytes 1048576 | tf_op jit(solution)/shard_map/other/pallas_call | solution.py:384
  6.6 0.1 collective-permute-start
  6.7 0.5 %collective-permute-start.1 = (f32[384,384]{1,0:T(8,128)S(1)}, f32[384,384]{1,0:T(8,128)S(1)}, u32[]{:S(2)}, u32[]{:S(2)}) collective-permute-start(f32[384,384]{1,0:T(8,128)S(1)} %get-tuple-element.31), channel_id=1, source_target_pairs={{0,1},{1,0},{2,3},{3,2},{4,5},{5,4},{6,7},{7,6},{8,9},{9,8},{10,11... | collective-permute-start | bytes 1769480 | tf_op jit(solution)/shard_map/ppermute | solution.py:888
  7.2 1.9 %collective-permute-start.2 = (f32[48,128]{1,0:T(8,128)S(1)}, f32[48,128]{1,0:T(8,128)S(1)}, u32[]{:S(2)}, u32[]{:S(2)}) collective-permute-start(f32[48,128]{1,0:T(8,128)S(1)} %get-tuple-element.25.planes), channel_id=1, source_target_pairs={{0,3},{1,2},{2,1},{3,0},{4,7},{5,6},{6,5},{7,4},{8,11},{9,10},{10,... | collective-permute-start | bytes 73736 | tf_op jit(solution)/shard_map/ppermute | solution.py:872
  9.1 0.0 copy-start
  9.1 2.4 %own.1 = f32[800,384]{1,0:T(8,128)S(1)} custom-call(f32[48,128]{1,0:T(8,128)S(1)} %get-tuple-element.25.planes, f32[384,384]{1,0:T(8,128)S(1)} %get-tuple-element.26.early.own_step, f32[384,384]{1,0:T(8,128)S(1)} %get-tuple-element.27.late, f32[2,384,384]{2,1,0:T(8,128)S(1)} %get-tuple-element.28.isos, f32[384,384]{1,0:T(8,128)S(1)} %get-tuple-element.29.lead), custom_call_target="tpu_custom_call" | custom-call | flops 2147483648 | bytes 1048576 | tf_op jit(solution)/shard_map/own/pallas_call | solution.py:384
  11.5 0.0 copy-start.5
  11.5 0.0 copy-start.4
  11.5 0.0 collective-permute-done.2.second
  11.5 0.0 collective-permute-done.1.got_step
  11.5 0.0 collective-permute-done.got
  11.5 0.0 copy-done
  11.5 1.5 %relay.1 = (f32[584,128]{1,0:T(8,128)S(1)}, f32[1536,384]{1,0:T(8,128)S(1)}, bf16[1536,1536]{1,0:T(8,128)(2,1)S(1)}, f32[26,8,128]{2,1,0:T(8,128)S(1)}, f32[8,12...) custom-call(f32[800,384]{1,0:T(8,128)S(1)} %own.1, f32[800,384]{1,0:T(8,128)S(1)} %collective-permute-done.got, ...), custom_call_target="tpu_custom_call" | custom-call | flops 679477248 | bytes 1048576 | tf_op jit(solution)/shard_map/relay/pallas_call | solution.py:384
  13.1 0.0 copy-start.2
  13.1 0.0 copy-start.3
  13.1 1.0 %collective-permute-start.4 = (f32[584,128]{1,0:T(8,128)S(1)}, f32[584,128]{1,0:T(8,128)S(1)}, u32[]{:S(2)}, u32[]{:S(2)}) collective-permute-start(f32[584,128]{1,0:T(8,128)S(1)} %get-tuple-element.34), channel_id=1, source_target_pairs={{0,2},{1,3},{2,0},{3,1},{4,6},{5,7},{6,4},{7,5},{8,10},{9,11},{10,... | collective-permute-start | bytes 897032 | tf_op jit(solution)/shard_map/ppermute | solution.py:912
  14.1 0.0 collective-permute-start.3
  14.1 0.0 copy-done.5
  14.1 1.6 %collective-permute-start.5 = (f32[136,128]{1,0:T(8,128)S(1)}, f32[136,128]{1,0:T(8,128)S(1)}, u32[]{:S(2)}, u32[]{:S(2)}) collective-permute-start(f32[136,128]{1,0:T(8,128)S(1)} %get-tuple-element.40), channel_id=1, source_target_pairs={{0,4},{4,0},{8,12},{12,8},{16,20},{20,16},{24,28},{28,24},{1,5},{5... | collective-permute-start | bytes 208904 | tf_op jit(solution)/shard_map/ppermute | solution.py:913
  15.7 0.2 collective-permute-start.6
  15.8 0.0 collective-permute-done.3.other_cells
  15.8 0.0 copy-done.4
  15.9 1.8 %atoms.1 = (f32[6,384,128]{2,1,0:T(8,128)S(1)}, bf16[480,512]{1,0:T(8,128)(2,1)S(1)}, f32[512,128]{1,0:T(8,128)S(1)}, f32[384,128]{1,0:T(8,128)S(1)}, f32[16,128]{1,0:T(8,128)S(1)}) custom-call(f32[1,4]{1,0:T(1,128)S(1)} %bitcast.5, s32[1,384]{1,0:T(1,128)S(1)} %reshape.17.orbital_atom, f32[8,128]{1,0:T(8,128)S(1)} %get-tuple-element.32.some_cells, ...), custom_call_target="tpu_custom_call" | custom-call | flops 536870912 | bytes 1048576 | tf_op jit(solution)/shard_map/atoms/pallas_call | solution.py:384
  17.7 0.0 copy-done.2
  17.7 0.0 copy-done.3
  17.7 0.0 copy-start.1
  17.7 1.2 %known.1 = (f32[8,128]{1,0:T(8,128)S(1)}, f32[32,128]{1,0:T(8,128)S(1)}) custom-call(f32[1,2]{1,0:T(1,128)S(1)} %bitcast.3, s32[1,2]{1,0:T(1,128)S(1)} %bitcast.4, s32[1,384]{1,0:T(1,128)S(1)} %reshape.17.orbital_atom, f32[384,128]{1,0:T(8,128)S(1)} %get-tuple-element.33.member, f32[800,384]{1,0:T(8,128)S(1)} %own.1, ...), custom_call_target="tpu_custom_call" | custom-call | flops 268435456 | bytes 1048576 | tf_op jit(solution)/shard_map/known/pallas_call | solution.py:384
  18.9 0.4 collective-permute-done.5.one_beside
  19.3 0.0 collective-permute-done.6.two_beside
  19.3 0.0 copy-done.1
  19.3 1.2 %moments.1 = (f32[24,128]{1,0:T(8,128)S(1)}, f32[20,24,128]{2,1,0:T(8,128)S(1)}) custom-call(f32[800,384]{1,0:T(8,128)S(1)} %own.1, f32[26,8,128]{2,1,0:T(8,128)S(1)} %get-tuple-element.39.field, f32[136,128]{1,0:T(8,128)S(1)} %collective-permute-done.5.one_beside, f32[136,128]{1,0:T(8,128)S(1)} %collective-permute-done.6.two_beside, s32[2,48]{1,0:T(2,128)S(1)} %copy-done.1), custom_call_target="tpu_custom_call" | custom-call | flops 67108864 | bytes 1048576 | tf_op jit(solution)/shard_map/moments/pallas_call | solution.py:384
  20.5 1.3 %collective-permute-done.4.packed = f32[584,128]{1,0:T(8,128)S(1)} collective-permute-done((f32[584,128]{1,0:T(8,128)S(1)}, f32[584,128]{1,0:T(8,128)S(1)}, u32[]{:S(2)}, u32[]{:S(2)}) %collective-permute-start.4) | collective-permute-done | bytes 299040 | tf_op jit(solution)/shard_map/ppermute | solution.py:912
  21.8 0.1 density.1
  21.9 0.0 collective-permute-start.7
  21.9 1.2 %collective-permute-done.7 = f32[40,128]{1,0:T(8,128)S(1)} collective-permute-done((f32[40,128]{1,0:T(8,128)S(1)}, f32[40,128]{1,0:T(8,128)S(1)}, u32[]{:S(2)}, u32[]{:S(2)}) %collective-permute-start.7) | collective-permute-done | bytes 20512 | tf_op jit(solution)/shard_map/ppermute | solution.py:788
  23.1 4.0 %collective-permute-start.10 = (f32[40,128]{1,0:T(8,128)S(1)}, f32[40,128]{1,0:T(8,128)S(1)}, u32[]{:S(2)}, u32[]{:S(2)}) collective-permute-start(f32[40,128]{1,0:T(8,128)S(1)} %add.21), channel_id=1, source_target_pairs={{0,6},{1,7},{2,4},{3,5},{4,2},{5,3},{6,0},{7,1},{8,14},{9,15},{10,... | collective-permute-start | bytes 61448 | tf_op jit(solution)/shard_map/ppermute | solution.py:788
  27.1 0.5 %collective-permute-start.9 = (f32[40,128]{1,0:T(8,128)S(1)}, f32[40,128]{1,0:T(8,128)S(1)}, u32[]{:S(2)}, u32[]{:S(2)}) collective-permute-start(f32[40,128]{1,0:T(8,128)S(1)} %add.21), channel_id=1, source_target_pairs={{0,4},{1,5},{2,6},{3,7},{4,0},{5,1},{6,2},{7,3},{8,12},{9,13},{10,... | collective-permute-start | bytes 61448 | tf_op jit(solution)/shard_map/ppermute | solution.py:788
  27.6 0.1 collective-permute-start.8
  27.7 1.2 %collective-permute-done.10 = f32[40,128]{1,0:T(8,128)S(1)} collective-permute-done((f32[40,128]{1,0:T(8,128)S(1)}, f32[40,128]{1,0:T(8,128)S(1)}, u32[]{:S(2)}, u32[]{:S(2)}) %collective-permute-start.10) | collective-permute-done | bytes 20512 | tf_op jit(solution)/shard_map/ppermute | solution.py:788
  28.9 2.0 %collective-permute-done.9 = f32[40,128]{1,0:T(8,128)S(1)} collective-permute-done((f32[40,128]{1,0:T(8,128)S(1)}, f32[40,128]{1,0:T(8,128)S(1)}, u32[]{:S(2)}, u32[]{:S(2)}) %collective-permute-start.9) | collective-permute-done | bytes 20512 | tf_op jit(solution)/shard_map/ppermute | solution.py:788
  30.9 0.5 %collective-permute-done.8 = f32[40,128]{1,0:T(8,128)S(1)} collective-permute-done((f32[40,128]{1,0:T(8,128)S(1)}, f32[40,128]{1,0:T(8,128)S(1)}, u32[]{:S(2)}, u32[]{:S(2)}) %collective-permute-start.8) | collective-permute-done | bytes 20512 | tf_op jit(solution)/shard_map/ppermute | solution.py:788
  31.4 3.9 %collective-permute-start.13 = (f32[40,128]{1,0:T(8,128)S(1)}, f32[40,128]{1,0:T(8,128)S(1)}, u32[]{:S(2)}, u32[]{:S(2)}) collective-permute-start(f32[40,128]{1,0:T(8,128)S(1)} %add_add_fusion.1), channel_id=1, source_target_pairs={{0,24},{4,28},{8,16},{12,20},{16,8},{20,12},{24,0},{28,4},{1,25},{... | collective-permute-start | bytes 61448 | tf_op jit(solution)/shard_map/ppermute | solution.py:788
  35.3 0.0 collective-permute-start.12
  35.3 0.6 %collective-permute-start.11 = (f32[40,128]{1,0:T(8,128)S(1)}, f32[40,128]{1,0:T(8,128)S(1)}, u32[]{:S(2)}, u32[]{:S(2)}) collective-permute-start(f32[40,128]{1,0:T(8,128)S(1)} %add_add_fusion.1), channel_id=1, source_target_pairs={{0,8},{4,12},{8,0},{12,4},{16,24},{20,28},{24,16},{28,20},{1,9},{5... | collective-permute-start | bytes 61448 | tf_op jit(solution)/shard_map/ppermute | solution.py:788
  35.9 1.1 %collective-permute-done.13 = f32[40,128]{1,0:T(8,128)S(1)} collective-permute-done((f32[40,128]{1,0:T(8,128)S(1)}, f32[40,128]{1,0:T(8,128)S(1)}, u32[]{:S(2)}, u32[]{:S(2)}) %collective-permute-start.13) | collective-permute-done | bytes 20512 | tf_op jit(solution)/shard_map/ppermute | solution.py:788
  37.1 2.9 %collective-permute-done.12 = f32[40,128]{1,0:T(8,128)S(1)} collective-permute-done((f32[40,128]{1,0:T(8,128)S(1)}, f32[40,128]{1,0:T(8,128)S(1)}, u32[]{:S(2)}, u32[]{:S(2)}) %collective-permute-start.12) | collective-permute-done | bytes 20512 | tf_op jit(solution)/shard_map/ppermute | solution.py:788
  40.0 0.0 collective-permute-done.11
  40.0 1.4 %finish.1 = (f32[4,2,48]{2,1,0:T(2,128)}, f32[16,8,128]{2,1,0:T(8,128)}) custom-call(f32[40,128]{1,0:T(8,128)S(1)} %add_add_fusion.payload, f32[6,384,128]{2,1,0:T(8,128)S(1)} %get-tuple-element.43.walks, bf16[480,512]{1,0:T(8,128)(2,1)S(1)} %get-tuple-element.44.row_hot, f32[512,128]{1,0:T(8,128)S(1)} %get-tuple-element.45.deep_hot, ...), custom_call_target="tpu_custom_call" | custom-call | flops 536870912 | bytes 1048576 | tf_op jit(solution)/shard_map/finish/pallas_call | solution.py:384
  (4 shorter events, 0.0 us)
Async XLA Ops:
  6.6 4.9 %collective-permute-start = (f32[800,384]{1,0:T(8,128)S(1)}, f32[800,384]{1,0:T(8,128)S(1)}, u32[]{:S(2)}, u32[]{:S(2)}) collective-permute-start(f32[800,384]{1,0:T(8,128)S(1)} %get-tuple-element.30), channel_id=1, source_target_pairs={{0,1},{1,0},{2,3},{3,2},{4,5},{5,4},{6,7},{7,6},{8,9},{9,8},{10,11... | collective-permute-start | bytes 3686408 | tf_op jit(solution)/shard_map/ppermute | solution.py:871
  6.7 4.8 %collective-permute-start.1 = (f32[384,384]{1,0:T(8,128)S(1)}, f32[384,384]{1,0:T(8,128)S(1)}, u32[]{:S(2)}, u32[]{:S(2)}) collective-permute-start(f32[384,384]{1,0:T(8,128)S(1)} %get-tuple-element.31), channel_id=1, source_target_pairs={{0,1},{1,0},{2,3},{3,2},{4,5},{5,4},{6,7},{7,6},{8,9},{9,8},{10,11... | collective-permute-start | bytes 1769480 | tf_op jit(solution)/shard_map/ppermute | solution.py:888
  7.2 4.3 %collective-permute-start.2 = (f32[48,128]{1,0:T(8,128)S(1)}, f32[48,128]{1,0:T(8,128)S(1)}, u32[]{:S(2)}, u32[]{:S(2)}) collective-permute-start(f32[48,128]{1,0:T(8,128)S(1)} %get-tuple-element.25.planes), channel_id=1, source_target_pairs={{0,3},{1,2},{2,1},{3,0},{4,7},{5,6},{6,5},{7,4},{8,11},{9,10},{10,... | collective-permute-start | bytes 73736 | tf_op jit(solution)/shard_map/ppermute | solution.py:872
  9.1 2.4 %copy-start = (f32[16,8,128]{2,1,0:T(8,128)S(1)}, f32[16,8,128]{2,1,0:T(8,128)}, u32[]{:S(2)}) copy-start(f32[16,8,128]{2,1,0:T(8,128)} %field.1) | copy-start | bytes 196612
  11.5 2.7 %copy-start.5 = (s32[384]{0:T(512)S(1)}, s32[384]{0:T(512)}, u32[]{:S(2)}) copy-start(s32[384]{0:T(512)} %param.15) | copy-start | bytes 4612
  11.5 4.4 %copy-start.4 = (f32[4]{0:T(128)S(1)}, f32[4]{0:T(128)}, u32[]{:S(2)}) copy-start(f32[4]{0:T(128)} %param.14) | copy-start | bytes 52
  13.1 4.6 %copy-start.2 = (f32[2]{0:T(128)S(1)}, f32[2]{0:T(128)}, u32[]{:S(2)}) copy-start(f32[2]{0:T(128)} %param.12) | copy-start | bytes 28
  13.1 4.6 %copy-start.3 = (s32[2]{0:T(128)S(1)}, s32[2]{0:T(128)}, u32[]{:S(2)}) copy-start(s32[2]{0:T(128)} %param.13) | copy-start | bytes 28
  13.1 8.7 %collective-permute-start.4 = (f32[584,128]{1,0:T(8,128)S(1)}, f32[584,128]{1,0:T(8,128)S(1)}, u32[]{:S(2)}, u32[]{:S(2)}) collective-permute-start(f32[584,128]{1,0:T(8,128)S(1)} %get-tuple-element.34), channel_id=1, source_target_pairs={{0,2},{1,3},{2,0},{3,1},{4,6},{5,7},{6,4},{7,5},{8,10},{9,11},{10,... | collective-permute-start | bytes 897032 | tf_op jit(solution)/shard_map/ppermute | solution.py:912
  14.1 1.7 %collective-permute-start.3 = (f32[8,128]{1,0:T(8,128)S(1)}, f32[8,128]{1,0:T(8,128)S(1)}, u32[]{:S(2)}, u32[]{:S(2)}) collective-permute-start(f32[8,128]{1,0:T(8,128)S(1)} %get-tuple-element.32.some_cells), channel_id=1, source_target_pairs={{0,1},{1,0},{2,3},{3,2},{4,5},{5,4},{6,7},{7,6},{8,9},{9,8},{10,11... | collective-permute-start | bytes 12296 | tf_op jit(solution)/shard_map/ppermute | solution.py:915
  14.1 5.1 %collective-permute-start.5 = (f32[136,128]{1,0:T(8,128)S(1)}, f32[136,128]{1,0:T(8,128)S(1)}, u32[]{:S(2)}, u32[]{:S(2)}) collective-permute-start(f32[136,128]{1,0:T(8,128)S(1)} %get-tuple-element.40), channel_id=1, source_target_pairs={{0,4},{4,0},{8,12},{12,8},{16,20},{20,16},{24,28},{28,24},{1,5},{5... | collective-permute-start | bytes 208904 | tf_op jit(solution)/shard_map/ppermute | solution.py:913
  15.7 3.6 %collective-permute-start.6 = (f32[136,128]{1,0:T(8,128)S(1)}, f32[136,128]{1,0:T(8,128)S(1)}, u32[]{:S(2)}, u32[]{:S(2)}) collective-permute-start(f32[136,128]{1,0:T(8,128)S(1)} %get-tuple-element.41), channel_id=1, source_target_pairs={{0,1},{1,0},{2,3},{3,2},{4,8},{5,9},{6,10},{7,11},{8,4},{9,5},{10,... | collective-permute-start | bytes 208904 | tf_op jit(solution)/shard_map/ppermute | solution.py:914
  17.7 1.6 %copy-start.1 = (s32[2,48]{1,0:T(2,128)S(1)}, s32[2,48]{1,0:T(2,128)}, u32[]{:S(2)}) copy-start(s32[2,48]{1,0:T(2,128)} %cells.1) | copy-start | bytes 1156
  21.9 1.2 %collective-permute-start.7 = (f32[40,128]{1,0:T(8,128)S(1)}, f32[40,128]{1,0:T(8,128)S(1)}, u32[]{:S(2)}, u32[]{:S(2)}) collective-permute-start(f32[40,128]{1,0:T(8,128)S(1)} %density.1), channel_id=1, source_target_pairs={{0,1},{1,0},{2,3},{3,2},{4,5},{5,4},{6,7},{7,6},{8,9},{9,8},{10,11... | collective-permute-start | bytes 61448 | tf_op jit(solution)/shard_map/ppermute | solution.py:788
  23.1 5.8 %collective-permute-start.10 = (f32[40,128]{1,0:T(8,128)S(1)}, f32[40,128]{1,0:T(8,128)S(1)}, u32[]{:S(2)}, u32[]{:S(2)}) collective-permute-start(f32[40,128]{1,0:T(8,128)S(1)} %add.21), channel_id=1, source_target_pairs={{0,6},{1,7},{2,4},{3,5},{4,2},{5,3},{6,0},{7,1},{8,14},{9,15},{10,... | collective-permute-start | bytes 61448 | tf_op jit(solution)/shard_map/ppermute | solution.py:788
  27.1 3.8 %collective-permute-start.9 = (f32[40,128]{1,0:T(8,128)S(1)}, f32[40,128]{1,0:T(8,128)S(1)}, u32[]{:S(2)}, u32[]{:S(2)}) collective-permute-start(f32[40,128]{1,0:T(8,128)S(1)} %add.21), channel_id=1, source_target_pairs={{0,4},{1,5},{2,6},{3,7},{4,0},{5,1},{6,2},{7,3},{8,12},{9,13},{10,... | collective-permute-start | bytes 61448 | tf_op jit(solution)/shard_map/ppermute | solution.py:788
  27.6 3.8 %collective-permute-start.8 = (f32[40,128]{1,0:T(8,128)S(1)}, f32[40,128]{1,0:T(8,128)S(1)}, u32[]{:S(2)}, u32[]{:S(2)}) collective-permute-start(f32[40,128]{1,0:T(8,128)S(1)} %add.21), channel_id=1, source_target_pairs={{0,2},{1,3},{2,0},{3,1},{4,6},{5,7},{6,4},{7,5},{8,10},{9,11},{10,... | collective-permute-start | bytes 61448 | tf_op jit(solution)/shard_map/ppermute | solution.py:788
  31.4 5.7 %collective-permute-start.13 = (f32[40,128]{1,0:T(8,128)S(1)}, f32[40,128]{1,0:T(8,128)S(1)}, u32[]{:S(2)}, u32[]{:S(2)}) collective-permute-start(f32[40,128]{1,0:T(8,128)S(1)} %add_add_fusion.1), channel_id=1, source_target_pairs={{0,24},{4,28},{8,16},{12,20},{16,8},{20,12},{24,0},{28,4},{1,25},{... | collective-permute-start | bytes 61448 | tf_op jit(solution)/shard_map/ppermute | solution.py:788
  35.3 4.7 %collective-permute-start.12 = (f32[40,128]{1,0:T(8,128)S(1)}, f32[40,128]{1,0:T(8,128)S(1)}, u32[]{:S(2)}, u32[]{:S(2)}) collective-permute-start(f32[40,128]{1,0:T(8,128)S(1)} %add_add_fusion.1), channel_id=1, source_target_pairs={{0,16},{4,20},{8,24},{12,28},{16,0},{20,4},{24,8},{28,12},{1,17},{... | collective-permute-start | bytes 61448 | tf_op jit(solution)/shard_map/ppermute | solution.py:788
  35.3 4.7 %collective-permute-start.11 = (f32[40,128]{1,0:T(8,128)S(1)}, f32[40,128]{1,0:T(8,128)S(1)}, u32[]{:S(2)}, u32[]{:S(2)}) collective-permute-start(f32[40,128]{1,0:T(8,128)S(1)} %add_add_fusion.1), channel_id=1, source_target_pairs={{0,8},{4,12},{8,0},{12,4},{16,24},{20,28},{24,16},{28,20},{1,9},{5... | collective-permute-start | bytes 61448 | tf_op jit(solution)/shard_map/ppermute | solution.py:788

commit v10 on v9

--- a/solution.py
+++ b/solution.py
@@ -792,19 +792,16 @@
 
 
 def total_over_all(value):
-    wires, slabs = (lax.axis_size("energy"), lax.axis_size("slab"))
+    size, slabs = (lax.axis_size("energy") * lax.axis_size("slab"), lax.axis_size("slab"))
     value = total_over(value, "slab", (1,))
-    stride = 2
-    while stride * 2 < slabs:
-        value = total_over(value, "slab", (stride,))
-        stride *= 2
-    value = total_over(value, BOTH, (stride, slabs, stride + slabs))
-    stride = 2
-    while stride * 4 <= wires:
-        value = total_over(value, "energy", (stride, 2 * stride, 3 * stride))
-        stride *= 4
-    if stride < wires:
-        value = total_over(value, "energy", (stride,))
+    strides = [1 << i for i in range(1, size.bit_length() - 1)]
+    far = [stride for stride in strides if stride > slabs // 2]
+    near = [stride for stride in strides if stride <= slabs // 2]
+    order = far[:2] + near + far[2:]
+    while order:
+        one, *rest = order[:2]
+        value = total_over(value, BOTH, (one, *rest, *[one + two for two in rest]))
+        order = order[2:]
     return value
 
 

time: 41.6 us -> 41.3 us (level)
  no operation moved by 1% of the time
where the time goes in v10:
time: 41.3 us; the launch traced here: 41.1 us
  Pallas kernels  15.6 us (38%)
  starting transfers between devices  14.2 us (34%)
  waiting for transfers between devices  10.5 us (25%)
  between operations  0.79 us (2%)
    pallas_call x8, Pallas kernels, local_call(): pl.pallas_call(kernel, out_shape=shapes, in_specs=[pl.BlockSpec(memory_sp...  15.6 us
    ppermute x7, starting transfers between devices, total_over(): lax.ppermute(value, axis, [(i, i ^ k) for i in range(size)])  8.96 us
    ppermute x7, waiting for transfers between devices, total_over(): lax.ppermute(value, axis, [(i, i ^ k) for i in range(size)])  8.82 us
    ppermute x1, starting transfers between devices, on_device(): second = lax.ppermute(edge, 'slab', neighbour_turn(devices))  1.92 us
    ppermute x1, starting transfers between devices, on_device(): one_beside = lax.ppermute(one_side, 'energy', pairs_of(wires))  1.55 us
    ppermute x1, waiting for transfers between devices, on_device(): packed = lax.ppermute(passed, 'slab', hop(devices, 1))  1.32 us
    ppermute x1, starting transfers between devices, on_device(): packed = lax.ppermute(passed, 'slab', hop(devices, 1))  1.04 us
  transfers between devices with their start and end apart: 14, of which 8 were waited for; matrix products, arithmetic and copies ran while one was open for 0% of the time, Pallas kernels for 16%

profile of v10, /device:TPU:0, one launch (start us, length us, event | category | flops | bytes accessed | tf_op | source)
XLA Modules:
  0.0 41.1 jit_solution(8925282225365348981)
XLA Ops:
  0.6 5.9 %other.1 = (f32[384,384]{1,0:T(8,128)S(1)}, f32[800,384]{1,0:T(8,128)S(1)}, f32[48,128]{1,0:T(8,128)S(1)}, f32[384,384]{1,0:T(8,128)S(1)}, f32[384,384]{1,0:T(8,...) custom-call(f32[2,2,384,384]{3,2,1,0:T(8,128)} %iso.1, f32[2,384,384]{2,1,0:T(8,128)} %coupling.1, ...), custom_call_target="tpu_custom_call" | custom-call | flops 2717908992 | bytes 1048576 | tf_op jit(solution)/shard_map/other/pallas_call | solution.py:384
  6.6 0.1 collective-permute-start
  6.7 0.5 %collective-permute-start.1 = (f32[384,384]{1,0:T(8,128)S(1)}, f32[384,384]{1,0:T(8,128)S(1)}, u32[]{:S(2)}, u32[]{:S(2)}) collective-permute-start(f32[384,384]{1,0:T(8,128)S(1)} %get-tuple-element.31), channel_id=1, source_target_pairs={{0,1},{1,0},{2,3},{3,2},{4,5},{5,4},{6,7},{7,6},{8,9},{9,8},{10,11... | collective-permute-start | bytes 1769480 | tf_op jit(solution)/shard_map/ppermute | solution.py:885
  7.2 1.9 %collective-permute-start.2 = (f32[48,128]{1,0:T(8,128)S(1)}, f32[48,128]{1,0:T(8,128)S(1)}, u32[]{:S(2)}, u32[]{:S(2)}) collective-permute-start(f32[48,128]{1,0:T(8,128)S(1)} %get-tuple-element.25.planes), channel_id=1, source_target_pairs={{0,3},{1,2},{2,1},{3,0},{4,7},{5,6},{6,5},{7,4},{8,11},{9,10},{10,... | collective-permute-start | bytes 73736 | tf_op jit(solution)/shard_map/ppermute | solution.py:869
  9.1 0.0 copy-start
  9.1 2.4 %own.1 = f32[800,384]{1,0:T(8,128)S(1)} custom-call(f32[48,128]{1,0:T(8,128)S(1)} %get-tuple-element.25.planes, f32[384,384]{1,0:T(8,128)S(1)} %get-tuple-element.26.early.own_step, f32[384,384]{1,0:T(8,128)S(1)} %get-tuple-element.27.late, f32[2,384,384]{2,1,0:T(8,128)S(1)} %get-tuple-element.28.isos, f32[384,384]{1,0:T(8,128)S(1)} %get-tuple-element.29.lead), custom_call_target="tpu_custom_call" | custom-call | flops 2147483648 | bytes 1048576 | tf_op jit(solution)/shard_map/own/pallas_call | solution.py:384
  11.5 0.0 copy-start.5
  11.5 0.0 copy-start.4
  11.5 0.0 collective-permute-done.2.second
  11.5 0.0 collective-permute-done.1.got_step
  11.5 0.0 collective-permute-done.got
  11.5 0.0 copy-done
  11.5 1.5 %relay.1 = (f32[584,128]{1,0:T(8,128)S(1)}, f32[1536,384]{1,0:T(8,128)S(1)}, bf16[1536,1536]{1,0:T(8,128)(2,1)S(1)}, f32[26,8,128]{2,1,0:T(8,128)S(1)}, f32[8,12...) custom-call(f32[800,384]{1,0:T(8,128)S(1)} %own.1, f32[800,384]{1,0:T(8,128)S(1)} %collective-permute-done.got, ...), custom_call_target="tpu_custom_call" | custom-call | flops 679477248 | bytes 1048576 | tf_op jit(solution)/shard_map/relay/pallas_call | solution.py:384
  13.1 0.0 copy-start.2
  13.1 0.0 copy-start.3
  13.1 1.0 %collective-permute-start.4 = (f32[584,128]{1,0:T(8,128)S(1)}, f32[584,128]{1,0:T(8,128)S(1)}, u32[]{:S(2)}, u32[]{:S(2)}) collective-permute-start(f32[584,128]{1,0:T(8,128)S(1)} %get-tuple-element.34), channel_id=1, source_target_pairs={{0,2},{1,3},{2,0},{3,1},{4,6},{5,7},{6,4},{7,5},{8,10},{9,11},{10,... | collective-permute-start | bytes 897032 | tf_op jit(solution)/shard_map/ppermute | solution.py:909
  14.1 0.0 collective-permute-start.3
  14.1 0.0 copy-done.5
  14.1 1.6 %collective-permute-start.5 = (f32[136,128]{1,0:T(8,128)S(1)}, f32[136,128]{1,0:T(8,128)S(1)}, u32[]{:S(2)}, u32[]{:S(2)}) collective-permute-start(f32[136,128]{1,0:T(8,128)S(1)} %get-tuple-element.40), channel_id=1, source_target_pairs={{0,4},{4,0},{8,12},{12,8},{16,20},{20,16},{24,28},{28,24},{1,5},{5... | collective-permute-start | bytes 208904 | tf_op jit(solution)/shard_map/ppermute | solution.py:910
  15.7 0.2 collective-permute-start.6
  15.8 0.0 collective-permute-done.3.other_cells
  15.8 0.0 copy-done.4
  15.9 1.8 %atoms.1 = (f32[6,384,128]{2,1,0:T(8,128)S(1)}, bf16[480,512]{1,0:T(8,128)(2,1)S(1)}, f32[512,128]{1,0:T(8,128)S(1)}, f32[384,128]{1,0:T(8,128)S(1)}, f32[16,128]{1,0:T(8,128)S(1)}) custom-call(f32[1,4]{1,0:T(1,128)S(1)} %bitcast.5, s32[1,384]{1,0:T(1,128)S(1)} %reshape.17.orbital_atom, f32[8,128]{1,0:T(8,128)S(1)} %get-tuple-element.32.some_cells, ...), custom_call_target="tpu_custom_call" | custom-call | flops 536870912 | bytes 1048576 | tf_op jit(solution)/shard_map/atoms/pallas_call | solution.py:384
  17.7 0.0 copy-done.2
  17.7 0.0 copy-done.3
  17.7 0.0 copy-start.1
  17.7 1.2 %known.1 = (f32[8,128]{1,0:T(8,128)S(1)}, f32[32,128]{1,0:T(8,128)S(1)}) custom-call(f32[1,2]{1,0:T(1,128)S(1)} %bitcast.3, s32[1,2]{1,0:T(1,128)S(1)} %bitcast.4, s32[1,384]{1,0:T(1,128)S(1)} %reshape.17.orbital_atom, f32[384,128]{1,0:T(8,128)S(1)} %get-tuple-element.33.member, f32[800,384]{1,0:T(8,128)S(1)} %own.1, ...), custom_call_target="tpu_custom_call" | custom-call | flops 268435456 | bytes 1048576 | tf_op jit(solution)/shard_map/known/pallas_call | solution.py:384
  18.9 0.4 collective-permute-done.5.one_beside
  19.3 0.0 collective-permute-done.6.two_beside
  19.3 0.0 copy-done.1
  19.3 1.2 %moments.1 = (f32[24,128]{1,0:T(8,128)S(1)}, f32[20,24,128]{2,1,0:T(8,128)S(1)}) custom-call(f32[800,384]{1,0:T(8,128)S(1)} %own.1, f32[26,8,128]{2,1,0:T(8,128)S(1)} %get-tuple-element.39.field, f32[136,128]{1,0:T(8,128)S(1)} %collective-permute-done.5.one_beside, f32[136,128]{1,0:T(8,128)S(1)} %collective-permute-done.6.two_beside, s32[2,48]{1,0:T(2,128)S(1)} %copy-done.1), custom_call_target="tpu_custom_call" | custom-call | flops 67108864 | bytes 1048576 | tf_op jit(solution)/shard_map/moments/pallas_call | solution.py:384
  20.5 1.3 %collective-permute-done.4.packed = f32[584,128]{1,0:T(8,128)S(1)} collective-permute-done((f32[584,128]{1,0:T(8,128)S(1)}, f32[584,128]{1,0:T(8,128)S(1)}, u32[]{:S(2)}, u32[]{:S(2)}) %collective-permute-start.4) | collective-permute-done | bytes 299040 | tf_op jit(solution)/shard_map/ppermute | solution.py:909
  21.8 0.1 density.1
  21.9 0.0 collective-permute-start.7
  21.9 1.2 %collective-permute-done.7 = f32[40,128]{1,0:T(8,128)S(1)} collective-permute-done((f32[40,128]{1,0:T(8,128)S(1)}, f32[40,128]{1,0:T(8,128)S(1)}, u32[]{:S(2)}, u32[]{:S(2)}) %collective-permute-start.7) | collective-permute-done | bytes 20512 | tf_op jit(solution)/shard_map/ppermute | solution.py:788
  23.1 3.3 %collective-permute-start.10 = (f32[40,128]{1,0:T(8,128)S(1)}, f32[40,128]{1,0:T(8,128)S(1)}, u32[]{:S(2)}, u32[]{:S(2)}) collective-permute-start(f32[40,128]{1,0:T(8,128)S(1)} %add.21), channel_id=1, source_target_pairs={{0,12},{1,13},{2,14},{3,15},{4,8},{5,9},{6,10},{7,11},{8,4},{9,5},... | collective-permute-start | bytes 61448 | tf_op jit(solution)/shard_map/ppermute | solution.py:788
  26.4 0.4 %collective-permute-start.9 = (f32[40,128]{1,0:T(8,128)S(1)}, f32[40,128]{1,0:T(8,128)S(1)}, u32[]{:S(2)}, u32[]{:S(2)}) collective-permute-start(f32[40,128]{1,0:T(8,128)S(1)} %add.21), channel_id=1, source_target_pairs={{0,8},{1,9},{2,10},{3,11},{4,12},{5,13},{6,14},{7,15},{8,0},{9,1},... | collective-permute-start | bytes 61448 | tf_op jit(solution)/shard_map/ppermute | solution.py:788
  26.8 0.2 collective-permute-start.8
  27.0 1.1 %collective-permute-done.10 = f32[40,128]{1,0:T(8,128)S(1)} collective-permute-done((f32[40,128]{1,0:T(8,128)S(1)}, f32[40,128]{1,0:T(8,128)S(1)}, u32[]{:S(2)}, u32[]{:S(2)}) %collective-permute-start.10) | collective-permute-done | bytes 20512 | tf_op jit(solution)/shard_map/ppermute | solution.py:788
  28.2 2.0 %collective-permute-done.9 = f32[40,128]{1,0:T(8,128)S(1)} collective-permute-done((f32[40,128]{1,0:T(8,128)S(1)}, f32[40,128]{1,0:T(8,128)S(1)}, u32[]{:S(2)}, u32[]{:S(2)}) %collective-permute-start.9) | collective-permute-done | bytes 20512 | tf_op jit(solution)/shard_map/ppermute | solution.py:788
  30.2 0.4 %collective-permute-done.8 = f32[40,128]{1,0:T(8,128)S(1)} collective-permute-done((f32[40,128]{1,0:T(8,128)S(1)}, f32[40,128]{1,0:T(8,128)S(1)}, u32[]{:S(2)}, u32[]{:S(2)}) %collective-permute-start.8) | collective-permute-done | bytes 20512 | tf_op jit(solution)/shard_map/ppermute | solution.py:788
  30.6 4.3 %collective-permute-start.13 = (f32[40,128]{1,0:T(8,128)S(1)}, f32[40,128]{1,0:T(8,128)S(1)}, u32[]{:S(2)}, u32[]{:S(2)}) collective-permute-start(f32[40,128]{1,0:T(8,128)S(1)} %add_add_fusion.1), channel_id=1, source_target_pairs={{0,18},{1,19},{2,16},{3,17},{4,22},{5,23},{6,20},{7,21},{8,26},{9,... | collective-permute-start | bytes 61448 | tf_op jit(solution)/shard_map/ppermute | solution.py:788
  35.0 0.3 collective-permute-start.12
  35.3 0.3 collective-permute-start.11
  35.6 1.1 %collective-permute-done.13 = f32[40,128]{1,0:T(8,128)S(1)} collective-permute-done((f32[40,128]{1,0:T(8,128)S(1)}, f32[40,128]{1,0:T(8,128)S(1)}, u32[]{:S(2)}, u32[]{:S(2)}) %collective-permute-start.13) | collective-permute-done | bytes 20512 | tf_op jit(solution)/shard_map/ppermute | solution.py:788
  36.7 2.9 %collective-permute-done.12 = f32[40,128]{1,0:T(8,128)S(1)} collective-permute-done((f32[40,128]{1,0:T(8,128)S(1)}, f32[40,128]{1,0:T(8,128)S(1)}, u32[]{:S(2)}, u32[]{:S(2)}) %collective-permute-start.12) | collective-permute-done | bytes 20512 | tf_op jit(solution)/shard_map/ppermute | solution.py:788
  39.7 0.0 collective-permute-done.11
  39.7 1.4 %finish.1 = (f32[4,2,48]{2,1,0:T(2,128)}, f32[16,8,128]{2,1,0:T(8,128)}) custom-call(f32[40,128]{1,0:T(8,128)S(1)} %add_add_fusion.payload, f32[6,384,128]{2,1,0:T(8,128)S(1)} %get-tuple-element.43.walks, bf16[480,512]{1,0:T(8,128)(2,1)S(1)} %get-tuple-element.44.row_hot, f32[512,128]{1,0:T(8,128)S(1)} %get-tuple-element.45.deep_hot, ...), custom_call_target="tpu_custom_call" | custom-call | flops 536870912 | bytes 1048576 | tf_op jit(solution)/shard_map/finish/pallas_call | solution.py:384
  (4 shorter events, 0.0 us)
Async XLA Ops:
  6.6 4.9 %collective-permute-start = (f32[800,384]{1,0:T(8,128)S(1)}, f32[800,384]{1,0:T(8,128)S(1)}, u32[]{:S(2)}, u32[]{:S(2)}) collective-permute-start(f32[800,384]{1,0:T(8,128)S(1)} %get-tuple-element.30), channel_id=1, source_target_pairs={{0,1},{1,0},{2,3},{3,2},{4,5},{5,4},{6,7},{7,6},{8,9},{9,8},{10,11... | collective-permute-start | bytes 3686408 | tf_op jit(solution)/shard_map/ppermute | solution.py:868
  6.7 4.8 %collective-permute-start.1 = (f32[384,384]{1,0:T(8,128)S(1)}, f32[384,384]{1,0:T(8,128)S(1)}, u32[]{:S(2)}, u32[]{:S(2)}) collective-permute-start(f32[384,384]{1,0:T(8,128)S(1)} %get-tuple-element.31), channel_id=1, source_target_pairs={{0,1},{1,0},{2,3},{3,2},{4,5},{5,4},{6,7},{7,6},{8,9},{9,8},{10,11... | collective-permute-start | bytes 1769480 | tf_op jit(solution)/shard_map/ppermute | solution.py:885
  7.2 4.3 %collective-permute-start.2 = (f32[48,128]{1,0:T(8,128)S(1)}, f32[48,128]{1,0:T(8,128)S(1)}, u32[]{:S(2)}, u32[]{:S(2)}) collective-permute-start(f32[48,128]{1,0:T(8,128)S(1)} %get-tuple-element.25.planes), channel_id=1, source_target_pairs={{0,3},{1,2},{2,1},{3,0},{4,7},{5,6},{6,5},{7,4},{8,11},{9,10},{10,... | collective-permute-start | bytes 73736 | tf_op jit(solution)/shard_map/ppermute | solution.py:869
  9.1 2.4 %copy-start = (f32[16,8,128]{2,1,0:T(8,128)S(1)}, f32[16,8,128]{2,1,0:T(8,128)}, u32[]{:S(2)}) copy-start(f32[16,8,128]{2,1,0:T(8,128)} %field.1) | copy-start | bytes 196612
  11.5 2.7 %copy-start.5 = (s32[384]{0:T(512)S(1)}, s32[384]{0:T(512)}, u32[]{:S(2)}) copy-start(s32[384]{0:T(512)} %param.15) | copy-start | bytes 4612
  11.5 4.4 %copy-start.4 = (f32[4]{0:T(128)S(1)}, f32[4]{0:T(128)}, u32[]{:S(2)}) copy-start(f32[4]{0:T(128)} %param.14) | copy-start | bytes 52
  13.1 4.6 %copy-start.2 = (f32[2]{0:T(128)S(1)}, f32[2]{0:T(128)}, u32[]{:S(2)}) copy-start(f32[2]{0:T(128)} %param.12) | copy-start | bytes 28
  13.1 4.6 %copy-start.3 = (s32[2]{0:T(128)S(1)}, s32[2]{0:T(128)}, u32[]{:S(2)}) copy-start(s32[2]{0:T(128)} %param.13) | copy-start | bytes 28
  13.1 8.7 %collective-permute-start.4 = (f32[584,128]{1,0:T(8,128)S(1)}, f32[584,128]{1,0:T(8,128)S(1)}, u32[]{:S(2)}, u32[]{:S(2)}) collective-permute-start(f32[584,128]{1,0:T(8,128)S(1)} %get-tuple-element.34), channel_id=1, source_target_pairs={{0,2},{1,3},{2,0},{3,1},{4,6},{5,7},{6,4},{7,5},{8,10},{9,11},{10,... | collective-permute-start | bytes 897032 | tf_op jit(solution)/shard_map/ppermute | solution.py:909
  14.1 1.7 %collective-permute-start.3 = (f32[8,128]{1,0:T(8,128)S(1)}, f32[8,128]{1,0:T(8,128)S(1)}, u32[]{:S(2)}, u32[]{:S(2)}) collective-permute-start(f32[8,128]{1,0:T(8,128)S(1)} %get-tuple-element.32.some_cells), channel_id=1, source_target_pairs={{0,1},{1,0},{2,3},{3,2},{4,5},{5,4},{6,7},{7,6},{8,9},{9,8},{10,11... | collective-permute-start | bytes 12296 | tf_op jit(solution)/shard_map/ppermute | solution.py:912
  14.1 5.1 %collective-permute-start.5 = (f32[136,128]{1,0:T(8,128)S(1)}, f32[136,128]{1,0:T(8,128)S(1)}, u32[]{:S(2)}, u32[]{:S(2)}) collective-permute-start(f32[136,128]{1,0:T(8,128)S(1)} %get-tuple-element.40), channel_id=1, source_target_pairs={{0,4},{4,0},{8,12},{12,8},{16,20},{20,16},{24,28},{28,24},{1,5},{5... | collective-permute-start | bytes 208904 | tf_op jit(solution)/shard_map/ppermute | solution.py:910
  15.7 3.6 %collective-permute-start.6 = (f32[136,128]{1,0:T(8,128)S(1)}, f32[136,128]{1,0:T(8,128)S(1)}, u32[]{:S(2)}, u32[]{:S(2)}) collective-permute-start(f32[136,128]{1,0:T(8,128)S(1)} %get-tuple-element.41), channel_id=1, source_target_pairs={{0,1},{1,0},{2,3},{3,2},{4,8},{5,9},{6,10},{7,11},{8,4},{9,5},{10,... | collective-permute-start | bytes 208904 | tf_op jit(solution)/shard_map/ppermute | solution.py:911
  17.7 1.6 %copy-start.1 = (s32[2,48]{1,0:T(2,128)S(1)}, s32[2,48]{1,0:T(2,128)}, u32[]{:S(2)}) copy-start(s32[2,48]{1,0:T(2,128)} %cells.1) | copy-start | bytes 1156
  21.9 1.2 %collective-permute-start.7 = (f32[40,128]{1,0:T(8,128)S(1)}, f32[40,128]{1,0:T(8,128)S(1)}, u32[]{:S(2)}, u32[]{:S(2)}) collective-permute-start(f32[40,128]{1,0:T(8,128)S(1)} %density.1), channel_id=1, source_target_pairs={{0,1},{1,0},{2,3},{3,2},{4,5},{5,4},{6,7},{7,6},{8,9},{9,8},{10,11... | collective-permute-start | bytes 61448 | tf_op jit(solution)/shard_map/ppermute | solution.py:788
  23.1 5.1 %collective-permute-start.10 = (f32[40,128]{1,0:T(8,128)S(1)}, f32[40,128]{1,0:T(8,128)S(1)}, u32[]{:S(2)}, u32[]{:S(2)}) collective-permute-start(f32[40,128]{1,0:T(8,128)S(1)} %add.21), channel_id=1, source_target_pairs={{0,12},{1,13},{2,14},{3,15},{4,8},{5,9},{6,10},{7,11},{8,4},{9,5},... | collective-permute-start | bytes 61448 | tf_op jit(solution)/shard_map/ppermute | solution.py:788
  26.4 3.8 %collective-permute-start.9 = (f32[40,128]{1,0:T(8,128)S(1)}, f32[40,128]{1,0:T(8,128)S(1)}, u32[]{:S(2)}, u32[]{:S(2)}) collective-permute-start(f32[40,128]{1,0:T(8,128)S(1)} %add.21), channel_id=1, source_target_pairs={{0,8},{1,9},{2,10},{3,11},{4,12},{5,13},{6,14},{7,15},{8,0},{9,1},... | collective-permute-start | bytes 61448 | tf_op jit(solution)/shard_map/ppermute | solution.py:788
  26.8 3.8 %collective-permute-start.8 = (f32[40,128]{1,0:T(8,128)S(1)}, f32[40,128]{1,0:T(8,128)S(1)}, u32[]{:S(2)}, u32[]{:S(2)}) collective-permute-start(f32[40,128]{1,0:T(8,128)S(1)} %add.21), channel_id=1, source_target_pairs={{0,4},{1,5},{2,6},{3,7},{4,0},{5,1},{6,2},{7,3},{8,12},{9,13},{10,... | collective-permute-start | bytes 61448 | tf_op jit(solution)/shard_map/ppermute | solution.py:788
  30.6 6.1 %collective-permute-start.13 = (f32[40,128]{1,0:T(8,128)S(1)}, f32[40,128]{1,0:T(8,128)S(1)}, u32[]{:S(2)}, u32[]{:S(2)}) collective-permute-start(f32[40,128]{1,0:T(8,128)S(1)} %add_add_fusion.1), channel_id=1, source_target_pairs={{0,18},{1,19},{2,16},{3,17},{4,22},{5,23},{6,20},{7,21},{8,26},{9,... | collective-permute-start | bytes 61448 | tf_op jit(solution)/shard_map/ppermute | solution.py:788
  35.0 4.7 %collective-permute-start.12 = (f32[40,128]{1,0:T(8,128)S(1)}, f32[40,128]{1,0:T(8,128)S(1)}, u32[]{:S(2)}, u32[]{:S(2)}) collective-permute-start(f32[40,128]{1,0:T(8,128)S(1)} %add_add_fusion.1), channel_id=1, source_target_pairs={{0,16},{1,17},{2,18},{3,19},{4,20},{5,21},{6,22},{7,23},{8,24},{9,... | collective-permute-start | bytes 61448 | tf_op jit(solution)/shard_map/ppermute | solution.py:788
  35.3 4.4 %collective-permute-start.11 = (f32[40,128]{1,0:T(8,128)S(1)}, f32[40,128]{1,0:T(8,128)S(1)}, u32[]{:S(2)}, u32[]{:S(2)}) collective-permute-start(f32[40,128]{1,0:T(8,128)S(1)} %add_add_fusion.1), channel_id=1, source_target_pairs={{0,2},{1,3},{2,0},{3,1},{4,6},{5,7},{6,4},{7,5},{8,10},{9,11},{10,... | collective-permute-start | bytes 61448 | tf_op jit(solution)/shard_map/ppermute | solution.py:788

commit v11 on v10

--- a/solution.py
+++ b/solution.py
@@ -356,17 +356,19 @@
         high, low = split(state[...])
         cut = n - TILE
         corner = [x[:cut, :cut] for x in (high, high, low)]
-        one = dot(wide[:, 2 * n :], jnp.concatenate(corner, axis=0), False)
+        corner = jnp.concatenate(corner, axis=0)
         last_high, last_low = (high[:, cut:], low[:, cut:])
         last = [
             jnp.concatenate([last_high, last_low], axis=1),
             jnp.concatenate([last_high, jnp.zeros_like(last_high)], axis=1),
         ]
-        two = dot(wide[:, : 2 * n], jnp.concatenate(last, axis=0), False)
-        both = jnp.concatenate([one, two[:, :TILE] + two[:, TILE:]], axis=1)
+        last = jnp.concatenate(last, axis=0)
         for number in range(4):
             rows = slice(number * n, (number + 1) * n)
-            value = jnp.sum(stack[rows, :] * both[rows], axis=1, keepdims=True) * member[...]
+            one = dot(wide[rows, 2 * n :], corner, False)
+            two = dot(wide[rows, : 2 * n], last, False)
+            both = jnp.concatenate([one, two[:, :TILE] + two[:, TILE:]], axis=1)
+            value = jnp.sum(stack[rows, :] * both, axis=1, keepdims=True) * member[...]
             fold[number : number + 1, :] += jnp.sum(value, axis=0, keepdims=True)
 
     plain = fold[...]

time: 41.3 us -> 41.2 us (level)
  no operation moved by 1% of the time
where the time goes in v11:
time: 41.2 us; the launch traced here: 41 us
  Pallas kernels  15.6 us (38%)
  starting transfers between devices  14.1 us (34%)
  waiting for transfers between devices  10.5 us (25%)
  between operations  0.79 us (2%)
    pallas_call x8, Pallas kernels, local_call(): pl.pallas_call(kernel, out_shape=shapes, in_specs=[pl.BlockSpec(memory_sp...  15.6 us
    ppermute x7, starting transfers between devices, total_over(): lax.ppermute(value, axis, [(i, i ^ k) for i in range(size)])  8.87 us
    ppermute x7, waiting for transfers between devices, total_over(): lax.ppermute(value, axis, [(i, i ^ k) for i in range(size)])  8.82 us
    ppermute x1, starting transfers between devices, on_device(): second = lax.ppermute(edge, 'slab', neighbour_turn(devices))  1.92 us
    ppermute x1, starting transfers between devices, on_device(): one_beside = lax.ppermute(one_side, 'energy', pairs_of(wires))  1.55 us
    ppermute x1, waiting for transfers between devices, on_device(): packed = lax.ppermute(passed, 'slab', hop(devices, 1))  1.32 us
    ppermute x1, starting transfers between devices, on_device(): packed = lax.ppermute(passed, 'slab', hop(devices, 1))  1.04 us
  transfers between devices with their start and end apart: 14, of which 8 were waited for; matrix products, arithmetic and copies ran while one was open for 0% of the time, Pallas kernels for 16%

profile of v11, /device:TPU:0, one launch (start us, length us, event | category | flops | bytes accessed | tf_op | source)
XLA Modules:
  0.0 41.0 jit_solution(5514179888852259600)
XLA Ops:
  0.6 5.9 %other.1 = (f32[384,384]{1,0:T(8,128)S(1)}, f32[800,384]{1,0:T(8,128)S(1)}, f32[48,128]{1,0:T(8,128)S(1)}, f32[384,384]{1,0:T(8,128)S(1)}, f32[384,384]{1,0:T(8,...) custom-call(f32[2,2,384,384]{3,2,1,0:T(8,128)} %iso.1, f32[2,384,384]{2,1,0:T(8,128)} %coupling.1, ...), custom_call_target="tpu_custom_call" | custom-call | flops 2717908992 | bytes 1048576 | tf_op jit(solution)/shard_map/other/pallas_call | solution.py:386
  6.6 0.1 collective-permute-start
  6.7 0.5 %collective-permute-start.1 = (f32[384,384]{1,0:T(8,128)S(1)}, f32[384,384]{1,0:T(8,128)S(1)}, u32[]{:S(2)}, u32[]{:S(2)}) collective-permute-start(f32[384,384]{1,0:T(8,128)S(1)} %get-tuple-element.31), channel_id=1, source_target_pairs={{0,1},{1,0},{2,3},{3,2},{4,5},{5,4},{6,7},{7,6},{8,9},{9,8},{10,11... | collective-permute-start | bytes 1769480 | tf_op jit(solution)/shard_map/ppermute | solution.py:887
  7.2 1.9 %collective-permute-start.2 = (f32[48,128]{1,0:T(8,128)S(1)}, f32[48,128]{1,0:T(8,128)S(1)}, u32[]{:S(2)}, u32[]{:S(2)}) collective-permute-start(f32[48,128]{1,0:T(8,128)S(1)} %get-tuple-element.25.planes), channel_id=1, source_target_pairs={{0,3},{1,2},{2,1},{3,0},{4,7},{5,6},{6,5},{7,4},{8,11},{9,10},{10,... | collective-permute-start | bytes 73736 | tf_op jit(solution)/shard_map/ppermute | solution.py:871
  9.1 0.0 copy-start
  9.1 2.4 %own.1 = f32[800,384]{1,0:T(8,128)S(1)} custom-call(f32[48,128]{1,0:T(8,128)S(1)} %get-tuple-element.25.planes, f32[384,384]{1,0:T(8,128)S(1)} %get-tuple-element.26.early.own_step, f32[384,384]{1,0:T(8,128)S(1)} %get-tuple-element.27.late, f32[2,384,384]{2,1,0:T(8,128)S(1)} %get-tuple-element.28.isos, f32[384,384]{1,0:T(8,128)S(1)} %get-tuple-element.29.lead), custom_call_target="tpu_custom_call" | custom-call | flops 2147483648 | bytes 1048576 | tf_op jit(solution)/shard_map/own/pallas_call | solution.py:386
  11.5 0.0 copy-start.5
  11.5 0.0 copy-start.4
  11.5 0.0 collective-permute-done.2.second
  11.5 0.0 collective-permute-done.1.got_step
  11.5 0.0 collective-permute-done.got
  11.5 0.0 copy-done
  11.5 1.5 %relay.1 = (f32[584,128]{1,0:T(8,128)S(1)}, f32[1536,384]{1,0:T(8,128)S(1)}, bf16[1536,1536]{1,0:T(8,128)(2,1)S(1)}, f32[26,8,128]{2,1,0:T(8,128)S(1)}, f32[8,12...) custom-call(f32[800,384]{1,0:T(8,128)S(1)} %own.1, f32[800,384]{1,0:T(8,128)S(1)} %collective-permute-done.got, ...), custom_call_target="tpu_custom_call" | custom-call | flops 679477248 | bytes 1048576 | tf_op jit(solution)/shard_map/relay/pallas_call | solution.py:386
  13.1 0.0 copy-start.2
  13.1 0.0 copy-start.3
  13.1 1.0 %collective-permute-start.4 = (f32[584,128]{1,0:T(8,128)S(1)}, f32[584,128]{1,0:T(8,128)S(1)}, u32[]{:S(2)}, u32[]{:S(2)}) collective-permute-start(f32[584,128]{1,0:T(8,128)S(1)} %get-tuple-element.34), channel_id=1, source_target_pairs={{0,2},{1,3},{2,0},{3,1},{4,6},{5,7},{6,4},{7,5},{8,10},{9,11},{10,... | collective-permute-start | bytes 897032 | tf_op jit(solution)/shard_map/ppermute | solution.py:911
  14.1 0.0 collective-permute-start.3
  14.1 0.0 copy-done.5
  14.1 1.6 %collective-permute-start.5 = (f32[136,128]{1,0:T(8,128)S(1)}, f32[136,128]{1,0:T(8,128)S(1)}, u32[]{:S(2)}, u32[]{:S(2)}) collective-permute-start(f32[136,128]{1,0:T(8,128)S(1)} %get-tuple-element.40), channel_id=1, source_target_pairs={{0,4},{4,0},{8,12},{12,8},{16,20},{20,16},{24,28},{28,24},{1,5},{5... | collective-permute-start | bytes 208904 | tf_op jit(solution)/shard_map/ppermute | solution.py:912
  15.7 0.2 collective-permute-start.6
  15.8 0.0 collective-permute-done.3.other_cells
  15.8 0.0 copy-done.4
  15.9 1.8 %atoms.1 = (f32[6,384,128]{2,1,0:T(8,128)S(1)}, bf16[480,512]{1,0:T(8,128)(2,1)S(1)}, f32[512,128]{1,0:T(8,128)S(1)}, f32[384,128]{1,0:T(8,128)S(1)}, f32[16,128]{1,0:T(8,128)S(1)}) custom-call(f32[1,4]{1,0:T(1,128)S(1)} %bitcast.5, s32[1,384]{1,0:T(1,128)S(1)} %reshape.17.orbital_atom, f32[8,128]{1,0:T(8,128)S(1)} %get-tuple-element.32.some_cells, ...), custom_call_target="tpu_custom_call" | custom-call | flops 536870912 | bytes 1048576 | tf_op jit(solution)/shard_map/atoms/pallas_call | solution.py:386
  17.7 0.0 copy-done.2
  17.7 0.0 copy-done.3
  17.7 0.0 copy-start.1
  17.7 1.2 %known.1 = (f32[8,128]{1,0:T(8,128)S(1)}, f32[32,128]{1,0:T(8,128)S(1)}) custom-call(f32[1,2]{1,0:T(1,128)S(1)} %bitcast.3, s32[1,2]{1,0:T(1,128)S(1)} %bitcast.4, s32[1,384]{1,0:T(1,128)S(1)} %reshape.17.orbital_atom, f32[384,128]{1,0:T(8,128)S(1)} %get-tuple-element.33.member, f32[800,384]{1,0:T(8,128)S(1)} %own.1, ...), custom_call_target="tpu_custom_call" | custom-call | flops 268435456 | bytes 1048576 | tf_op jit(solution)/shard_map/known/pallas_call | solution.py:386
  18.9 0.4 collective-permute-done.5.one_beside
  19.3 0.0 collective-permute-done.6.two_beside
  19.3 0.0 copy-done.1
  19.3 1.2 %moments.1 = (f32[24,128]{1,0:T(8,128)S(1)}, f32[20,24,128]{2,1,0:T(8,128)S(1)}) custom-call(f32[800,384]{1,0:T(8,128)S(1)} %own.1, f32[26,8,128]{2,1,0:T(8,128)S(1)} %get-tuple-element.39.field, f32[136,128]{1,0:T(8,128)S(1)} %collective-permute-done.5.one_beside, f32[136,128]{1,0:T(8,128)S(1)} %collective-permute-done.6.two_beside, s32[2,48]{1,0:T(2,128)S(1)} %copy-done.1), custom_call_target="tpu_custom_call" | custom-call | flops 67108864 | bytes 1048576 | tf_op jit(solution)/shard_map/moments/pallas_call | solution.py:386
  20.5 1.3 %collective-permute-done.4.packed = f32[584,128]{1,0:T(8,128)S(1)} collective-permute-done((f32[584,128]{1,0:T(8,128)S(1)}, f32[584,128]{1,0:T(8,128)S(1)}, u32[]{:S(2)}, u32[]{:S(2)}) %collective-permute-start.4) | collective-permute-done | bytes 299040 | tf_op jit(solution)/shard_map/ppermute | solution.py:911
  21.8 0.1 density.1
  21.9 0.0 collective-permute-start.7
  21.9 1.2 %collective-permute-done.7 = f32[40,128]{1,0:T(8,128)S(1)} collective-permute-done((f32[40,128]{1,0:T(8,128)S(1)}, f32[40,128]{1,0:T(8,128)S(1)}, u32[]{:S(2)}, u32[]{:S(2)}) %collective-permute-start.7) | collective-permute-done | bytes 20512 | tf_op jit(solution)/shard_map/ppermute | solution.py:790
  23.1 3.3 %collective-permute-start.10 = (f32[40,128]{1,0:T(8,128)S(1)}, f32[40,128]{1,0:T(8,128)S(1)}, u32[]{:S(2)}, u32[]{:S(2)}) collective-permute-start(f32[40,128]{1,0:T(8,128)S(1)} %add.21), channel_id=1, source_target_pairs={{0,12},{1,13},{2,14},{3,15},{4,8},{5,9},{6,10},{7,11},{8,4},{9,5},... | collective-permute-start | bytes 61448 | tf_op jit(solution)/shard_map/ppermute | solution.py:790
  26.4 0.4 %collective-permute-start.9 = (f32[40,128]{1,0:T(8,128)S(1)}, f32[40,128]{1,0:T(8,128)S(1)}, u32[]{:S(2)}, u32[]{:S(2)}) collective-permute-start(f32[40,128]{1,0:T(8,128)S(1)} %add.21), channel_id=1, source_target_pairs={{0,8},{1,9},{2,10},{3,11},{4,12},{5,13},{6,14},{7,15},{8,0},{9,1},... | collective-permute-start | bytes 61448 | tf_op jit(solution)/shard_map/ppermute | solution.py:790
  26.8 0.2 collective-permute-start.8
  27.0 1.1 %collective-permute-done.10 = f32[40,128]{1,0:T(8,128)S(1)} collective-permute-done((f32[40,128]{1,0:T(8,128)S(1)}, f32[40,128]{1,0:T(8,128)S(1)}, u32[]{:S(2)}, u32[]{:S(2)}) %collective-permute-start.10) | collective-permute-done | bytes 20512 | tf_op jit(solution)/shard_map/ppermute | solution.py:790
  28.2 2.0 %collective-permute-done.9 = f32[40,128]{1,0:T(8,128)S(1)} collective-permute-done((f32[40,128]{1,0:T(8,128)S(1)}, f32[40,128]{1,0:T(8,128)S(1)}, u32[]{:S(2)}, u32[]{:S(2)}) %collective-permute-start.9) | collective-permute-done | bytes 20512 | tf_op jit(solution)/shard_map/ppermute | solution.py:790
  30.2 0.4 %collective-permute-done.8 = f32[40,128]{1,0:T(8,128)S(1)} collective-permute-done((f32[40,128]{1,0:T(8,128)S(1)}, f32[40,128]{1,0:T(8,128)S(1)}, u32[]{:S(2)}, u32[]{:S(2)}) %collective-permute-start.8) | collective-permute-done | bytes 20512 | tf_op jit(solution)/shard_map/ppermute | solution.py:790
  30.6 4.2 %collective-permute-start.13 = (f32[40,128]{1,0:T(8,128)S(1)}, f32[40,128]{1,0:T(8,128)S(1)}, u32[]{:S(2)}, u32[]{:S(2)}) collective-permute-start(f32[40,128]{1,0:T(8,128)S(1)} %add_add_fusion.1), channel_id=1, source_target_pairs={{0,18},{1,19},{2,16},{3,17},{4,22},{5,23},{6,20},{7,21},{8,26},{9,... | collective-permute-start | bytes 61448 | tf_op jit(solution)/shard_map/ppermute | solution.py:790
  34.9 0.3 collective-permute-start.12
  35.2 0.3 collective-permute-start.11
  35.5 1.1 %collective-permute-done.13 = f32[40,128]{1,0:T(8,128)S(1)} collective-permute-done((f32[40,128]{1,0:T(8,128)S(1)}, f32[40,128]{1,0:T(8,128)S(1)}, u32[]{:S(2)}, u32[]{:S(2)}) %collective-permute-start.13) | collective-permute-done | bytes 20512 | tf_op jit(solution)/shard_map/ppermute | solution.py:790
  36.6 2.9 %collective-permute-done.12 = f32[40,128]{1,0:T(8,128)S(1)} collective-permute-done((f32[40,128]{1,0:T(8,128)S(1)}, f32[40,128]{1,0:T(8,128)S(1)}, u32[]{:S(2)}, u32[]{:S(2)}) %collective-permute-start.12) | collective-permute-done | bytes 20512 | tf_op jit(solution)/shard_map/ppermute | solution.py:790
  39.6 0.0 collective-permute-done.11
  39.6 1.4 %finish.1 = (f32[4,2,48]{2,1,0:T(2,128)}, f32[16,8,128]{2,1,0:T(8,128)}) custom-call(f32[40,128]{1,0:T(8,128)S(1)} %add_add_fusion.payload, f32[6,384,128]{2,1,0:T(8,128)S(1)} %get-tuple-element.43.walks, bf16[480,512]{1,0:T(8,128)(2,1)S(1)} %get-tuple-element.44.row_hot, f32[512,128]{1,0:T(8,128)S(1)} %get-tuple-element.45.deep_hot, ...), custom_call_target="tpu_custom_call" | custom-call | flops 536870912 | bytes 1048576 | tf_op jit(solution)/shard_map/finish/pallas_call | solution.py:386
  (4 shorter events, 0.0 us)
Async XLA Ops:
  6.6 4.9 %collective-permute-start = (f32[800,384]{1,0:T(8,128)S(1)}, f32[800,384]{1,0:T(8,128)S(1)}, u32[]{:S(2)}, u32[]{:S(2)}) collective-permute-start(f32[800,384]{1,0:T(8,128)S(1)} %get-tuple-element.30), channel_id=1, source_target_pairs={{0,1},{1,0},{2,3},{3,2},{4,5},{5,4},{6,7},{7,6},{8,9},{9,8},{10,11... | collective-permute-start | bytes 3686408 | tf_op jit(solution)/shard_map/ppermute | solution.py:870
  6.7 4.8 %collective-permute-start.1 = (f32[384,384]{1,0:T(8,128)S(1)}, f32[384,384]{1,0:T(8,128)S(1)}, u32[]{:S(2)}, u32[]{:S(2)}) collective-permute-start(f32[384,384]{1,0:T(8,128)S(1)} %get-tuple-element.31), channel_id=1, source_target_pairs={{0,1},{1,0},{2,3},{3,2},{4,5},{5,4},{6,7},{7,6},{8,9},{9,8},{10,11... | collective-permute-start | bytes 1769480 | tf_op jit(solution)/shard_map/ppermute | solution.py:887
  7.2 4.3 %collective-permute-start.2 = (f32[48,128]{1,0:T(8,128)S(1)}, f32[48,128]{1,0:T(8,128)S(1)}, u32[]{:S(2)}, u32[]{:S(2)}) collective-permute-start(f32[48,128]{1,0:T(8,128)S(1)} %get-tuple-element.25.planes), channel_id=1, source_target_pairs={{0,3},{1,2},{2,1},{3,0},{4,7},{5,6},{6,5},{7,4},{8,11},{9,10},{10,... | collective-permute-start | bytes 73736 | tf_op jit(solution)/shard_map/ppermute | solution.py:871
  9.1 2.4 %copy-start = (f32[16,8,128]{2,1,0:T(8,128)S(1)}, f32[16,8,128]{2,1,0:T(8,128)}, u32[]{:S(2)}) copy-start(f32[16,8,128]{2,1,0:T(8,128)} %field.1) | copy-start | bytes 196612
  11.5 2.7 %copy-start.5 = (s32[384]{0:T(512)S(1)}, s32[384]{0:T(512)}, u32[]{:S(2)}) copy-start(s32[384]{0:T(512)} %param.15) | copy-start | bytes 4612
  11.5 4.4 %copy-start.4 = (f32[4]{0:T(128)S(1)}, f32[4]{0:T(128)}, u32[]{:S(2)}) copy-start(f32[4]{0:T(128)} %param.14) | copy-start | bytes 52
  13.1 4.6 %copy-start.2 = (f32[2]{0:T(128)S(1)}, f32[2]{0:T(128)}, u32[]{:S(2)}) copy-start(f32[2]{0:T(128)} %param.12) | copy-start | bytes 28
  13.1 4.6 %copy-start.3 = (s32[2]{0:T(128)S(1)}, s32[2]{0:T(128)}, u32[]{:S(2)}) copy-start(s32[2]{0:T(128)} %param.13) | copy-start | bytes 28
  13.1 8.7 %collective-permute-start.4 = (f32[584,128]{1,0:T(8,128)S(1)}, f32[584,128]{1,0:T(8,128)S(1)}, u32[]{:S(2)}, u32[]{:S(2)}) collective-permute-start(f32[584,128]{1,0:T(8,128)S(1)} %get-tuple-element.34), channel_id=1, source_target_pairs={{0,2},{1,3},{2,0},{3,1},{4,6},{5,7},{6,4},{7,5},{8,10},{9,11},{10,... | collective-permute-start | bytes 897032 | tf_op jit(solution)/shard_map/ppermute | solution.py:911
  14.1 1.7 %collective-permute-start.3 = (f32[8,128]{1,0:T(8,128)S(1)}, f32[8,128]{1,0:T(8,128)S(1)}, u32[]{:S(2)}, u32[]{:S(2)}) collective-permute-start(f32[8,128]{1,0:T(8,128)S(1)} %get-tuple-element.32.some_cells), channel_id=1, source_target_pairs={{0,1},{1,0},{2,3},{3,2},{4,5},{5,4},{6,7},{7,6},{8,9},{9,8},{10,11... | collective-permute-start | bytes 12296 | tf_op jit(solution)/shard_map/ppermute | solution.py:914
  14.1 5.1 %collective-permute-start.5 = (f32[136,128]{1,0:T(8,128)S(1)}, f32[136,128]{1,0:T(8,128)S(1)}, u32[]{:S(2)}, u32[]{:S(2)}) collective-permute-start(f32[136,128]{1,0:T(8,128)S(1)} %get-tuple-element.40), channel_id=1, source_target_pairs={{0,4},{4,0},{8,12},{12,8},{16,20},{20,16},{24,28},{28,24},{1,5},{5... | collective-permute-start | bytes 208904 | tf_op jit(solution)/shard_map/ppermute | solution.py:912
  15.7 3.6 %collective-permute-start.6 = (f32[136,128]{1,0:T(8,128)S(1)}, f32[136,128]{1,0:T(8,128)S(1)}, u32[]{:S(2)}, u32[]{:S(2)}) collective-permute-start(f32[136,128]{1,0:T(8,128)S(1)} %get-tuple-element.41), channel_id=1, source_target_pairs={{0,1},{1,0},{2,3},{3,2},{4,8},{5,9},{6,10},{7,11},{8,4},{9,5},{10,... | collective-permute-start | bytes 208904 | tf_op jit(solution)/shard_map/ppermute | solution.py:913
  17.7 1.6 %copy-start.1 = (s32[2,48]{1,0:T(2,128)S(1)}, s32[2,48]{1,0:T(2,128)}, u32[]{:S(2)}) copy-start(s32[2,48]{1,0:T(2,128)} %cells.1) | copy-start | bytes 1156
  21.9 1.2 %collective-permute-start.7 = (f32[40,128]{1,0:T(8,128)S(1)}, f32[40,128]{1,0:T(8,128)S(1)}, u32[]{:S(2)}, u32[]{:S(2)}) collective-permute-start(f32[40,128]{1,0:T(8,128)S(1)} %density.1), channel_id=1, source_target_pairs={{0,1},{1,0},{2,3},{3,2},{4,5},{5,4},{6,7},{7,6},{8,9},{9,8},{10,11... | collective-permute-start | bytes 61448 | tf_op jit(solution)/shard_map/ppermute | solution.py:790
  23.1 5.1 %collective-permute-start.10 = (f32[40,128]{1,0:T(8,128)S(1)}, f32[40,128]{1,0:T(8,128)S(1)}, u32[]{:S(2)}, u32[]{:S(2)}) collective-permute-start(f32[40,128]{1,0:T(8,128)S(1)} %add.21), channel_id=1, source_target_pairs={{0,12},{1,13},{2,14},{3,15},{4,8},{5,9},{6,10},{7,11},{8,4},{9,5},... | collective-permute-start | bytes 61448 | tf_op jit(solution)/shard_map/ppermute | solution.py:790
  26.4 3.8 %collective-permute-start.9 = (f32[40,128]{1,0:T(8,128)S(1)}, f32[40,128]{1,0:T(8,128)S(1)}, u32[]{:S(2)}, u32[]{:S(2)}) collective-permute-start(f32[40,128]{1,0:T(8,128)S(1)} %add.21), channel_id=1, source_target_pairs={{0,8},{1,9},{2,10},{3,11},{4,12},{5,13},{6,14},{7,15},{8,0},{9,1},... | collective-permute-start | bytes 61448 | tf_op jit(solution)/shard_map/ppermute | solution.py:790
  26.8 3.8 %collective-permute-start.8 = (f32[40,128]{1,0:T(8,128)S(1)}, f32[40,128]{1,0:T(8,128)S(1)}, u32[]{:S(2)}, u32[]{:S(2)}) collective-permute-start(f32[40,128]{1,0:T(8,128)S(1)} %add.21), channel_id=1, source_target_pairs={{0,4},{1,5},{2,6},{3,7},{4,0},{5,1},{6,2},{7,3},{8,12},{9,13},{10,... | collective-permute-start | bytes 61448 | tf_op jit(solution)/shard_map/ppermute | solution.py:790
  30.6 6.0 %collective-permute-start.13 = (f32[40,128]{1,0:T(8,128)S(1)}, f32[40,128]{1,0:T(8,128)S(1)}, u32[]{:S(2)}, u32[]{:S(2)}) collective-permute-start(f32[40,128]{1,0:T(8,128)S(1)} %add_add_fusion.1), channel_id=1, source_target_pairs={{0,18},{1,19},{2,16},{3,17},{4,22},{5,23},{6,20},{7,21},{8,26},{9,... | collective-permute-start | bytes 61448 | tf_op jit(solution)/shard_map/ppermute | solution.py:790
  34.9 4.7 %collective-permute-start.12 = (f32[40,128]{1,0:T(8,128)S(1)}, f32[40,128]{1,0:T(8,128)S(1)}, u32[]{:S(2)}, u32[]{:S(2)}) collective-permute-start(f32[40,128]{1,0:T(8,128)S(1)} %add_add_fusion.1), channel_id=1, source_target_pairs={{0,16},{1,17},{2,18},{3,19},{4,20},{5,21},{6,22},{7,23},{8,24},{9,... | collective-permute-start | bytes 61448 | tf_op jit(solution)/shard_map/ppermute | solution.py:790
  35.2 4.4 %collective-permute-start.11 = (f32[40,128]{1,0:T(8,128)S(1)}, f32[40,128]{1,0:T(8,128)S(1)}, u32[]{:S(2)}, u32[]{:S(2)}) collective-permute-start(f32[40,128]{1,0:T(8,128)S(1)} %add_add_fusion.1), channel_id=1, source_target_pairs={{0,2},{1,3},{2,0},{3,1},{4,6},{5,7},{6,4},{7,5},{8,10},{9,11},{10,... | collective-permute-start | bytes 61448 | tf_op jit(solution)/shard_map/ppermute | solution.py:790
